TPU v7x, 32 devices: a whole 2x2x4 slice. The times are simulated.
32 devices in a mesh: dp: 8 (over z, x), chan: 4 (over y, core).
Axes of the slice: x: 2, y: 2, z: 4, core: 2. Of those that a mesh axis runs over, the one named last changes fastest.
Arguments:
- inputs: bfloat16 [64, 128, 512], P(('dp', 'chan')), may hold values from -6 to 6
- cotangent: bfloat16 [64, 128, 512], P(('dp', 'chan')), may hold values from -6 to 6
- expand_w: bfloat16 [512, 2048], P(None, 'chan'), may hold values from -0.25 to 0.25
- expand_b: float32 [2048], P('chan'), may hold values from -3 to 3
- depth_k: float32 [25, 2048], P(None, 'chan'), may hold values from -1.25 to 1.25
- depth_b: float32 [2048], P('chan'), may hold values from -3 to 3
- project_w: bfloat16 [2048, 512], P('chan'), may hold values from -0.125 to 0.125
Outputs:
- input_grad: bfloat16 [64, 128, 512], P(('dp', 'chan'))
- expand_w_grad: float32 [512, 2048], P(None, 'chan')
- expand_b_grad: float32 [2048], P('chan')
- depth_k_grad: float32 [25, 2048], P(None, 'chan')
- depth_b_grad: float32 [2048], P('chan')
- project_w_grad: float32 [2048, 512], P('chan')
All inputs are finite; a program needn't handle non-finite values.
Results may differ from a plain program's by a relative error of at most 0.007.
Values may be sent and summed in bfloat16 or wider, within the bound.
No kernel may reach another device: no remote copies, remote signals or barrier semaphores. Data moves between devices by JAX's collectives and lax.ppermute only.
A program may use at most 64 MiB of HBM per device.

v0:
```python
import jax
import jax.numpy as jnp
from jax import lax
from jax.sharding import PartitionSpec as P


def extended(block, sides, width):
    for axis, dim in sides:
        count = lax.axis_size(axis)
        forward = [(i, i + 1) for i in range(count - 1)]
        backward = [(target, source) for source, target in forward]
        low = lax.ppermute(
            lax.slice_in_dim(block, block.shape[dim] - width, None, axis=dim), axis, forward
        )
        high = lax.ppermute(lax.slice_in_dim(block, 0, width, axis=dim), axis, backward)
        block = jnp.concatenate([low, block, high], axis=dim)
    return block


def gelu_parts(pre):
    cdf = 0.5 * (1.0 + lax.erf(pre * 0.7071067811865476))
    dens = jnp.exp(-0.5 * pre * pre) * 0.3989422804014327
    return (pre * cdf, cdf + pre * dens)


def shards(inputs, cotangent, expand_w, expand_b, depth_k, depth_b, project_w):
    rows_in, rows_cot = (
        lax.all_gather(inputs, "chan", axis=0, tiled=True),
        lax.all_gather(cotangent, "chan", axis=0, tiled=True),
    )
    nrows, ncols, cin = rows_in.shape
    hslice = expand_w.shape[1]
    flat_inputs = rows_in.reshape(nrows * ncols, cin)
    flat_cotan = rows_cot.reshape(nrows * ncols, cin)
    pre_one = (
        jnp.dot(flat_inputs, expand_w, preferred_element_type=jnp.float32).reshape(
            nrows, ncols, hslice
        )
        + expand_b
    )
    hidden, slope_one = gelu_parts(pre_one)
    hidden = hidden.astype(jnp.bfloat16)
    rimmed = extended(hidden, (("dp", 0),), 2)
    padded = jnp.pad(rimmed, ((0, 0), (2, 2), (0, 0))).astype(jnp.float32)
    pre_two = jnp.zeros((nrows, ncols, hslice), jnp.float32) + depth_b
    for row_tap in range(5):
        for col_tap in range(5):
            pre_two = (
                pre_two
                + depth_k[5 * row_tap + col_tap]
                * padded[row_tap : row_tap + nrows, col_tap : col_tap + ncols]
            )
    mixed, slope_two = gelu_parts(pre_two)
    mixed = mixed.astype(jnp.bfloat16).reshape(nrows * ncols, hslice)
    grad_w2 = jnp.dot(mixed.T, flat_cotan, preferred_element_type=jnp.float32)
    grad_mixed = jnp.dot(flat_cotan, project_w.T, preferred_element_type=jnp.float32).reshape(
        nrows, ncols, hslice
    )
    grad_pre = (grad_mixed * slope_two).astype(jnp.bfloat16)
    grad_pre_f = grad_pre.astype(jnp.float32)
    grad_bd = jnp.sum(grad_pre_f, axis=(0, 1))
    grad_rimmed = extended(grad_pre, (("dp", 0),), 2)
    grad_pad = jnp.pad(grad_rimmed, ((0, 0), (2, 2), (0, 0))).astype(jnp.float32)
    taps = []
    grad_hidden = jnp.zeros((nrows, ncols, hslice), jnp.float32)
    for row_tap in range(5):
        for col_tap in range(5):
            taps.append(
                jnp.sum(
                    padded[row_tap : row_tap + nrows, col_tap : col_tap + ncols] * grad_pre_f,
                    axis=(0, 1),
                )
            )
            grad_hidden = (
                grad_hidden
                + depth_k[5 * row_tap + col_tap]
                * grad_pad[4 - row_tap : 4 - row_tap + nrows, 4 - col_tap : 4 - col_tap + ncols]
            )
    grad_k = jnp.stack(taps, axis=0)
    grad_act = (grad_hidden * slope_one).astype(jnp.bfloat16)
    flat_act = grad_act.reshape(nrows * ncols, hslice)
    grad_b1 = jnp.sum(flat_act.astype(jnp.float32), axis=0)
    grad_w1 = jnp.dot(flat_inputs.T, flat_act, preferred_element_type=jnp.float32)
    summed = lax.psum((grad_w1, grad_b1, grad_k, grad_bd, grad_w2), "dp")
    own_part = lax.psum_scatter(
        jnp.einsum("rwh,ch->rwc", grad_act, expand_w, preferred_element_type=jnp.float32),
        "chan",
        scatter_dimension=0,
        tiled=True,
    )
    input_grad = (cotangent.astype(jnp.float32) + own_part).astype(jnp.bfloat16)
    return (input_grad, summed[0], summed[1], summed[2], summed[3], summed[4])


def solution(mesh):
    in_specs = (
        P(("dp", "chan"), None, None),
        P(("dp", "chan"), None, None),
        P(None, "chan"),
        P("chan"),
        P(None, "chan"),
        P("chan"),
        P("chan", None),
    )
    out_specs = (
        P(("dp", "chan"), None, None),
        P(None, "chan"),
        P("chan"),
        P(None, "chan"),
        P("chan"),
        P("chan", None),
    )
    return jax.shard_map(shards, mesh=mesh, in_specs=in_specs, out_specs=out_specs, check_vma=False)
```

profile of v0, /device:TPU:0, one launch (start us, length us, event | category | flops | bytes accessed | tf_op | source)
XLA Modules:
  0.0 259.4 jit_solution(5204955824896270988)
XLA Ops:
  7.2 0.0 copy-start
  7.2 0.0 all-gather.5.cloned.1.call-start
  7.2 0.7 all-gather.5.cloned.1.call-update
  7.9 0.0 all-gather.3.cloned.1.call-start
  8.0 0.7 all-gather.3.cloned.1.call-update
  8.7 0.0 copy-start.5
  8.7 0.0 all-reduce.6.cloned.1.call-start
  8.7 20.3 %all-gather.5.cloned.1.call-done = bf16[8,128,512]{2,1,0:T(8,128)(2,1)} async-done(((bf16[2,128,512]{2,1,0:T(8,128)(2,1)}), bf16[8,128,512]{2,1,0:T(8,128)(2,1)}) %all-gather.5.cloned.1.call-update) | async-done | bytes 1048592 | tf_op jit(solution)/shard_map/all_gather | solution.py:28
  29.0 0.0 copy-done
  29.0 3.4 %multiply_convert_fusion.1 = (bf16[8,128,512]{2,1,0:T(8,128)(2,1)S(1)}, f32[8,128,512]{2,1,0:T(8,128)}) fusion(f32[512]{0:T(512)} %param.10, bf16[8,128,512]{2,1,0:T(8,128)(2,1)} %all-gather.5.cloned.1.call-done, bf16[512,512]{1,0:T(8,128)(2,1)S(1)} %copy-done), kind=kOutput, calls=%fused_computation.121 | convolution fusion | flops 540016640 | bytes 4720640 | tf_op jit(solution)/shard_map/dot_general | solution.py:36
  32.5 3.4 %collective-permute-start = (bf16[2,128,512]{2,1,0:T(8,128)(2,1)S(1)}, bf16[2,128,512]{2,1,0:T(8,128)(2,1)S(1)}, u32[]{:S(2)}, u32[]{:S(2)}) collective-permute-start(bf16[2,128,512]{2,1,0:T(8,128)(2,1)S(1)} %get-tuple-element.53), channel_id=1, source_target_pairs={{0,4},{4,8},{8,12},{12,16},{16,20},{20,24},{24,28},{1,5},{5,9},{9,... | collective-permute-start | bytes 786440 | tf_op jit(solution)/shard_map/ppermute | solution.py:12
  35.9 1.3 collective-permute-start.1
  37.2 0.0 copy-done.5
  37.2 0.0 copy-start.6
  37.2 10.2 %collective-permute-done = bf16[2,128,512]{2,1,0:T(8,128)(2,1)S(1)} collective-permute-done((bf16[2,128,512]{2,1,0:T(8,128)(2,1)S(1)}, bf16[2,128,512]{2,1,0:T(8,128)(2,1)S(1)}, u32[]{:S(2)}, u32[]{:S(2)}) %collective-permute-start) | collective-permute-done | bytes 262176 | tf_op jit(solution)/shard_map/ppermute | solution.py:12
  47.4 0.0 collective-permute-done.1
  47.4 2.2 fusion.68
  49.6 0.0 copy-done.6
  49.6 27.2 %multiply_add_fusion = f32[8,128,512]{2,1,0:T(8,128)} fusion(f32[12,132,512]{2,1,0:T(8,128)} %fusion.68, f32[512]{0:T(512)S(1)} %bitcast.82, f32[512]{0:T(512)S(1)} %bitcast.84, f32[512]{0:T(512)S(1)} %bitcast.88, f32[512]{0:T(512)S(1)} %bitcast.90, f32[512]{0:T(512)S(1)} %bitcast.92, f32[512]{0:T(512)S(1)} %bitcast.94, f32[512]{0:T(512)S(1)} %bitcast.96, ...), kind=kLoop, calls=%fused_computation.120 | loop fusion | flops 26214400 | bytes 54579200 | tf_op jit(solution)/shard_map/add | solution.py:49
  76.8 0.0 all-gather.3.cloned.1.call-done
  76.8 0.0 copy-done.10
  76.8 0.0 copy-start.2
  76.9 0.0 copy-start.9
  76.9 8.8 %fusion.36 = (f32[512]{0:T(512)S(1)}, f32[512]{0:T(512)S(1)}, f32[512]{0:T(512)S(1)}, f32[512]{0:T(512)S(1)}, f32[512]{0:T(512)S(1)}, /*index=5*/f32[512]{0:T(51...) fusion(f32[12,132,512]{2,1,0:T(8,128)} %fusion.68, f32[8,128,512]{2,1,0:T(8,128)} %multiply_add_fusion, ...), kind=kOutput, calls=%fused_computation.66 | convolution fusion | flops 550498304 | bytes 19415040 | tf_op jit(solution)/shard_map/dot_general | solution.py:56
  85.7 4.4 %collective-permute-start.2 = (bf16[2,128,512]{2,1,0:T(8,128)(2,1)S(1)}, bf16[2,128,512]{2,1,0:T(8,128)(2,1)S(1)}, u32[]{:S(2)}, u32[]{:S(2)}) collective-permute-start(bf16[2,128,512]{2,1,0:T(8,128)(2,1)S(1)} %get-tuple-element.51), channel_id=1, source_target_pairs={{0,4},{4,8},{8,12},{12,16},{16,20},{20,24},{24,28},{1,5},{5,9},{9,... | collective-permute-start | bytes 786440 | tf_op jit(solution)/shard_map/ppermute | solution.py:12
  90.1 1.3 collective-permute-start.3
  91.4 0.0 copy-done.2
  91.4 0.0 copy-done.9
  91.4 1.7 convolution_bitcast_fusion
  93.2 2.2 collective-permute-done.2
  95.4 5.3 %collective-permute-done.3 = bf16[2,128,512]{2,1,0:T(8,128)(2,1)S(1)} collective-permute-done((bf16[2,128,512]{2,1,0:T(8,128)(2,1)S(1)}, bf16[2,128,512]{2,1,0:T(8,128)(2,1)S(1)}, u32[]{:S(2)}, u32[]{:S(2)}) %collective-permute-start.3) | collective-permute-done | bytes 262176 | tf_op jit(solution)/shard_map/ppermute | solution.py:15
  100.6 0.5 fusion.62
  101.2 7.3 %convert_reduce_fusion.1 = (f32[512]{0:T(512)S(1)}, bf16[8,128,512]{2,1,0:T(8,128)(2,1)S(1)}) fusion(f32[8,128,512]{2,1,0:T(8,128)S(1)} %copy-done.1, f32[512]{0:T(512)S(1)} %copy-done.7, f32[12,132,512]{2,1,0:T(8,128)S(1)} %fusion.62, f32[512]{0:T(512)S(1)} %bitcast.83, f32[512]{0:T(512)S(1)} %bitcast.85, f32[512]{0:T(512)S(1)} %bitcast.89, ...), kind=kLoop, calls=%fused_computation.118 | loop fusion | flops 32505344 | bytes 55629824 | tf_op jit(solution)/shard_map/reduce_sum | solution.py:82
  108.4 1.7 convolution_bitcast_fusion.1
  110.2 0.0 all-reduce.6.cloned.1.call-update
  110.2 0.2 reduce-scatter.2.cloned.1.call-start
  110.4 2.1 fusion.69
  112.5 0.0 reduce-scatter.2.cloned.1.call-update
  112.5 18.6 %fusion.37 = (f32[512]{0:T(512)S(1)}, f32[512]{0:T(512)S(1)}, f32[512]{0:T(512)S(1)}, f32[512]{0:T(512)S(1)}, f32[512]{0:T(512)S(1)}, /*index=5*/f32[512]{0:T(51...) fusion(bf16[8,128,512]{2,1,0:T(8,128)(2,1)S(1)} %get-tuple-elem, ...), kind=kLoop, calls=%fused_computation.67 | loop fusion | flops 19389440 | bytes 38834176 | tf_op jit(solution)/shard_map/reduce_sum | solution.py:69
  131.2 0.0 copy-start.4
  131.2 0.1 stack.103
  131.3 40.9 %all-reduce.2 = (f32[512]{0:T(512)}, f32[25,512]{1,0:T(8,128)}, f32[512]{0:T(512)}) all-reduce(f32[512]{0:T(512)S(1)} %get-tuple-element.49, f32[25,512]{1,0:T(8,128)S(1)} %stack.103, f32[512]{0:T(512)S(1)} %get-tuple-element.43), channel_id=1, replica_groups=mesh['dp'=8,'chan'=4] {'dp'}, use_global_device_ids=true, to_apply=%region_3.4 | all-reduce | flops 13824 | bytes 110592 | tf_op jit(solution)/shard_map/psum | solution.py:84
  172.2 44.2 %all-reduce.6.cloned.1.call-done = (f32[512,512]{0,1:T(8,128)}, f32[512,512]{1,0:T(8,128)}) async-done(((f32[512,512]{0,1:T(8,128)}, f32[512,512]{1,0:T(8,128)}), (f32[512,512]{0,1:T(8,128)}, f32[512,512]{1,0:T(8,128)})) %all-reduce.6.cloned.1.call-update) | async-done | bytes 2097168 | tf_op jit(solution)/shard_map/psum | solution.py:84
  216.5 2.6 %copy.18 = f32[512,512]{1,0:T(8,128)} copy(f32[512,512]{0,1:T(8,128)} %get-tuple-element.47) | data formatting | bytes 2097152
  219.1 31.0 %reduce-scatter.2.cloned.1.call-done = f32[2,128,512]{2,1,0:T(8,128)} async-done(((f32[8,128,512]{2,1,0:T(8,128)}), f32[2,128,512]{2,1,0:T(8,128)}) %reduce-scatter.2.cloned.1.call-update) | async-done | bytes 524304 | tf_op jit(solution)/shard_map/reduce_scatter | solution.py:85
  250.0 0.0 copy-done.4
  250.0 1.8 add_convert_fusion
  251.9 1.0 copy.23
  (13 shorter events, 0.1 us)
Async XLA Ops:
  7.2 21.9 %copy-start = (bf16[512,512]{1,0:T(8,128)(2,1)S(1)}, bf16[512,512]{1,0:T(8,128)(2,1)}, u32[]{:S(2)}) copy-start(bf16[512,512]{1,0:T(8,128)(2,1)} %param.9) | copy-start | bytes 1572868
  7.2 21.9 %all-gather.5.cloned.1.call-start = ((), (), s32[]{:S(2)}) async-start(), calls=%async_computation.2 | async-start | bytes 1310720 | tf_op jit(solution)/shard_map/all_gather | solution.py:28
  7.9 68.9 %all-gather.3.cloned.1.call-start = ((), (), s32[]{:S(2)}) async-start(), calls=%async_computation.1 | async-start | bytes 1310720 | tf_op jit(solution)/shard_map/all_gather | solution.py:29
  8.7 28.5 %copy-start.5 = (f32[25,512]{1,0:T(8,128)S(1)}, f32[25,512]{1,0:T(8,128)}, u32[]{:S(2)}) copy-start(f32[25,512]{1,0:T(8,128)} %param.11) | copy-start | bytes 153604
  8.7 207.8 %all-reduce.6.cloned.1.call-start = ((), (), s32[]{:S(2)}) async-start(), calls=%async_computation.4 | async-start | bytes 4194304 | tf_op jit(solution)/shard_map/psum | solution.py:84
  32.5 14.9 %collective-permute-start = (bf16[2,128,512]{2,1,0:T(8,128)(2,1)S(1)}, bf16[2,128,512]{2,1,0:T(8,128)(2,1)S(1)}, u32[]{:S(2)}, u32[]{:S(2)}) collective-permute-start(bf16[2,128,512]{2,1,0:T(8,128)(2,1)S(1)} %get-tuple-element.53), channel_id=1, source_target_pairs={{0,4},{4,8},{8,12},{12,16},{16,20},{20,24},{24,28},{1,5},{5,9},{9,... | collective-permute-start | bytes 786440 | tf_op jit(solution)/shard_map/ppermute | solution.py:12
  35.9 11.6 %collective-permute-start.1 = (bf16[2,128,512]{2,1,0:T(8,128)(2,1)S(1)}, bf16[2,128,512]{2,1,0:T(8,128)(2,1)S(1)}, u32[]{:S(2)}, u32[]{:S(2)}) collective-permute-start(bf16[2,128,512]{2,1,0:T(8,128)(2,1)S(1)} %get-tuple-element.54), channel_id=1, source_target_pairs={{4,0},{8,4},{12,8},{16,12},{20,16},{24,20},{28,24},{5,1},{9,5},{13... | collective-permute-start | bytes 786440 | tf_op jit(solution)/shard_map/ppermute | solution.py:15
  37.2 12.4 %copy-start.6 = (f32[512]{0:T(512)S(1)}, f32[512]{0:T(512)}, u32[]{:S(2)}) copy-start(f32[512]{0:T(512)} %param.12) | copy-start | bytes 6148
  49.6 27.2 %copy-start.10 = (bf16[512,512]{1,0:T(8,128)(2,1)S(1)}, bf16[512,512]{1,0:T(8,128)(2,1)}, u32[]{:S(2)}) copy-start(bf16[512,512]{1,0:T(8,128)(2,1)} %param.13) | copy-start | bytes 1572868
  76.8 14.6 %copy-start.2 = (f32[8,128,512]{2,1,0:T(8,128)S(1)}, f32[8,128,512]{2,1,0:T(8,128)}, u32[]{:S(2)}) copy-start(f32[8,128,512]{2,1,0:T(8,128)} %multiply_add_fusion) | copy-start | bytes 6291460
  76.9 14.6 %copy-start.9 = (bf16[8,128,512]{2,1,0:T(8,128)(2,1)S(1)}, bf16[8,128,512]{2,1,0:T(8,128)(2,1)}, u32[]{:S(2)}) copy-start(bf16[8,128,512]{2,1,0:T(8,128)(2,1)} %all-gather.3.cloned.1.call-done) | copy-start | bytes 3145732
  85.7 9.6 %collective-permute-start.2 = (bf16[2,128,512]{2,1,0:T(8,128)(2,1)S(1)}, bf16[2,128,512]{2,1,0:T(8,128)(2,1)S(1)}, u32[]{:S(2)}, u32[]{:S(2)}) collective-permute-start(bf16[2,128,512]{2,1,0:T(8,128)(2,1)S(1)} %get-tuple-element.51), channel_id=1, source_target_pairs={{0,4},{4,8},{8,12},{12,16},{16,20},{20,24},{24,28},{1,5},{5,9},{9,... | collective-permute-start | bytes 786440 | tf_op jit(solution)/shard_map/ppermute | solution.py:12
  90.1 10.5 %collective-permute-start.3 = (bf16[2,128,512]{2,1,0:T(8,128)(2,1)S(1)}, bf16[2,128,512]{2,1,0:T(8,128)(2,1)S(1)}, u32[]{:S(2)}, u32[]{:S(2)}) collective-permute-start(bf16[2,128,512]{2,1,0:T(8,128)(2,1)S(1)} %get-tuple-element.52), channel_id=1, source_target_pairs={{4,0},{8,4},{12,8},{16,12},{20,16},{24,20},{28,24},{5,1},{9,5},{13... | collective-permute-start | bytes 786440 | tf_op jit(solution)/shard_map/ppermute | solution.py:15
  93.2 7.9 %copy-start.1 = (f32[8,128,512]{2,1,0:T(8,128)S(1)}, f32[8,128,512]{2,1,0:T(8,128)}, u32[]{:S(2)}) copy-start(f32[8,128,512]{2,1,0:T(8,128)} %get-tuple-element.81) | copy-start | bytes 6291460
  93.2 8.0 %copy-start.7 = (f32[512]{0:T(512)S(1)}, f32[512]{0:T(512)}, u32[]{:S(2)}) copy-start(f32[512]{0:T(512)} %param.10) | copy-start | bytes 6148
  101.1 7.3 %copy-start.8 = (bf16[8,128,512]{2,1,0:T(8,128)(2,1)S(1)}, bf16[8,128,512]{2,1,0:T(8,128)(2,1)}, u32[]{:S(2)}) copy-start(bf16[8,128,512]{2,1,0:T(8,128)(2,1)} %all-gather.5.cloned.1.call-done) | copy-start | bytes 3145732
  110.2 139.9 %reduce-scatter.2.cloned.1.call-start = ((), (), s32[]{:S(2)}) async-start(), calls=%async_computation.3 | async-start | bytes 2621440 | tf_op jit(solution)/shard_map/reduce_scatter | solution.py:85
  131.2 118.9 %copy-start.4 = (bf16[2,128,512]{2,1,0:T(8,128)(2,1)S(1)}, bf16[2,128,512]{2,1,0:T(8,128)(2,1)}, u32[]{:S(2)}) copy-start(bf16[2,128,512]{2,1,0:T(8,128)(2,1)} %param.8) | copy-start | bytes 786436
  216.5 35.4 %copy-start.3 = (f32[512,512]{1,0:T(8,128)S(1)}, f32[512,512]{1,0:T(8,128)}, u32[]{:S(2)}) copy-start(f32[512,512]{1,0:T(8,128)} %get-tuple-element.88) | copy-start | bytes 3145732
Sparse Core Ops, SparseCore 0:
  9.6 19.4 all-gather.4
  30.6 16.7 all-gather.2
  110.3 106.1 all-reduce.5
  218.8 31.1 reduce-scatter.1
where the time goes:
time: 260 us; the launch traced here: 259 us
  waiting for transfers between devices  115 us (44%)
  other arithmetic  57.6 us (22%)
  blocking collectives  40.9 us (16%)
  matrix products  17.7 us (7%)
  between operations  14 us (5%)
  starting transfers between devices  10.7 us (4%)
  local copies, waits for them, and re-layouts  3.89 us (1%)
    psum x1, waiting for transfers between devices, shards(): summed = lax.psum((grad_w1, grad_b1, grad_k, grad_bd, grad_w2), 'dp')  44.2 us
    psum x1, blocking collectives, shards(): summed = lax.psum((grad_w1, grad_b1, grad_k, grad_bd, grad_w2), 'dp')  40.9 us
    reduce_scatter x1, waiting for transfers between devices, shards(): lax.psum_scatter(jnp.einsum('rwh,ch->rwc', grad_act, expand_w, preferred_...  31 us
    add x1, other arithmetic, shards(): pre_two + depth_k[5 * row_tap + col_tap] * padded[row_tap:row_tap + nrows...  27.2 us
    all_gather x1, waiting for transfers between devices, shards(): lax.all_gather(inputs, 'chan', axis=0, tiled=True)  20.3 us
    reduce_sum x1, other arithmetic, shards(): jnp.sum(padded[row_tap:row_tap + nrows, col_tap:col_tap + ncols] * grad_p...  18.6 us
    ppermute x2, waiting for transfers between devices, extended(): lax.ppermute(lax.slice_in_dim(block, block.shape[dim] - width, None, axis...  12.3 us
    dot_general x1, matrix products, shards(): jnp.dot(flat_cotan, project_w.T, preferred_element_type=jnp.float32)  8.8 us
  transfers between devices with their start and end apart: 8, of which 6 were waited for; matrix products, arithmetic and copies ran while one was open for 22% of the time, Pallas kernels for 0%

commit v1 on v0

v1 whole, which is shorter than its diff:
```python
import jax
import jax.numpy as jnp
from jax import lax
from jax.experimental import pallas as pl
from jax.experimental.pallas import tpu as pltpu
from jax.sharding import PartitionSpec as P

BF = jnp.bfloat16
F32 = jnp.float32
AXES = ("dp", "chan")
VMEM = pl.BlockSpec(memory_space=pltpu.VMEM)
SMEM = pl.BlockSpec(memory_space=pltpu.SMEM)
EDGE = 8


def params():
    return pltpu.CompilerParams(vmem_limit_bytes=48 * 1024 * 1024)


def cost(flops, nbytes, trans=0):
    return pl.CostEstimate(flops=flops, bytes_accessed=nbytes, transcendentals=trans)


def gelu_parts(pre):
    cdf = 0.5 * (1.0 + lax.erf(pre * 0.7071067811865476))
    dens = jnp.exp(-0.5 * pre * pre) * 0.3989422804014327
    return pre * cdf, cdf + pre * dens


def hop(value, dp_xor, chan_xor):
    ndp, nchan = lax.axis_size("dp"), lax.axis_size("chan")
    pairs = [
        (d * nchan + c, (d ^ dp_xor) * nchan + (c ^ chan_xor))
        for d in range(ndp)
        for c in range(nchan)
    ]
    return lax.ppermute(value, AXES, pairs)


def shift(value, step):
    ndp, nchan = lax.axis_size("dp"), lax.axis_size("chan")
    pairs = [
        (d * nchan + c, (d + step) * nchan + c)
        for d in range(ndp)
        if 0 <= d + step < ndp
        for c in range(nchan)
    ]
    return lax.ppermute(value, AXES, pairs)


def gathered(block):
    across, beside, corner = hop(block, 1, 0), hop(block, 0, 2), hop(block, 1, 2)
    near = {0: block, 2: beside, 4: across, 6: corner}
    return [near[k] if k in near else hop(near[k - 1], 0, 1) for k in range(8)]


def scattered(chunks, zpos, groups):
    own = lax.dynamic_index_in_dim(chunks, zpos, 0, keepdims=False).astype(F32)
    for k in range(1, groups):
        part = lax.dynamic_index_in_dim(chunks, zpos ^ k, 0, keepdims=False)
        own = own + hop(part.astype(BF), 2 * k, 0).astype(F32)
    return own.astype(BF)


def spread(chunk, groups):
    return [[hop(chunk, 2 * k + m, 0) if k + m else chunk for m in range(2)] for k in range(groups)]


def expand_kernel(me, *refs):
    pieces, (w, b, hid, slope, rows, pre) = refs[:8], refs[8:]
    n, ncols, cin = pieces[0].shape
    step = 64
    for k, piece in enumerate(pieces):
        at = (me[0] ^ k) * n
        rows[pl.ds(at, n)] = piece[...]
        pre[...] = jnp.dot(piece[...].reshape(n * ncols, cin), w[...], preferred_element_type=F32) + b[...]
        for r in range(n):

            def body(i, carry, r=r, at=at):
                src = pl.ds(pl.multiple_of(r * ncols + i * step, step), step)
                dst = pl.ds(pl.multiple_of(i * step, step), step)
                h, s = gelu_parts(pre[src, :])
                hid[at + r, dst, :] = h.astype(BF)
                slope[at + r, dst, :] = s.astype(BF)
                return carry

            lax.fori_loop(0, ncols // step, body, 0)


def project_kernel(me, *refs):
    pieces, (w, out, rows) = refs[:8], refs[8:]
    n, ncols, cin = pieces[0].shape
    for k, piece in enumerate(pieces):
        at = (me[0] ^ k) * n
        rows[pl.ds(at, n)] = piece[...]
        res = lax.dot_general(
            piece[...].reshape(n * ncols, cin), w[...], (((1,), (1,)), ((), ())), preferred_element_type=F32
        )
        out[pl.ds(at, n)] = res.reshape(n, ncols, -1)


def load_padded(pad, top, mid, bottom):
    nrows, ncols, lanes = mid.shape
    zeros = jnp.zeros((nrows + 4, EDGE, lanes), F32)
    pad[:, 0:EDGE, :] = zeros
    pad[:, EDGE + ncols :, :] = zeros
    pad[0:2, EDGE : EDGE + ncols, :] = top[...].astype(F32)
    pad[nrows + 2 :, EDGE : EDGE + ncols, :] = bottom[...].astype(F32)

    def body(r, carry):
        pad[r + 2, EDGE : EDGE + ncols, :] = mid[r].astype(F32)
        return carry

    lax.fori_loop(0, nrows, body, 0)


def conv_tiles(pad, taps, nrows, ncols, flip, emit):
    cols = 16

    def body(i, carry):
        w0 = i * cols
        for r0 in range(0, nrows, 4):
            acc = [None] * 4
            for j in range(5):
                xs = [pad[r0 + q, pl.ds(w0 + (EDGE - 2) + j, cols), :] for q in range(8)]
                for q in range(5):
                    t = 5 * q + j
                    tap = taps[(24 - t if flip else t) : (25 - t if flip else t + 1), :]
                    for r in range(4):
                        term = tap * xs[r + q]
                        acc[r] = term if acc[r] is None else acc[r] + term
            emit(r0, pl.ds(pl.multiple_of(w0, cols), cols), acc)
        return carry

    lax.fori_loop(0, ncols // cols, body, 0)


def middle_kernel(top, mid, bottom, gm, taps, bias, mixed, gp, pad):
    nrows, ncols, _ = mid.shape
    load_padded(pad, top, mid, bottom)

    def emit(r0, w, acc):
        for r in range(4):
            m, s = gelu_parts(acc[r] + bias[...])
            mixed[r0 + r, w, :] = m.astype(BF)
            gp[r0 + r, w, :] = (gm[r0 + r, w, :] * s).astype(BF)

    conv_tiles(pad, taps, nrows, ncols, False, emit)


def taps_kernel(top, mid, bottom, gp, grad_k, grad_b, pad, gpf):
    nrows, ncols, lanes = mid.shape
    load_padded(pad, top, mid, bottom)

    def widen(r, carry):
        gpf[r] = gp[r].astype(F32)
        return carry

    lax.fori_loop(0, nrows, widen, 0)

    def body(i, accs):
        accs = list(accs)
        w0 = i * 8
        for j in range(5):
            xs = [pad[q, pl.ds(w0 + (EDGE - 2) + j, 8), :] for q in range(4)]
            for r in range(nrows):
                xs.append(pad[r + 4, pl.ds(w0 + (EDGE - 2) + j, 8), :])
                g = gpf[r, pl.ds(pl.multiple_of(w0, 8), 8), :]
                for q in range(5):
                    accs[5 * q + j] = accs[5 * q + j] + xs[r + q] * g
                if j == 0:
                    accs[25] = accs[25] + g
        return tuple(accs)

    accs = lax.fori_loop(0, ncols // 8, body, tuple(jnp.zeros((8, lanes), F32) for _ in range(26)))
    for t in range(25):
        grad_k[t : t + 1, :] = jnp.sum(accs[t], axis=0, keepdims=True)
    grad_b[...] = jnp.sum(accs[25], axis=0, keepdims=True)


def back_kernel(top, mid, bottom, slope, taps, act, grad_b, pad, total):
    nrows, ncols, lanes = mid.shape
    load_padded(pad, top, mid, bottom)
    total[...] = jnp.zeros_like(total)

    def emit(r0, w, acc):
        part = jnp.zeros((8, lanes), F32)
        for r in range(4):
            a = (acc[r] * slope[r0 + r, w, :].astype(F32)).astype(BF)
            act[r0 + r, w, :] = a
            part = part + jnp.sum(a.astype(F32).reshape(-1, 8, lanes), axis=0)
        total[...] += part

    conv_tiles(pad, taps, nrows, ncols, True, emit)
    grad_b[...] = jnp.sum(total[...], axis=0, keepdims=True)


def place_kernel(where, *refs):
    blocks, out = refs[:-1], refs[-1]
    n, lanes = blocks[0].shape
    for k, block in enumerate(blocks):
        r, c = where[2 * k], where[2 * k + 1]
        out[pl.ds(pl.multiple_of(r * n, n), n), pl.ds(pl.multiple_of(c * lanes, lanes), lanes)] = block[...].astype(F32)


def shards(inputs, cotangent, expand_w, expand_b, depth_k, depth_b, project_w):
    chan = lax.axis_index("chan")
    pair = lax.rem(lax.axis_index("dp"), 2)
    zpos = lax.div(lax.axis_index("dp"), 2)
    groups = lax.axis_size("dp") // 2
    own_rows, ncols, cin = inputs.shape
    nrows = 8 * own_rows
    hslice = expand_w.shape[1]
    half = hslice // 2
    lanes = 128
    npix = nrows * ncols
    me = (pair * 4 + chan).astype(jnp.int32).reshape(1)

    w1 = lax.dynamic_slice_in_dim(expand_w, pair * half, half, axis=1)
    w2 = lax.dynamic_slice_in_dim(project_w, pair * half, half, axis=0)
    b1 = lax.dynamic_slice_in_dim(expand_b, pair * half, half).reshape(1, half)
    bd = lax.dynamic_slice_in_dim(depth_b, pair * half, half).reshape(1, half)
    taps = lax.dynamic_slice_in_dim(depth_k, pair * half, half, axis=1)

    def array(*shape, dtype=BF):
        return jax.ShapeDtypeStruct(shape, dtype)

    full = array(nrows, ncols, half)
    in_pieces = gathered(inputs)
    hidden, slope_one, rows_in = pl.pallas_call(
        expand_kernel,
        out_shape=(full, full, array(nrows, ncols, cin)),
        in_specs=[SMEM] + [VMEM] * 10,
        out_specs=(VMEM,) * 3,
        scratch_shapes=[pltpu.VMEM((own_rows * ncols, half), F32)],
        compiler_params=params(),
        cost_estimate=cost(2 * npix * cin * half, 4 * npix * cin),
        name="expand",
    )(me, *in_pieces, w1, b1)

    hid_top = shift(hidden[nrows - 2 :], 2)
    hid_bottom = shift(hidden[:2], -2)
    cot_pieces = gathered(cotangent)
    grad_mixed, rows_cot = pl.pallas_call(
        project_kernel,
        out_shape=(array(nrows, ncols, half, dtype=F32), array(nrows, ncols, cin)),
        in_specs=[SMEM] + [VMEM] * 9,
        out_specs=(VMEM,) * 2,
        compiler_params=params(),
        cost_estimate=cost(2 * npix * cin * half, 4 * npix * cin),
        name="project",
    )(me, *cot_pieces, w2)

    def rows_spec(n):
        return pl.BlockSpec((n, ncols, lanes), lambda i: (0, 0, i))

    def flat_spec(n):
        return pl.BlockSpec((n, lanes), lambda i: (0, i))

    grid = (half // lanes,)
    padded = pltpu.VMEM((nrows + 4, ncols + 2 * EDGE, lanes), F32)
    halo_specs = [rows_spec(2), rows_spec(nrows), rows_spec(2)]
    vpu = cost(100 * npix * half, 8 * npix * half)
    mixed, grad_pre = pl.pallas_call(
        middle_kernel,
        grid=grid,
        out_shape=(full, full),
        in_specs=halo_specs + [rows_spec(nrows), flat_spec(25), flat_spec(1)],
        out_specs=(rows_spec(nrows),) * 2,
        scratch_shapes=[padded],
        compiler_params=params(),
        cost_estimate=vpu,
        name="middle",
    )(hid_top, hidden, hid_bottom, grad_mixed, taps, bd)

    gp_top = shift(grad_pre[nrows - 2 :], 2)
    gp_bottom = shift(grad_pre[:2], -2)
    flat_cot = rows_cot.reshape(npix, cin)
    grad_w2 = jnp.dot(mixed.reshape(npix, half).T, flat_cot, preferred_element_type=F32)
    w2_own = scattered(grad_w2.reshape(groups, half // groups, cin), zpos, groups)

    grad_k, grad_bd = pl.pallas_call(
        taps_kernel,
        grid=grid,
        out_shape=(array(25, half, dtype=F32), array(1, half, dtype=F32)),
        in_specs=halo_specs + [rows_spec(nrows)],
        out_specs=(flat_spec(25), flat_spec(1)),
        scratch_shapes=[padded, pltpu.VMEM((nrows, ncols, lanes), F32)],
        compiler_params=params(),
        cost_estimate=vpu,
        name="taps",
    )(hid_top, hidden, hid_bottom, grad_pre)

    grad_act, grad_b1 = pl.pallas_call(
        back_kernel,
        grid=grid,
        out_shape=(full, array(1, half, dtype=F32)),
        in_specs=halo_specs + [rows_spec(nrows), flat_spec(25)],
        out_specs=(rows_spec(nrows), flat_spec(1)),
        scratch_shapes=[padded, pltpu.VMEM((8, lanes), F32)],
        compiler_params=params(),
        cost_estimate=vpu,
        name="back",
    )(gp_top, grad_pre, gp_bottom, slope_one, taps)

    core = lax.rem(chan, 2)
    by_core = grad_act.reshape(4, 2, own_rows * ncols, half)

    def share(which):
        act = lax.dynamic_index_in_dim(by_core, which, 1, keepdims=False)
        return jnp.einsum("pth,ch->ptc", act, w1, preferred_element_type=F32)

    other = hop(share(1 - core).astype(BF), 0, 1)
    flat_act = grad_act.reshape(npix, half)
    grad_w1 = jnp.dot(rows_in.reshape(npix, cin).T, flat_act, preferred_element_type=F32)
    tail_rows = 16 * groups
    small = jnp.concatenate([grad_k, grad_bd, grad_b1, jnp.zeros((tail_rows - 27, half), F32)], axis=0)
    w1_chunks = jnp.concatenate(
        [grad_w1.reshape(groups, cin // groups, half), small.reshape(groups, 16, half)], axis=1
    )
    chip_sum = share(core) + other.astype(F32)
    chip = pair * 2 + lax.div(chan, 2)

    def chip_part(k):
        return lax.dynamic_index_in_dim(chip_sum, chip ^ k, 0, keepdims=False)

    own_part = chip_part(0)
    for k, (a, b) in ((1, (0, 2)), (2, (1, 0)), (3, (1, 2))):
        own_part = own_part + hop(chip_part(k).astype(BF), a, b).astype(F32)
    input_grad = (cotangent.astype(F32) + own_part.reshape(cotangent.shape)).astype(BF)

    w1_own = scattered(w1_chunks, zpos, groups)

    def placed(blocks, where, shape):
        return pl.pallas_call(
            place_kernel,
            out_shape=jax.ShapeDtypeStruct(shape, F32),
            in_specs=[SMEM] + [VMEM] * len(blocks),
            out_specs=VMEM,
            compiler_params=params(),
            name="place",
        )(jnp.stack(where).astype(jnp.int32), *blocks)

    w2_blocks, w2_where, w1_blocks, small_blocks, w1_where = [], [], [], [], []
    w2_all, w1_all = spread(w2_own, groups), spread(w1_own, groups)
    for k in range(groups):
        for m in range(2):
            w2_blocks.append(w2_all[k][m])
            w2_where += [(pair ^ m) * groups + (zpos ^ k), 0 * zpos]
            w1_blocks.append(w1_all[k][m][: cin // groups])
            small_blocks.append(w1_all[k][m][cin // groups :])
            w1_where += [zpos ^ k, pair ^ m]
    out_w2 = placed(w2_blocks, w2_where, (hslice, cin))
    out_w1 = placed(w1_blocks, w1_where, (cin, hslice))
    out_small = placed(small_blocks, w1_where, (tail_rows, hslice))
    return (input_grad, out_w1, out_small[26], out_small[:25], out_small[25], out_w2)


def solution(mesh):
    in_specs = (
        P(("dp", "chan"), None, None),
        P(("dp", "chan"), None, None),
        P(None, "chan"),
        P("chan"),
        P(None, "chan"),
        P("chan"),
        P("chan", None),
    )
    out_specs = (
        P(("dp", "chan"), None, None),
        P(None, "chan"),
        P("chan"),
        P(None, "chan"),
        P("chan"),
        P("chan", None),
    )
    return jax.shard_map(shards, mesh=mesh, in_specs=in_specs, out_specs=out_specs, check_vma=False)
```

time: 260 us -> 142 us (0.55)
  waiting for transfers between devices: 115 us -> 25.6 us
  other arithmetic: 57.6 us -> 2.13 us
  starting transfers between devices: 10.7 us -> 59.1 us
  blocking collectives: 40.9 us -> 0 us
  Pallas kernels: 0 us -> 28.6 us
  local copies, waits for them, and re-layouts: 3.89 us -> 20.9 us
  matrix products: 17.7 us -> 4.27 us
  between operations: 14 us -> 1.13 us
    ppermute x4 -> x42, starting transfers between devices: 10.4 us -> 59.1 us  [the longest x38 48.3 us: hop(): return lax.ppermute(value, AXES, pairs)]
    psum x1 -> x0, waiting for transfers between devices: 44.2 us -> none  [shards(): summed = lax.psum((grad_w1, grad_b1, grad_k, grad_bd, grad_w2), 'dp')]
    psum x1 -> x0, blocking collectives: 40.9 us -> none  [shards(): summed = lax.psum((grad_w1, grad_b1, grad_k, grad_bd, grad_w2), 'dp')]
    reduce_scatter x1 -> x0, waiting for transfers between devices: 31 us -> none  [shards(): lax.psum_scatter(jnp.einsum('rwh,ch->rwc', grad_act, expand_w, preferred_...]
    pallas_call x0 -> x8, Pallas kernels: none -> 28.6 us  [the longest x1 6.26 us: shards(): pl.pallas_call(middle_kernel, grid=grid, out_shape=(full, full), in_specs...]
    add x1, other arithmetic: 27.2 us -> 1.17 us  [shards(): own_part = own_part + hop(chip_part(k).astype(BF), a, b).astype(F32)]
    reduce_sum x2 -> x0, other arithmetic: 25.9 us -> none  [the longest x1 18.6 us: shards(): jnp.sum(padded[row_tap:row_tap + nrows, col_tap:col_tap + ncols] * grad_p...]
    all_gather x2 -> x0, waiting for transfers between devices: 20.3 us -> none  [the longest x1 20.3 us: shards(): lax.all_gather(inputs, 'chan', axis=0, tiled=True)]
  transfers between devices with their start and end apart: 8 -> 42, of which waited for: 6 -> 12; matrix products, arithmetic and copies ran while one was open for 22% -> 9% of each run, Pallas kernels for 0% -> 16%
where the time goes in v1:
time: 142 us
  starting transfers between devices  59.1 us (42%)
  Pallas kernels  28.6 us (20%)
  waiting for transfers between devices  25.6 us (18%)
  local copies, waits for them, and re-layouts  20.9 us (15%)
  matrix products  4.27 us (3%)
  other arithmetic  2.13 us (2%)
    ppermute x38, starting transfers between devices, hop(): return lax.ppermute(value, AXES, pairs)  48.3 us
    ppermute x38, waiting for transfers between devices, hop(): return lax.ppermute(value, AXES, pairs)  25.6 us
    ppermute x4, starting transfers between devices, shift(): return lax.ppermute(value, AXES, pairs)  10.7 us
    unnamed x38, local copies, waits for them, and re-layouts  9.77 us
    pallas_call x1, Pallas kernels, shards(): pl.pallas_call(middle_kernel, grid=grid, out_shape=(full, full), in_specs...  6.26 us
    pallas_call x1, Pallas kernels, shards(): pl.pallas_call(expand_kernel, out_shape=(full, full, array(nrows, ncols,...  5.85 us
    pallas_call x1, Pallas kernels, shards(): pl.pallas_call(taps_kernel, grid=grid, out_shape=(array(25, half, dtype=F...  4.76 us
    pallas_call x1, Pallas kernels, shards(): pl.pallas_call(back_kernel, grid=grid, out_shape=(full, array(1, half, dt...  4.74 us
  transfers between devices with their start and end apart: 42, of which 12 were waited for; matrix products, arithmetic and copies ran while one was open for 9% of the time, Pallas kernels for 16%

profile of v1, /device:TPU:0, one launch (start us, length us, event | category | flops | bytes accessed | tf_op | source)
XLA Modules:
  0.0 141.8 jit_solution(18174581064446593984)
XLA Ops:
  0.7 3.0 %collective-permute-start.1 = (bf16[2,128,512]{2,1,0:T(8,128)(2,1)}, bf16[2,128,512]{2,1,0:T(8,128)(2,1)S(1)}, u32[]{:S(2)}, u32[]{:S(2)}) collective-permute-start(bf16[2,128,512]{2,1,0:T(8,128)(2,1)} %refs_0_.2), channel_id=1, source_target_pairs={{0,2},{1,3},{2,0},{3,1},{4,6},{5,7},{6,4},{7,5},{8,10},{9,11},{10,... | collective-permute-start | bytes 786440 | tf_op jit(solution)/shard_map/ppermute | solution.py:37
  3.7 1.5 %collective-permute-start.3 = (bf16[2,128,512]{2,1,0:T(8,128)(2,1)}, bf16[2,128,512]{2,1,0:T(8,128)(2,1)S(1)}, u32[]{:S(2)}, u32[]{:S(2)}) collective-permute-start(bf16[2,128,512]{2,1,0:T(8,128)(2,1)} %refs_0_.2), channel_id=1, source_target_pairs={{0,4},{1,5},{2,6},{3,7},{4,0},{5,1},{6,2},{7,3},{8,12},{9,13},{10,... | collective-permute-start | bytes 786440 | tf_op jit(solution)/shard_map/ppermute | solution.py:37
  5.2 1.9 %collective-permute-start.10 = (bf16[2,128,512]{2,1,0:T(8,128)(2,1)}, bf16[2,128,512]{2,1,0:T(8,128)(2,1)S(1)}, u32[]{:S(2)}, u32[]{:S(2)}) collective-permute-start(bf16[2,128,512]{2,1,0:T(8,128)(2,1)} %refs_0_.3), channel_id=1, source_target_pairs={{0,2},{1,3},{2,0},{3,1},{4,6},{5,7},{6,4},{7,5},{8,10},{9,11},{10,... | collective-permute-start | bytes 786440 | tf_op jit(solution)/shard_map/ppermute | solution.py:37
  7.2 4.6 %collective-permute-done.1.refs_2_ = bf16[2,128,512]{2,1,0:T(8,128)(2,1)S(1)} collective-permute-done((bf16[2,128,512]{2,1,0:T(8,128)(2,1)}, bf16[2,128,512]{2,1,0:T(8,128)(2,1)S(1)}, u32[]{:S(2)}, u32[]{:S(2)}) %collective-permute-start.1) | collective-permute-done | bytes 262176 | tf_op jit(solution)/shard_map/ppermute | solution.py:37
  11.8 2.7 %collective-permute-start.12 = (bf16[2,128,512]{2,1,0:T(8,128)(2,1)}, bf16[2,128,512]{2,1,0:T(8,128)(2,1)S(1)}, u32[]{:S(2)}, u32[]{:S(2)}) collective-permute-start(bf16[2,128,512]{2,1,0:T(8,128)(2,1)} %refs_0_.3), channel_id=1, source_target_pairs={{0,4},{1,5},{2,6},{3,7},{4,0},{5,1},{6,2},{7,3},{8,12},{9,13},{10,... | collective-permute-start | bytes 786440 | tf_op jit(solution)/shard_map/ppermute | solution.py:37
  14.5 1.5 %collective-permute-start.14 = (bf16[2,128,512]{2,1,0:T(8,128)(2,1)}, bf16[2,128,512]{2,1,0:T(8,128)(2,1)S(1)}, u32[]{:S(2)}, u32[]{:S(2)}) collective-permute-start(bf16[2,128,512]{2,1,0:T(8,128)(2,1)} %refs_0_.3), channel_id=1, source_target_pairs={{0,6},{1,7},{2,4},{3,5},{4,2},{5,3},{6,0},{7,1},{8,14},{9,15},{10,... | collective-permute-start | bytes 786440 | tf_op jit(solution)/shard_map/ppermute | solution.py:37
  16.0 2.3 %collective-permute-done.5.refs_6_ = bf16[2,128,512]{2,1,0:T(8,128)(2,1)S(1)} collective-permute-done((bf16[2,128,512]{2,1,0:T(8,128)(2,1)}, bf16[2,128,512]{2,1,0:T(8,128)(2,1)S(1)}, u32[]{:S(2)}, u32[]{:S(2)}) %collective-permute-start.5) | collective-permute-done | bytes 262176 | tf_op jit(solution)/shard_map/ppermute | solution.py:37
  18.8 2.7 %collective-permute-done.10.refs_2_ = bf16[2,128,512]{2,1,0:T(8,128)(2,1)S(1)} collective-permute-done((bf16[2,128,512]{2,1,0:T(8,128)(2,1)}, bf16[2,128,512]{2,1,0:T(8,128)(2,1)S(1)}, u32[]{:S(2)}, u32[]{:S(2)}) %collective-permute-start.10) | collective-permute-done | bytes 262176 | tf_op jit(solution)/shard_map/ppermute | solution.py:37
  23.1 1.0 constant_dynamic-slice_fusion.1.refs_8_
  24.6 3.7 %collective-permute-done.14.refs_6_ = bf16[2,128,512]{2,1,0:T(8,128)(2,1)S(1)} collective-permute-done((bf16[2,128,512]{2,1,0:T(8,128)(2,1)}, bf16[2,128,512]{2,1,0:T(8,128)(2,1)S(1)}, u32[]{:S(2)}, u32[]{:S(2)}) %collective-permute-start.14) | collective-permute-done | bytes 262176 | tf_op jit(solution)/shard_map/ppermute | solution.py:37
  35.1 5.9 %expand.1 = (bf16[16,128,256]{2,1,0:T(8,128)(2,1)S(1)}, bf16[16,128,256]{2,1,0:T(8,128)(2,1)S(1)}, bf16[16,128,512]{2,1,0:T(8,128)(2,1)}) custom-call(s32[1]{0:T(128)} %bitcast.me, bf16[2,128,512]{2,1,0:T(8,128)(2,1)S(1)} %copy-done.5, bf16[2,128,512]{2,1,0:T(8,128)(2,1)S(1)} %copy-done.9, bf16[2,128,512]{2,1,0:T(8,128)(2,1)S(1)} %collective-permute-done.1.refs_2_, ...), custom_call_target="tpu_custom_call" | custom-call | flops 536870912 | bytes 4194304 | tf_op jit(solution)/shard_map/expand/pallas_call | solution.py:230
  40.9 1.0 copy-done.1
  42.6 3.6 %collective-permute-start.7 = (bf16[2,128,256]{2,1,0:T(8,128)(2,1)}, bf16[2,128,256]{2,1,0:T(8,128)(2,1)S(1)}, u32[]{:S(2)}, u32[]{:S(2)}) collective-permute-start(bf16[2,128,256]{2,1,0:T(8,128)(2,1)} %get-tuple-element.34), channel_id=1, source_target_pairs={{0,8},{1,9},{2,10},{3,11},{4,12},{5,13},{6,14},{7,15},{8,16},{9,17... | collective-permute-start | bytes 393224 | tf_op jit(solution)/shard_map/ppermute | solution.py:48
  46.9 1.3 collective-permute-start.8
  48.3 4.0 %copy.13 = bf16[512,2048]{1,0:T(8,128)(2,1)} copy(bf16[512,2048]{0,1:T(8,128)(2,1)} %bitcast.102) | data formatting | bytes 4194304 | tf_op jit(solution)/shard_map/dot_general | solution.py:315
  53.2 3.3 %project.1 = (f32[16,128,256]{2,1,0:T(8,128)S(1)}, bf16[16,128,512]{2,1,0:T(8,128)(2,1)}) custom-call(s32[1]{0:T(128)} %bitcast.me, bf16[2,128,512]{2,1,0:T(8,128)(2,1)S(1)} %copy-done.4, bf16[2,128,512]{2,1,0:T(8,128)(2,1)S(1)} %copy-done.15, bf16[2,128,512]{2,1,0:T(8,128)(2,1)S(1)} %collective-permute-done.10.refs_2_, ...), custom_call_target="tpu_custom_call" | custom-call | flops 536870912 | bytes 4194304 | tf_op jit(solution)/shard_map/project/pallas_call | solution.py:244
  56.5 6.3 %middle.1 = (bf16[16,128,256]{2,1,0:T(8,128)(2,1)S(1)}, bf16[16,128,256]{2,1,0:T(8,128)(2,1)S(1)}) custom-call(bf16[2,128,256]{2,1,0:T(8,128)(2,1)S(1)} %collective-permute-done.7.top, bf16[16,128,256]{2,1,0:T(8,128)(2,1)S(1)} %get-tuple-element.17.mid, bf16[2,128,256]{2,1,0:T(8,128)(2,1)S(1)} %collective-permute-done.8.bottom, ...), custom_call_target="tpu_custom_call" | custom-call | flops 52428800 | bytes 4194304 | tf_op jit(solution)/shard_map/middle/pallas_call | solution.py:264
  62.8 1.0 copy-done.3
  63.8 2.3 %copy.14 = bf16[256,2048]{1,0:T(8,128)(2,1)} copy(bf16[256,2048]{0,1:T(8,128)(2,1)} %bitcast.98) | data formatting | bytes 2097152 | tf_op jit(solution)/shard_map/dot_general | solution.py:279
  66.0 4.6 %collective-permute-start.16 = (bf16[2,128,256]{2,1,0:T(8,128)(2,1)S(1)}, bf16[2,128,256]{2,1,0:T(8,128)(2,1)S(1)}, u32[]{:S(2)}, u32[]{:S(2)}) collective-permute-start(bf16[2,128,256]{2,1,0:T(8,128)(2,1)S(1)} %get-tuple-element.32), channel_id=1, source_target_pairs={{0,8},{1,9},{2,10},{3,11},{4,12},{5,13},{6,14},{7,15},{8,16},{9,17... | collective-permute-start | bytes 393224 | tf_op jit(solution)/shard_map/ppermute | solution.py:48
  70.6 1.3 collective-permute-start.17
  71.9 2.6 %fusion.41 = f32[4,64,512]{2,1,0:T(8,128)S(1)} fusion(bf16[4,64,2048]{2,1,0:T(8,128)(2,1)} %bitcast.104, bf16[2048,512,1]{1,0,2:T(8,128)(2,1)} %bitcast.109), kind=kOutput, calls=%fused_computation.62 | convolution fusion | flops 536870912 | bytes 3670016 | tf_op jit(solution)/shard_map/dot_general | solution.py:279
  74.6 2.7 %collective-permute-start.32 = (bf16[64,512]{1,0:T(8,128)(2,1)S(1)}, bf16[64,512]{1,0:T(8,128)(2,1)S(1)}, u32[]{:S(2)}, u32[]{:S(2)}) collective-permute-start(bf16[64,512]{1,0:T(8,128)(2,1)S(1)} %get-tuple-element.38), channel_id=1, source_target_pairs={{0,8},{1,9},{2,10},{3,11},{4,12},{5,13},{6,14},{7,15},{8,0},{9,1},... | collective-permute-start | bytes 196616 | tf_op jit(solution)/shard_map/ppermute | solution.py:37
  77.3 2.6 %collective-permute-start.33 = (bf16[64,512]{1,0:T(8,128)(2,1)S(1)}, bf16[64,512]{1,0:T(8,128)(2,1)S(1)}, u32[]{:S(2)}, u32[]{:S(2)}) collective-permute-start(bf16[64,512]{1,0:T(8,128)(2,1)S(1)} %get-tuple-element.40), channel_id=1, source_target_pairs={{0,16},{1,17},{2,18},{3,19},{4,20},{5,21},{6,22},{7,23},{8,24},{9,... | collective-permute-start | bytes 196616 | tf_op jit(solution)/shard_map/ppermute | solution.py:37
  79.9 4.8 %taps.1 = (f32[25,256]{1,0:T(8,128)S(1)}, f32[1,256]{1,0:T(1,128)S(1)}) custom-call(bf16[2,128,256]{2,1,0:T(8,128)(2,1)S(1)} %collective-permute-done.7.top, bf16[16,128,256]{2,1,0:T(8,128)(2,1)S(1)} %get-tuple-element.17.mid, bf16[2,128,256]{2,1,0:T(8,128)(2,1)S(1)} %collective-permute-done.8.bottom, bf16[16,128,256]{2,1,0:T(8,128)(2,1)S(1)} %get-tuple-element.19.mid.gp), custom_call_target="tpu_custom_call" | custom-call | flops 52428800 | bytes 4194304 | tf_op jit(solution)/shard_map/taps/pallas_call | solution.py:282
  84.7 4.7 %back.1 = (bf16[16,128,256]{2,1,0:T(8,128)(2,1)S(1)}, f32[1,256]{1,0:T(1,128)S(1)}) custom-call(bf16[2,128,256]{2,1,0:T(8,128)(2,1)S(1)} %collective-permute-done.16.top, bf16[16,128,256]{2,1,0:T(8,128)(2,1)S(1)} %get-tuple-element.19.mid.gp, bf16[2,128,256]{2,1,0:T(8,128)(2,1)S(1)} %collective-permute-done.17.bottom, bf16[16,128,256]{2,1,0:T(8,128)(2,1)S(1)} %copy-done.2, ...), custom_call_target="tpu_custom_call" | custom-call | flops 52428800 | bytes 4194304 | tf_op jit(solution)/shard_map/back/pallas_call | solution.py:294
  91.8 3.5 %collective-permute-start.23 = (bf16[144,256]{1,0:T(8,128)(2,1)S(1)}, bf16[144,256]{1,0:T(8,128)(2,1)S(1)}, u32[]{:S(2)}, u32[]{:S(2)}) collective-permute-start(bf16[144,256]{1,0:T(8,128)(2,1)S(1)} %get-tuple-element.36), channel_id=1, source_target_pairs={{0,16},{1,17},{2,18},{3,19},{4,20},{5,21},{6,22},{7,23},{8,24},{9,... | collective-permute-start | bytes 221192 | tf_op jit(solution)/shard_map/ppermute | solution.py:37
  95.4 1.6 %collective-permute-start.35 = (bf16[64,512]{1,0:T(8,128)(2,1)S(1)}, bf16[64,512]{1,0:T(8,128)(2,1)S(1)}, u32[]{:S(2)}, u32[]{:S(2)}) collective-permute-start(bf16[64,512]{1,0:T(8,128)(2,1)S(1)} %fusion.28.refs_0_), channel_id=1, source_target_pairs={{0,4},{1,5},{2,6},{3,7},{4,0},{5,1},{6,2},{7,3},{8,12},{9,13},{10,... | collective-permute-start | bytes 196616 | tf_op jit(solution)/shard_map/ppermute | solution.py:37
  97.5 3.7 %collective-permute-done.23 = bf16[144,256]{1,0:T(8,128)(2,1)S(1)} collective-permute-done((bf16[144,256]{1,0:T(8,128)(2,1)S(1)}, bf16[144,256]{1,0:T(8,128)(2,1)S(1)}, u32[]{:S(2)}, u32[]{:S(2)}) %collective-permute-start.23) | collective-permute-done | bytes 73760 | tf_op jit(solution)/shard_map/ppermute | solution.py:37
  101.9 3.6 %collective-permute-start.38 = (bf16[64,512]{1,0:T(8,128)(2,1)S(1)}, bf16[64,512]{1,0:T(8,128)(2,1)S(1)}, u32[]{:S(2)}, u32[]{:S(2)}) collective-permute-start(bf16[64,512]{1,0:T(8,128)(2,1)S(1)} %fusion.28.refs_0_), channel_id=1, source_target_pairs={{0,16},{1,17},{2,18},{3,19},{4,20},{5,21},{6,22},{7,23},{8,24},{9,... | collective-permute-start | bytes 196616 | tf_op jit(solution)/shard_map/ppermute | solution.py:37
  105.8 2.1 %collective-permute-start.40 = (bf16[64,512]{1,0:T(8,128)(2,1)S(1)}, bf16[64,512]{1,0:T(8,128)(2,1)S(1)}, u32[]{:S(2)}, u32[]{:S(2)}) collective-permute-start(bf16[64,512]{1,0:T(8,128)(2,1)S(1)} %fusion.28.refs_0_), channel_id=1, source_target_pairs={{0,24},{1,25},{2,26},{3,27},{4,28},{5,29},{6,30},{7,31},{8,16},{9,... | collective-permute-start | bytes 196616 | tf_op jit(solution)/shard_map/ppermute | solution.py:37
  108.0 2.4 %collective-permute-start.41 = (bf16[64,512]{1,0:T(8,128)(2,1)S(1)}, bf16[64,512]{1,0:T(8,128)(2,1)S(1)}, u32[]{:S(2)}, u32[]{:S(2)}) collective-permute-start(bf16[64,512]{1,0:T(8,128)(2,1)S(1)} %fusion.28.refs_0_), channel_id=1, source_target_pairs={{0,28},{1,29},{2,30},{3,31},{4,24},{5,25},{6,26},{7,27},{8,20},{9,... | collective-permute-start | bytes 196616 | tf_op jit(solution)/shard_map/ppermute | solution.py:37
  110.3 1.8 %collective-permute-done.38.refs_4_ = bf16[64,512]{1,0:T(8,128)(2,1)S(1)} collective-permute-done((bf16[64,512]{1,0:T(8,128)(2,1)S(1)}, bf16[64,512]{1,0:T(8,128)(2,1)S(1)}, u32[]{:S(2)}, u32[]{:S(2)}) %collective-permute-start.38) | collective-permute-done | bytes 65568 | tf_op jit(solution)/shard_map/ppermute | solution.py:37
  112.1 1.6 %collective-permute-start.25 = (bf16[144,256]{1,0:T(8,128)(2,1)S(1)}, bf16[144,256]{1,0:T(8,128)(2,1)S(1)}, u32[]{:S(2)}, u32[]{:S(2)}) collective-permute-start(bf16[144,256]{1,0:T(8,128)(2,1)S(1)} %fusion.21), channel_id=1, source_target_pairs={{0,4},{1,5},{2,6},{3,7},{4,0},{5,1},{6,2},{7,3},{8,12},{9,13},{10,... | collective-permute-start | bytes 221192 | tf_op jit(solution)/shard_map/ppermute | solution.py:37
  114.3 1.0 collective-permute-done.39.refs_5_
  116.2 1.8 %collective-permute-start.28 = (bf16[144,256]{1,0:T(8,128)(2,1)S(1)}, bf16[144,256]{1,0:T(8,128)(2,1)S(1)}, u32[]{:S(2)}, u32[]{:S(2)}) collective-permute-start(bf16[144,256]{1,0:T(8,128)(2,1)S(1)} %fusion.21), channel_id=1, source_target_pairs={{0,16},{1,17},{2,18},{3,19},{4,20},{5,21},{6,22},{7,23},{8,24},{9,... | collective-permute-start | bytes 221192 | tf_op jit(solution)/shard_map/ppermute | solution.py:37
  118.0 2.2 %collective-permute-start.29 = (bf16[144,256]{1,0:T(8,128)(2,1)S(1)}, bf16[144,256]{1,0:T(8,128)(2,1)S(1)}, u32[]{:S(2)}, u32[]{:S(2)}) collective-permute-start(bf16[144,256]{1,0:T(8,128)(2,1)S(1)} %fusion.21), channel_id=1, source_target_pairs={{0,20},{1,21},{2,22},{3,23},{4,16},{5,17},{6,18},{7,19},{8,28},{9,... | collective-permute-start | bytes 221192 | tf_op jit(solution)/shard_map/ppermute | solution.py:37
  120.2 2.5 %collective-permute-start.30 = (bf16[144,256]{1,0:T(8,128)(2,1)S(1)}, bf16[144,256]{1,0:T(8,128)(2,1)S(1)}, u32[]{:S(2)}, u32[]{:S(2)}) collective-permute-start(bf16[144,256]{1,0:T(8,128)(2,1)S(1)} %fusion.21), channel_id=1, source_target_pairs={{0,24},{1,25},{2,26},{3,27},{4,28},{5,29},{6,30},{7,31},{8,16},{9,... | collective-permute-start | bytes 221192 | tf_op jit(solution)/shard_map/ppermute | solution.py:37
  122.7 1.4 %collective-permute-start.31 = (bf16[144,256]{1,0:T(8,128)(2,1)S(1)}, bf16[144,256]{1,0:T(8,128)(2,1)S(1)}, u32[]{:S(2)}, u32[]{:S(2)}) collective-permute-start(bf16[144,256]{1,0:T(8,128)(2,1)S(1)} %fusion.21), channel_id=1, source_target_pairs={{0,28},{1,29},{2,30},{3,31},{4,24},{5,25},{6,26},{7,27},{8,20},{9,... | collective-permute-start | bytes 221192 | tf_op jit(solution)/shard_map/ppermute | solution.py:37
  124.2 1.6 %collective-permute-start.19 = (bf16[256,512]{1,0:T(8,128)(2,1)S(1)}, bf16[256,512]{1,0:T(8,128)(2,1)S(1)}, u32[]{:S(2)}, u32[]{:S(2)}) collective-permute-start(bf16[256,512]{1,0:T(8,128)(2,1)S(1)} %get-tuple-element.28), channel_id=1, source_target_pairs={{0,2},{1,3},{2,0},{3,1},{4,6},{5,7},{6,4},{7,5},{8,10},{9,11},{10,... | collective-permute-start | bytes 786440 | tf_op jit(solution)/shard_map/ppermute | solution.py:37
  125.8 1.1 collective-permute-done.28
  126.9 1.7 %collective-permute-start.20 = (bf16[256,512]{1,0:T(8,128)(2,1)S(1)}, bf16[256,512]{1,0:T(8,128)(2,1)S(1)}, u32[]{:S(2)}, u32[]{:S(2)}) collective-permute-start(bf16[256,512]{1,0:T(8,128)(2,1)S(1)} %get-tuple-element.30), channel_id=1, source_target_pairs={{0,4},{1,5},{2,6},{3,7},{4,0},{5,1},{6,2},{7,3},{8,12},{9,13},{10,... | collective-permute-start | bytes 786440 | tf_op jit(solution)/shard_map/ppermute | solution.py:37
  128.6 1.5 %collective-permute-done.29 = bf16[144,256]{1,0:T(8,128)(2,1)S(1)} collective-permute-done((bf16[144,256]{1,0:T(8,128)(2,1)S(1)}, bf16[144,256]{1,0:T(8,128)(2,1)S(1)}, u32[]{:S(2)}, u32[]{:S(2)}) %collective-permute-start.29) | collective-permute-done | bytes 73760 | tf_op jit(solution)/shard_map/ppermute | solution.py:37
  130.1 1.6 %collective-permute-start.21 = (bf16[256,512]{1,0:T(8,128)(2,1)S(1)}, bf16[256,512]{1,0:T(8,128)(2,1)S(1)}, u32[]{:S(2)}, u32[]{:S(2)}) collective-permute-start(bf16[256,512]{1,0:T(8,128)(2,1)S(1)} %get-tuple-element.29), channel_id=1, source_target_pairs={{0,6},{1,7},{2,4},{3,5},{4,2},{5,3},{6,0},{7,1},{8,14},{9,15},{10,... | collective-permute-start | bytes 786440 | tf_op jit(solution)/shard_map/ppermute | solution.py:37
  131.9 1.6 %place.5 = f32[512,512]{1,0:T(8,128)} custom-call(s32[16]{0:T(128)S(1)} %stack.90.where, bf16[64,512]{1,0:T(8,128)(2,1)S(1)} %fusion.28.refs_0_, bf16[64,512]{1,0:T(8,128)(2,1)S(1)} %collective-permute-done.35.refs_1_, bf16[64,512]{1,0:T(8,128)(2,1)S(1)} %collective-permute-done.36.refs_2_, bf16[64,512]{1,0:T(8,128)(2,1)S(1)} %collective-permute-done.37.refs_3_, ...), custom_call_target="tpu_custom_call" | custom-call | tf_op jit(solution)/shard_map/place/pallas_call | solution.py:335
  134.9 1.6 %place.3 = f32[512,512]{1,0:T(8,128)} custom-call(s32[16]{0:T(128)S(1)} %stack.38.where, bf16[128,256]{1,0:T(8,128)(2,1)S(1)} %slice.92.refs_0_, bf16[128,256]{1,0:T(8,128)(2,1)S(1)} %slice.93.refs_1_, bf16[128,256]{1,0:T(8,128)(2,1)S(1)} %slice.94.refs_2_, bf16[128,256]{1,0:T(8,128)(2,1)S(1)} %slice.95.refs_3_, bf16[128,256]{1,0:T(8,128)(2,1)S(1)} %slice.96.refs_4_, ...), custom_call_target="tpu_custom_call" | custom-call | tf_op jit(solution)/shard_map/place/pallas_call | solution.py:335
  137.0 2.8 %collective-permute-done.21 = bf16[256,512]{1,0:T(8,128)(2,1)S(1)} collective-permute-done((bf16[256,512]{1,0:T(8,128)(2,1)S(1)}, bf16[256,512]{1,0:T(8,128)(2,1)S(1)}, u32[]{:S(2)}, u32[]{:S(2)}) %collective-permute-start.21) | collective-permute-done | bytes 262176 | tf_op jit(solution)/shard_map/ppermute | solution.py:37
  139.9 1.2 fusion.1
  (125 shorter events, 20.3 us)
Async XLA Ops:
  0.6 22.4 %copy-start = (bf16[512,512]{1,0:T(8,128)(2,1)S(1)}, bf16[512,512]{1,0:T(8,128)(2,1)}, u32[]{:S(2)}) copy-start(bf16[512,512]{1,0:T(8,128)(2,1)} %param.9) | copy-start | bytes 1572868
  0.6 47.6 %copy-start.18 = (f32[25,512]{1,0:T(8,128)S(1)}, f32[25,512]{1,0:T(8,128)}, u32[]{:S(2)}) copy-start(f32[25,512]{1,0:T(8,128)} %param.11) | copy-start | bytes 153604
  0.7 11.1 %collective-permute-start.1 = (bf16[2,128,512]{2,1,0:T(8,128)(2,1)}, bf16[2,128,512]{2,1,0:T(8,128)(2,1)S(1)}, u32[]{:S(2)}, u32[]{:S(2)}) collective-permute-start(bf16[2,128,512]{2,1,0:T(8,128)(2,1)} %refs_0_.2), channel_id=1, source_target_pairs={{0,2},{1,3},{2,0},{3,1},{4,6},{5,7},{6,4},{7,5},{8,10},{9,11},{10,... | collective-permute-start | bytes 786440 | tf_op jit(solution)/shard_map/ppermute | solution.py:37
  3.7 10.8 %collective-permute-start.3 = (bf16[2,128,512]{2,1,0:T(8,128)(2,1)}, bf16[2,128,512]{2,1,0:T(8,128)(2,1)S(1)}, u32[]{:S(2)}, u32[]{:S(2)}) collective-permute-start(bf16[2,128,512]{2,1,0:T(8,128)(2,1)} %refs_0_.2), channel_id=1, source_target_pairs={{0,4},{1,5},{2,6},{3,7},{4,0},{5,1},{6,2},{7,3},{8,12},{9,13},{10,... | collective-permute-start | bytes 786440 | tf_op jit(solution)/shard_map/ppermute | solution.py:37
  5.2 13.1 %collective-permute-start.5 = (bf16[2,128,512]{2,1,0:T(8,128)(2,1)}, bf16[2,128,512]{2,1,0:T(8,128)(2,1)S(1)}, u32[]{:S(2)}, u32[]{:S(2)}) collective-permute-start(bf16[2,128,512]{2,1,0:T(8,128)(2,1)} %refs_0_.2), channel_id=1, source_target_pairs={{0,6},{1,7},{2,4},{3,5},{4,2},{5,3},{6,0},{7,1},{8,14},{9,15},{10,... | collective-permute-start | bytes 786440 | tf_op jit(solution)/shard_map/ppermute | solution.py:37
  5.2 13.0 %collective-permute-start = (bf16[2,128,512]{2,1,0:T(8,128)(2,1)}, bf16[2,128,512]{2,1,0:T(8,128)(2,1)S(1)}, u32[]{:S(2)}, u32[]{:S(2)}) collective-permute-start(bf16[2,128,512]{2,1,0:T(8,128)(2,1)} %refs_0_.2), channel_id=1, source_target_pairs={{0,1},{1,0},{2,3},{3,2},{4,5},{5,4},{6,7},{7,6},{8,9},{9,8},{10,11... | collective-permute-start | bytes 786440 | tf_op jit(solution)/shard_map/ppermute | solution.py:37
  5.2 16.2 %collective-permute-start.10 = (bf16[2,128,512]{2,1,0:T(8,128)(2,1)}, bf16[2,128,512]{2,1,0:T(8,128)(2,1)S(1)}, u32[]{:S(2)}, u32[]{:S(2)}) collective-permute-start(bf16[2,128,512]{2,1,0:T(8,128)(2,1)} %refs_0_.3), channel_id=1, source_target_pairs={{0,2},{1,3},{2,0},{3,1},{4,6},{5,7},{6,4},{7,5},{8,10},{9,11},{10,... | collective-permute-start | bytes 786440 | tf_op jit(solution)/shard_map/ppermute | solution.py:37
  11.8 12.7 %collective-permute-start.12 = (bf16[2,128,512]{2,1,0:T(8,128)(2,1)}, bf16[2,128,512]{2,1,0:T(8,128)(2,1)S(1)}, u32[]{:S(2)}, u32[]{:S(2)}) collective-permute-start(bf16[2,128,512]{2,1,0:T(8,128)(2,1)} %refs_0_.3), channel_id=1, source_target_pairs={{0,4},{1,5},{2,6},{3,7},{4,0},{5,1},{6,2},{7,3},{8,12},{9,13},{10,... | collective-permute-start | bytes 786440 | tf_op jit(solution)/shard_map/ppermute | solution.py:37
  14.5 13.9 %collective-permute-start.14 = (bf16[2,128,512]{2,1,0:T(8,128)(2,1)}, bf16[2,128,512]{2,1,0:T(8,128)(2,1)S(1)}, u32[]{:S(2)}, u32[]{:S(2)}) collective-permute-start(bf16[2,128,512]{2,1,0:T(8,128)(2,1)} %refs_0_.3), channel_id=1, source_target_pairs={{0,6},{1,7},{2,4},{3,5},{4,2},{5,3},{6,0},{7,1},{8,14},{9,15},{10,... | collective-permute-start | bytes 786440 | tf_op jit(solution)/shard_map/ppermute | solution.py:37
  18.3 12.0 %copy-start.6 = (bf16[2,128,512]{2,1,0:T(8,128)(2,1)}, bf16[2,128,512]{2,1,0:T(8,128)(2,1)S(1)}, u32[]{:S(2)}) copy-start(bf16[2,128,512]{2,1,0:T(8,128)(2,1)S(1)} %collective-permute-done.5.refs_6_) | copy-start | bytes 786436
  18.3 10.1 %collective-permute-start.2 = (bf16[2,128,512]{2,1,0:T(8,128)(2,1)S(1)}, bf16[2,128,512]{2,1,0:T(8,128)(2,1)S(1)}, u32[]{:S(2)}, u32[]{:S(2)}) collective-permute-start(bf16[2,128,512]{2,1,0:T(8,128)(2,1)S(1)} %collective-permute-done.1.refs_2_), channel_id=1, source_target_pairs={{0,1},{1,0},{2,3},{3,2},{4,5},{5,4},{6,7},{7,6},{8,9},{9,8},{10,11... | collective-permute-start | bytes 786440 | tf_op jit(solution)/shard_map/ppermute | solution.py:37
  18.3 12.0 %copy-start.8 = (bf16[2,128,512]{2,1,0:T(8,128)(2,1)}, bf16[2,128,512]{2,1,0:T(8,128)(2,1)S(1)}, u32[]{:S(2)}) copy-start(bf16[2,128,512]{2,1,0:T(8,128)(2,1)S(1)} %collective-permute-done.refs_1_) | copy-start | bytes 786436
  18.3 11.3 %collective-permute-start.4 = (bf16[2,128,512]{2,1,0:T(8,128)(2,1)S(1)}, bf16[2,128,512]{2,1,0:T(8,128)(2,1)S(1)}, u32[]{:S(2)}, u32[]{:S(2)}) collective-permute-start(bf16[2,128,512]{2,1,0:T(8,128)(2,1)S(1)} %collective-permute-done.3.refs_4_), channel_id=1, source_target_pairs={{0,1},{1,0},{2,3},{3,2},{4,5},{5,4},{6,7},{7,6},{8,9},{9,8},{10,11... | collective-permute-start | bytes 786440 | tf_op jit(solution)/shard_map/ppermute | solution.py:37
  21.4 8.8 %collective-permute-start.6 = (bf16[2,128,512]{2,1,0:T(8,128)(2,1)S(1)}, bf16[2,128,512]{2,1,0:T(8,128)(2,1)}, u32[]{:S(2)}, u32[]{:S(2)}) collective-permute-start(bf16[2,128,512]{2,1,0:T(8,128)(2,1)S(1)} %collective-permute-done.5.refs_6_), channel_id=1, source_target_pairs={{0,1},{1,0},{2,3},{3,2},{4,5},{5,4},{6,7},{7,6},{8,9},{9,8},{10,11... | collective-permute-start | bytes 786440 | tf_op jit(solution)/shard_map/ppermute | solution.py:37
  24.4 21.8 %collective-permute-start.9 = (bf16[2,128,512]{2,1,0:T(8,128)(2,1)}, bf16[2,128,512]{2,1,0:T(8,128)(2,1)S(1)}, u32[]{:S(2)}, u32[]{:S(2)}) collective-permute-start(bf16[2,128,512]{2,1,0:T(8,128)(2,1)} %refs_0_.3), channel_id=1, source_target_pairs={{0,1},{1,0},{2,3},{3,2},{4,5},{5,4},{6,7},{7,6},{8,9},{9,8},{10,11... | collective-permute-start | bytes 786440 | tf_op jit(solution)/shard_map/ppermute | solution.py:37
  28.4 23.9 %collective-permute-start.11 = (bf16[2,128,512]{2,1,0:T(8,128)(2,1)S(1)}, bf16[2,128,512]{2,1,0:T(8,128)(2,1)}, u32[]{:S(2)}, u32[]{:S(2)}) collective-permute-start(bf16[2,128,512]{2,1,0:T(8,128)(2,1)S(1)} %collective-permute-done.10.refs_2_), channel_id=1, source_target_pairs={{0,1},{1,0},{2,3},{3,2},{4,5},{5,4},{6,7},{7,6},{8,9},{9,8},{10,11... | collective-permute-start | bytes 786440 | tf_op jit(solution)/shard_map/ppermute | solution.py:37
  29.1 23.2 %collective-permute-start.13 = (bf16[2,128,512]{2,1,0:T(8,128)(2,1)S(1)}, bf16[2,128,512]{2,1,0:T(8,128)(2,1)}, u32[]{:S(2)}, u32[]{:S(2)}) collective-permute-start(bf16[2,128,512]{2,1,0:T(8,128)(2,1)S(1)} %collective-permute-done.12.refs_4_), channel_id=1, source_target_pairs={{0,1},{1,0},{2,3},{3,2},{4,5},{5,4},{6,7},{7,6},{8,9},{9,8},{10,11... | collective-permute-start | bytes 786440 | tf_op jit(solution)/shard_map/ppermute | solution.py:37
  30.3 22.0 %collective-permute-start.15 = (bf16[2,128,512]{2,1,0:T(8,128)(2,1)S(1)}, bf16[2,128,512]{2,1,0:T(8,128)(2,1)}, u32[]{:S(2)}, u32[]{:S(2)}) collective-permute-start(bf16[2,128,512]{2,1,0:T(8,128)(2,1)S(1)} %collective-permute-done.14.refs_6_), channel_id=1, source_target_pairs={{0,1},{1,0},{2,3},{3,2},{4,5},{5,4},{6,7},{7,6},{8,9},{9,8},{10,11... | collective-permute-start | bytes 786440 | tf_op jit(solution)/shard_map/ppermute | solution.py:37
  42.6 13.9 %collective-permute-start.7 = (bf16[2,128,256]{2,1,0:T(8,128)(2,1)}, bf16[2,128,256]{2,1,0:T(8,128)(2,1)S(1)}, u32[]{:S(2)}, u32[]{:S(2)}) collective-permute-start(bf16[2,128,256]{2,1,0:T(8,128)(2,1)} %get-tuple-element.34), channel_id=1, source_target_pairs={{0,8},{1,9},{2,10},{3,11},{4,12},{5,13},{6,14},{7,15},{8,16},{9,17... | collective-permute-start | bytes 393224 | tf_op jit(solution)/shard_map/ppermute | solution.py:48
  46.9 9.6 %collective-permute-start.8 = (bf16[2,128,256]{2,1,0:T(8,128)(2,1)}, bf16[2,128,256]{2,1,0:T(8,128)(2,1)S(1)}, u32[]{:S(2)}, u32[]{:S(2)}) collective-permute-start(bf16[2,128,256]{2,1,0:T(8,128)(2,1)} %get-tuple-element.33), channel_id=1, source_target_pairs={{8,0},{9,1},{10,2},{11,3},{12,4},{13,5},{14,6},{15,7},{16,8},{17,9... | collective-permute-start | bytes 393224 | tf_op jit(solution)/shard_map/ppermute | solution.py:48
  66.0 18.6 %collective-permute-start.16 = (bf16[2,128,256]{2,1,0:T(8,128)(2,1)S(1)}, bf16[2,128,256]{2,1,0:T(8,128)(2,1)S(1)}, u32[]{:S(2)}, u32[]{:S(2)}) collective-permute-start(bf16[2,128,256]{2,1,0:T(8,128)(2,1)S(1)} %get-tuple-element.32), channel_id=1, source_target_pairs={{0,8},{1,9},{2,10},{3,11},{4,12},{5,13},{6,14},{7,15},{8,16},{9,17... | collective-permute-start | bytes 393224 | tf_op jit(solution)/shard_map/ppermute | solution.py:48
  70.6 14.1 %collective-permute-start.17 = (bf16[2,128,256]{2,1,0:T(8,128)(2,1)S(1)}, bf16[2,128,256]{2,1,0:T(8,128)(2,1)S(1)}, u32[]{:S(2)}, u32[]{:S(2)}) collective-permute-start(bf16[2,128,256]{2,1,0:T(8,128)(2,1)S(1)} %get-tuple-element.31), channel_id=1, source_target_pairs={{8,0},{9,1},{10,2},{11,3},{12,4},{13,5},{14,6},{15,7},{16,8},{17,9... | collective-permute-start | bytes 393224 | tf_op jit(solution)/shard_map/ppermute | solution.py:48
  74.5 10.1 %copy-start.2 = (bf16[16,128,256]{2,1,0:T(8,128)(2,1)S(1)}, bf16[16,128,256]{2,1,0:T(8,128)(2,1)}, u32[]{:S(2)}) copy-start(bf16[16,128,256]{2,1,0:T(8,128)(2,1)} %copy-done.1) | copy-start | bytes 3145732
  74.6 17.2 %collective-permute-start.32 = (bf16[64,512]{1,0:T(8,128)(2,1)S(1)}, bf16[64,512]{1,0:T(8,128)(2,1)S(1)}, u32[]{:S(2)}, u32[]{:S(2)}) collective-permute-start(bf16[64,512]{1,0:T(8,128)(2,1)S(1)} %get-tuple-element.38), channel_id=1, source_target_pairs={{0,8},{1,9},{2,10},{3,11},{4,12},{5,13},{6,14},{7,15},{8,0},{9,1},... | collective-permute-start | bytes 196616 | tf_op jit(solution)/shard_map/ppermute | solution.py:37
  77.3 18.0 %collective-permute-start.33 = (bf16[64,512]{1,0:T(8,128)(2,1)S(1)}, bf16[64,512]{1,0:T(8,128)(2,1)S(1)}, u32[]{:S(2)}, u32[]{:S(2)}) collective-permute-start(bf16[64,512]{1,0:T(8,128)(2,1)S(1)} %get-tuple-element.40), channel_id=1, source_target_pairs={{0,16},{1,17},{2,18},{3,19},{4,20},{5,21},{6,22},{7,23},{8,24},{9,... | collective-permute-start | bytes 196616 | tf_op jit(solution)/shard_map/ppermute | solution.py:37
  79.9 15.4 %collective-permute-start.34 = (bf16[64,512]{1,0:T(8,128)(2,1)S(1)}, bf16[64,512]{1,0:T(8,128)(2,1)S(1)}, u32[]{:S(2)}, u32[]{:S(2)}) collective-permute-start(bf16[64,512]{1,0:T(8,128)(2,1)S(1)} %get-tuple-element.39), channel_id=1, source_target_pairs={{0,24},{1,25},{2,26},{3,27},{4,28},{5,29},{6,30},{7,31},{8,16},{9,... | collective-permute-start | bytes 196616 | tf_op jit(solution)/shard_map/ppermute | solution.py:37
  89.9 23.8 %collective-permute-start.18 = (bf16[4,256,512]{2,1,0:T(8,128)(2,1)S(1)}, bf16[4,256,512]{2,1,0:T(8,128)(2,1)S(1)}, u32[]{:S(2)}, u32[]{:S(2)}) collective-permute-start(bf16[4,256,512]{2,1,0:T(8,128)(2,1)S(1)} %convolution_convert_fusion), channel_id=1, source_target_pairs={{0,1},{1,0},{2,3},{3,2},{4,5},{5,4},{6,7},{7,6},{8,9},{9,8},{10,11... | collective-permute-start | bytes 3145736 | tf_op jit(solution)/shard_map/ppermute | solution.py:37
  90.8 6.1 %collective-permute-start.22 = (bf16[144,256]{1,0:T(8,128)(2,1)S(1)}, bf16[144,256]{1,0:T(8,128)(2,1)S(1)}, u32[]{:S(2)}, u32[]{:S(2)}) collective-permute-start(bf16[144,256]{1,0:T(8,128)(2,1)S(1)} %get-tuple-element.35), channel_id=1, source_target_pairs={{0,8},{1,9},{2,10},{3,11},{4,12},{5,13},{6,14},{7,15},{8,0},{9,1},... | collective-permute-start | bytes 221192 | tf_op jit(solution)/shard_map/ppermute | solution.py:37
  91.8 9.4 %collective-permute-start.23 = (bf16[144,256]{1,0:T(8,128)(2,1)S(1)}, bf16[144,256]{1,0:T(8,128)(2,1)S(1)}, u32[]{:S(2)}, u32[]{:S(2)}) collective-permute-start(bf16[144,256]{1,0:T(8,128)(2,1)S(1)} %get-tuple-element.36), channel_id=1, source_target_pairs={{0,16},{1,17},{2,18},{3,19},{4,20},{5,21},{6,22},{7,23},{8,24},{9,... | collective-permute-start | bytes 221192 | tf_op jit(solution)/shard_map/ppermute | solution.py:37
  95.3 6.6 %collective-permute-start.24 = (bf16[144,256]{1,0:T(8,128)(2,1)S(1)}, bf16[144,256]{1,0:T(8,128)(2,1)S(1)}, u32[]{:S(2)}, u32[]{:S(2)}) collective-permute-start(bf16[144,256]{1,0:T(8,128)(2,1)S(1)} %get-tuple-element.37), channel_id=1, source_target_pairs={{0,24},{1,25},{2,26},{3,27},{4,28},{5,29},{6,30},{7,31},{8,16},{9,... | collective-permute-start | bytes 221192 | tf_op jit(solution)/shard_map/ppermute | solution.py:37
  95.4 10.2 %collective-permute-start.35 = (bf16[64,512]{1,0:T(8,128)(2,1)S(1)}, bf16[64,512]{1,0:T(8,128)(2,1)S(1)}, u32[]{:S(2)}, u32[]{:S(2)}) collective-permute-start(bf16[64,512]{1,0:T(8,128)(2,1)S(1)} %fusion.28.refs_0_), channel_id=1, source_target_pairs={{0,4},{1,5},{2,6},{3,7},{4,0},{5,1},{6,2},{7,3},{8,12},{9,13},{10,... | collective-permute-start | bytes 196616 | tf_op jit(solution)/shard_map/ppermute | solution.py:37
  96.9 8.9 %collective-permute-start.36 = (bf16[64,512]{1,0:T(8,128)(2,1)S(1)}, bf16[64,512]{1,0:T(8,128)(2,1)S(1)}, u32[]{:S(2)}, u32[]{:S(2)}) collective-permute-start(bf16[64,512]{1,0:T(8,128)(2,1)S(1)} %fusion.28.refs_0_), channel_id=1, source_target_pairs={{0,8},{1,9},{2,10},{3,11},{4,12},{5,13},{6,14},{7,15},{8,0},{9,1},... | collective-permute-start | bytes 196616 | tf_op jit(solution)/shard_map/ppermute | solution.py:37
  101.2 6.8 %collective-permute-start.37 = (bf16[64,512]{1,0:T(8,128)(2,1)S(1)}, bf16[64,512]{1,0:T(8,128)(2,1)S(1)}, u32[]{:S(2)}, u32[]{:S(2)}) collective-permute-start(bf16[64,512]{1,0:T(8,128)(2,1)S(1)} %fusion.28.refs_0_), channel_id=1, source_target_pairs={{0,12},{1,13},{2,14},{3,15},{4,8},{5,9},{6,10},{7,11},{8,4},{9,5},... | collective-permute-start | bytes 196616 | tf_op jit(solution)/shard_map/ppermute | solution.py:37
  101.9 10.3 %collective-permute-start.38 = (bf16[64,512]{1,0:T(8,128)(2,1)S(1)}, bf16[64,512]{1,0:T(8,128)(2,1)S(1)}, u32[]{:S(2)}, u32[]{:S(2)}) collective-permute-start(bf16[64,512]{1,0:T(8,128)(2,1)S(1)} %fusion.28.refs_0_), channel_id=1, source_target_pairs={{0,16},{1,17},{2,18},{3,19},{4,20},{5,21},{6,22},{7,23},{8,24},{9,... | collective-permute-start | bytes 196616 | tf_op jit(solution)/shard_map/ppermute | solution.py:37
  105.5 9.7 %collective-permute-start.39 = (bf16[64,512]{1,0:T(8,128)(2,1)S(1)}, bf16[64,512]{1,0:T(8,128)(2,1)S(1)}, u32[]{:S(2)}, u32[]{:S(2)}) collective-permute-start(bf16[64,512]{1,0:T(8,128)(2,1)S(1)} %fusion.28.refs_0_), channel_id=1, source_target_pairs={{0,20},{1,21},{2,22},{3,23},{4,16},{5,17},{6,18},{7,19},{8,28},{9,... | collective-permute-start | bytes 196616 | tf_op jit(solution)/shard_map/ppermute | solution.py:37
  105.8 10.4 %collective-permute-start.40 = (bf16[64,512]{1,0:T(8,128)(2,1)S(1)}, bf16[64,512]{1,0:T(8,128)(2,1)S(1)}, u32[]{:S(2)}, u32[]{:S(2)}) collective-permute-start(bf16[64,512]{1,0:T(8,128)(2,1)S(1)} %fusion.28.refs_0_), channel_id=1, source_target_pairs={{0,24},{1,25},{2,26},{3,27},{4,28},{5,29},{6,30},{7,31},{8,16},{9,... | collective-permute-start | bytes 196616 | tf_op jit(solution)/shard_map/ppermute | solution.py:37
  108.0 10.1 %collective-permute-start.41 = (bf16[64,512]{1,0:T(8,128)(2,1)S(1)}, bf16[64,512]{1,0:T(8,128)(2,1)S(1)}, u32[]{:S(2)}, u32[]{:S(2)}) collective-permute-start(bf16[64,512]{1,0:T(8,128)(2,1)S(1)} %fusion.28.refs_0_), channel_id=1, source_target_pairs={{0,28},{1,29},{2,30},{3,31},{4,24},{5,25},{6,26},{7,27},{8,20},{9,... | collective-permute-start | bytes 196616 | tf_op jit(solution)/shard_map/ppermute | solution.py:37
  112.1 8.0 %collective-permute-start.25 = (bf16[144,256]{1,0:T(8,128)(2,1)S(1)}, bf16[144,256]{1,0:T(8,128)(2,1)S(1)}, u32[]{:S(2)}, u32[]{:S(2)}) collective-permute-start(bf16[144,256]{1,0:T(8,128)(2,1)S(1)} %fusion.21), channel_id=1, source_target_pairs={{0,4},{1,5},{2,6},{3,7},{4,0},{5,1},{6,2},{7,3},{8,12},{9,13},{10,... | collective-permute-start | bytes 221192 | tf_op jit(solution)/shard_map/ppermute | solution.py:37
  113.8 8.9 %collective-permute-start.26 = (bf16[144,256]{1,0:T(8,128)(2,1)S(1)}, bf16[144,256]{1,0:T(8,128)(2,1)S(1)}, u32[]{:S(2)}, u32[]{:S(2)}) collective-permute-start(bf16[144,256]{1,0:T(8,128)(2,1)S(1)} %fusion.21), channel_id=1, source_target_pairs={{0,8},{1,9},{2,10},{3,11},{4,12},{5,13},{6,14},{7,15},{8,0},{9,1},... | collective-permute-start | bytes 221192 | tf_op jit(solution)/shard_map/ppermute | solution.py:37
  114.2 9.9 %copy-start.16 = (f32[4,256,512]{2,1,0:T(8,128)}, f32[4,256,512]{2,1,0:T(8,128)S(1)}, u32[]{:S(2)}) copy-start(f32[4,256,512]{2,1,0:T(8,128)S(1)} %convert_add_fusion) | copy-start | bytes 6291460
  115.2 9.0 %collective-permute-start.27 = (bf16[144,256]{1,0:T(8,128)(2,1)S(1)}, bf16[144,256]{1,0:T(8,128)(2,1)S(1)}, u32[]{:S(2)}, u32[]{:S(2)}) collective-permute-start(bf16[144,256]{1,0:T(8,128)(2,1)S(1)} %fusion.21), channel_id=1, source_target_pairs={{0,12},{1,13},{2,14},{3,15},{4,8},{5,9},{6,10},{7,11},{8,4},{9,5},... | collective-permute-start | bytes 221192 | tf_op jit(solution)/shard_map/ppermute | solution.py:37
  116.2 10.7 %collective-permute-start.28 = (bf16[144,256]{1,0:T(8,128)(2,1)S(1)}, bf16[144,256]{1,0:T(8,128)(2,1)S(1)}, u32[]{:S(2)}, u32[]{:S(2)}) collective-permute-start(bf16[144,256]{1,0:T(8,128)(2,1)S(1)} %fusion.21), channel_id=1, source_target_pairs={{0,16},{1,17},{2,18},{3,19},{4,20},{5,21},{6,22},{7,23},{8,24},{9,... | collective-permute-start | bytes 221192 | tf_op jit(solution)/shard_map/ppermute | solution.py:37
  118.0 12.1 %collective-permute-start.29 = (bf16[144,256]{1,0:T(8,128)(2,1)S(1)}, bf16[144,256]{1,0:T(8,128)(2,1)S(1)}, u32[]{:S(2)}, u32[]{:S(2)}) collective-permute-start(bf16[144,256]{1,0:T(8,128)(2,1)S(1)} %fusion.21), channel_id=1, source_target_pairs={{0,20},{1,21},{2,22},{3,23},{4,16},{5,17},{6,18},{7,19},{8,28},{9,... | collective-permute-start | bytes 221192 | tf_op jit(solution)/shard_map/ppermute | solution.py:37
  120.2 13.3 %collective-permute-start.30 = (bf16[144,256]{1,0:T(8,128)(2,1)S(1)}, bf16[144,256]{1,0:T(8,128)(2,1)S(1)}, u32[]{:S(2)}, u32[]{:S(2)}) collective-permute-start(bf16[144,256]{1,0:T(8,128)(2,1)S(1)} %fusion.21), channel_id=1, source_target_pairs={{0,24},{1,25},{2,26},{3,27},{4,28},{5,29},{6,30},{7,31},{8,16},{9,... | collective-permute-start | bytes 221192 | tf_op jit(solution)/shard_map/ppermute | solution.py:37
  122.7 10.9 %collective-permute-start.31 = (bf16[144,256]{1,0:T(8,128)(2,1)S(1)}, bf16[144,256]{1,0:T(8,128)(2,1)S(1)}, u32[]{:S(2)}, u32[]{:S(2)}) collective-permute-start(bf16[144,256]{1,0:T(8,128)(2,1)S(1)} %fusion.21), channel_id=1, source_target_pairs={{0,28},{1,29},{2,30},{3,31},{4,24},{5,25},{6,26},{7,27},{8,20},{9,... | collective-permute-start | bytes 221192 | tf_op jit(solution)/shard_map/ppermute | solution.py:37
  124.2 12.8 %collective-permute-start.19 = (bf16[256,512]{1,0:T(8,128)(2,1)S(1)}, bf16[256,512]{1,0:T(8,128)(2,1)S(1)}, u32[]{:S(2)}, u32[]{:S(2)}) collective-permute-start(bf16[256,512]{1,0:T(8,128)(2,1)S(1)} %get-tuple-element.28), channel_id=1, source_target_pairs={{0,2},{1,3},{2,0},{3,1},{4,6},{5,7},{6,4},{7,5},{8,10},{9,11},{10,... | collective-permute-start | bytes 786440 | tf_op jit(solution)/shard_map/ppermute | solution.py:37
  126.9 10.2 %collective-permute-start.20 = (bf16[256,512]{1,0:T(8,128)(2,1)S(1)}, bf16[256,512]{1,0:T(8,128)(2,1)S(1)}, u32[]{:S(2)}, u32[]{:S(2)}) collective-permute-start(bf16[256,512]{1,0:T(8,128)(2,1)S(1)} %get-tuple-element.30), channel_id=1, source_target_pairs={{0,4},{1,5},{2,6},{3,7},{4,0},{5,1},{6,2},{7,3},{8,12},{9,13},{10,... | collective-permute-start | bytes 786440 | tf_op jit(solution)/shard_map/ppermute | solution.py:37
  130.1 9.8 %collective-permute-start.21 = (bf16[256,512]{1,0:T(8,128)(2,1)S(1)}, bf16[256,512]{1,0:T(8,128)(2,1)S(1)}, u32[]{:S(2)}, u32[]{:S(2)}) collective-permute-start(bf16[256,512]{1,0:T(8,128)(2,1)S(1)} %get-tuple-element.29), channel_id=1, source_target_pairs={{0,6},{1,7},{2,4},{3,5},{4,2},{5,3},{6,0},{7,1},{8,14},{9,15},{10,... | collective-permute-start | bytes 786440 | tf_op jit(solution)/shard_map/ppermute | solution.py:37
  (13 other events, 19.2 us)

commit v2 on v0

v2 whole, which is shorter than its diff:
```python
import jax
import jax.numpy as jnp
from jax import lax
from jax.experimental import pallas as pl
from jax.experimental.pallas import tpu as pltpu
from jax.sharding import PartitionSpec as P

BF = jnp.bfloat16
F32 = jnp.float32
AXES = ("dp", "chan")
VMEM = pl.BlockSpec(memory_space=pltpu.VMEM)
SMEM = pl.BlockSpec(memory_space=pltpu.SMEM)
ANY = pl.BlockSpec(memory_space=pl.ANY)
EDGE = 8
LANES = 128


def array(*shape, dtype=BF):
    return jax.ShapeDtypeStruct(shape, dtype)


def kernel(body, name, out, args, scratch=(), flops=0, nbytes=0, after=(), into=()):
    first, last = len(args), len(args) + len(after) + len(into)

    def run(*refs):
        body(*refs[:first], *refs[last:])

    return pl.pallas_call(
        run,
        out_shape=out,
        in_specs=[SMEM] + [VMEM] * (len(args) - 1) + [ANY] * len(after) + [VMEM] * len(into),
        out_specs=jax.tree.map(lambda _: VMEM, out),
        scratch_shapes=list(scratch),
        compiler_params=pltpu.CompilerParams(vmem_limit_bytes=16 * 1024 * 1024),
        cost_estimate=pl.CostEstimate(flops=flops, bytes_accessed=nbytes, transcendentals=0),
        input_output_aliases={len(args) + len(after) + i: i for i in range(len(into))},
        name=name,
    )(*args, *after, *into)


def gelu_parts(pre):
    cdf = 0.5 * (1.0 + lax.erf(pre * 0.7071067811865476))
    dens = jnp.exp(-0.5 * pre * pre) * 0.3989422804014327
    return pre * cdf, cdf + pre * dens


def hop(value, dp_xor, chan_xor):
    ndp, nchan = lax.axis_size("dp"), lax.axis_size("chan")
    pairs = [
        (d * nchan + c, (d ^ dp_xor) * nchan + (c ^ chan_xor))
        for d in range(ndp)
        for c in range(nchan)
    ]
    return lax.ppermute(value, AXES, pairs)


def cross(value, turn):
    ndp, nchan = lax.axis_size("dp"), lax.axis_size("chan")
    pairs = []
    for d in range(ndp):
        for c in range(nchan):
            to = (d ^ 1, c) if (c & 1) == turn else (d, c ^ 2)
            pairs.append((d * nchan + c, to[0] * nchan + to[1]))
    return lax.ppermute(value, AXES, pairs)


def meet(value, odd):
    ndp, nchan = lax.axis_size("dp"), lax.axis_size("chan")
    pairs = []
    for d in range(ndp):
        to = d + 2 if (d // 2) % 2 == odd else d - 2
        if 0 <= to < ndp:
            pairs += [(d * nchan + c, to * nchan + c) for c in range(nchan)]
    return lax.ppermute(value, AXES, pairs)


def tied(value, *others):
    return lax.optimization_barrier((value, *others))[0]


def prepare_kernel(pos, w1, b1, taps, b2, w2, rows, cot, w1_own, b1_own, taps_own, b2_own, w2_own, rows_own, cot_own):
    half = b1_own.shape[1]
    cut = pl.ds(pl.multiple_of(pos[1] * half, half), half)
    w1_own[...] = w1[:, cut]
    b1_own[...] = b1[:, cut]
    taps_own[...] = taps[:, cut]
    b2_own[...] = b2[:, cut]
    w2_own[...] = w2[cut, :]
    rows_own[...] = rows[...]
    cot_own[...] = cot[...]


def put_edges(pos, rows, edges):
    last = rows.shape[0] - 2
    odd = pos[2] & 1
    edges[0][...] = rows[pl.ds(last * (1 - odd), 2)]
    edges[1][...] = rows[pl.ds(last * odd, 2)]


def expand_kernel(order, pos, w, b, *refs):
    pieces, (hid, slope, *edges, pre) = refs[: len(order)], refs[len(order) :]
    n, ncols, cin = pieces[0].shape
    half = hid.shape[2]
    for k, piece in zip(order, pieces):
        at = (pos[0] ^ k) * n
        pre[...] = (
            jnp.dot(piece[...].reshape(n * ncols, cin), w[...], preferred_element_type=F32) + b[...]
        ).reshape(n, ncols, half)

        def body(r, carry, at=at):
            h, s = gelu_parts(pre[r])
            hid[at + r] = h.astype(BF)
            slope[at + r] = s.astype(BF)
            return carry

        lax.fori_loop(0, n, body, 0)
    if edges:
        put_edges(pos, hid, edges)


def load_padded(pos, pad, cut, mid, near=None, far=None, rows=None):
    nrows, ncols, _ = mid.shape
    zeros = jnp.zeros((nrows + 4, EDGE, LANES), F32)
    pad[:, 0:EDGE, :] = zeros
    pad[:, EDGE + ncols :, :] = zeros
    if near is not None:
        a, b = near[:, :, cut].astype(F32), far[:, :, cut].astype(F32)
        odd = (pos[2] & 1) == 1
        pad[0:2, EDGE : EDGE + ncols, :] = jnp.where(odd, a, b)
        pad[nrows + 2 :, EDGE : EDGE + ncols, :] = jnp.where(odd, b, a)

    def body(r, carry):
        pad[r + 2, EDGE : EDGE + ncols, :] = mid[r, :, cut].astype(F32)
        return carry

    for lo, hi in rows or ((0, nrows),):
        lax.fori_loop(lo, hi, body, 0)


def conv_tiles(pad, taps, cut, ncols, starts, nr, cols, flip, emit):
    def body(i, carry):
        w0 = i * cols
        for r0 in starts:
            acc = [None] * nr
            for j in range(5):
                xs = [pad[r0 + q, pl.ds(w0 + (EDGE - 2) + j, cols), :] for q in range(nr + 4)]
                for q in range(5):
                    t = 5 * q + j
                    t = 24 - t if flip else t
                    for r in range(nr):
                        term = taps[t : t + 1, cut] * xs[r + q]
                        acc[r] = term if acc[r] is None else acc[r] + term
            emit(r0, pl.ds(pl.multiple_of(w0, cols), cols), acc)
        return carry

    lax.fori_loop(0, ncols // cols, body, 0)


def cuts(half):
    return [slice(c, c + LANES) for c in range(0, half, LANES)]


def middle_kernel(inner, pos, taps, bias, *refs):
    (mid, mixed, slope, pad) = refs if inner else (refs[0], *refs[3:])
    near, far = (None, None) if inner else refs[1:3]
    nrows, ncols, half = mid.shape
    for cut in cuts(half):
        load_padded(pos, pad, cut, mid, near, far, None if inner else ((0, 4), (nrows - 4, nrows)))
        add = bias[:, cut]

        def emit(r0, w, acc, cut=cut, add=add):
            for r in range(len(acc)):
                m, s = gelu_parts(acc[r] + add)
                mixed[r0 + r, w, cut] = m.astype(BF)
                slope[r0 + r, w, cut] = s

        if inner:
            conv_tiles(pad, taps, cut, ncols, range(2, nrows - 2, 4), 4, 16, False, emit)
        else:
            conv_tiles(pad, taps, cut, ncols, (0, nrows - 2), 2, 32, False, emit)


def project_kernel(order, pos, weights, slope, *refs):
    pieces, (gp, *edges) = refs[: len(order)], refs[len(order) :]
    n, ncols, cin = pieces[0].shape
    half = gp.shape[2]
    for k, piece in zip(order, pieces):
        at = (pos[0] ^ k) * n
        res = lax.dot_general(
            piece[...].reshape(n * ncols, cin), weights[...], (((1,), (1,)), ((), ())), preferred_element_type=F32
        )
        gp[pl.ds(at, n)] = (res.reshape(n, ncols, half) * slope[pl.ds(at, n)]).astype(BF)
    if edges:
        put_edges(pos, gp, edges)


def outer_sum(pos, total, pieces, values, swap):
    n, ncols, _ = pieces[0].shape
    for k, piece in enumerate(pieces):
        a = piece[...].reshape(n * ncols, -1)
        b = values[pl.ds((pos[0] ^ k) * n, n)].reshape(n * ncols, -1)
        if swap:
            a, b = b, a
        part = lax.dot_general(a, b, (((0,), (0,)), ((), ())), preferred_element_type=F32)
        if k == 0:
            total[0 : part.shape[0], :] = part
        else:
            total[0 : part.shape[0], :] += part


def w2_kernel(pos, mixed, *refs):
    pieces, outs, total = refs[:8], refs[8:-1], refs[-1]
    outer_sum(pos, total, pieces, mixed, True)
    n = outs[0].shape[0]
    for k, ref in enumerate(outs):
        ref[...] = total[pl.ds(pl.multiple_of((pos[2] ^ k) * n, n), n), :].astype(ref.dtype)


def taps_kernel(pos, mid, near, far, gp, small, pad, gpf):
    nrows, ncols, half = mid.shape
    small[...] = jnp.zeros_like(small)
    for cut in cuts(half):
        load_padded(pos, pad, cut, mid, near, far)

        def widen(r, carry, cut=cut):
            gpf[r] = gp[r, :, cut].astype(F32)
            return carry

        lax.fori_loop(0, nrows, widen, 0)

        def body(i, accs):
            accs = list(accs)
            w0 = i * 8
            for j in range(5):
                xs = [pad[q, pl.ds(w0 + (EDGE - 2) + j, 8), :] for q in range(4)]
                for r in range(nrows):
                    xs.append(pad[r + 4, pl.ds(w0 + (EDGE - 2) + j, 8), :])
                    g = gpf[r, pl.ds(pl.multiple_of(w0, 8), 8), :]
                    for q in range(5):
                        accs[5 * q + j] = accs[5 * q + j] + xs[r + q] * g
                    if j == 0:
                        accs[25] = accs[25] + g
            return tuple(accs)

        zero = jnp.zeros((8, LANES), F32)
        accs = lax.fori_loop(0, ncols // 8, body, (zero,) * 26)
        for t in range(26):
            small[t : t + 1, cut] = jnp.sum(accs[t], axis=0, keepdims=True)


def back_kernel(pos, taps, mid, near, far, slope, act, grad_b, pad, total):
    nrows, ncols, half = mid.shape
    for cut in cuts(half):
        load_padded(pos, pad, cut, mid, near, far)
        total[...] = jnp.zeros_like(total)

        def emit(r0, w, acc, cut=cut):
            part = jnp.zeros((8, LANES), F32)
            for r in range(4):
                a = (acc[r] * slope[r0 + r, w, cut].astype(F32)).astype(BF)
                act[r0 + r, w, cut] = a
                part = part + jnp.sum(a.astype(F32).reshape(-1, 8, LANES), axis=0)
            total[...] += part

        conv_tiles(pad, taps, cut, ncols, range(0, nrows, 4), 4, 16, True, emit)
        grad_b[:, cut] = jnp.sum(total[...], axis=0, keepdims=True)


def w1_kernel(pos, act, small, grad_b, *refs):
    pieces, outs, total = refs[:8], refs[8:-1], refs[-1]
    outer_sum(pos, total, pieces, act, False)
    cin = pieces[0].shape[2]
    total[cin:, :] = small[...]
    total[cin + 26 : cin + 27, :] = grad_b[...]
    chunks = len(outs)
    n, m = cin // chunks, small.shape[0] // chunks
    for k, ref in enumerate(outs):
        at = pos[2] ^ k
        ref[0:n, :] = total[pl.ds(pl.multiple_of(at * n, n), n), :].astype(ref.dtype)
        ref[n:, :] = total[pl.ds(pl.multiple_of(cin + at * m, m), m), :].astype(ref.dtype)


def share(pos, act, w, chip_xor, core):
    ncols, half = act.shape[1:]
    n = act.shape[0] // 8
    at = (((pos[0] // 2) ^ chip_xor) * 2 + core) * n
    return lax.dot_general(
        act[pl.ds(at, n)].reshape(n * ncols, half), w[...], (((1,), (1,)), ((), ())), preferred_element_type=F32
    ).reshape(n, ncols, -1)


def core_kernel(pos, act, w, out):
    for k in range(4):
        out[k] = share(pos, act, w, k, 1 - pos[3]).astype(BF)


def chip_send_kernel(pos, act, w, other, out):
    for i, k in enumerate((2 - pos[3], 3)):
        out[i] = (share(pos, act, w, k, pos[3]) + other[k].astype(F32)).astype(BF)


def chip_keep_kernel(pos, act, w, other, out):
    for i, k in enumerate((0, 1 + pos[3])):
        out[i] = share(pos, act, w, k, pos[3]) + other[k].astype(F32)


def forward_kernel(pos, kept, arrived, out):
    out[...] = (kept[1] + arrived[1].astype(F32)).astype(BF)


def finish_kernel(pos, cot, kept, arrived, last, out):
    out[...] = (cot[...].astype(F32) + (kept[0] + arrived[0].astype(F32) + last[...].astype(F32))).astype(BF)


def column_kernel(pos, *refs):
    blocks, out = refs[:-1], refs[-1]
    for k, block in enumerate(blocks):
        out[pos[2] ^ k] = block[...]


def w2_place_kernel(pos, blocks, out):
    some, _, n, _ = blocks[0].shape
    groups = some * len(blocks)
    for b, block in enumerate(blocks):
        for a in range(some):
            for x in range(2):
                at = (pos[1] ^ x) * groups + (pos[2] ^ (len(blocks) * a + b))
                out[pl.ds(pl.multiple_of(at * n, n), n), :] = block[a, x].astype(F32)


def w1_place_kernel(pos, mine, other, out, grad_k, grad_bd, grad_b1, small):
    g, rows, half = mine.shape
    n = out.shape[0] // g
    m = rows - n
    for k, col in enumerate((mine, other)):
        cut = pl.ds(pl.multiple_of((pos[1] ^ k) * half, half), half)
        for i in range(g):
            out[i * n : (i + 1) * n, cut] = col[i, 0:n, :].astype(F32)
            small[i * m : (i + 1) * m, cut] = col[i, n:, :].astype(F32)
    grad_k[...] = small[0:25, :]
    grad_bd[...] = small[25:26, :]
    grad_b1[...] = small[26:27, :]


def last_kernel(pos, cot, kept, arrived, last, mine, other, *refs):
    blocks, (out, out_w2, out_w1, grad_k, grad_bd, grad_b1, small) = refs[:-7], refs[-7:]
    finish_kernel(pos, cot, kept, arrived, last, out)
    w2_place_kernel(pos, blocks, out_w2)
    w1_place_kernel(pos, mine, other, out_w1, grad_k, grad_bd, grad_b1, small)


def summed(own, sends):
    for k, send in enumerate(sends):
        own = own + hop(send, 2 * (k + 1), 0).astype(F32)
    return own.astype(BF)


def halved(chunks):
    arrived = hop(jnp.stack([chunks[1], chunks[3]]), 2, 0).astype(F32)
    return chunks[0] + arrived[0], chunks[2] + arrived[1]


def column(pos, chunk, groups, after=()):
    blocks = [hop(chunk, 2 * k, 0) if k else chunk for k in range(groups)]
    return kernel(column_kernel, "column", array(groups, *chunk.shape), (pos, *blocks), after=after)


def shards(inputs, cotangent, expand_w, expand_b, depth_k, depth_b, project_w):
    chan, dp = lax.axis_index("chan"), lax.axis_index("dp")
    pair, zpos = dp & 1, dp >> 1
    groups = lax.axis_size("dp") // 2
    own_rows, ncols, cin = inputs.shape
    nrows = 8 * own_rows
    hslice = expand_w.shape[1]
    half = hslice // 2
    npix = nrows * ncols
    pos = jnp.stack([pair * 4 + chan, pair, zpos, chan & 1]).astype(jnp.int32)

    full = array(nrows, ncols, half)
    mm = vpu = dict(flops=1024, nbytes=1024)
    pad = pltpu.VMEM((nrows + 4, ncols + 2 * EDGE, LANES), F32)

    mine = array(*inputs.shape)
    w1, b1, taps, bd, w2, rows_own, cot_own = kernel(
        prepare_kernel, "prepare",
        (array(cin, half), array(1, half, dtype=F32), array(25, half, dtype=F32), array(1, half, dtype=F32),
         array(half, cin), mine, mine),
        (pos, expand_w, expand_b.reshape(1, hslice), depth_k, depth_b.reshape(1, hslice), project_w, inputs, cotangent),
    )

    def expand(order, into=(), after=(), edges=()):
        return kernel(
            lambda *refs: expand_kernel(order, *refs), "expand%d" % order[0], (full, full) + edges,
            (pos, w1, b1, *(in_pieces[k] for k in order)), [pltpu.VMEM((own_rows, ncols, half), F32)],
            into=into, after=after, **mm,
        )

    in_pieces = {0: rows_own, 1: hop(inputs, 0, 1)}
    cot_pieces = {0: cot_own, 1: hop(cotangent, 0, 1)}
    steps = {4: (1, 0), 2: (0, 2), 6: (1, 2)}
    for k, step in steps.items():
        in_pieces[k] = hop(inputs, *step)
    first = expand((0, 1), after=(cot_pieces[1],))
    for k in steps:
        in_pieces[k + 1] = hop(tied(in_pieces[k], first[0]), 0, 1)
    cot_start = tied(cotangent, in_pieces[2], in_pieces[4])
    for k, step in steps.items():
        cot_pieces[k] = hop(tied(cot_start, in_pieces[6]) if k == 6 else cot_start, *step)
    in_pieces = [in_pieces[k] for k in range(8)]
    edges = (array(2, ncols, half),) * 2
    hidden, slope_one, *sent = expand((3, 5, 7), expand((2, 4, 6), first), edges=edges)
    hid_near, hid_far = meet(sent[0], 0), meet(sent[1], 1)

    mixed, slope_two = kernel(
        lambda *refs: middle_kernel(True, *refs), "inner", (full, array(nrows, ncols, half, dtype=F32)),
        (pos, taps, bd, hidden), [pad], **vpu,
    )
    mixed, slope_two = kernel(
        lambda *refs: middle_kernel(False, *refs), "outer", (full, array(nrows, ncols, half, dtype=F32)),
        (pos, taps, bd, hidden, hid_near, hid_far), [pad], into=(mixed, slope_two), **vpu,
    )
    for k in steps:
        cot_pieces[k + 1] = hop(tied(cot_pieces[k], mixed), 0, 1)

    def project(order, into=(), after=(), edges=()):
        return kernel(
            lambda *refs: project_kernel(order, *refs), "project%d" % order[0], (full,) + edges,
            (pos, w2, slope_two, *(cot_pieces[k] for k in order)), into=into, after=after, **mm,
        )

    def chunk_outs(rows, width):
        return (array(rows, width, dtype=F32),) + (array(rows, width),) * (groups - 1)

    half_done = project((0, 1, 2, 4, 6))
    w2_chunks = kernel(
        w2_kernel, "w2", chunk_outs(half // groups, cin), (pos, mixed, *(cot_pieces[k] for k in range(8))),
        [pltpu.VMEM((half, cin), F32)], after=half_done, **mm,
    )
    grad_pre, *sent = project((3, 5, 7), half_done, (w2_chunks[0],), edges)
    gp_near, gp_far = meet(sent[0], 0), meet(sent[1], 1)
    tail = 16 * groups
    small = kernel(
        taps_kernel, "taps", array(tail, half, dtype=F32), (pos, hidden, hid_near, hid_far, grad_pre),
        [pad, pltpu.VMEM((nrows, ncols, LANES), F32)], **vpu,
    )
    four = groups == 4
    w2_halves = halved(w2_chunks) if four else w2_chunks[:1]
    grad_act, grad_b1 = kernel(
        back_kernel, "back", (full, array(1, half, dtype=F32)),
        (pos, taps, grad_pre, gp_near, gp_far, slope_one), [pad, pltpu.VMEM((8, LANES), F32)],
        after=(small, *w2_halves), **vpu,
    )
    if four:
        w2_sent = hop(tied(w2_halves[1], small).astype(BF), 4, 0).astype(F32)
        w2_chunk = (tied(w2_halves[0], grad_act) + w2_sent).astype(BF)
    else:
        w2_chunk = summed(tied(w2_chunks[0], grad_act), w2_chunks[1:])
    w2_pair = jnp.stack([w2_chunk, hop(w2_chunk, 1, 0)])

    block = (own_rows, ncols, cin)
    two = (2, *block)
    to_core = kernel(core_kernel, "core", array(4, *block), (pos, grad_act, w1), after=(w2_chunk,), **mm)
    from_core = hop(to_core, 0, 1)
    w1_own, *w1_sends = kernel(
        w1_kernel, "w1", chunk_outs((cin + tail) // groups, half), (pos, grad_act, small, grad_b1, *in_pieces),
        [pltpu.VMEM((cin + tail, half), F32)], after=(w2_chunk, to_core), **mm,
    )
    going = kernel(
        chip_send_kernel, "chip_send", array(*two), (pos, grad_act, w1, from_core), after=(w1_own,), **mm
    )
    w2_pair = tied(w2_pair, going)
    if four:
        w2_quad = jnp.stack([w2_pair, hop(w2_pair, 4, 0)])
        w2_all = (w2_quad, hop(w2_quad, 2, 0))
    else:
        w2_all = [(hop(w2_pair, 2 * k, 0) if k else w2_pair)[None] for k in range(groups)]
    arrived = cross(going, 0)
    kept = kernel(
        chip_keep_kernel, "chip_keep", array(*two, dtype=F32), (pos, grad_act, w1, from_core), after=(going,), **mm
    )
    forward = kernel(forward_kernel, "forward", array(*block), (pos, kept, arrived), **mm)
    onward = cross(forward, 1)

    w1_chunk = summed(tied(w1_own, kept), w1_sends)
    w1_col = column(pos, w1_chunk, groups)
    line = array(1, hslice, dtype=F32)
    input_grad, out_w2, out_w1, out_k, out_bd, out_b1 = kernel(
        last_kernel, "last",
        (array(*block), array(hslice, cin, dtype=F32), array(cin, hslice, dtype=F32), array(25, hslice, dtype=F32), line, line),
        (pos, cot_own, kept, arrived, onward, w1_col, hop(w1_col, 1, 0), *w2_all),
        [pltpu.VMEM((tail, hslice), F32)],
    )
    return (input_grad, out_w1, out_b1.reshape(hslice), out_k, out_bd.reshape(hslice), out_w2)


def solution(mesh):
    in_specs = (
        P(("dp", "chan"), None, None),
        P(("dp", "chan"), None, None),
        P(None, "chan"),
        P("chan"),
        P(None, "chan"),
        P("chan"),
        P("chan", None),
    )
    out_specs = (
        P(("dp", "chan"), None, None),
        P(None, "chan"),
        P("chan"),
        P(None, "chan"),
        P("chan"),
        P("chan", None),
    )
    return jax.shard_map(shards, mesh=mesh, in_specs=in_specs, out_specs=out_specs, check_vma=False)
```

time: 260 us -> 97 us (0.37)
  waiting for transfers between devices: 115 us -> 18.8 us
  other arithmetic: 57.6 us -> 0.26 us
  blocking collectives: 40.9 us -> 0 us
  Pallas kernels: 0 us -> 32.4 us
  starting transfers between devices: 10.7 us -> 36.9 us
  matrix products: 17.7 us -> 0 us
  between operations: 14 us -> 0.98 us
    psum x1 -> x0, waiting for transfers between devices: 44.2 us -> none  [shards(): summed = lax.psum((grad_w1, grad_b1, grad_k, grad_bd, grad_w2), 'dp')]
    psum x1 -> x0, blocking collectives: 40.9 us -> none  [shards(): summed = lax.psum((grad_w1, grad_b1, grad_k, grad_bd, grad_w2), 'dp')]
    pallas_call x0 -> x18, Pallas kernels: none -> 32.4 us  [kernel(): pl.pallas_call(run, out_shape=out, in_specs=[SMEM] + [VMEM] * (len(args)...]
    reduce_scatter x1 -> x0, waiting for transfers between devices: 31 us -> none  [shards(): lax.psum_scatter(jnp.einsum('rwh,ch->rwc', grad_act, expand_w, preferred_...]
    add x1, other arithmetic: 27.2 us -> 0.04 us  [halved(): return (chunks[0] + arrived[0], chunks[2] + arrived[1])]
    ppermute x4 -> x33, starting transfers between devices: 10.4 us -> 36.9 us  [the longest x27 32.3 us: hop(): return lax.ppermute(value, AXES, pairs)]
    reduce_sum x2 -> x0, other arithmetic: 25.9 us -> none  [the longest x1 18.6 us: shards(): jnp.sum(padded[row_tap:row_tap + nrows, col_tap:col_tap + ncols] * grad_p...]
    all_gather x2 -> x0, waiting for transfers between devices: 20.3 us -> none  [the longest x1 20.3 us: shards(): lax.all_gather(inputs, 'chan', axis=0, tiled=True)]
  transfers between devices with their start and end apart: 8 -> 33, of which waited for: 6 -> 8; matrix products, arithmetic and copies ran while one was open for 22% -> 0% of each run, Pallas kernels for 0% -> 29%
where the time goes in v2:
time: 97 us; the launch traced here: 95.5 us
  starting transfers between devices  36.9 us (38%)
  Pallas kernels  32.4 us (33%)
  waiting for transfers between devices  18.8 us (19%)
  local copies, waits for them, and re-layouts  6.18 us (6%)
  between operations  0.98 us (1%)
    pallas_call x18, Pallas kernels, kernel(): pl.pallas_call(run, out_shape=out, in_specs=[SMEM] + [VMEM] * (len(args)...  32.4 us
    ppermute x27, starting transfers between devices, hop(): return lax.ppermute(value, AXES, pairs)  32.3 us
    ppermute x27, waiting for transfers between devices, hop(): return lax.ppermute(value, AXES, pairs)  18.8 us
    unnamed x14, local copies, waits for them, and re-layouts  6.18 us
    ppermute x4, starting transfers between devices, meet(): return lax.ppermute(value, AXES, pairs)  3.27 us
  transfers between devices with their start and end apart: 33, of which 8 were waited for; matrix products, arithmetic and copies ran while one was open for 0% of the time, Pallas kernels for 29%

profile of v2, /device:TPU:0, one launch (start us, length us, event | category | flops | bytes accessed | tf_op | source)
XLA Modules:
  0.0 95.5 jit_solution(15835527643065233798)
XLA Ops:
  1.2 2.9 %collective-permute-start = (bf16[2,128,512]{2,1,0:T(8,128)(2,1)}, bf16[2,128,512]{2,1,0:T(8,128)(2,1)S(1)}, u32[]{:S(2)}, u32[]{:S(2)}) collective-permute-start(bf16[2,128,512]{2,1,0:T(8,128)(2,1)} %refs_6_.1), channel_id=1, source_target_pairs={{0,2},{1,3},{2,0},{3,1},{4,6},{5,7},{6,4},{7,5},{8,10},{9,11},{10,... | collective-permute-start | bytes 786440 | tf_op jit(solution)/shard_map/ppermute | solution.py:54
  4.2 1.5 %collective-permute-start.4 = (bf16[2,128,512]{2,1,0:T(8,128)(2,1)}, bf16[2,128,512]{2,1,0:T(8,128)(2,1)S(1)}, u32[]{:S(2)}, u32[]{:S(2)}) collective-permute-start(bf16[2,128,512]{2,1,0:T(8,128)(2,1)} %refs_6_.1), channel_id=1, source_target_pairs={{0,4},{1,5},{2,6},{3,7},{4,0},{5,1},{6,2},{7,3},{8,12},{9,13},{10,... | collective-permute-start | bytes 786440 | tf_op jit(solution)/shard_map/ppermute | solution.py:54
  5.7 1.0 %copy-done = bf16[512,512]{1,0:T(8,128)(2,1)S(1)} copy-done((bf16[512,512]{1,0:T(8,128)(2,1)S(1)}, bf16[512,512]{1,0:T(8,128)(2,1)}, u32[]{:S(2)}) %copy-start) | copy-done | bytes 524312
  6.8 1.0 %copy-done.1 = bf16[512,512]{1,0:T(8,128)(2,1)S(1)} copy-done((bf16[512,512]{1,0:T(8,128)(2,1)S(1)}, bf16[512,512]{1,0:T(8,128)(2,1)}, u32[]{:S(2)}) %copy-start.1) | copy-done | bytes 524312
  7.8 0.9 copy-done.2
  8.8 0.9 copy-done.3
  9.7 0.8 copy-done.4
  10.6 0.7 copy-done.5
  11.3 0.7 copy-done.6
  11.9 0.6 prepare.1
  12.6 1.4 %expand0.1 = (bf16[16,128,256]{2,1,0:T(8,128)(2,1)S(1)}, bf16[16,128,256]{2,1,0:T(8,128)(2,1)S(1)}) custom-call(s32[4]{0:T(128)S(1)} %pad_add_fusion.refs_0_, bf16[512,256]{1,0:T(8,128)(2,1)S(1)} %get-tuple-element.60.refs_1_.refs_2_, f32[1,256]{1,0:T(1,128)S(1)} %get-tuple-element.61.refs_2_, bf16[2,128,512]{2,1,0:T(8,128)(2,1)S(1)} %get-tuple-element.62.refs_3_.refs_4_, ...), custom_call_target="tpu_custom_call" | custom-call | flops 1024 | bytes 1024 | tf_op jit(solution)/shard_map/expand0/pallas_call | solution.py:28
  14.5 3.2 %collective-permute-done.6.refs_5_.refs_10_ = bf16[2,128,512]{2,1,0:T(8,128)(2,1)S(1)} collective-permute-done((bf16[2,128,512]{2,1,0:T(8,128)(2,1)}, bf16[2,128,512]{2,1,0:T(8,128)(2,1)S(1)}, u32[]{:S(2)}, u32[]{:S(2)}) %collective-permute-start.6) | collective-permute-done | bytes 262176 | tf_op jit(solution)/shard_map/ppermute | solution.py:54
  17.7 1.7 %collective-permute-start.10 = (bf16[2,128,512]{2,1,0:T(8,128)(2,1)S(1)}, bf16[2,128,512]{2,1,0:T(8,128)(2,1)S(1)}, u32[]{:S(2)}, u32[]{:S(2)}) collective-permute-start(bf16[2,128,512]{2,1,0:T(8,128)(2,1)S(1)} %copy-done.3), channel_id=1, source_target_pairs={{0,2},{1,3},{2,0},{3,1},{4,6},{5,7},{6,4},{7,5},{8,10},{9,11},{10,... | collective-permute-start | bytes 786440 | tf_op jit(solution)/shard_map/ppermute | solution.py:54
  19.5 1.5 %collective-permute-start.12 = (bf16[2,128,512]{2,1,0:T(8,128)(2,1)S(1)}, bf16[2,128,512]{2,1,0:T(8,128)(2,1)S(1)}, u32[]{:S(2)}, u32[]{:S(2)}) collective-permute-start(bf16[2,128,512]{2,1,0:T(8,128)(2,1)S(1)} %copy-done.3), channel_id=1, source_target_pairs={{0,4},{1,5},{2,6},{3,7},{4,0},{5,1},{6,2},{7,3},{8,12},{9,13},{10,... | collective-permute-start | bytes 786440 | tf_op jit(solution)/shard_map/ppermute | solution.py:54
  21.2 1.7 %expand2.1 = (bf16[16,128,256]{2,1,0:T(8,128)(2,1)S(1)}, bf16[16,128,256]{2,1,0:T(8,128)(2,1)S(1)}) custom-call(s32[4]{0:T(128)S(1)} %pad_add_fusion.refs_0_, bf16[512,256]{1,0:T(8,128)(2,1)S(1)} %get-tuple-element.60.refs_1_.refs_2_, f32[1,256]{1,0:T(1,128)S(1)} %get-tuple-element.61.refs_2_, ...), custom_call_target="tpu_custom_call", output_to_operand_aliasing={{0}: (6, {}), {1}: (7, {})} | custom-call | flops 1024 | bytes 1024 | tf_op jit(solution)/shard_map/expand2/pallas_call | solution.py:28
  23.0 1.7 %expand3.1 = (bf16[16,128,256]{2,1,0:T(8,128)(2,1)S(1)}, bf16[16,128,256]{2,1,0:T(8,128)(2,1)S(1)}, bf16[2,128,256]{2,1,0:T(8,128)(2,1)S(1)}, bf16[2,128,256]{2,1,0:T(8,128)(2,1)S(1)}) custom-call(s32[4]{0:T(128)S(1)} %pad_add_fusion.refs_0_, bf16[512,256]{1,0:T(8,128)(2,1)S(1)} %get-tuple-element.60.refs_1_.refs_2_, ...), custom_call_target="tpu_custom_call", output_to_operand_aliasing={{0}: (6, {}), {1}: (7, {})} | custom-call | flops 1024 | bytes 1024 | tf_op jit(solution)/shard_map/expand3/pallas_call | solution.py:28
  24.7 1.9 %collective-permute-start.8 = (bf16[2,128,256]{2,1,0:T(8,128)(2,1)S(1)}, bf16[2,128,256]{2,1,0:T(8,128)(2,1)S(1)}, u32[]{:S(2)}, u32[]{:S(2)}) collective-permute-start(bf16[2,128,256]{2,1,0:T(8,128)(2,1)S(1)} %get-tuple-element.71), channel_id=1, source_target_pairs={{0,8},{1,9},{2,10},{3,11},{4,12},{5,13},{6,14},{7,15},{8,0},{9,1},... | collective-permute-start | bytes 393224 | tf_op jit(solution)/shard_map/ppermute | solution.py:74
  26.6 0.7 collective-permute-start.9
  27.3 4.7 %inner.1 = (bf16[16,128,256]{2,1,0:T(8,128)(2,1)S(1)}, f32[16,128,256]{2,1,0:T(8,128)S(1)}) custom-call(s32[4]{0:T(128)S(1)} %pad_add_fusion.refs_0_, f32[25,256]{1,0:T(8,128)S(1)} %get-tuple-element.57.refs_1_, f32[1,256]{1,0:T(1,128)S(1)} %get-tuple-element.59.refs_2_, bf16[16,128,256]{2,1,0:T(8,128)(2,1)S(1)} %get-tuple-element.70.refs_3_.refs_1_), custom_call_target="tpu_custom_call" | custom-call | flops 1024 | bytes 1024 | tf_op jit(solution)/shard_map/inner/pallas_call | solution.py:28
  32.0 2.0 %outer.1 = (bf16[16,128,256]{2,1,0:T(8,128)(2,1)S(1)}, f32[16,128,256]{2,1,0:T(8,128)S(1)}) custom-call(s32[4]{0:T(128)S(1)} %pad_add_fusion.refs_0_, f32[25,256]{1,0:T(8,128)S(1)} %get-tuple-element.57.refs_1_, f32[1,256]{1,0:T(1,128)S(1)} %get-tuple-element.59.refs_2_, ...), custom_call_target="tpu_custom_call", output_to_operand_aliasing={{0}: (6, {}), {1}: (7, {})} | custom-call | flops 1024 | bytes 1024 | tf_op jit(solution)/shard_map/outer/pallas_call | solution.py:28
  34.7 1.1 %project0.1.refs_10_.refs_7_ = bf16[16,128,256]{2,1,0:T(8,128)(2,1)S(1)} custom-call(s32[4]{0:T(128)S(1)} %pad_add_fusion.refs_0_, bf16[256,512]{1,0:T(8,128)(2,1)S(1)} %get-tuple-element.58.refs_1_, f32[16,128,256]{2,1,0:T(8,128)S(1)} %get-tuple-element.75.refs_2_, bf16[2,128,512]{2,1,0:T(8,128)(2,1)S(1)} %get-tuple-element.56.refs_3_.refs_2_.refs_1_, ...), custom_call_target="tpu_custom_call" | custom-call | flops 1024 | bytes 1024 | tf_op jit(solution)/shard_map/project0/pallas_call | solution.py:28
  36.4 1.3 %w2.1 = (f32[64,512]{1,0:T(8,128)S(1)}, bf16[64,512]{1,0:T(8,128)(2,1)S(1)}, bf16[64,512]{1,0:T(8,128)(2,1)S(1)}, bf16[64,512]{1,0:T(8,128)(2,1)S(1)}) custom-call(s32[4]{0:T(128)S(1)} %pad_add_fusion.refs_0_, bf16[16,128,256]{2,1,0:T(8,128)(2,1)S(1)} %get-tuple-element.77.refs_1_, bf16[2,128,512]{2,1,0:T(8,128)(2,1)S(1)} %get-tuple-element.56.refs_3_.refs_2_.refs_1_, ...), custom_call_target="tpu_custom_call" | custom-call | flops 1024 | bytes 1024 | tf_op jit(solution)/shard_map/w2/pallas_call | solution.py:28
  37.8 4.5 %collective-permute-start.18 = (bf16[2,64,512]{2,1,0:T(8,128)(2,1)S(1)}, bf16[2,64,512]{2,1,0:T(8,128)(2,1)S(1)}, u32[]{:S(2)}, u32[]{:S(2)}) collective-permute-start(bf16[2,64,512]{2,1,0:T(8,128)(2,1)S(1)} %pad_maximum_fusion.1), channel_id=1, source_target_pairs={{0,8},{1,9},{2,10},{3,11},{4,12},{5,13},{6,14},{7,15},{8,0},{9,1},... | collective-permute-start | bytes 393224 | tf_op jit(solution)/shard_map/ppermute | solution.py:54
  42.2 1.0 %project3.1 = (bf16[16,128,256]{2,1,0:T(8,128)(2,1)S(1)}, bf16[2,128,256]{2,1,0:T(8,128)(2,1)S(1)}, bf16[2,128,256]{2,1,0:T(8,128)(2,1)S(1)}) custom-call(s32[4]{0:T(128)S(1)} %pad_add_fusion.refs_0_, bf16[256,512]{1,0:T(8,128)(2,1)S(1)} %get-tuple-element.58.refs_1_, ...), custom_call_target="tpu_custom_call", output_to_operand_aliasing={{0}: (7, {})} | custom-call | flops 1024 | bytes 1024 | tf_op jit(solution)/shard_map/project3/pallas_call | solution.py:28
  43.3 0.7 collective-permute-start.17
  43.9 4.8 %taps.1.refs_6_.refs_2_ = f32[64,256]{1,0:T(8,128)S(1)} custom-call(s32[4]{0:T(128)S(1)} %pad_add_fusion.refs_0_, bf16[16,128,256]{2,1,0:T(8,128)(2,1)S(1)} %get-tuple-element.70.refs_3_.refs_1_, bf16[2,128,256]{2,1,0:T(8,128)(2,1)S(1)} %collective-permute-done.8.refs_4_.refs_2_, bf16[2,128,256]{2,1,0:T(8,128)(2,1)S(1)} %collective-permute-done.9.refs_5_.refs_3_, ...), custom_call_target="tpu_custom_call" | custom-call | flops 1024 | bytes 1024 | tf_op jit(solution)/shard_map/taps/pallas_call | solution.py:28
  48.9 4.8 %collective-permute-start.19 = (bf16[64,512]{1,0:T(8,128)(2,1)S(1)}, bf16[64,512]{1,0:T(8,128)(2,1)S(1)}, u32[]{:S(2)}, u32[]{:S(2)}) collective-permute-start(bf16[64,512]{1,0:T(8,128)(2,1)S(1)} %convert_element_type.29), channel_id=1, source_target_pairs={{0,16},{1,17},{2,18},{3,19},{4,20},{5,21},{6,22},{7,23},{8,24},{9,... | collective-permute-start | bytes 196616 | tf_op jit(solution)/shard_map/ppermute | solution.py:54
  53.7 4.7 %back.1 = (bf16[16,128,256]{2,1,0:T(8,128)(2,1)S(1)}, f32[1,256]{1,0:T(1,128)S(1)}) custom-call(s32[4]{0:T(128)S(1)} %pad_add_fusion.refs_0_, f32[25,256]{1,0:T(8,128)S(1)} %get-tuple-element.57.refs_1_, bf16[16,128,256]{2,1,0:T(8,128)(2,1)S(1)} %get-tuple-element.83.refs_4_.refs_2_, bf16[2,128,256]{2,1,0:T(8,128)(2,1)S(1)} %collective-permute-done.16.refs_3_, ...), custom_call_target="tpu_custom_call" | custom-call | flops 1024 | bytes 1024 | tf_op jit(solution)/shard_map/back/pallas_call | solution.py:28
  58.4 1.0 %core.1.refs_13_ = bf16[4,2,128,512]{3,2,1,0:T(8,128)(2,1)S(1)} custom-call(s32[4]{0:T(128)S(1)} %pad_add_fusion.refs_0_, bf16[16,128,256]{2,1,0:T(8,128)(2,1)S(1)} %get-tuple-element.90.refs_1_, bf16[512,256]{1,0:T(8,128)(2,1)S(1)} %get-tuple-element.60.refs_1_.refs_2_, bf16[64,512]{1,0:T(8,128)(2,1)S(1)} %add_convert_fusion.1.refs_3_.refs_12_), custom_call_target="tpu_custom_call" | custom-call | flops 1024 | bytes 1024 | tf_op jit(solution)/shard_map/core/pallas_call | solution.py:28
  59.5 1.6 %collective-permute-start.30 = (bf16[64,512]{1,0:T(8,128)(2,1)S(1)}, bf16[64,512]{1,0:T(8,128)(2,1)S(1)}, u32[]{:S(2)}, u32[]{:S(2)}) collective-permute-start(bf16[64,512]{1,0:T(8,128)(2,1)S(1)} %add_convert_fusion.1.refs_3_.refs_12_), channel_id=1, source_target_pairs={{0,4},{1,5},{2,6},{3,7},{4,0},{5,1},{6,2},{7,3},{8,12},{9,13},{10,... | collective-permute-start | bytes 196616 | tf_op jit(solution)/shard_map/ppermute | solution.py:54
  61.0 1.3 %w1.1 = (f32[144,256]{1,0:T(8,128)S(1)}, bf16[144,256]{1,0:T(8,128)(2,1)S(1)}, bf16[144,256]{1,0:T(8,128)(2,1)S(1)}, bf16[144,256]{1,0:T(8,128)(2,1)S(1)}) custom-call(s32[4]{0:T(128)S(1)} %pad_add_fusion.refs_0_, bf16[16,128,256]{2,1,0:T(8,128)(2,1)S(1)} %get-tuple-element.90.refs_1_, f32[64,256]{1,0:T(8,128)S(1)} %taps.1.refs_6_.refs_2_, ...), custom_call_target="tpu_custom_call" | custom-call | flops 1024 | bytes 1024 | tf_op jit(solution)/shard_map/w1/pallas_call | solution.py:28
  62.4 1.2 %collective-permute-start.25 = (bf16[144,256]{1,0:T(8,128)(2,1)S(1)}, bf16[144,256]{1,0:T(8,128)(2,1)S(1)}, u32[]{:S(2)}, u32[]{:S(2)}) collective-permute-start(bf16[144,256]{1,0:T(8,128)(2,1)S(1)} %get-tuple-element.98), channel_id=1, source_target_pairs={{0,24},{1,25},{2,26},{3,27},{4,28},{5,29},{6,30},{7,31},{8,16},{9,... | collective-permute-start | bytes 221192 | tf_op jit(solution)/shard_map/ppermute | solution.py:54
  63.5 3.3 %collective-permute-start.23 = (bf16[144,256]{1,0:T(8,128)(2,1)S(1)}, bf16[144,256]{1,0:T(8,128)(2,1)S(1)}, u32[]{:S(2)}, u32[]{:S(2)}) collective-permute-start(bf16[144,256]{1,0:T(8,128)(2,1)S(1)} %get-tuple-element.96), channel_id=1, source_target_pairs={{0,8},{1,9},{2,10},{3,11},{4,12},{5,13},{6,14},{7,15},{8,0},{9,1},... | collective-permute-start | bytes 221192 | tf_op jit(solution)/shard_map/ppermute | solution.py:54
  66.8 0.9 chip_send.1.refs_4_
  67.7 0.6 collective-permute-start.21
  68.3 0.9 chip_keep.1.refs_1_.refs_2_
  69.4 2.2 %collective-permute-done.24 = bf16[144,256]{1,0:T(8,128)(2,1)S(1)} collective-permute-done((bf16[144,256]{1,0:T(8,128)(2,1)S(1)}, bf16[144,256]{1,0:T(8,128)(2,1)S(1)}, u32[]{:S(2)}, u32[]{:S(2)}) %collective-permute-start.24) | collective-permute-done | bytes 73760 | tf_op jit(solution)/shard_map/ppermute | solution.py:54
  71.8 1.8 %collective-permute-start.27 = (bf16[144,256]{1,0:T(8,128)(2,1)S(1)}, bf16[144,256]{1,0:T(8,128)(2,1)S(1)}, u32[]{:S(2)}, u32[]{:S(2)}) collective-permute-start(bf16[144,256]{1,0:T(8,128)(2,1)S(1)} %add_convert_fusion.refs_1_), channel_id=1, source_target_pairs={{0,16},{1,17},{2,18},{3,19},{4,20},{5,21},{6,22},{7,23},{8,24},{9,... | collective-permute-start | bytes 221192 | tf_op jit(solution)/shard_map/ppermute | solution.py:54
  73.5 2.6 %collective-permute-start.28 = (bf16[144,256]{1,0:T(8,128)(2,1)S(1)}, bf16[144,256]{1,0:T(8,128)(2,1)S(1)}, u32[]{:S(2)}, u32[]{:S(2)}) collective-permute-start(bf16[144,256]{1,0:T(8,128)(2,1)S(1)} %add_convert_fusion.refs_1_), channel_id=1, source_target_pairs={{0,24},{1,25},{2,26},{3,27},{4,28},{5,29},{6,30},{7,31},{8,16},{9,... | collective-permute-start | bytes 221192 | tf_op jit(solution)/shard_map/ppermute | solution.py:54
  76.1 1.2 %collective-permute-done.26.refs_2_ = bf16[144,256]{1,0:T(8,128)(2,1)S(1)} collective-permute-done((bf16[144,256]{1,0:T(8,128)(2,1)S(1)}, bf16[144,256]{1,0:T(8,128)(2,1)S(1)}, u32[]{:S(2)}, u32[]{:S(2)}) %collective-permute-start.26) | collective-permute-done | bytes 73760 | tf_op jit(solution)/shard_map/ppermute | solution.py:54
  77.3 5.6 %collective-permute-done.27.refs_3_ = bf16[144,256]{1,0:T(8,128)(2,1)S(1)} collective-permute-done((bf16[144,256]{1,0:T(8,128)(2,1)S(1)}, bf16[144,256]{1,0:T(8,128)(2,1)S(1)}, u32[]{:S(2)}, u32[]{:S(2)}) %collective-permute-start.27) | collective-permute-done | bytes 73760 | tf_op jit(solution)/shard_map/ppermute | solution.py:54
  83.0 0.6 column.1.refs_5_
  83.5 1.1 %collective-permute-start.29 = (bf16[4,144,256]{2,1,0:T(8,128)(2,1)S(1)}, bf16[4,144,256]{2,1,0:T(8,128)(2,1)S(1)}, u32[]{:S(2)}, u32[]{:S(2)}) collective-permute-start(bf16[4,144,256]{2,1,0:T(8,128)(2,1)S(1)} %column.1.refs_5_), channel_id=1, source_target_pairs={{0,4},{1,5},{2,6},{3,7},{4,0},{5,1},{6,2},{7,3},{8,12},{9,13},{10,... | collective-permute-start | bytes 884744 | tf_op jit(solution)/shard_map/ppermute | solution.py:54
  84.6 1.7 %collective-permute-start.32 = (bf16[2,2,64,512]{3,2,1,0:T(8,128)(2,1)S(1)}, bf16[2,2,64,512]{3,2,1,0:T(8,128)(2,1)S(1)}, u32[]{:S(2)}, u32[]{:S(2)}) collective-permute-start(bf16[2,2,64,512]{3,2,1,0:T(8,128)(2,1)S(1)} %pad_maximum_fusion.refs_7_), channel_id=1, source_target_pairs={{0,8},{1,9},{2,10},{3,11},{4,12},{5,13},{6,14},{7,15},{8,0},{9,1},... | collective-permute-start | bytes 786440 | tf_op jit(solution)/shard_map/ppermute | solution.py:54
  86.3 0.6 forward.1
  86.9 0.7 collective-permute-start.22
  87.6 5.8 %collective-permute-done.29.refs_6_ = bf16[4,144,256]{2,1,0:T(8,128)(2,1)S(1)} collective-permute-done((bf16[4,144,256]{2,1,0:T(8,128)(2,1)S(1)}, bf16[4,144,256]{2,1,0:T(8,128)(2,1)S(1)}, u32[]{:S(2)}, u32[]{:S(2)}) %collective-permute-start.29) | collective-permute-done | bytes 294944 | tf_op jit(solution)/shard_map/ppermute | solution.py:54
  93.5 2.0 %last.1 = (bf16[2,128,512]{2,1,0:T(8,128)(2,1)}, f32[512,512]{1,0:T(8,128)}, f32[512,512]{1,0:T(8,128)}, f32[25,512]{1,0:T(8,128)}, f32[1,512]{1,0:T(1,128)}, /*index=5*/f32[1,512]{1,0:T(1,128)}) custom-call(s32[4]{0:T(128)S(1)} %pad_add_fusion.refs_0_, bf16[2,128,512]{2,1,0:T(8,128)(2,1)S(1)} %get-tuple-element.56.refs_3_.refs_2_.refs_1_, ...), custom_call_target="tpu_custom_call" | custom-call | tf_op jit(solution)/shard_map/last/pallas_call | solution.py:28
  (59 shorter events, 3.4 us)
Async XLA Ops:
  0.6 11.9 %collective-permute-start.1 = (bf16[2,128,512]{2,1,0:T(8,128)(2,1)}, bf16[2,128,512]{2,1,0:T(8,128)(2,1)S(1)}, u32[]{:S(2)}, u32[]{:S(2)}) collective-permute-start(bf16[2,128,512]{2,1,0:T(8,128)(2,1)} %refs_6_.1), channel_id=1, source_target_pairs={{0,1},{1,0},{2,3},{3,2},{4,5},{5,4},{6,7},{7,6},{8,9},{9,8},{10,11... | collective-permute-start | bytes 786440 | tf_op jit(solution)/shard_map/ppermute | solution.py:54
  1.1 11.4 %collective-permute-start.2 = (bf16[2,128,512]{2,1,0:T(8,128)(2,1)}, bf16[2,128,512]{2,1,0:T(8,128)(2,1)S(1)}, u32[]{:S(2)}, u32[]{:S(2)}) collective-permute-start(bf16[2,128,512]{2,1,0:T(8,128)(2,1)} %refs_7_.1), channel_id=1, source_target_pairs={{0,1},{1,0},{2,3},{3,2},{4,5},{5,4},{6,7},{7,6},{8,9},{9,8},{10,11... | collective-permute-start | bytes 786440 | tf_op jit(solution)/shard_map/ppermute | solution.py:54
  1.2 12.7 %collective-permute-start = (bf16[2,128,512]{2,1,0:T(8,128)(2,1)}, bf16[2,128,512]{2,1,0:T(8,128)(2,1)S(1)}, u32[]{:S(2)}, u32[]{:S(2)}) collective-permute-start(bf16[2,128,512]{2,1,0:T(8,128)(2,1)} %refs_6_.1), channel_id=1, source_target_pairs={{0,2},{1,3},{2,0},{3,1},{4,6},{5,7},{6,4},{7,5},{8,10},{9,11},{10,... | collective-permute-start | bytes 786440 | tf_op jit(solution)/shard_map/ppermute | solution.py:54
  4.2 9.9 %collective-permute-start.4 = (bf16[2,128,512]{2,1,0:T(8,128)(2,1)}, bf16[2,128,512]{2,1,0:T(8,128)(2,1)S(1)}, u32[]{:S(2)}, u32[]{:S(2)}) collective-permute-start(bf16[2,128,512]{2,1,0:T(8,128)(2,1)} %refs_6_.1), channel_id=1, source_target_pairs={{0,4},{1,5},{2,6},{3,7},{4,0},{5,1},{6,2},{7,3},{8,12},{9,13},{10,... | collective-permute-start | bytes 786440 | tf_op jit(solution)/shard_map/ppermute | solution.py:54
  5.7 12.1 %collective-permute-start.6 = (bf16[2,128,512]{2,1,0:T(8,128)(2,1)}, bf16[2,128,512]{2,1,0:T(8,128)(2,1)S(1)}, u32[]{:S(2)}, u32[]{:S(2)}) collective-permute-start(bf16[2,128,512]{2,1,0:T(8,128)(2,1)} %refs_6_.1), channel_id=1, source_target_pairs={{0,6},{1,7},{2,4},{3,5},{4,2},{5,3},{6,0},{7,1},{8,14},{9,15},{10,... | collective-permute-start | bytes 786440 | tf_op jit(solution)/shard_map/ppermute | solution.py:54
  5.7 1.0 %copy-start = (bf16[512,512]{1,0:T(8,128)(2,1)S(1)}, bf16[512,512]{1,0:T(8,128)(2,1)}, u32[]{:S(2)}) copy-start(bf16[512,512]{1,0:T(8,128)(2,1)} %refs_1_.1) | copy-start | bytes 1572868
  6.8 1.0 %copy-start.1 = (bf16[512,512]{1,0:T(8,128)(2,1)S(1)}, bf16[512,512]{1,0:T(8,128)(2,1)}, u32[]{:S(2)}) copy-start(bf16[512,512]{1,0:T(8,128)(2,1)} %refs_5_.1) | copy-start | bytes 1572868
  7.8 0.9 copy-start.2
  8.8 0.9 copy-start.3
  9.7 0.8 copy-start.4
  10.6 0.7 copy-start.5
  11.3 0.7 copy-start.6
  14.0 7.0 %collective-permute-start.3 = (bf16[2,128,512]{2,1,0:T(8,128)(2,1)S(1)}, bf16[2,128,512]{2,1,0:T(8,128)(2,1)S(1)}, u32[]{:S(2)}, u32[]{:S(2)}) collective-permute-start(bf16[2,128,512]{2,1,0:T(8,128)(2,1)S(1)} %collective-permute-done.refs_3_.refs_6_), channel_id=1, source_target_pairs={{0,1},{1,0},{2,3},{3,2},{4,5},{5,4},{6,7},{7,6},{8,9},{9,8},{10,11... | collective-permute-start | bytes 786440 | tf_op jit(solution)/shard_map/ppermute | solution.py:54
  14.1 8.9 %collective-permute-start.5 = (bf16[2,128,512]{2,1,0:T(8,128)(2,1)S(1)}, bf16[2,128,512]{2,1,0:T(8,128)(2,1)S(1)}, u32[]{:S(2)}, u32[]{:S(2)}) collective-permute-start(bf16[2,128,512]{2,1,0:T(8,128)(2,1)S(1)} %collective-permute-done.4.refs_4_.refs_8_), channel_id=1, source_target_pairs={{0,1},{1,0},{2,3},{3,2},{4,5},{5,4},{6,7},{7,6},{8,9},{9,8},{10,11... | collective-permute-start | bytes 786440 | tf_op jit(solution)/shard_map/ppermute | solution.py:54
  17.7 5.2 %collective-permute-start.7 = (bf16[2,128,512]{2,1,0:T(8,128)(2,1)S(1)}, bf16[2,128,512]{2,1,0:T(8,128)(2,1)S(1)}, u32[]{:S(2)}, u32[]{:S(2)}) collective-permute-start(bf16[2,128,512]{2,1,0:T(8,128)(2,1)S(1)} %collective-permute-done.6.refs_5_.refs_10_), channel_id=1, source_target_pairs={{0,1},{1,0},{2,3},{3,2},{4,5},{5,4},{6,7},{7,6},{8,9},{9,8},{10,11... | collective-permute-start | bytes 786440 | tf_op jit(solution)/shard_map/ppermute | solution.py:54
  17.7 16.3 %collective-permute-start.10 = (bf16[2,128,512]{2,1,0:T(8,128)(2,1)S(1)}, bf16[2,128,512]{2,1,0:T(8,128)(2,1)S(1)}, u32[]{:S(2)}, u32[]{:S(2)}) collective-permute-start(bf16[2,128,512]{2,1,0:T(8,128)(2,1)S(1)} %copy-done.3), channel_id=1, source_target_pairs={{0,2},{1,3},{2,0},{3,1},{4,6},{5,7},{6,4},{7,5},{8,10},{9,11},{10,... | collective-permute-start | bytes 786440 | tf_op jit(solution)/shard_map/ppermute | solution.py:54
  19.5 14.7 %collective-permute-start.12 = (bf16[2,128,512]{2,1,0:T(8,128)(2,1)S(1)}, bf16[2,128,512]{2,1,0:T(8,128)(2,1)S(1)}, u32[]{:S(2)}, u32[]{:S(2)}) collective-permute-start(bf16[2,128,512]{2,1,0:T(8,128)(2,1)S(1)} %copy-done.3), channel_id=1, source_target_pairs={{0,4},{1,5},{2,6},{3,7},{4,0},{5,1},{6,2},{7,3},{8,12},{9,13},{10,... | collective-permute-start | bytes 786440 | tf_op jit(solution)/shard_map/ppermute | solution.py:54
  21.0 13.7 %collective-permute-start.14 = (bf16[2,128,512]{2,1,0:T(8,128)(2,1)S(1)}, bf16[2,128,512]{2,1,0:T(8,128)(2,1)S(1)}, u32[]{:S(2)}, u32[]{:S(2)}) collective-permute-start(bf16[2,128,512]{2,1,0:T(8,128)(2,1)S(1)} %copy-done.3), channel_id=1, source_target_pairs={{0,6},{1,7},{2,4},{3,5},{4,2},{5,3},{6,0},{7,1},{8,14},{9,15},{10,... | collective-permute-start | bytes 786440 | tf_op jit(solution)/shard_map/ppermute | solution.py:54
  24.7 7.3 %collective-permute-start.8 = (bf16[2,128,256]{2,1,0:T(8,128)(2,1)S(1)}, bf16[2,128,256]{2,1,0:T(8,128)(2,1)S(1)}, u32[]{:S(2)}, u32[]{:S(2)}) collective-permute-start(bf16[2,128,256]{2,1,0:T(8,128)(2,1)S(1)} %get-tuple-element.71), channel_id=1, source_target_pairs={{0,8},{1,9},{2,10},{3,11},{4,12},{5,13},{6,14},{7,15},{8,0},{9,1},... | collective-permute-start | bytes 393224 | tf_op jit(solution)/shard_map/ppermute | solution.py:74
  26.6 5.4 %collective-permute-start.9 = (bf16[2,128,256]{2,1,0:T(8,128)(2,1)S(1)}, bf16[2,128,256]{2,1,0:T(8,128)(2,1)S(1)}, u32[]{:S(2)}, u32[]{:S(2)}) collective-permute-start(bf16[2,128,256]{2,1,0:T(8,128)(2,1)S(1)} %get-tuple-element.72), channel_id=1, source_target_pairs={{8,16},{9,17},{10,18},{11,19},{12,20},{13,21},{14,22},{15,23},{16,... | collective-permute-start | bytes 393224 | tf_op jit(solution)/shard_map/ppermute | solution.py:74
  34.1 1.8 %collective-permute-start.11 = (bf16[2,128,512]{2,1,0:T(8,128)(2,1)S(1)}, bf16[2,128,512]{2,1,0:T(8,128)(2,1)S(1)}, u32[]{:S(2)}, u32[]{:S(2)}) collective-permute-start(bf16[2,128,512]{2,1,0:T(8,128)(2,1)S(1)} %collective-permute-done.10.refs_5_.refs_4_), channel_id=1, source_target_pairs={{0,1},{1,0},{2,3},{3,2},{4,5},{5,4},{6,7},{7,6},{8,9},{9,8},{10,11... | collective-permute-start | bytes 786440 | tf_op jit(solution)/shard_map/ppermute | solution.py:54
  34.2 1.9 %collective-permute-start.13 = (bf16[2,128,512]{2,1,0:T(8,128)(2,1)S(1)}, bf16[2,128,512]{2,1,0:T(8,128)(2,1)S(1)}, u32[]{:S(2)}, u32[]{:S(2)}) collective-permute-start(bf16[2,128,512]{2,1,0:T(8,128)(2,1)S(1)} %collective-permute-done.12.refs_6_), channel_id=1, source_target_pairs={{0,1},{1,0},{2,3},{3,2},{4,5},{5,4},{6,7},{7,6},{8,9},{9,8},{10,11... | collective-permute-start | bytes 786440 | tf_op jit(solution)/shard_map/ppermute | solution.py:54
  34.6 1.8 %collective-permute-start.15 = (bf16[2,128,512]{2,1,0:T(8,128)(2,1)S(1)}, bf16[2,128,512]{2,1,0:T(8,128)(2,1)S(1)}, u32[]{:S(2)}, u32[]{:S(2)}) collective-permute-start(bf16[2,128,512]{2,1,0:T(8,128)(2,1)S(1)} %collective-permute-done.14.refs_7_.refs_8_), channel_id=1, source_target_pairs={{0,1},{1,0},{2,3},{3,2},{4,5},{5,4},{6,7},{7,6},{8,9},{9,8},{10,11... | collective-permute-start | bytes 786440 | tf_op jit(solution)/shard_map/ppermute | solution.py:54
  37.8 11.0 %collective-permute-start.18 = (bf16[2,64,512]{2,1,0:T(8,128)(2,1)S(1)}, bf16[2,64,512]{2,1,0:T(8,128)(2,1)S(1)}, u32[]{:S(2)}, u32[]{:S(2)}) collective-permute-start(bf16[2,64,512]{2,1,0:T(8,128)(2,1)S(1)} %pad_maximum_fusion.1), channel_id=1, source_target_pairs={{0,8},{1,9},{2,10},{3,11},{4,12},{5,13},{6,14},{7,15},{8,0},{9,1},... | collective-permute-start | bytes 393224 | tf_op jit(solution)/shard_map/ppermute | solution.py:54
  43.2 10.5 %collective-permute-start.16 = (bf16[2,128,256]{2,1,0:T(8,128)(2,1)S(1)}, bf16[2,128,256]{2,1,0:T(8,128)(2,1)S(1)}, u32[]{:S(2)}, u32[]{:S(2)}) collective-permute-start(bf16[2,128,256]{2,1,0:T(8,128)(2,1)S(1)} %get-tuple-element.84), channel_id=1, source_target_pairs={{0,8},{1,9},{2,10},{3,11},{4,12},{5,13},{6,14},{7,15},{8,0},{9,1},... | collective-permute-start | bytes 393224 | tf_op jit(solution)/shard_map/ppermute | solution.py:74
  43.3 10.4 %collective-permute-start.17 = (bf16[2,128,256]{2,1,0:T(8,128)(2,1)S(1)}, bf16[2,128,256]{2,1,0:T(8,128)(2,1)S(1)}, u32[]{:S(2)}, u32[]{:S(2)}) collective-permute-start(bf16[2,128,256]{2,1,0:T(8,128)(2,1)S(1)} %get-tuple-element.85), channel_id=1, source_target_pairs={{8,16},{9,17},{10,18},{11,19},{12,20},{13,21},{14,22},{15,23},{16,... | collective-permute-start | bytes 393224 | tf_op jit(solution)/shard_map/ppermute | solution.py:74
  48.9 9.5 %collective-permute-start.19 = (bf16[64,512]{1,0:T(8,128)(2,1)S(1)}, bf16[64,512]{1,0:T(8,128)(2,1)S(1)}, u32[]{:S(2)}, u32[]{:S(2)}) collective-permute-start(bf16[64,512]{1,0:T(8,128)(2,1)S(1)} %convert_element_type.29), channel_id=1, source_target_pairs={{0,16},{1,17},{2,18},{3,19},{4,20},{5,21},{6,22},{7,23},{8,24},{9,... | collective-permute-start | bytes 196616 | tf_op jit(solution)/shard_map/ppermute | solution.py:54
  59.4 7.4 %collective-permute-start.20 = (bf16[4,2,128,512]{3,2,1,0:T(8,128)(2,1)S(1)}, bf16[4,2,128,512]{3,2,1,0:T(8,128)(2,1)S(1)}, u32[]{:S(2)}, u32[]{:S(2)}) collective-permute-start(bf16[4,2,128,512]{3,2,1,0:T(8,128)(2,1)S(1)} %core.1.refs_13_), channel_id=1, source_target_pairs={{0,1},{1,0},{2,3},{3,2},{4,5},{5,4},{6,7},{7,6},{8,9},{9,8},{10,11... | collective-permute-start | bytes 3145736 | tf_op jit(solution)/shard_map/ppermute | solution.py:54
  59.5 8.8 %collective-permute-start.30 = (bf16[64,512]{1,0:T(8,128)(2,1)S(1)}, bf16[64,512]{1,0:T(8,128)(2,1)S(1)}, u32[]{:S(2)}, u32[]{:S(2)}) collective-permute-start(bf16[64,512]{1,0:T(8,128)(2,1)S(1)} %add_convert_fusion.1.refs_3_.refs_12_), channel_id=1, source_target_pairs={{0,4},{1,5},{2,6},{3,7},{4,0},{5,1},{6,2},{7,3},{8,12},{9,13},{10,... | collective-permute-start | bytes 196616 | tf_op jit(solution)/shard_map/ppermute | solution.py:54
  62.4 7.1 %collective-permute-start.25 = (bf16[144,256]{1,0:T(8,128)(2,1)S(1)}, bf16[144,256]{1,0:T(8,128)(2,1)S(1)}, u32[]{:S(2)}, u32[]{:S(2)}) collective-permute-start(bf16[144,256]{1,0:T(8,128)(2,1)S(1)} %get-tuple-element.98), channel_id=1, source_target_pairs={{0,24},{1,25},{2,26},{3,27},{4,28},{5,29},{6,30},{7,31},{8,16},{9,... | collective-permute-start | bytes 221192 | tf_op jit(solution)/shard_map/ppermute | solution.py:54
  63.5 8.1 %collective-permute-start.24 = (bf16[144,256]{1,0:T(8,128)(2,1)S(1)}, bf16[144,256]{1,0:T(8,128)(2,1)S(1)}, u32[]{:S(2)}, u32[]{:S(2)}) collective-permute-start(bf16[144,256]{1,0:T(8,128)(2,1)S(1)} %get-tuple-element.97), channel_id=1, source_target_pairs={{0,16},{1,17},{2,18},{3,19},{4,20},{5,21},{6,22},{7,23},{8,24},{9,... | collective-permute-start | bytes 221192 | tf_op jit(solution)/shard_map/ppermute | solution.py:54
  63.5 8.1 %collective-permute-start.23 = (bf16[144,256]{1,0:T(8,128)(2,1)S(1)}, bf16[144,256]{1,0:T(8,128)(2,1)S(1)}, u32[]{:S(2)}, u32[]{:S(2)}) collective-permute-start(bf16[144,256]{1,0:T(8,128)(2,1)S(1)} %get-tuple-element.96), channel_id=1, source_target_pairs={{0,8},{1,9},{2,10},{3,11},{4,12},{5,13},{6,14},{7,15},{8,0},{9,1},... | collective-permute-start | bytes 221192 | tf_op jit(solution)/shard_map/ppermute | solution.py:54
  67.7 18.6 %collective-permute-start.21 = (bf16[2,2,128,512]{3,2,1,0:T(8,128)(2,1)S(1)}, bf16[2,2,128,512]{3,2,1,0:T(8,128)(2,1)S(1)}, u32[]{:S(2)}, u32[]{:S(2)}) collective-permute-start(bf16[2,2,128,512]{3,2,1,0:T(8,128)(2,1)S(1)} %chip_send.1.refs_4_), channel_id=1, source_target_pairs={{0,4},{1,3},{2,6},{3,1},{4,0},{5,7},{6,2},{7,5},{8,12},{9,11},{10,... | collective-permute-start | bytes 1572872 | tf_op jit(solution)/shard_map/ppermute | solution.py:64
  69.2 15.4 %collective-permute-start.31 = (bf16[2,64,512]{2,1,0:T(8,128)(2,1)S(1)}, bf16[2,64,512]{2,1,0:T(8,128)(2,1)S(1)}, u32[]{:S(2)}, u32[]{:S(2)}) collective-permute-start(bf16[2,64,512]{2,1,0:T(8,128)(2,1)S(1)} %pad_maximum_fusion.2), channel_id=1, source_target_pairs={{0,16},{1,17},{2,18},{3,19},{4,20},{5,21},{6,22},{7,23},{8,24},{9,... | collective-permute-start | bytes 393224 | tf_op jit(solution)/shard_map/ppermute | solution.py:54
  71.7 5.7 %collective-permute-start.26 = (bf16[144,256]{1,0:T(8,128)(2,1)S(1)}, bf16[144,256]{1,0:T(8,128)(2,1)S(1)}, u32[]{:S(2)}, u32[]{:S(2)}) collective-permute-start(bf16[144,256]{1,0:T(8,128)(2,1)S(1)} %add_convert_fusion.refs_1_), channel_id=1, source_target_pairs={{0,8},{1,9},{2,10},{3,11},{4,12},{5,13},{6,14},{7,15},{8,0},{9,1},... | collective-permute-start | bytes 221192 | tf_op jit(solution)/shard_map/ppermute | solution.py:54
  71.8 11.2 %collective-permute-start.27 = (bf16[144,256]{1,0:T(8,128)(2,1)S(1)}, bf16[144,256]{1,0:T(8,128)(2,1)S(1)}, u32[]{:S(2)}, u32[]{:S(2)}) collective-permute-start(bf16[144,256]{1,0:T(8,128)(2,1)S(1)} %add_convert_fusion.refs_1_), channel_id=1, source_target_pairs={{0,16},{1,17},{2,18},{3,19},{4,20},{5,21},{6,22},{7,23},{8,24},{9,... | collective-permute-start | bytes 221192 | tf_op jit(solution)/shard_map/ppermute | solution.py:54
  73.5 9.4 %collective-permute-start.28 = (bf16[144,256]{1,0:T(8,128)(2,1)S(1)}, bf16[144,256]{1,0:T(8,128)(2,1)S(1)}, u32[]{:S(2)}, u32[]{:S(2)}) collective-permute-start(bf16[144,256]{1,0:T(8,128)(2,1)S(1)} %add_convert_fusion.refs_1_), channel_id=1, source_target_pairs={{0,24},{1,25},{2,26},{3,27},{4,28},{5,29},{6,30},{7,31},{8,16},{9,... | collective-permute-start | bytes 221192 | tf_op jit(solution)/shard_map/ppermute | solution.py:54
  83.5 9.9 %collective-permute-start.29 = (bf16[4,144,256]{2,1,0:T(8,128)(2,1)S(1)}, bf16[4,144,256]{2,1,0:T(8,128)(2,1)S(1)}, u32[]{:S(2)}, u32[]{:S(2)}) collective-permute-start(bf16[4,144,256]{2,1,0:T(8,128)(2,1)S(1)} %column.1.refs_5_), channel_id=1, source_target_pairs={{0,4},{1,5},{2,6},{3,7},{4,0},{5,1},{6,2},{7,3},{8,12},{9,13},{10,... | collective-permute-start | bytes 884744 | tf_op jit(solution)/shard_map/ppermute | solution.py:54
  84.6 8.9 %collective-permute-start.32 = (bf16[2,2,64,512]{3,2,1,0:T(8,128)(2,1)S(1)}, bf16[2,2,64,512]{3,2,1,0:T(8,128)(2,1)S(1)}, u32[]{:S(2)}, u32[]{:S(2)}) collective-permute-start(bf16[2,2,64,512]{3,2,1,0:T(8,128)(2,1)S(1)} %pad_maximum_fusion.refs_7_), channel_id=1, source_target_pairs={{0,8},{1,9},{2,10},{3,11},{4,12},{5,13},{6,14},{7,15},{8,0},{9,1},... | collective-permute-start | bytes 786440 | tf_op jit(solution)/shard_map/ppermute | solution.py:54
  86.9 6.6 %collective-permute-start.22 = (bf16[2,128,512]{2,1,0:T(8,128)(2,1)S(1)}, bf16[2,128,512]{2,1,0:T(8,128)(2,1)S(1)}, u32[]{:S(2)}, u32[]{:S(2)}) collective-permute-start(bf16[2,128,512]{2,1,0:T(8,128)(2,1)S(1)} %forward.1), channel_id=1, source_target_pairs={{0,2},{1,5},{2,0},{3,7},{4,6},{5,1},{6,4},{7,3},{8,10},{9,13},{10,... | collective-permute-start | bytes 786440 | tf_op jit(solution)/shard_map/ppermute | solution.py:64

commit v3 on v2

--- a/solution.py
+++ b/solution.py
@@ -13,6 +13,7 @@
 ANY = pl.BlockSpec(memory_space=pl.ANY)
 EDGE = 8
 LANES = 128
+ROOM = 0
 
 
 def array(*shape, dtype=BF):
@@ -78,7 +79,7 @@
     return lax.optimization_barrier((value, *others))[0]
 
 
-def prepare_kernel(pos, w1, b1, taps, b2, w2, rows, cot, w1_own, b1_own, taps_own, b2_own, w2_own, rows_own, cot_own):
+def prepare_kernel(pos, w1, b1, taps, b2, w2, rows, cot, w1_own, b1_own, taps_own, b2_own, w2_own, rows_own, cot_own, *pads):
     half = b1_own.shape[1]
     cut = pl.ds(pl.multiple_of(pos[1] * half, half), half)
     w1_own[...] = w1[:, cut]
@@ -88,19 +89,45 @@
     w2_own[...] = w2[cut, :]
     rows_own[...] = rows[...]
     cot_own[...] = cot[...]
-
-
-def put_edges(pos, rows, edges):
-    last = rows.shape[0] - 2
+    for pad in pads:
+        zeros = jnp.zeros((pad.shape[0], pad.shape[1], EDGE, LANES), F32)
+        pad[:, :, 0:EDGE, :] = zeros
+        pad[:, :, pad.shape[2] - EDGE :, :] = zeros
+
+
+def cuts(half):
+    return [(c, slice(c * LANES, (c + 1) * LANES)) for c in range(half // LANES)]
+
+
+def put_rows(pad, at, value):
+    rows, ncols, half = value.shape
+    value = value.astype(BF).astype(F32)
+    for c, cut in cuts(half):
+        pad[c, pl.ds(at + 2, rows), EDGE : EDGE + ncols, :] = value[:, :, cut]
+
+
+def put_edges(pos, pad, edges):
+    _, ncols, half = edges[0].shape
+    last = pad.shape[1] - 6
     odd = pos[2] & 1
-    edges[0][...] = rows[pl.ds(last * (1 - odd), 2)]
-    edges[1][...] = rows[pl.ds(last * odd, 2)]
+    for edge, at in zip(edges, (last * (1 - odd), last * odd)):
+        for c, cut in cuts(half):
+            edge[:, :, cut] = pad[c, pl.ds(at + 2, 2), EDGE : EDGE + ncols, :].astype(BF)
+
+
+def put_halo(pos, pad, near, far):
+    _, ncols, half = near.shape
+    last = pad.shape[1] - 2
+    odd = pos[2] & 1
+    for edge, at in zip((near, far), (last * (1 - odd), last * odd)):
+        for c, cut in cuts(half):
+            pad[c, pl.ds(at, 2), EDGE : EDGE + ncols, :] = edge[:, :, cut].astype(F32)
 
 
 def expand_kernel(order, pos, w, b, *refs):
     pieces, (hid, slope, *edges, pre) = refs[: len(order)], refs[len(order) :]
     n, ncols, cin = pieces[0].shape
-    half = hid.shape[2]
+    half = slope.shape[2]
     for k, piece in zip(order, pieces):
         at = (pos[0] ^ k) * n
         pre[...] = (
@@ -108,33 +135,14 @@
         ).reshape(n, ncols, half)
 
         def body(r, carry, at=at):
-            h, s = gelu_parts(pre[r])
-            hid[at + r] = h.astype(BF)
-            slope[at + r] = s.astype(BF)
+            h, s = gelu_parts(pre[pl.ds(r, 1)])
+            put_rows(hid, at + r, h)
+            slope[pl.ds(at + r, 1)] = s.astype(BF)
             return carry
 
         lax.fori_loop(0, n, body, 0)
     if edges:
         put_edges(pos, hid, edges)
-
-
-def load_padded(pos, pad, cut, mid, near=None, far=None, rows=None):
-    nrows, ncols, _ = mid.shape
-    zeros = jnp.zeros((nrows + 4, EDGE, LANES), F32)
-    pad[:, 0:EDGE, :] = zeros
-    pad[:, EDGE + ncols :, :] = zeros
-    if near is not None:
-        a, b = near[:, :, cut].astype(F32), far[:, :, cut].astype(F32)
-        odd = (pos[2] & 1) == 1
-        pad[0:2, EDGE : EDGE + ncols, :] = jnp.where(odd, a, b)
-        pad[nrows + 2 :, EDGE : EDGE + ncols, :] = jnp.where(odd, b, a)
-
-    def body(r, carry):
-        pad[r + 2, EDGE : EDGE + ncols, :] = mid[r, :, cut].astype(F32)
-        return carry
-
-    for lo, hi in rows or ((0, nrows),):
-        lax.fori_loop(lo, hi, body, 0)
 
 
 def conv_tiles(pad, taps, cut, ncols, starts, nr, cols, flip, emit):
@@ -156,16 +164,14 @@
     lax.fori_loop(0, ncols // cols, body, 0)
 
 
-def cuts(half):
-    return [slice(c, c + LANES) for c in range(0, half, LANES)]
-
-
 def middle_kernel(inner, pos, taps, bias, *refs):
-    (mid, mixed, slope, pad) = refs if inner else (refs[0], *refs[3:])
-    near, far = (None, None) if inner else refs[1:3]
-    nrows, ncols, half = mid.shape
-    for cut in cuts(half):
-        load_padded(pos, pad, cut, mid, near, far, None if inner else ((0, 4), (nrows - 4, nrows)))
+    if inner:
+        pad, mixed, slope = refs
+    else:
+        near, far, mixed, slope, pad = refs
+        put_halo(pos, pad, near, far)
+    nrows, ncols, half = mixed.shape
+    for c, cut in cuts(half):
         add = bias[:, cut]
 
         def emit(r0, w, acc, cut=cut, add=add):
@@ -175,21 +181,21 @@
                 slope[r0 + r, w, cut] = s
 
         if inner:
-            conv_tiles(pad, taps, cut, ncols, range(2, nrows - 2, 4), 4, 16, False, emit)
+            conv_tiles(pad.at[c], taps, cut, ncols, range(2, nrows - 2, 4), 4, 16, False, emit)
         else:
-            conv_tiles(pad, taps, cut, ncols, (0, nrows - 2), 2, 32, False, emit)
+            conv_tiles(pad.at[c], taps, cut, ncols, (0, nrows - 2), 2, 32, False, emit)
 
 
 def project_kernel(order, pos, weights, slope, *refs):
     pieces, (gp, *edges) = refs[: len(order)], refs[len(order) :]
     n, ncols, cin = pieces[0].shape
-    half = gp.shape[2]
+    half = slope.shape[2]
     for k, piece in zip(order, pieces):
         at = (pos[0] ^ k) * n
         res = lax.dot_general(
             piece[...].reshape(n * ncols, cin), weights[...], (((1,), (1,)), ((), ())), preferred_element_type=F32
         )
-        gp[pl.ds(at, n)] = (res.reshape(n, ncols, half) * slope[pl.ds(at, n)]).astype(BF)
+        put_rows(gp, at, res.reshape(n, ncols, half) * slope[pl.ds(at, n)])
     if edges:
         put_edges(pos, gp, edges)
 
@@ -216,26 +222,20 @@
         ref[...] = total[pl.ds(pl.multiple_of((pos[2] ^ k) * n, n), n), :].astype(ref.dtype)
 
 
-def taps_kernel(pos, mid, near, far, gp, small, pad, gpf):
-    nrows, ncols, half = mid.shape
+def taps_kernel(pos, hid, gp, small):
+    _, nrows, ncols, _ = hid.shape
+    nrows, ncols = nrows - 4, ncols - 2 * EDGE
     small[...] = jnp.zeros_like(small)
-    for cut in cuts(half):
-        load_padded(pos, pad, cut, mid, near, far)
-
-        def widen(r, carry, cut=cut):
-            gpf[r] = gp[r, :, cut].astype(F32)
-            return carry
-
-        lax.fori_loop(0, nrows, widen, 0)
-
-        def body(i, accs):
+    for c, cut in cuts(small.shape[1]):
+
+        def body(i, accs, c=c):
             accs = list(accs)
             w0 = i * 8
             for j in range(5):
-                xs = [pad[q, pl.ds(w0 + (EDGE - 2) + j, 8), :] for q in range(4)]
+                xs = [hid[c, q, pl.ds(w0 + (EDGE - 2) + j, 8), :] for q in range(4)]
                 for r in range(nrows):
-                    xs.append(pad[r + 4, pl.ds(w0 + (EDGE - 2) + j, 8), :])
-                    g = gpf[r, pl.ds(pl.multiple_of(w0, 8), 8), :]
+                    xs.append(hid[c, r + 4, pl.ds(w0 + (EDGE - 2) + j, 8), :])
+                    g = gp[c, r + 2, pl.ds(pl.multiple_of(w0 + EDGE, 8), 8), :]
                     for q in range(5):
                         accs[5 * q + j] = accs[5 * q + j] + xs[r + q] * g
                     if j == 0:
@@ -248,10 +248,10 @@
             small[t : t + 1, cut] = jnp.sum(accs[t], axis=0, keepdims=True)
 
 
-def back_kernel(pos, taps, mid, near, far, slope, act, grad_b, pad, total):
-    nrows, ncols, half = mid.shape
-    for cut in cuts(half):
-        load_padded(pos, pad, cut, mid, near, far)
+def back_kernel(pos, taps, near, far, slope, pad, act, grad_b, total):
+    nrows, ncols, half = act.shape
+    put_halo(pos, pad, near, far)
+    for c, cut in cuts(half):
         total[...] = jnp.zeros_like(total)
 
         def emit(r0, w, acc, cut=cut):
@@ -262,7 +262,7 @@
                 part = part + jnp.sum(a.astype(F32).reshape(-1, 8, LANES), axis=0)
             total[...] += part
 
-        conv_tiles(pad, taps, cut, ncols, range(0, nrows, 4), 4, 16, True, emit)
+        conv_tiles(pad.at[c], taps, cut, ncols, range(0, nrows, 4), 4, 16, True, emit)
         grad_b[:, cut] = jnp.sum(total[...], axis=0, keepdims=True)
 
 
@@ -312,31 +312,44 @@
     out[...] = (cot[...].astype(F32) + (kept[0] + arrived[0].astype(F32) + last[...].astype(F32))).astype(BF)
 
 
+def sum_kernel(pos, own, *refs):
+    total = own[...]
+    for part in refs[:-1]:
+        total = total + part[...].astype(F32)
+    refs[-1][...] = total.astype(BF)
+
+
+def copy_kernel(pos, value, out):
+    out[...] = value[...]
+
+
 def column_kernel(pos, *refs):
     blocks, out = refs[:-1], refs[-1]
+    n = blocks[0].shape[0]
     for k, block in enumerate(blocks):
-        out[pos[2] ^ k] = block[...]
-
-
-def w2_place_kernel(pos, blocks, out):
-    some, _, n, _ = blocks[0].shape
-    groups = some * len(blocks)
-    for b, block in enumerate(blocks):
-        for a in range(some):
-            for x in range(2):
-                at = (pos[1] ^ x) * groups + (pos[2] ^ (len(blocks) * a + b))
-                out[pl.ds(pl.multiple_of(at * n, n), n), :] = block[a, x].astype(F32)
-
-
-def w1_place_kernel(pos, mine, other, out, grad_k, grad_bd, grad_b1, small):
-    g, rows, half = mine.shape
+        out[pos[2] ^ k, 0:n] = block[...]
+        if n < out.shape[1]:
+            out[pos[2] ^ k, n:] = jnp.zeros((out.shape[1] - n, out.shape[2]), out.dtype)
+
+
+def w2_place_kernel(pos, mine, other, out):
+    g, _, cin = mine.shape
+    n = out.shape[0] // (2 * g)
+    for k, col in enumerate((mine, other)):
+        for i in range(g):
+            out[pl.ds(pl.multiple_of(((pos[1] ^ k) * g + i) * n, n), n), :] = col[i, 0:n].astype(F32)
+
+
+def w1_place_kernel(pos, blocks, out, grad_k, grad_bd, grad_b1, small):
+    g = len(blocks) // 2
+    half = blocks[0].shape[1]
     n = out.shape[0] // g
-    m = rows - n
-    for k, col in enumerate((mine, other)):
-        cut = pl.ds(pl.multiple_of((pos[1] ^ k) * half, half), half)
-        for i in range(g):
-            out[i * n : (i + 1) * n, cut] = col[i, 0:n, :].astype(F32)
-            small[i * m : (i + 1) * m, cut] = col[i, n:, :].astype(F32)
+    m = small.shape[0] // g
+    for i, block in enumerate(blocks):
+        cut = pl.ds(pl.multiple_of((pos[1] ^ (i // g)) * half, half), half)
+        at = pos[2] ^ (i % g)
+        out[pl.ds(pl.multiple_of(at * n, n), n), cut] = block[0:n, :].astype(F32)
+        small[pl.ds(pl.multiple_of(at * m, m), m), cut] = block[n:, :].astype(F32)
     grad_k[...] = small[0:25, :]
     grad_bd[...] = small[25:26, :]
     grad_b1[...] = small[26:27, :]
@@ -345,8 +358,8 @@
 def last_kernel(pos, cot, kept, arrived, last, mine, other, *refs):
     blocks, (out, out_w2, out_w1, grad_k, grad_bd, grad_b1, small) = refs[:-7], refs[-7:]
     finish_kernel(pos, cot, kept, arrived, last, out)
-    w2_place_kernel(pos, blocks, out_w2)
-    w1_place_kernel(pos, mine, other, out_w1, grad_k, grad_bd, grad_b1, small)
+    w2_place_kernel(pos, mine, other, out_w2)
+    w1_place_kernel(pos, blocks, out_w1, grad_k, grad_bd, grad_b1, small)
 
 
 def summed(own, sends):
@@ -358,11 +371,6 @@
 def halved(chunks):
     arrived = hop(jnp.stack([chunks[1], chunks[3]]), 2, 0).astype(F32)
     return chunks[0] + arrived[0], chunks[2] + arrived[1]
-
-
-def column(pos, chunk, groups, after=()):
-    blocks = [hop(chunk, 2 * k, 0) if k else chunk for k in range(groups)]
-    return kernel(column_kernel, "column", array(groups, *chunk.shape), (pos, *blocks), after=after)
 
 
 def shards(inputs, cotangent, expand_w, expand_b, depth_k, depth_b, project_w):
@@ -378,19 +386,20 @@
 
     full = array(nrows, ncols, half)
     mm = vpu = dict(flops=1024, nbytes=1024)
-    pad = pltpu.VMEM((nrows + 4, ncols + 2 * EDGE, LANES), F32)
+    long = dict(flops=2 * 10**10, nbytes=10**8)
+    padded = array(half // LANES, nrows + 4, ncols + 2 * EDGE, LANES, dtype=F32)
 
     mine = array(*inputs.shape)
-    w1, b1, taps, bd, w2, rows_own, cot_own = kernel(
+    w1, b1, taps, bd, w2, rows_own, cot_own, hidden, grad_pre = kernel(
         prepare_kernel, "prepare",
         (array(cin, half), array(1, half, dtype=F32), array(25, half, dtype=F32), array(1, half, dtype=F32),
-         array(half, cin), mine, mine),
+         array(half, cin), mine, mine, padded, padded),
         (pos, expand_w, expand_b.reshape(1, hslice), depth_k, depth_b.reshape(1, hslice), project_w, inputs, cotangent),
     )
 
     def expand(order, into=(), after=(), edges=()):
         return kernel(
-            lambda *refs: expand_kernel(order, *refs), "expand%d" % order[0], (full, full) + edges,
+            lambda *refs: expand_kernel(order, *refs), "expand%d" % order[0], (padded, full) + edges,
             (pos, w1, b1, *(in_pieces[k] for k in order)), [pltpu.VMEM((own_rows, ncols, half), F32)],
             into=into, after=after, **mm,
         )
@@ -400,38 +409,39 @@
     steps = {4: (1, 0), 2: (0, 2), 6: (1, 2)}
     for k, step in steps.items():
         in_pieces[k] = hop(inputs, *step)
-    first = expand((0, 1), after=(cot_pieces[1],))
+    first = expand((0, 1), (hidden,), after=(cot_pieces[1],))
     for k in steps:
         in_pieces[k + 1] = hop(tied(in_pieces[k], first[0]), 0, 1)
-    cot_start = tied(cotangent, in_pieces[2], in_pieces[4])
+    second = expand((2, 4), first)
+    cot_start = tied(cotangent, in_pieces[2], in_pieces[4], second[1])
     for k, step in steps.items():
         cot_pieces[k] = hop(tied(cot_start, in_pieces[6]) if k == 6 else cot_start, *step)
     in_pieces = [in_pieces[k] for k in range(8)]
     edges = (array(2, ncols, half),) * 2
-    hidden, slope_one, *sent = expand((3, 5, 7), expand((2, 4, 6), first), edges=edges)
+    hidden, slope_one, *sent = expand((7,), expand((6, 3, 5), second), edges=edges)
     hid_near, hid_far = meet(sent[0], 0), meet(sent[1], 1)
 
-    mixed, slope_two = kernel(
-        lambda *refs: middle_kernel(True, *refs), "inner", (full, array(nrows, ncols, half, dtype=F32)),
-        (pos, taps, bd, hidden), [pad], **vpu,
-    )
-    mixed, slope_two = kernel(
-        lambda *refs: middle_kernel(False, *refs), "outer", (full, array(nrows, ncols, half, dtype=F32)),
-        (pos, taps, bd, hidden, hid_near, hid_far), [pad], into=(mixed, slope_two), **vpu,
+    f32_full = array(nrows, ncols, half, dtype=F32)
+    inner = kernel(
+        lambda *refs: middle_kernel(True, *refs), "inner", (full, f32_full), (pos, taps, bd, hidden), **vpu
+    )
+    mixed, slope_two, hidden = kernel(
+        lambda *refs: middle_kernel(False, *refs), "outer", (full, f32_full, padded),
+        (pos, taps, bd, hid_near, hid_far), into=(*inner, hidden), **vpu,
     )
     for k in steps:
         cot_pieces[k + 1] = hop(tied(cot_pieces[k], mixed), 0, 1)
 
     def project(order, into=(), after=(), edges=()):
         return kernel(
-            lambda *refs: project_kernel(order, *refs), "project%d" % order[0], (full,) + edges,
+            lambda *refs: project_kernel(order, *refs), "project%d" % order[0], (padded,) + edges,
             (pos, w2, slope_two, *(cot_pieces[k] for k in order)), into=into, after=after, **mm,
         )
 
     def chunk_outs(rows, width):
         return (array(rows, width, dtype=F32),) + (array(rows, width),) * (groups - 1)
 
-    half_done = project((0, 1, 2, 4, 6))
+    half_done = project((0, 1, 2, 4, 6), (grad_pre,))
     w2_chunks = kernel(
         w2_kernel, "w2", chunk_outs(half // groups, cin), (pos, mixed, *(cot_pieces[k] for k in range(8))),
         [pltpu.VMEM((half, cin), F32)], after=half_done, **mm,
@@ -439,23 +449,19 @@
     grad_pre, *sent = project((3, 5, 7), half_done, (w2_chunks[0],), edges)
     gp_near, gp_far = meet(sent[0], 0), meet(sent[1], 1)
     tail = 16 * groups
-    small = kernel(
-        taps_kernel, "taps", array(tail, half, dtype=F32), (pos, hidden, hid_near, hid_far, grad_pre),
-        [pad, pltpu.VMEM((nrows, ncols, LANES), F32)], **vpu,
-    )
+    small = kernel(taps_kernel, "taps", array(tail, half, dtype=F32), (pos, hidden, grad_pre), **vpu)
     four = groups == 4
     w2_halves = halved(w2_chunks) if four else w2_chunks[:1]
-    grad_act, grad_b1 = kernel(
-        back_kernel, "back", (full, array(1, half, dtype=F32)),
-        (pos, taps, grad_pre, gp_near, gp_far, slope_one), [pad, pltpu.VMEM((8, LANES), F32)],
-        after=(small, *w2_halves), **vpu,
+    _, grad_act, grad_b1 = kernel(
+        back_kernel, "back", (padded, full, array(1, half, dtype=F32)), (pos, taps, gp_near, gp_far, slope_one),
+        [pltpu.VMEM((8, LANES), F32)], after=(small, *w2_halves), into=(grad_pre,), **vpu,
     )
     if four:
         w2_sent = hop(tied(w2_halves[1], small).astype(BF), 4, 0).astype(F32)
         w2_chunk = (tied(w2_halves[0], grad_act) + w2_sent).astype(BF)
     else:
         w2_chunk = summed(tied(w2_chunks[0], grad_act), w2_chunks[1:])
-    w2_pair = jnp.stack([w2_chunk, hop(w2_chunk, 1, 0)])
+    w2_two = jnp.stack([w2_chunk, hop(w2_chunk, 4, 0)]) if four else None
 
     block = (own_rows, ncols, cin)
     two = (2, *block)
@@ -468,26 +474,32 @@
     going = kernel(
         chip_send_kernel, "chip_send", array(*two), (pos, grad_act, w1, from_core), after=(w1_own,), **mm
     )
-    w2_pair = tied(w2_pair, going)
     if four:
-        w2_quad = jnp.stack([w2_pair, hop(w2_pair, 4, 0)])
-        w2_all = (w2_quad, hop(w2_quad, 2, 0))
+        w2_far = hop(tied(w2_two, going), 2, 0)
+        w2_blocks = [w2_two[0], w2_far[0], w2_two[1], w2_far[1]]
     else:
-        w2_all = [(hop(w2_pair, 2 * k, 0) if k else w2_pair)[None] for k in range(groups)]
+        w2_blocks = [hop(w2_chunk, 2 * k, 0) if k else w2_chunk for k in range(groups)]
     arrived = cross(going, 0)
+    w1_parts = [hop(send, 2 * (k + 1), 0) for k, send in enumerate(w1_sends)]
+    w1_chunk = kernel(sum_kernel, "sum", array(*w1_own.shape), (pos, w1_own, *w1_parts), after=(going,), **long)
+    w1_side = hop(w1_chunk, 1, 0)
+    w1_near = [hop(w1_chunk, 2 * k, 0) if k else w1_chunk for k in range(groups)]
     kept = kernel(
-        chip_keep_kernel, "chip_keep", array(*two, dtype=F32), (pos, grad_act, w1, from_core), after=(going,), **mm
-    )
+        chip_keep_kernel, "chip_keep", array(*two, dtype=F32), (pos, grad_act, w1, from_core), after=(w1_chunk,), **mm
+    )
+    w2_col = kernel(
+        column_kernel, "column", array(groups, half // groups + ROOM, cin), (pos, *w2_blocks), after=(kept,), **mm
+    )
+    w2_other = hop(w2_col, 1, 0)
     forward = kernel(forward_kernel, "forward", array(*block), (pos, kept, arrived), **mm)
     onward = cross(forward, 1)
-
-    w1_chunk = summed(tied(w1_own, kept), w1_sends)
-    w1_col = column(pos, w1_chunk, groups)
+    w1_side = kernel(copy_kernel, "side", array(*w1_side.shape), (pos, w1_side), after=(w1_near[-1],), **long)
+    w1_blocks = w1_near + [hop(w1_side, 2 * k, 0) if k else w1_side for k in range(groups)]
     line = array(1, hslice, dtype=F32)
     input_grad, out_w2, out_w1, out_k, out_bd, out_b1 = kernel(
         last_kernel, "last",
         (array(*block), array(hslice, cin, dtype=F32), array(cin, hslice, dtype=F32), array(25, hslice, dtype=F32), line, line),
-        (pos, cot_own, kept, arrived, onward, w1_col, hop(w1_col, 1, 0), *w2_all),
+        (pos, cot_own, kept, arrived, onward, w2_col, w2_other, *w1_blocks),
         [pltpu.VMEM((tail, hslice), F32)],
     )
     return (input_grad, out_w1, out_b1.reshape(hslice), out_k, out_bd.reshape(hslice), out_w2)

time: 97 us -> 94.4 us (0.973); the launches traced: 95.5 us -> 94 us
  waiting for transfers between devices: 18.8 us -> 11.5 us
  starting transfers between devices: 36.9 us -> 42 us
  Pallas kernels: 32.4 us -> 34.1 us
    ppermute x27 -> x30, waiting for transfers between devices: 18.8 us -> 11.5 us  [hop(): return lax.ppermute(value, AXES, pairs)]
    ppermute x27 -> x30, starting transfers between devices: 32.3 us -> 35.4 us  [hop(): return lax.ppermute(value, AXES, pairs)]
    ppermute x2, starting transfers between devices: 1.35 us -> 3.33 us  [cross(): return lax.ppermute(value, AXES, pairs)]
    pallas_call x18 -> x21, Pallas kernels: 32.4 us -> 34.1 us  [kernel(): pl.pallas_call(run, out_shape=out, in_specs=[SMEM] + [VMEM] * (len(args)...]
    unnamed x14 -> x12, local copies, waits for them, and re-layouts: 6.18 us -> 5.23 us
  transfers between devices with their start and end apart: 33 -> 36, of which waited for: 8 -> 6; matrix products, arithmetic and copies ran while one was open for 0% -> 0% of each run, Pallas kernels for 29% -> 32%
where the time goes in v3:
time: 94.4 us; the launch traced here: 94 us
  starting transfers between devices  42 us (44%)
  Pallas kernels  34.1 us (36%)
  waiting for transfers between devices  11.5 us (12%)
  local copies, waits for them, and re-layouts  5.24 us (6%)
  between operations  1 us (1%)
    ppermute x30, starting transfers between devices, hop(): return lax.ppermute(value, AXES, pairs)  35.4 us
    pallas_call x21, Pallas kernels, kernel(): pl.pallas_call(run, out_shape=out, in_specs=[SMEM] + [VMEM] * (len(args)...  34.1 us
    ppermute x30, waiting for transfers between devices, hop(): return lax.ppermute(value, AXES, pairs)  11.5 us
    unnamed x12, local copies, waits for them, and re-layouts  5.23 us
    ppermute x2, starting transfers between devices, cross(): return lax.ppermute(value, AXES, pairs)  3.33 us
    ppermute x4, starting transfers between devices, meet(): return lax.ppermute(value, AXES, pairs)  3.27 us
  transfers between devices with their start and end apart: 36, of which 6 were waited for; matrix products, arithmetic and copies ran while one was open for 0% of the time, Pallas kernels for 32%

profile of v3, /device:TPU:0, one launch (start us, length us, event | category | flops | bytes accessed | tf_op | source)
XLA Modules:
  0.0 94.0 jit_solution(9064821537686362739)
XLA Ops:
  1.2 2.9 %collective-permute-start.4 = (bf16[2,128,512]{2,1,0:T(8,128)(2,1)}, bf16[2,128,512]{2,1,0:T(8,128)(2,1)S(1)}, u32[]{:S(2)}, u32[]{:S(2)}) collective-permute-start(bf16[2,128,512]{2,1,0:T(8,128)(2,1)} %refs_6_.1), channel_id=1, source_target_pairs={{0,2},{1,3},{2,0},{3,1},{4,6},{5,7},{6,4},{7,5},{8,10},{9,11},{10,... | collective-permute-start | bytes 786440 | tf_op jit(solution)/shard_map/ppermute | solution.py:55
  4.2 1.5 %collective-permute-start.6 = (bf16[2,128,512]{2,1,0:T(8,128)(2,1)}, bf16[2,128,512]{2,1,0:T(8,128)(2,1)S(1)}, u32[]{:S(2)}, u32[]{:S(2)}) collective-permute-start(bf16[2,128,512]{2,1,0:T(8,128)(2,1)} %refs_6_.1), channel_id=1, source_target_pairs={{0,4},{1,5},{2,6},{3,7},{4,0},{5,1},{6,2},{7,3},{8,12},{9,13},{10,... | collective-permute-start | bytes 786440 | tf_op jit(solution)/shard_map/ppermute | solution.py:55
  5.7 1.0 %copy-done = bf16[512,512]{1,0:T(8,128)(2,1)S(1)} copy-done((bf16[512,512]{1,0:T(8,128)(2,1)S(1)}, bf16[512,512]{1,0:T(8,128)(2,1)}, u32[]{:S(2)}) %copy-start) | copy-done | bytes 524312
  6.8 1.0 %copy-done.1 = bf16[512,512]{1,0:T(8,128)(2,1)S(1)} copy-done((bf16[512,512]{1,0:T(8,128)(2,1)S(1)}, bf16[512,512]{1,0:T(8,128)(2,1)}, u32[]{:S(2)}) %copy-start.1) | copy-done | bytes 524312
  7.8 0.9 %copy-done.2 = bf16[2,128,512]{2,1,0:T(8,128)(2,1)S(1)} copy-done((bf16[2,128,512]{2,1,0:T(8,128)(2,1)S(1)}, bf16[2,128,512]{2,1,0:T(8,128)(2,1)}, u32[]{:S(2)}) %copy-start.2) | copy-done | bytes 262168
  8.8 0.8 copy-done.3
  9.6 0.7 copy-done.4
  10.3 0.7 copy-done.5
  11.0 1.1 %prepare.1 = (bf16[512,256]{1,0:T(8,128)(2,1)S(1)}, f32[1,256]{1,0:T(1,128)S(1)}, f32[25,256]{1,0:T(8,128)S(1)}, f32[1,256]{1,0:T(1,128)S(1)}, bf16[256,512]{1,0...) custom-call(s32[4]{0:T(128)S(1)} %pad_add_fusion.refs_0_, ...), custom_call_target="tpu_custom_call" | custom-call | tf_op jit(solution)/shard_map/prepare/pallas_call | solution.py:29
  12.1 1.4 %expand0.1 = (f32[2,20,144,128]{3,2,1,0:T(8,128)S(1)}, bf16[16,128,256]{2,1,0:T(8,128)(2,1)S(1)}) custom-call(s32[4]{0:T(128)S(1)} %pad_add_fusion.refs_0_, bf16[512,256]{1,0:T(8,128)(2,1)S(1)} %get-tuple-element.64.refs_1_.refs_2_, f32[1,256]{1,0:T(1,128)S(1)} %get-tuple-element.65.refs_2_, ...), custom_call_target="tpu_custom_call", output_to_operand_aliasing={{0}: (6, {})} | custom-call | flops 1024 | bytes 1024 | tf_op jit(solution)/shard_map/expand0/pallas_call | solution.py:29
  14.1 3.7 %collective-permute-done.refs_3_.refs_10_ = bf16[2,128,512]{2,1,0:T(8,128)(2,1)S(1)} collective-permute-done((bf16[2,128,512]{2,1,0:T(8,128)(2,1)}, bf16[2,128,512]{2,1,0:T(8,128)(2,1)S(1)}, u32[]{:S(2)}, u32[]{:S(2)}) %collective-permute-start) | collective-permute-done | bytes 262176 | tf_op jit(solution)/shard_map/ppermute | solution.py:55
  17.7 1.4 %expand2.1 = (f32[2,20,144,128]{3,2,1,0:T(8,128)S(1)}, bf16[16,128,256]{2,1,0:T(8,128)(2,1)S(1)}) custom-call(s32[4]{0:T(128)S(1)} %pad_add_fusion.refs_0_, bf16[512,256]{1,0:T(8,128)(2,1)S(1)} %get-tuple-element.64.refs_1_.refs_2_, f32[1,256]{1,0:T(1,128)S(1)} %get-tuple-element.65.refs_2_, ...), custom_call_target="tpu_custom_call", output_to_operand_aliasing={{0}: (5, {}), {1}: (6, {})} | custom-call | flops 1024 | bytes 1024 | tf_op jit(solution)/shard_map/expand2/pallas_call | solution.py:29
  19.1 2.7 %collective-permute-start.14 = (bf16[2,128,512]{2,1,0:T(8,128)(2,1)}, bf16[2,128,512]{2,1,0:T(8,128)(2,1)S(1)}, u32[]{:S(2)}, u32[]{:S(2)}) collective-permute-start(bf16[2,128,512]{2,1,0:T(8,128)(2,1)} %refs_7_.1), channel_id=1, source_target_pairs={{0,6},{1,7},{2,4},{3,5},{4,2},{5,3},{6,0},{7,1},{8,14},{9,15},{10,... | collective-permute-start | bytes 786440 | tf_op jit(solution)/shard_map/ppermute | solution.py:55
  22.7 1.8 %expand6.1 = (f32[2,20,144,128]{3,2,1,0:T(8,128)S(1)}, bf16[16,128,256]{2,1,0:T(8,128)(2,1)S(1)}) custom-call(s32[4]{0:T(128)S(1)} %pad_add_fusion.refs_0_, bf16[512,256]{1,0:T(8,128)(2,1)S(1)} %get-tuple-element.64.refs_1_.refs_2_, f32[1,256]{1,0:T(1,128)S(1)} %get-tuple-element.65.refs_2_, ...), custom_call_target="tpu_custom_call", output_to_operand_aliasing={{0}: (6, {}), {1}: (7, {})} | custom-call | flops 1024 | bytes 1024 | tf_op jit(solution)/shard_map/expand6/pallas_call | solution.py:29
  24.5 0.9 %expand7.1 = (f32[2,20,144,128]{3,2,1,0:T(8,128)S(1)}, bf16[16,128,256]{2,1,0:T(8,128)(2,1)S(1)}, bf16[2,128,256]{2,1,0:T(8,128)(2,1)S(1)}, bf16[2,128,256]{2,1,0:T(8,128)(2,1)S(1)}) custom-call(s32[4]{0:T(128)S(1)} %pad_add_fusion.refs_0_, bf16[512,256]{1,0:T(8,128)(2,1)S(1)} %get-tuple-element.64.refs_1_.refs_2_, ...), custom_call_target="tpu_custom_call", output_to_operand_aliasing={{0}: (4, {}), {1}: (5, {})} | custom-call | flops 1024 | bytes 1024 | tf_op jit(solution)/shard_map/expand7/pallas_call | solution.py:29
  25.4 1.9 %collective-permute-start.8 = (bf16[2,128,256]{2,1,0:T(8,128)(2,1)S(1)}, bf16[2,128,256]{2,1,0:T(8,128)(2,1)S(1)}, u32[]{:S(2)}, u32[]{:S(2)}) collective-permute-start(bf16[2,128,256]{2,1,0:T(8,128)(2,1)S(1)} %get-tuple-element.77), channel_id=1, source_target_pairs={{0,8},{1,9},{2,10},{3,11},{4,12},{5,13},{6,14},{7,15},{8,0},{9,1},... | collective-permute-start | bytes 393224 | tf_op jit(solution)/shard_map/ppermute | solution.py:75
  27.3 0.7 collective-permute-start.9
  28.0 4.8 %inner.1 = (bf16[16,128,256]{2,1,0:T(8,128)(2,1)S(1)}, f32[16,128,256]{2,1,0:T(8,128)S(1)}) custom-call(s32[4]{0:T(128)S(1)} %pad_add_fusion.refs_0_, f32[25,256]{1,0:T(8,128)S(1)} %get-tuple-element.61.refs_1_, f32[1,256]{1,0:T(1,128)S(1)} %get-tuple-element.63.refs_2_, f32[2,20,144,128]{3,2,1,0:T(8,128)S(1)} %get-tuple-element.79.refs_3_.refs_7_), custom_call_target="tpu_custom_call" | custom-call | flops 1024 | bytes 1024 | tf_op jit(solution)/shard_map/inner/pallas_call | solution.py:29
  32.8 2.1 %outer.1 = (bf16[16,128,256]{2,1,0:T(8,128)(2,1)S(1)}, f32[16,128,256]{2,1,0:T(8,128)S(1)}, f32[2,20,144,128]{3,2,1,0:T(8,128)S(1)}) custom-call(s32[4]{0:T(128)S(1)} %pad_add_fusion.refs_0_, f32[25,256]{1,0:T(8,128)S(1)} %get-tuple-element.61.refs_1_, ...), custom_call_target="tpu_custom_call", output_to_operand_aliasing={{0}: (5, {}), {1}: (6, {}), {2}: (7, {})} | custom-call | flops 1024 | bytes 1024 | tf_op jit(solution)/shard_map/outer/pallas_call | solution.py:29
  35.6 1.1 %project0.1.refs_10_.refs_7_ = f32[2,20,144,128]{3,2,1,0:T(8,128)S(1)} custom-call(s32[4]{0:T(128)S(1)} %pad_add_fusion.refs_0_, bf16[256,512]{1,0:T(8,128)(2,1)S(1)} %get-tuple-element.62.refs_1_, f32[16,128,256]{2,1,0:T(8,128)S(1)} %get-tuple-element.82.refs_2_, ...), custom_call_target="tpu_custom_call", output_to_operand_aliasing={{}: (8, {})} | custom-call | flops 1024 | bytes 1024 | tf_op jit(solution)/shard_map/project0/pallas_call | solution.py:29
  37.2 1.3 %w2.1 = (f32[64,512]{1,0:T(8,128)S(1)}, bf16[64,512]{1,0:T(8,128)(2,1)S(1)}, bf16[64,512]{1,0:T(8,128)(2,1)S(1)}, bf16[64,512]{1,0:T(8,128)(2,1)S(1)}) custom-call(s32[4]{0:T(128)S(1)} %pad_add_fusion.refs_0_, bf16[16,128,256]{2,1,0:T(8,128)(2,1)S(1)} %get-tuple-element.84.refs_1_, bf16[2,128,512]{2,1,0:T(8,128)(2,1)S(1)} %get-tuple-element.60.refs_3_.refs_2_.refs_1_, ...), custom_call_target="tpu_custom_call" | custom-call | flops 1024 | bytes 1024 | tf_op jit(solution)/shard_map/w2/pallas_call | solution.py:29
  38.6 4.5 %collective-permute-start.18 = (bf16[2,64,512]{2,1,0:T(8,128)(2,1)S(1)}, bf16[2,64,512]{2,1,0:T(8,128)(2,1)S(1)}, u32[]{:S(2)}, u32[]{:S(2)}) collective-permute-start(bf16[2,64,512]{2,1,0:T(8,128)(2,1)S(1)} %pad_maximum_fusion), channel_id=1, source_target_pairs={{0,8},{1,9},{2,10},{3,11},{4,12},{5,13},{6,14},{7,15},{8,0},{9,1},... | collective-permute-start | bytes 393224 | tf_op jit(solution)/shard_map/ppermute | solution.py:55
  43.0 1.0 %project3.1 = (f32[2,20,144,128]{3,2,1,0:T(8,128)S(1)}, bf16[2,128,256]{2,1,0:T(8,128)(2,1)S(1)}, bf16[2,128,256]{2,1,0:T(8,128)(2,1)S(1)}) custom-call(s32[4]{0:T(128)S(1)} %pad_add_fusion.refs_0_, bf16[256,512]{1,0:T(8,128)(2,1)S(1)} %get-tuple-element.62.refs_1_, f32[16,128,256]{2,1,0:T(8,128)S(1)} %get-tuple-element.82.refs_2_, ...), custom_call_target="tpu_custom_call", output_to_operand_aliasing={{0}: (7, {})} | custom-call | flops 1024 | bytes 1024 | tf_op jit(solution)/shard_map/project3/pallas_call | solution.py:29
  44.1 0.7 collective-permute-start.17
  44.8 4.3 %taps.1.refs_5_.refs_2_ = f32[64,256]{1,0:T(8,128)S(1)} custom-call(s32[4]{0:T(128)S(1)} %pad_add_fusion.refs_0_, f32[2,20,144,128]{3,2,1,0:T(8,128)S(1)} %get-tuple-element.94.refs_1_, f32[2,20,144,128]{3,2,1,0:T(8,128)S(1)} %get-tuple-element.95.refs_2_.refs_8_), custom_call_target="tpu_custom_call" | custom-call | flops 1024 | bytes 1024 | tf_op jit(solution)/shard_map/taps/pallas_call | solution.py:29
  49.2 4.8 %collective-permute-start.19 = (bf16[64,512]{1,0:T(8,128)(2,1)S(1)}, bf16[64,512]{1,0:T(8,128)(2,1)S(1)}, u32[]{:S(2)}, u32[]{:S(2)}) collective-permute-start(bf16[64,512]{1,0:T(8,128)(2,1)S(1)} %convert_element_type.17), channel_id=1, source_target_pairs={{0,16},{1,17},{2,18},{3,19},{4,20},{5,21},{6,22},{7,23},{8,24},{9,... | collective-permute-start | bytes 196616 | tf_op jit(solution)/shard_map/ppermute | solution.py:55
  54.0 4.5 %back.1 = (f32[2,20,144,128]{3,2,1,0:T(8,128)S(1)}, bf16[16,128,256]{2,1,0:T(8,128)(2,1)S(1)}, f32[1,256]{1,0:T(1,128)S(1)}) custom-call(s32[4]{0:T(128)S(1)} %pad_add_fusion.refs_0_, f32[25,256]{1,0:T(8,128)S(1)} %get-tuple-element.61.refs_1_, bf16[2,128,256]{2,1,0:T(8,128)(2,1)S(1)} %collective-permute-done.16.refs_2_, ...), custom_call_target="tpu_custom_call", output_to_operand_aliasing={{0}: (8, {})} | custom-call | flops 1024 | bytes 1024 | tf_op jit(solution)/shard_map/back/pallas_call | solution.py:29
  58.5 1.0 %core.1.refs_13_ = bf16[4,2,128,512]{3,2,1,0:T(8,128)(2,1)S(1)} custom-call(s32[4]{0:T(128)S(1)} %pad_add_fusion.refs_0_, bf16[16,128,256]{2,1,0:T(8,128)(2,1)S(1)} %get-tuple-element.99.refs_1_, bf16[512,256]{1,0:T(8,128)(2,1)S(1)} %get-tuple-element.64.refs_1_.refs_2_, bf16[64,512]{1,0:T(8,128)(2,1)S(1)} %add_convert_fusion.refs_3_.refs_12_.refs_1_), custom_call_target="tpu_custom_call" | custom-call | flops 1024 | bytes 1024 | tf_op jit(solution)/shard_map/core/pallas_call | solution.py:29
  59.6 0.7 collective-permute-start.26
  60.3 1.3 %w1.1 = (f32[144,256]{1,0:T(8,128)S(1)}, bf16[144,256]{1,0:T(8,128)(2,1)S(1)}, bf16[144,256]{1,0:T(8,128)(2,1)S(1)}, bf16[144,256]{1,0:T(8,128)(2,1)S(1)}) custom-call(s32[4]{0:T(128)S(1)} %pad_add_fusion.refs_0_, bf16[16,128,256]{2,1,0:T(8,128)(2,1)S(1)} %get-tuple-element.99.refs_1_, f32[64,256]{1,0:T(8,128)S(1)} %taps.1.refs_5_.refs_2_, ...), custom_call_target="tpu_custom_call" | custom-call | flops 1024 | bytes 1024 | tf_op jit(solution)/shard_map/w1/pallas_call | solution.py:29
  61.6 1.1 %collective-permute-start.21 = (bf16[144,256]{1,0:T(8,128)(2,1)S(1)}, bf16[144,256]{1,0:T(8,128)(2,1)S(1)}, u32[]{:S(2)}, u32[]{:S(2)}) collective-permute-start(bf16[144,256]{1,0:T(8,128)(2,1)S(1)} %get-tuple-element.104), channel_id=1, source_target_pairs={{0,8},{1,9},{2,10},{3,11},{4,12},{5,13},{6,14},{7,15},{8,0},{9,1},... | collective-permute-start | bytes 221192 | tf_op jit(solution)/shard_map/ppermute | solution.py:55
  62.7 1.4 %collective-permute-start.22 = (bf16[144,256]{1,0:T(8,128)(2,1)S(1)}, bf16[144,256]{1,0:T(8,128)(2,1)S(1)}, u32[]{:S(2)}, u32[]{:S(2)}) collective-permute-start(bf16[144,256]{1,0:T(8,128)(2,1)S(1)} %get-tuple-element.105), channel_id=1, source_target_pairs={{0,16},{1,17},{2,18},{3,19},{4,20},{5,21},{6,22},{7,23},{8,24},{9,... | collective-permute-start | bytes 221192 | tf_op jit(solution)/shard_map/ppermute | solution.py:55
  64.1 2.0 %collective-permute-start.23 = (bf16[144,256]{1,0:T(8,128)(2,1)S(1)}, bf16[144,256]{1,0:T(8,128)(2,1)S(1)}, u32[]{:S(2)}, u32[]{:S(2)}) collective-permute-start(bf16[144,256]{1,0:T(8,128)(2,1)S(1)} %get-tuple-element.106), channel_id=1, source_target_pairs={{0,24},{1,25},{2,26},{3,27},{4,28},{5,29},{6,30},{7,31},{8,16},{9,... | collective-permute-start | bytes 221192 | tf_op jit(solution)/shard_map/ppermute | solution.py:55
  66.1 0.9 chip_send.1.refs_5_
  67.0 1.6 %collective-permute-start.24 = (bf16[2,2,128,512]{3,2,1,0:T(8,128)(2,1)S(1)}, bf16[2,2,128,512]{3,2,1,0:T(8,128)(2,1)S(1)}, u32[]{:S(2)}, u32[]{:S(2)}) collective-permute-start(bf16[2,2,128,512]{3,2,1,0:T(8,128)(2,1)S(1)} %chip_send.1.refs_5_), channel_id=1, source_target_pairs={{0,4},{1,3},{2,6},{3,1},{4,0},{5,7},{6,2},{7,5},{8,12},{9,11},{10,... | collective-permute-start | bytes 1572872 | tf_op jit(solution)/shard_map/ppermute | solution.py:65
  68.6 2.9 %collective-permute-done.22.refs_3_ = bf16[144,256]{1,0:T(8,128)(2,1)S(1)} collective-permute-done((bf16[144,256]{1,0:T(8,128)(2,1)S(1)}, bf16[144,256]{1,0:T(8,128)(2,1)S(1)}, u32[]{:S(2)}, u32[]{:S(2)}) %collective-permute-start.22) | collective-permute-done | bytes 73760 | tf_op jit(solution)/shard_map/ppermute | solution.py:55
  72.1 2.2 %collective-permute-start.31 = (bf16[144,256]{1,0:T(8,128)(2,1)S(1)}, bf16[144,256]{1,0:T(8,128)(2,1)S(1)}, u32[]{:S(2)}, u32[]{:S(2)}) collective-permute-start(bf16[144,256]{1,0:T(8,128)(2,1)S(1)} %sum.1.refs_4_.refs_7_), channel_id=1, source_target_pairs={{0,24},{1,25},{2,26},{3,27},{4,28},{5,29},{6,30},{7,31},{8,16},{9,... | collective-permute-start | bytes 221192 | tf_op jit(solution)/shard_map/ppermute | solution.py:55
  74.3 1.5 %collective-permute-start.32 = (bf16[144,256]{1,0:T(8,128)(2,1)S(1)}, bf16[144,256]{1,0:T(8,128)(2,1)S(1)}, u32[]{:S(2)}, u32[]{:S(2)}) collective-permute-start(bf16[144,256]{1,0:T(8,128)(2,1)S(1)} %sum.1.refs_4_.refs_7_), channel_id=1, source_target_pairs={{0,4},{1,5},{2,6},{3,7},{4,0},{5,1},{6,2},{7,3},{8,12},{9,13},{10,... | collective-permute-start | bytes 221192 | tf_op jit(solution)/shard_map/ppermute | solution.py:55
  75.8 1.0 %collective-permute-start.29 = (bf16[144,256]{1,0:T(8,128)(2,1)S(1)}, bf16[144,256]{1,0:T(8,128)(2,1)S(1)}, u32[]{:S(2)}, u32[]{:S(2)}) collective-permute-start(bf16[144,256]{1,0:T(8,128)(2,1)S(1)} %sum.1.refs_4_.refs_7_), channel_id=1, source_target_pairs={{0,8},{1,9},{2,10},{3,11},{4,12},{5,13},{6,14},{7,15},{8,0},{9,1},... | collective-permute-start | bytes 221192 | tf_op jit(solution)/shard_map/ppermute | solution.py:55
  76.8 0.9 chip_keep.1.refs_1_.refs_5_.refs_2_
  77.7 1.3 %collective-permute-start.30 = (bf16[144,256]{1,0:T(8,128)(2,1)S(1)}, bf16[144,256]{1,0:T(8,128)(2,1)S(1)}, u32[]{:S(2)}, u32[]{:S(2)}) collective-permute-start(bf16[144,256]{1,0:T(8,128)(2,1)S(1)} %sum.1.refs_4_.refs_7_), channel_id=1, source_target_pairs={{0,16},{1,17},{2,18},{3,19},{4,20},{5,21},{6,22},{7,23},{8,24},{9,... | collective-permute-start | bytes 221192 | tf_op jit(solution)/shard_map/ppermute | solution.py:55
  79.6 0.6 collective-permute-start.28
  80.8 1.8 %collective-permute-start.25 = (bf16[2,128,512]{2,1,0:T(8,128)(2,1)S(1)}, bf16[2,128,512]{2,1,0:T(8,128)(2,1)S(1)}, u32[]{:S(2)}, u32[]{:S(2)}) collective-permute-start(bf16[2,128,512]{2,1,0:T(8,128)(2,1)S(1)} %forward.1), channel_id=1, source_target_pairs={{0,2},{1,5},{2,0},{3,7},{4,6},{5,1},{6,4},{7,3},{8,10},{9,13},{10,... | collective-permute-start | bytes 786440 | tf_op jit(solution)/shard_map/ppermute | solution.py:65
  83.8 2.0 %collective-permute-start.34 = (bf16[144,256]{1,0:T(8,128)(2,1)S(1)}, bf16[144,256]{1,0:T(8,128)(2,1)S(1)}, u32[]{:S(2)}, u32[]{:S(2)}) collective-permute-start(bf16[144,256]{1,0:T(8,128)(2,1)S(1)} %side.1.refs_11_), channel_id=1, source_target_pairs={{0,16},{1,17},{2,18},{3,19},{4,20},{5,21},{6,22},{7,23},{8,24},{9,... | collective-permute-start | bytes 221192 | tf_op jit(solution)/shard_map/ppermute | solution.py:55
  85.8 1.9 %collective-permute-start.35 = (bf16[144,256]{1,0:T(8,128)(2,1)S(1)}, bf16[144,256]{1,0:T(8,128)(2,1)S(1)}, u32[]{:S(2)}, u32[]{:S(2)}) collective-permute-start(bf16[144,256]{1,0:T(8,128)(2,1)S(1)} %side.1.refs_11_), channel_id=1, source_target_pairs={{0,24},{1,25},{2,26},{3,27},{4,28},{5,29},{6,30},{7,31},{8,16},{9,... | collective-permute-start | bytes 221192 | tf_op jit(solution)/shard_map/ppermute | solution.py:55
  87.6 2.5 %collective-permute-done.34.refs_13_ = bf16[144,256]{1,0:T(8,128)(2,1)S(1)} collective-permute-done((bf16[144,256]{1,0:T(8,128)(2,1)S(1)}, bf16[144,256]{1,0:T(8,128)(2,1)S(1)}, u32[]{:S(2)}, u32[]{:S(2)}) %collective-permute-start.34) | collective-permute-done | bytes 73760 | tf_op jit(solution)/shard_map/ppermute | solution.py:55
  90.1 1.8 %collective-permute-done.35.refs_14_ = bf16[144,256]{1,0:T(8,128)(2,1)S(1)} collective-permute-done((bf16[144,256]{1,0:T(8,128)(2,1)S(1)}, bf16[144,256]{1,0:T(8,128)(2,1)S(1)}, u32[]{:S(2)}, u32[]{:S(2)}) %collective-permute-start.35) | collective-permute-done | bytes 73760 | tf_op jit(solution)/shard_map/ppermute | solution.py:55
  91.9 2.0 %last.1 = (bf16[2,128,512]{2,1,0:T(8,128)(2,1)}, f32[512,512]{1,0:T(8,128)}, f32[512,512]{1,0:T(8,128)}, f32[25,512]{1,0:T(8,128)}, f32[1,512]{1,0:T(1,128)}, /*index=5*/f32[1,512]{1,0:T(1,128)}) custom-call(s32[4]{0:T(128)S(1)} %pad_add_fusion.refs_0_, bf16[2,128,512]{2,1,0:T(8,128)(2,1)S(1)} %get-tuple-element.60.refs_3_.refs_2_.refs_1_, ...), custom_call_target="tpu_custom_call" | custom-call | tf_op jit(solution)/shard_map/last/pallas_call | solution.py:29
  (65 shorter events, 6.6 us)
Async XLA Ops:
  0.6 11.4 %collective-permute-start.2 = (bf16[2,128,512]{2,1,0:T(8,128)(2,1)}, bf16[2,128,512]{2,1,0:T(8,128)(2,1)S(1)}, u32[]{:S(2)}, u32[]{:S(2)}) collective-permute-start(bf16[2,128,512]{2,1,0:T(8,128)(2,1)} %refs_7_.1), channel_id=1, source_target_pairs={{0,1},{1,0},{2,3},{3,2},{4,5},{5,4},{6,7},{7,6},{8,9},{9,8},{10,11... | collective-permute-start | bytes 786440 | tf_op jit(solution)/shard_map/ppermute | solution.py:55
  1.1 10.9 %collective-permute-start.1 = (bf16[2,128,512]{2,1,0:T(8,128)(2,1)}, bf16[2,128,512]{2,1,0:T(8,128)(2,1)S(1)}, u32[]{:S(2)}, u32[]{:S(2)}) collective-permute-start(bf16[2,128,512]{2,1,0:T(8,128)(2,1)} %refs_6_.1), channel_id=1, source_target_pairs={{0,1},{1,0},{2,3},{3,2},{4,5},{5,4},{6,7},{7,6},{8,9},{9,8},{10,11... | collective-permute-start | bytes 786440 | tf_op jit(solution)/shard_map/ppermute | solution.py:55
  1.2 12.3 %collective-permute-start.4 = (bf16[2,128,512]{2,1,0:T(8,128)(2,1)}, bf16[2,128,512]{2,1,0:T(8,128)(2,1)S(1)}, u32[]{:S(2)}, u32[]{:S(2)}) collective-permute-start(bf16[2,128,512]{2,1,0:T(8,128)(2,1)} %refs_6_.1), channel_id=1, source_target_pairs={{0,2},{1,3},{2,0},{3,1},{4,6},{5,7},{6,4},{7,5},{8,10},{9,11},{10,... | collective-permute-start | bytes 786440 | tf_op jit(solution)/shard_map/ppermute | solution.py:55
  4.2 9.4 %collective-permute-start.6 = (bf16[2,128,512]{2,1,0:T(8,128)(2,1)}, bf16[2,128,512]{2,1,0:T(8,128)(2,1)S(1)}, u32[]{:S(2)}, u32[]{:S(2)}) collective-permute-start(bf16[2,128,512]{2,1,0:T(8,128)(2,1)} %refs_6_.1), channel_id=1, source_target_pairs={{0,4},{1,5},{2,6},{3,7},{4,0},{5,1},{6,2},{7,3},{8,12},{9,13},{10,... | collective-permute-start | bytes 786440 | tf_op jit(solution)/shard_map/ppermute | solution.py:55
  5.7 12.1 %collective-permute-start = (bf16[2,128,512]{2,1,0:T(8,128)(2,1)}, bf16[2,128,512]{2,1,0:T(8,128)(2,1)S(1)}, u32[]{:S(2)}, u32[]{:S(2)}) collective-permute-start(bf16[2,128,512]{2,1,0:T(8,128)(2,1)} %refs_6_.1), channel_id=1, source_target_pairs={{0,6},{1,7},{2,4},{3,5},{4,2},{5,3},{6,0},{7,1},{8,14},{9,15},{10,... | collective-permute-start | bytes 786440 | tf_op jit(solution)/shard_map/ppermute | solution.py:55
  5.7 1.0 %copy-start = (bf16[512,512]{1,0:T(8,128)(2,1)S(1)}, bf16[512,512]{1,0:T(8,128)(2,1)}, u32[]{:S(2)}) copy-start(bf16[512,512]{1,0:T(8,128)(2,1)} %refs_1_.1) | copy-start | bytes 1572868
  6.8 1.0 %copy-start.1 = (bf16[512,512]{1,0:T(8,128)(2,1)S(1)}, bf16[512,512]{1,0:T(8,128)(2,1)}, u32[]{:S(2)}) copy-start(bf16[512,512]{1,0:T(8,128)(2,1)} %refs_5_.1) | copy-start | bytes 1572868
  7.8 0.9 %copy-start.2 = (bf16[2,128,512]{2,1,0:T(8,128)(2,1)S(1)}, bf16[2,128,512]{2,1,0:T(8,128)(2,1)}, u32[]{:S(2)}) copy-start(bf16[2,128,512]{2,1,0:T(8,128)(2,1)} %refs_6_.1) | copy-start | bytes 786436
  8.8 0.8 copy-start.3
  9.6 0.7 copy-start.4
  10.3 0.7 copy-start.5
  13.5 8.9 %collective-permute-start.5 = (bf16[2,128,512]{2,1,0:T(8,128)(2,1)S(1)}, bf16[2,128,512]{2,1,0:T(8,128)(2,1)S(1)}, u32[]{:S(2)}, u32[]{:S(2)}) collective-permute-start(bf16[2,128,512]{2,1,0:T(8,128)(2,1)S(1)} %collective-permute-done.4.refs_3_.refs_6_), channel_id=1, source_target_pairs={{0,1},{1,0},{2,3},{3,2},{4,5},{5,4},{6,7},{7,6},{8,9},{9,8},{10,11... | collective-permute-start | bytes 786440 | tf_op jit(solution)/shard_map/ppermute | solution.py:55
  13.6 9.1 %collective-permute-start.7 = (bf16[2,128,512]{2,1,0:T(8,128)(2,1)S(1)}, bf16[2,128,512]{2,1,0:T(8,128)(2,1)S(1)}, u32[]{:S(2)}, u32[]{:S(2)}) collective-permute-start(bf16[2,128,512]{2,1,0:T(8,128)(2,1)S(1)} %collective-permute-done.6.refs_4_.refs_8_), channel_id=1, source_target_pairs={{0,1},{1,0},{2,3},{3,2},{4,5},{5,4},{6,7},{7,6},{8,9},{9,8},{10,11... | collective-permute-start | bytes 786440 | tf_op jit(solution)/shard_map/ppermute | solution.py:55
  17.7 6.7 %collective-permute-start.3 = (bf16[2,128,512]{2,1,0:T(8,128)(2,1)S(1)}, bf16[2,128,512]{2,1,0:T(8,128)(2,1)S(1)}, u32[]{:S(2)}, u32[]{:S(2)}) collective-permute-start(bf16[2,128,512]{2,1,0:T(8,128)(2,1)S(1)} %collective-permute-done.refs_3_.refs_10_), channel_id=1, source_target_pairs={{0,1},{1,0},{2,3},{3,2},{4,5},{5,4},{6,7},{7,6},{8,9},{9,8},{10,11... | collective-permute-start | bytes 786440 | tf_op jit(solution)/shard_map/ppermute | solution.py:55
  19.1 15.7 %collective-permute-start.14 = (bf16[2,128,512]{2,1,0:T(8,128)(2,1)}, bf16[2,128,512]{2,1,0:T(8,128)(2,1)S(1)}, u32[]{:S(2)}, u32[]{:S(2)}) collective-permute-start(bf16[2,128,512]{2,1,0:T(8,128)(2,1)} %refs_7_.1), channel_id=1, source_target_pairs={{0,6},{1,7},{2,4},{3,5},{4,2},{5,3},{6,0},{7,1},{8,14},{9,15},{10,... | collective-permute-start | bytes 786440 | tf_op jit(solution)/shard_map/ppermute | solution.py:55
  21.9 13.1 %collective-permute-start.12 = (bf16[2,128,512]{2,1,0:T(8,128)(2,1)}, bf16[2,128,512]{2,1,0:T(8,128)(2,1)S(1)}, u32[]{:S(2)}, u32[]{:S(2)}) collective-permute-start(bf16[2,128,512]{2,1,0:T(8,128)(2,1)} %refs_7_.1), channel_id=1, source_target_pairs={{0,4},{1,5},{2,6},{3,7},{4,0},{5,1},{6,2},{7,3},{8,12},{9,13},{10,... | collective-permute-start | bytes 786440 | tf_op jit(solution)/shard_map/ppermute | solution.py:55
  22.4 13.1 %collective-permute-start.10 = (bf16[2,128,512]{2,1,0:T(8,128)(2,1)}, bf16[2,128,512]{2,1,0:T(8,128)(2,1)S(1)}, u32[]{:S(2)}, u32[]{:S(2)}) collective-permute-start(bf16[2,128,512]{2,1,0:T(8,128)(2,1)} %refs_7_.1), channel_id=1, source_target_pairs={{0,2},{1,3},{2,0},{3,1},{4,6},{5,7},{6,4},{7,5},{8,10},{9,11},{10,... | collective-permute-start | bytes 786440 | tf_op jit(solution)/shard_map/ppermute | solution.py:55
  25.4 7.3 %collective-permute-start.8 = (bf16[2,128,256]{2,1,0:T(8,128)(2,1)S(1)}, bf16[2,128,256]{2,1,0:T(8,128)(2,1)S(1)}, u32[]{:S(2)}, u32[]{:S(2)}) collective-permute-start(bf16[2,128,256]{2,1,0:T(8,128)(2,1)S(1)} %get-tuple-element.77), channel_id=1, source_target_pairs={{0,8},{1,9},{2,10},{3,11},{4,12},{5,13},{6,14},{7,15},{8,0},{9,1},... | collective-permute-start | bytes 393224 | tf_op jit(solution)/shard_map/ppermute | solution.py:75
  27.3 5.4 %collective-permute-start.9 = (bf16[2,128,256]{2,1,0:T(8,128)(2,1)S(1)}, bf16[2,128,256]{2,1,0:T(8,128)(2,1)S(1)}, u32[]{:S(2)}, u32[]{:S(2)}) collective-permute-start(bf16[2,128,256]{2,1,0:T(8,128)(2,1)S(1)} %get-tuple-element.78), channel_id=1, source_target_pairs={{8,16},{9,17},{10,18},{11,19},{12,20},{13,21},{14,22},{15,23},{16,... | collective-permute-start | bytes 393224 | tf_op jit(solution)/shard_map/ppermute | solution.py:75
  34.9 1.8 %collective-permute-start.15 = (bf16[2,128,512]{2,1,0:T(8,128)(2,1)S(1)}, bf16[2,128,512]{2,1,0:T(8,128)(2,1)S(1)}, u32[]{:S(2)}, u32[]{:S(2)}) collective-permute-start(bf16[2,128,512]{2,1,0:T(8,128)(2,1)S(1)} %collective-permute-done.14.refs_7_.refs_8_), channel_id=1, source_target_pairs={{0,1},{1,0},{2,3},{3,2},{4,5},{5,4},{6,7},{7,6},{8,9},{9,8},{10,11... | collective-permute-start | bytes 786440 | tf_op jit(solution)/shard_map/ppermute | solution.py:55
  35.0 1.9 %collective-permute-start.13 = (bf16[2,128,512]{2,1,0:T(8,128)(2,1)S(1)}, bf16[2,128,512]{2,1,0:T(8,128)(2,1)S(1)}, u32[]{:S(2)}, u32[]{:S(2)}) collective-permute-start(bf16[2,128,512]{2,1,0:T(8,128)(2,1)S(1)} %collective-permute-done.12.refs_6_), channel_id=1, source_target_pairs={{0,1},{1,0},{2,3},{3,2},{4,5},{5,4},{6,7},{7,6},{8,9},{9,8},{10,11... | collective-permute-start | bytes 786440 | tf_op jit(solution)/shard_map/ppermute | solution.py:55
  35.5 1.8 %collective-permute-start.11 = (bf16[2,128,512]{2,1,0:T(8,128)(2,1)S(1)}, bf16[2,128,512]{2,1,0:T(8,128)(2,1)S(1)}, u32[]{:S(2)}, u32[]{:S(2)}) collective-permute-start(bf16[2,128,512]{2,1,0:T(8,128)(2,1)S(1)} %collective-permute-done.10.refs_5_.refs_4_), channel_id=1, source_target_pairs={{0,1},{1,0},{2,3},{3,2},{4,5},{5,4},{6,7},{7,6},{8,9},{9,8},{10,11... | collective-permute-start | bytes 786440 | tf_op jit(solution)/shard_map/ppermute | solution.py:55
  38.6 10.5 %collective-permute-start.18 = (bf16[2,64,512]{2,1,0:T(8,128)(2,1)S(1)}, bf16[2,64,512]{2,1,0:T(8,128)(2,1)S(1)}, u32[]{:S(2)}, u32[]{:S(2)}) collective-permute-start(bf16[2,64,512]{2,1,0:T(8,128)(2,1)S(1)} %pad_maximum_fusion), channel_id=1, source_target_pairs={{0,8},{1,9},{2,10},{3,11},{4,12},{5,13},{6,14},{7,15},{8,0},{9,1},... | collective-permute-start | bytes 393224 | tf_op jit(solution)/shard_map/ppermute | solution.py:55
  44.0 9.9 %collective-permute-start.16 = (bf16[2,128,256]{2,1,0:T(8,128)(2,1)S(1)}, bf16[2,128,256]{2,1,0:T(8,128)(2,1)S(1)}, u32[]{:S(2)}, u32[]{:S(2)}) collective-permute-start(bf16[2,128,256]{2,1,0:T(8,128)(2,1)S(1)} %get-tuple-element.91), channel_id=1, source_target_pairs={{0,8},{1,9},{2,10},{3,11},{4,12},{5,13},{6,14},{7,15},{8,0},{9,1},... | collective-permute-start | bytes 393224 | tf_op jit(solution)/shard_map/ppermute | solution.py:75
  44.1 9.8 %collective-permute-start.17 = (bf16[2,128,256]{2,1,0:T(8,128)(2,1)S(1)}, bf16[2,128,256]{2,1,0:T(8,128)(2,1)S(1)}, u32[]{:S(2)}, u32[]{:S(2)}) collective-permute-start(bf16[2,128,256]{2,1,0:T(8,128)(2,1)S(1)} %get-tuple-element.92), channel_id=1, source_target_pairs={{8,16},{9,17},{10,18},{11,19},{12,20},{13,21},{14,22},{15,23},{16,... | collective-permute-start | bytes 393224 | tf_op jit(solution)/shard_map/ppermute | solution.py:75
  49.2 9.3 %collective-permute-start.19 = (bf16[64,512]{1,0:T(8,128)(2,1)S(1)}, bf16[64,512]{1,0:T(8,128)(2,1)S(1)}, u32[]{:S(2)}, u32[]{:S(2)}) collective-permute-start(bf16[64,512]{1,0:T(8,128)(2,1)S(1)} %convert_element_type.17), channel_id=1, source_target_pairs={{0,16},{1,17},{2,18},{3,19},{4,20},{5,21},{6,22},{7,23},{8,24},{9,... | collective-permute-start | bytes 196616 | tf_op jit(solution)/shard_map/ppermute | solution.py:55
  59.5 6.6 %collective-permute-start.20 = (bf16[4,2,128,512]{3,2,1,0:T(8,128)(2,1)S(1)}, bf16[4,2,128,512]{3,2,1,0:T(8,128)(2,1)S(1)}, u32[]{:S(2)}, u32[]{:S(2)}) collective-permute-start(bf16[4,2,128,512]{3,2,1,0:T(8,128)(2,1)S(1)} %core.1.refs_13_), channel_id=1, source_target_pairs={{0,1},{1,0},{2,3},{3,2},{4,5},{5,4},{6,7},{7,6},{8,9},{9,8},{10,11... | collective-permute-start | bytes 3145736 | tf_op jit(solution)/shard_map/ppermute | solution.py:55
  59.6 6.5 %collective-permute-start.26 = (bf16[64,512]{1,0:T(8,128)(2,1)S(1)}, bf16[64,512]{1,0:T(8,128)(2,1)S(1)}, u32[]{:S(2)}, u32[]{:S(2)}) collective-permute-start(bf16[64,512]{1,0:T(8,128)(2,1)S(1)} %add_convert_fusion.refs_3_.refs_12_.refs_1_), channel_id=1, source_target_pairs={{0,16},{1,17},{2,18},{3,19},{4,20},{5,21},{6,22},{7,23},{8,24},{9,... | collective-permute-start | bytes 196616 | tf_op jit(solution)/shard_map/ppermute | solution.py:55
  61.6 7.0 %collective-permute-start.21 = (bf16[144,256]{1,0:T(8,128)(2,1)S(1)}, bf16[144,256]{1,0:T(8,128)(2,1)S(1)}, u32[]{:S(2)}, u32[]{:S(2)}) collective-permute-start(bf16[144,256]{1,0:T(8,128)(2,1)S(1)} %get-tuple-element.104), channel_id=1, source_target_pairs={{0,8},{1,9},{2,10},{3,11},{4,12},{5,13},{6,14},{7,15},{8,0},{9,1},... | collective-permute-start | bytes 221192 | tf_op jit(solution)/shard_map/ppermute | solution.py:55
  62.7 8.9 %collective-permute-start.22 = (bf16[144,256]{1,0:T(8,128)(2,1)S(1)}, bf16[144,256]{1,0:T(8,128)(2,1)S(1)}, u32[]{:S(2)}, u32[]{:S(2)}) collective-permute-start(bf16[144,256]{1,0:T(8,128)(2,1)S(1)} %get-tuple-element.105), channel_id=1, source_target_pairs={{0,16},{1,17},{2,18},{3,19},{4,20},{5,21},{6,22},{7,23},{8,24},{9,... | collective-permute-start | bytes 221192 | tf_op jit(solution)/shard_map/ppermute | solution.py:55
  64.1 7.5 %collective-permute-start.23 = (bf16[144,256]{1,0:T(8,128)(2,1)S(1)}, bf16[144,256]{1,0:T(8,128)(2,1)S(1)}, u32[]{:S(2)}, u32[]{:S(2)}) collective-permute-start(bf16[144,256]{1,0:T(8,128)(2,1)S(1)} %get-tuple-element.106), channel_id=1, source_target_pairs={{0,24},{1,25},{2,26},{3,27},{4,28},{5,29},{6,30},{7,31},{8,16},{9,... | collective-permute-start | bytes 221192 | tf_op jit(solution)/shard_map/ppermute | solution.py:55
  67.0 12.6 %collective-permute-start.24 = (bf16[2,2,128,512]{3,2,1,0:T(8,128)(2,1)S(1)}, bf16[2,2,128,512]{3,2,1,0:T(8,128)(2,1)S(1)}, u32[]{:S(2)}, u32[]{:S(2)}) collective-permute-start(bf16[2,2,128,512]{3,2,1,0:T(8,128)(2,1)S(1)} %chip_send.1.refs_5_), channel_id=1, source_target_pairs={{0,4},{1,3},{2,6},{3,1},{4,0},{5,7},{6,2},{7,5},{8,12},{9,11},{10,... | collective-permute-start | bytes 1572872 | tf_op jit(solution)/shard_map/ppermute | solution.py:65
  68.6 9.2 %collective-permute-start.27 = (bf16[2,64,512]{2,1,0:T(8,128)(2,1)S(1)}, bf16[2,64,512]{2,1,0:T(8,128)(2,1)S(1)}, u32[]{:S(2)}, u32[]{:S(2)}) collective-permute-start(bf16[2,64,512]{2,1,0:T(8,128)(2,1)S(1)} %pad_maximum_fusion.1), channel_id=1, source_target_pairs={{0,8},{1,9},{2,10},{3,11},{4,12},{5,13},{6,14},{7,15},{8,0},{9,1},... | collective-permute-start | bytes 393224 | tf_op jit(solution)/shard_map/ppermute | solution.py:55
  72.1 8.7 %collective-permute-start.31 = (bf16[144,256]{1,0:T(8,128)(2,1)S(1)}, bf16[144,256]{1,0:T(8,128)(2,1)S(1)}, u32[]{:S(2)}, u32[]{:S(2)}) collective-permute-start(bf16[144,256]{1,0:T(8,128)(2,1)S(1)} %sum.1.refs_4_.refs_7_), channel_id=1, source_target_pairs={{0,24},{1,25},{2,26},{3,27},{4,28},{5,29},{6,30},{7,31},{8,16},{9,... | collective-permute-start | bytes 221192 | tf_op jit(solution)/shard_map/ppermute | solution.py:55
  74.3 8.3 %collective-permute-start.32 = (bf16[144,256]{1,0:T(8,128)(2,1)S(1)}, bf16[144,256]{1,0:T(8,128)(2,1)S(1)}, u32[]{:S(2)}, u32[]{:S(2)}) collective-permute-start(bf16[144,256]{1,0:T(8,128)(2,1)S(1)} %sum.1.refs_4_.refs_7_), channel_id=1, source_target_pairs={{0,4},{1,5},{2,6},{3,7},{4,0},{5,1},{6,2},{7,3},{8,12},{9,13},{10,... | collective-permute-start | bytes 221192 | tf_op jit(solution)/shard_map/ppermute | solution.py:55
  75.8 7.9 %collective-permute-start.29 = (bf16[144,256]{1,0:T(8,128)(2,1)S(1)}, bf16[144,256]{1,0:T(8,128)(2,1)S(1)}, u32[]{:S(2)}, u32[]{:S(2)}) collective-permute-start(bf16[144,256]{1,0:T(8,128)(2,1)S(1)} %sum.1.refs_4_.refs_7_), channel_id=1, source_target_pairs={{0,8},{1,9},{2,10},{3,11},{4,12},{5,13},{6,14},{7,15},{8,0},{9,1},... | collective-permute-start | bytes 221192 | tf_op jit(solution)/shard_map/ppermute | solution.py:55
  77.7 8.1 %collective-permute-start.30 = (bf16[144,256]{1,0:T(8,128)(2,1)S(1)}, bf16[144,256]{1,0:T(8,128)(2,1)S(1)}, u32[]{:S(2)}, u32[]{:S(2)}) collective-permute-start(bf16[144,256]{1,0:T(8,128)(2,1)S(1)} %sum.1.refs_4_.refs_7_), channel_id=1, source_target_pairs={{0,16},{1,17},{2,18},{3,19},{4,20},{5,21},{6,22},{7,23},{8,24},{9,... | collective-permute-start | bytes 221192 | tf_op jit(solution)/shard_map/ppermute | solution.py:55
  79.6 12.3 %collective-permute-start.28 = (bf16[4,64,512]{2,1,0:T(8,128)(2,1)S(1)}, bf16[4,64,512]{2,1,0:T(8,128)(2,1)S(1)}, u32[]{:S(2)}, u32[]{:S(2)}) collective-permute-start(bf16[4,64,512]{2,1,0:T(8,128)(2,1)S(1)} %column.1.refs_5_), channel_id=1, source_target_pairs={{0,4},{1,5},{2,6},{3,7},{4,0},{5,1},{6,2},{7,3},{8,12},{9,13},{10,... | collective-permute-start | bytes 786440 | tf_op jit(solution)/shard_map/ppermute | solution.py:55
  80.8 11.1 %collective-permute-start.25 = (bf16[2,128,512]{2,1,0:T(8,128)(2,1)S(1)}, bf16[2,128,512]{2,1,0:T(8,128)(2,1)S(1)}, u32[]{:S(2)}, u32[]{:S(2)}) collective-permute-start(bf16[2,128,512]{2,1,0:T(8,128)(2,1)S(1)} %forward.1), channel_id=1, source_target_pairs={{0,2},{1,5},{2,0},{3,7},{4,6},{5,1},{6,4},{7,3},{8,10},{9,13},{10,... | collective-permute-start | bytes 786440 | tf_op jit(solution)/shard_map/ppermute | solution.py:65
  83.2 4.5 %collective-permute-start.33 = (bf16[144,256]{1,0:T(8,128)(2,1)S(1)}, bf16[144,256]{1,0:T(8,128)(2,1)S(1)}, u32[]{:S(2)}, u32[]{:S(2)}) collective-permute-start(bf16[144,256]{1,0:T(8,128)(2,1)S(1)} %side.1.refs_11_), channel_id=1, source_target_pairs={{0,8},{1,9},{2,10},{3,11},{4,12},{5,13},{6,14},{7,15},{8,0},{9,1},... | collective-permute-start | bytes 221192 | tf_op jit(solution)/shard_map/ppermute | solution.py:55
  83.8 6.4 %collective-permute-start.34 = (bf16[144,256]{1,0:T(8,128)(2,1)S(1)}, bf16[144,256]{1,0:T(8,128)(2,1)S(1)}, u32[]{:S(2)}, u32[]{:S(2)}) collective-permute-start(bf16[144,256]{1,0:T(8,128)(2,1)S(1)} %side.1.refs_11_), channel_id=1, source_target_pairs={{0,16},{1,17},{2,18},{3,19},{4,20},{5,21},{6,22},{7,23},{8,24},{9,... | collective-permute-start | bytes 221192 | tf_op jit(solution)/shard_map/ppermute | solution.py:55
  85.8 6.2 %collective-permute-start.35 = (bf16[144,256]{1,0:T(8,128)(2,1)S(1)}, bf16[144,256]{1,0:T(8,128)(2,1)S(1)}, u32[]{:S(2)}, u32[]{:S(2)}) collective-permute-start(bf16[144,256]{1,0:T(8,128)(2,1)S(1)} %side.1.refs_11_), channel_id=1, source_target_pairs={{0,24},{1,25},{2,26},{3,27},{4,28},{5,29},{6,30},{7,31},{8,16},{9,... | collective-permute-start | bytes 221192 | tf_op jit(solution)/shard_map/ppermute | solution.py:55

commit v4 on v3

--- a/solution.py
+++ b/solution.py
@@ -13,6 +13,8 @@
 ANY = pl.BlockSpec(memory_space=pl.ANY)
 EDGE = 8
 LANES = 128
+FLIP_HID, FLIP_GP = 0, 1
+FIRST = 2
 ROOM = 0
 
 
@@ -106,19 +108,19 @@
         pad[c, pl.ds(at + 2, rows), EDGE : EDGE + ncols, :] = value[:, :, cut]
 
 
-def put_edges(pos, pad, edges):
+def put_edges(pos, pad, edges, flip):
     _, ncols, half = edges[0].shape
     last = pad.shape[1] - 6
-    odd = pos[2] & 1
+    odd = (pos[2] & 1) ^ flip
     for edge, at in zip(edges, (last * (1 - odd), last * odd)):
         for c, cut in cuts(half):
             edge[:, :, cut] = pad[c, pl.ds(at + 2, 2), EDGE : EDGE + ncols, :].astype(BF)
 
 
-def put_halo(pos, pad, near, far):
+def put_halo(pos, pad, near, far, flip):
     _, ncols, half = near.shape
     last = pad.shape[1] - 2
-    odd = pos[2] & 1
+    odd = (pos[2] & 1) ^ flip
     for edge, at in zip((near, far), (last * (1 - odd), last * odd)):
         for c, cut in cuts(half):
             pad[c, pl.ds(at, 2), EDGE : EDGE + ncols, :] = edge[:, :, cut].astype(F32)
@@ -142,7 +144,7 @@
 
         lax.fori_loop(0, n, body, 0)
     if edges:
-        put_edges(pos, hid, edges)
+        put_edges(pos, hid, edges, FLIP_HID)
 
 
 def conv_tiles(pad, taps, cut, ncols, starts, nr, cols, flip, emit):
@@ -169,7 +171,7 @@
         pad, mixed, slope = refs
     else:
         near, far, mixed, slope, pad = refs
-        put_halo(pos, pad, near, far)
+        put_halo(pos, pad, near, far, FLIP_HID)
     nrows, ncols, half = mixed.shape
     for c, cut in cuts(half):
         add = bias[:, cut]
@@ -186,36 +188,47 @@
             conv_tiles(pad.at[c], taps, cut, ncols, (0, nrows - 2), 2, 32, False, emit)
 
 
-def project_kernel(order, pos, weights, slope, *refs):
-    pieces, (gp, *edges) = refs[: len(order)], refs[len(order) :]
-    n, ncols, cin = pieces[0].shape
+def cot_blocks(pos, which, refs):
+    core = pos[3]
+    found = []
+    for i, ref in zip(which, refs):
+        if i in (2, 4):
+            found += [((4 - 2 * core if i == 2 else 3 + 2 * core) + (j if i == 2 else -j), ref.at[j]) for j in range(2)]
+        else:
+            found.append(({0: 0, 1: 1, 3: 6, 5: 7}[i], ref))
+    return found
+
+
+def project_kernel(which, pos, weights, slope, *refs):
+    pieces, (gp, *edges) = cot_blocks(pos, which, refs[: len(which)]), refs[len(which) :]
+    n, ncols, cin = pieces[0][1].shape
     half = slope.shape[2]
-    for k, piece in zip(order, pieces):
+    for k, piece in pieces:
         at = (pos[0] ^ k) * n
         res = lax.dot_general(
             piece[...].reshape(n * ncols, cin), weights[...], (((1,), (1,)), ((), ())), preferred_element_type=F32
         )
         put_rows(gp, at, res.reshape(n, ncols, half) * slope[pl.ds(at, n)])
     if edges:
-        put_edges(pos, gp, edges)
+        put_edges(pos, gp, edges, FLIP_GP)
 
 
 def outer_sum(pos, total, pieces, values, swap):
-    n, ncols, _ = pieces[0].shape
-    for k, piece in enumerate(pieces):
+    n, ncols, _ = pieces[0][1].shape
+    for i, (k, piece) in enumerate(pieces):
         a = piece[...].reshape(n * ncols, -1)
         b = values[pl.ds((pos[0] ^ k) * n, n)].reshape(n * ncols, -1)
         if swap:
             a, b = b, a
         part = lax.dot_general(a, b, (((0,), (0,)), ((), ())), preferred_element_type=F32)
-        if k == 0:
+        if i == 0:
             total[0 : part.shape[0], :] = part
         else:
             total[0 : part.shape[0], :] += part
 
 
 def w2_kernel(pos, mixed, *refs):
-    pieces, outs, total = refs[:8], refs[8:-1], refs[-1]
+    pieces, outs, total = cot_blocks(pos, range(6), refs[:6]), refs[6:-1], refs[-1]
     outer_sum(pos, total, pieces, mixed, True)
     n = outs[0].shape[0]
     for k, ref in enumerate(outs):
@@ -250,7 +263,7 @@
 
 def back_kernel(pos, taps, near, far, slope, pad, act, grad_b, total):
     nrows, ncols, half = act.shape
-    put_halo(pos, pad, near, far)
+    put_halo(pos, pad, near, far, FLIP_GP)
     for c, cut in cuts(half):
         total[...] = jnp.zeros_like(total)
 
@@ -268,7 +281,7 @@
 
 def w1_kernel(pos, act, small, grad_b, *refs):
     pieces, outs, total = refs[:8], refs[8:-1], refs[-1]
-    outer_sum(pos, total, pieces, act, False)
+    outer_sum(pos, total, list(enumerate(pieces)), act, False)
     cin = pieces[0].shape[2]
     total[cin:, :] = small[...]
     total[cin + 26 : cin + 27, :] = grad_b[...]
@@ -369,8 +382,9 @@
 
 
 def halved(chunks):
-    arrived = hop(jnp.stack([chunks[1], chunks[3]]), 2, 0).astype(F32)
-    return chunks[0] + arrived[0], chunks[2] + arrived[1]
+    other = 3 - FIRST
+    arrived = hop(jnp.stack([chunks[FIRST], chunks[3]]), 2 * FIRST, 0).astype(F32)
+    return chunks[0] + arrived[0], chunks[other] + arrived[1]
 
 
 def shards(inputs, cotangent, expand_w, expand_b, depth_k, depth_b, project_w):
@@ -405,21 +419,20 @@
         )
 
     in_pieces = {0: rows_own, 1: hop(inputs, 0, 1)}
-    cot_pieces = {0: cot_own, 1: hop(cotangent, 0, 1)}
+    cot_core = hop(cotangent, 0, 1)
     steps = {4: (1, 0), 2: (0, 2), 6: (1, 2)}
     for k, step in steps.items():
         in_pieces[k] = hop(inputs, *step)
-    first = expand((0, 1), (hidden,), after=(cot_pieces[1],))
+    first = expand((0, 1), (hidden,), after=(cot_core,))
     for k in steps:
         in_pieces[k + 1] = hop(tied(in_pieces[k], first[0]), 0, 1)
     second = expand((2, 4), first)
-    cot_start = tied(cotangent, in_pieces[2], in_pieces[4], second[1])
-    for k, step in steps.items():
-        cot_pieces[k] = hop(tied(cot_start, in_pieces[6]) if k == 6 else cot_start, *step)
+    cot_pair = cross(tied(jnp.stack([cot_own, cot_core]), in_pieces[2], in_pieces[4]), 0)
+    cot_far = hop(tied(cotangent, in_pieces[6]), *steps[6])
     in_pieces = [in_pieces[k] for k in range(8)]
     edges = (array(2, ncols, half),) * 2
     hidden, slope_one, *sent = expand((7,), expand((6, 3, 5), second), edges=edges)
-    hid_near, hid_far = meet(sent[0], 0), meet(sent[1], 1)
+    hid_near, hid_far = meet(sent[0], FLIP_HID), meet(sent[1], 1 - FLIP_HID)
 
     f32_full = array(nrows, ncols, half, dtype=F32)
     inner = kernel(
@@ -429,25 +442,26 @@
         lambda *refs: middle_kernel(False, *refs), "outer", (full, f32_full, padded),
         (pos, taps, bd, hid_near, hid_far), into=(*inner, hidden), **vpu,
     )
-    for k in steps:
-        cot_pieces[k + 1] = hop(tied(cot_pieces[k], mixed), 0, 1)
-
-    def project(order, into=(), after=(), edges=()):
+    cot_swap = hop(tied(cot_pair, slope_one), 0, 1)
+    cot_last = hop(tied(cot_far, mixed), 0, 1)
+    cot_pieces = (cot_own, cot_core, cot_pair, cot_far, cot_swap, cot_last)
+
+    def project(pieces, into=(), after=(), edges=()):
         return kernel(
-            lambda *refs: project_kernel(order, *refs), "project%d" % order[0], (padded,) + edges,
-            (pos, w2, slope_two, *(cot_pieces[k] for k in order)), into=into, after=after, **mm,
+            lambda *refs: project_kernel(pieces, *refs), "project%d" % pieces[0], (padded,) + edges,
+            (pos, w2, slope_two, *(cot_pieces[i] for i in pieces)), into=into, after=after, **mm,
         )
 
     def chunk_outs(rows, width):
         return (array(rows, width, dtype=F32),) + (array(rows, width),) * (groups - 1)
 
-    half_done = project((0, 1, 2, 4, 6), (grad_pre,))
+    half_done = project((0, 1, 2, 3), (grad_pre,))
     w2_chunks = kernel(
-        w2_kernel, "w2", chunk_outs(half // groups, cin), (pos, mixed, *(cot_pieces[k] for k in range(8))),
+        w2_kernel, "w2", chunk_outs(half // groups, cin), (pos, mixed, *cot_pieces),
         [pltpu.VMEM((half, cin), F32)], after=half_done, **mm,
     )
-    grad_pre, *sent = project((3, 5, 7), half_done, (w2_chunks[0],), edges)
-    gp_near, gp_far = meet(sent[0], 0), meet(sent[1], 1)
+    grad_pre, *sent = project((4, 5), half_done, (w2_chunks[0],), edges)
+    gp_near, gp_far = meet(sent[0], FLIP_GP), meet(sent[1], 1 - FLIP_GP)
     tail = 16 * groups
     small = kernel(taps_kernel, "taps", array(tail, half, dtype=F32), (pos, hidden, grad_pre), **vpu)
     four = groups == 4
@@ -457,7 +471,7 @@
         [pltpu.VMEM((8, LANES), F32)], after=(small, *w2_halves), into=(grad_pre,), **vpu,
     )
     if four:
-        w2_sent = hop(tied(w2_halves[1], small).astype(BF), 4, 0).astype(F32)
+        w2_sent = hop(tied(w2_halves[1], small).astype(BF), 2 * (3 - FIRST), 0).astype(F32)
         w2_chunk = (tied(w2_halves[0], grad_act) + w2_sent).astype(BF)
     else:
         w2_chunk = summed(tied(w2_chunks[0], grad_act), w2_chunks[1:])
@@ -480,18 +494,18 @@
     else:
         w2_blocks = [hop(w2_chunk, 2 * k, 0) if k else w2_chunk for k in range(groups)]
     arrived = cross(going, 0)
+    kept = kernel(chip_keep_kernel, "chip_keep", array(*two, dtype=F32), (pos, grad_act, w1, from_core), after=(going,), **mm)
     w1_parts = [hop(send, 2 * (k + 1), 0) for k, send in enumerate(w1_sends)]
-    w1_chunk = kernel(sum_kernel, "sum", array(*w1_own.shape), (pos, w1_own, *w1_parts), after=(going,), **long)
+    w1_chunk = kernel(sum_kernel, "sum", array(*w1_own.shape), (pos, w1_own, *w1_parts), after=(kept,), **long)
     w1_side = hop(w1_chunk, 1, 0)
     w1_near = [hop(w1_chunk, 2 * k, 0) if k else w1_chunk for k in range(groups)]
-    kept = kernel(
-        chip_keep_kernel, "chip_keep", array(*two, dtype=F32), (pos, grad_act, w1, from_core), after=(w1_chunk,), **mm
-    )
     w2_col = kernel(
-        column_kernel, "column", array(groups, half // groups + ROOM, cin), (pos, *w2_blocks), after=(kept,), **mm
+        column_kernel, "column", array(groups, half // groups + ROOM, cin), (pos, *w2_blocks), after=(w1_chunk,), **mm
     )
     w2_other = hop(w2_col, 1, 0)
-    forward = kernel(forward_kernel, "forward", array(*block), (pos, kept, arrived), **mm)
+    forward = kernel(
+        forward_kernel, "forward", array(*block), (pos, kept, arrived), after=(w1_side,), **mm
+    )
     onward = cross(forward, 1)
     w1_side = kernel(copy_kernel, "side", array(*w1_side.shape), (pos, w1_side), after=(w1_near[-1],), **long)
     w1_blocks = w1_near + [hop(w1_side, 2 * k, 0) if k else w1_side for k in range(groups)]

time: 94.4 us -> 91.1 us (0.965)
  waiting for transfers between devices: 11.5 us -> 9.12 us
  starting transfers between devices: 42 us -> 41 us
    ppermute x30 -> x27, waiting for transfers between devices: 11.5 us -> 8.84 us  [hop(): return lax.ppermute(value, AXES, pairs)]
    ppermute x30 -> x27, starting transfers between devices: 35.4 us -> 32.9 us  [hop(): return lax.ppermute(value, AXES, pairs)]
    ppermute x4, starting transfers between devices: 3.27 us -> 4.78 us  [meet(): return lax.ppermute(value, AXES, pairs)]
    ppermute x2 -> x3, starting transfers between devices: 3.33 us -> 3.37 us  [cross(): return lax.ppermute(value, AXES, pairs)]
  transfers between devices with their start and end apart: 36 -> 34, of which waited for: 6 -> 7; matrix products, arithmetic and copies ran while one was open for 0% -> 0% of each run, Pallas kernels for 32% -> 33%
where the time goes in v4:
time: 91.1 us; the launch traced here: 90.7 us
  starting transfers between devices  41 us (45%)
  Pallas kernels  34.1 us (37%)
  waiting for transfers between devices  9.12 us (10%)
  local copies, waits for them, and re-layouts  5.24 us (6%)
  between operations  0.98 us (1%)
    pallas_call x21, Pallas kernels, kernel(): pl.pallas_call(run, out_shape=out, in_specs=[SMEM] + [VMEM] * (len(args)...  34.1 us
    ppermute x27, starting transfers between devices, hop(): return lax.ppermute(value, AXES, pairs)  32.9 us
    ppermute x27, waiting for transfers between devices, hop(): return lax.ppermute(value, AXES, pairs)  8.84 us
    unnamed x12, local copies, waits for them, and re-layouts  5.23 us
    ppermute x4, starting transfers between devices, meet(): return lax.ppermute(value, AXES, pairs)  4.78 us
    ppermute x3, starting transfers between devices, cross(): return lax.ppermute(value, AXES, pairs)  3.37 us
  transfers between devices with their start and end apart: 34, of which 7 were waited for; matrix products, arithmetic and copies ran while one was open for 0% of the time, Pallas kernels for 33%

profile of v4, /device:TPU:0, one launch (start us, length us, event | category | flops | bytes accessed | tf_op | source)
XLA Modules:
  0.0 90.7 jit_solution(10921843221535668064)
XLA Ops:
  1.1 2.6 %collective-permute-start.4 = (bf16[2,128,512]{2,1,0:T(8,128)(2,1)}, bf16[2,128,512]{2,1,0:T(8,128)(2,1)S(1)}, u32[]{:S(2)}, u32[]{:S(2)}) collective-permute-start(bf16[2,128,512]{2,1,0:T(8,128)(2,1)} %refs_6_.1), channel_id=1, source_target_pairs={{0,2},{1,3},{2,0},{3,1},{4,6},{5,7},{6,4},{7,5},{8,10},{9,11},{10,... | collective-permute-start | bytes 786440 | tf_op jit(solution)/shard_map/ppermute | solution.py:57
  3.7 1.5 %collective-permute-start.6 = (bf16[2,128,512]{2,1,0:T(8,128)(2,1)}, bf16[2,128,512]{2,1,0:T(8,128)(2,1)S(1)}, u32[]{:S(2)}, u32[]{:S(2)}) collective-permute-start(bf16[2,128,512]{2,1,0:T(8,128)(2,1)} %refs_6_.1), channel_id=1, source_target_pairs={{0,4},{1,5},{2,6},{3,7},{4,0},{5,1},{6,2},{7,3},{8,12},{9,13},{10,... | collective-permute-start | bytes 786440 | tf_op jit(solution)/shard_map/ppermute | solution.py:57
  5.4 1.0 %copy-done = bf16[512,512]{1,0:T(8,128)(2,1)S(1)} copy-done((bf16[512,512]{1,0:T(8,128)(2,1)S(1)}, bf16[512,512]{1,0:T(8,128)(2,1)}, u32[]{:S(2)}) %copy-start) | copy-done | bytes 524312
  6.5 1.0 %copy-done.1 = bf16[512,512]{1,0:T(8,128)(2,1)S(1)} copy-done((bf16[512,512]{1,0:T(8,128)(2,1)S(1)}, bf16[512,512]{1,0:T(8,128)(2,1)}, u32[]{:S(2)}) %copy-start.1) | copy-done | bytes 524312
  7.5 0.9 %copy-done.2 = bf16[2,128,512]{2,1,0:T(8,128)(2,1)S(1)} copy-done((bf16[2,128,512]{2,1,0:T(8,128)(2,1)S(1)}, bf16[2,128,512]{2,1,0:T(8,128)(2,1)}, u32[]{:S(2)}) %copy-start.2) | copy-done | bytes 262168
  8.5 0.8 copy-done.3
  9.3 0.7 copy-done.4
  10.0 0.7 copy-done.5
  10.7 1.1 %prepare.1 = (bf16[512,256]{1,0:T(8,128)(2,1)S(1)}, f32[1,256]{1,0:T(1,128)S(1)}, f32[25,256]{1,0:T(8,128)S(1)}, f32[1,256]{1,0:T(1,128)S(1)}, bf16[256,512]{1,0...) custom-call(s32[4]{0:T(128)S(1)} %pad_add_fusion.refs_0_, ...), custom_call_target="tpu_custom_call" | custom-call | tf_op jit(solution)/shard_map/prepare/pallas_call | solution.py:31
  11.8 1.3 %collective-permute-done.6.refs_4_.refs_8_ = bf16[2,128,512]{2,1,0:T(8,128)(2,1)S(1)} collective-permute-done((bf16[2,128,512]{2,1,0:T(8,128)(2,1)}, bf16[2,128,512]{2,1,0:T(8,128)(2,1)S(1)}, u32[]{:S(2)}, u32[]{:S(2)}) %collective-permute-start.6) | collective-permute-done | bytes 262176 | tf_op jit(solution)/shard_map/ppermute | solution.py:57
  13.1 1.5 %collective-permute-start.10 = (bf16[2,2,128,512]{3,2,1,0:T(8,128)(2,1)S(1)}, bf16[2,2,128,512]{3,2,1,0:T(8,128)(2,1)S(1)}, u32[]{:S(2)}, u32[]{:S(2)}) collective-permute-start(bf16[2,2,128,512]{3,2,1,0:T(8,128)(2,1)S(1)} %pad_maximum_fusion), channel_id=1, source_target_pairs={{0,4},{1,3},{2,6},{3,1},{4,0},{5,7},{6,2},{7,5},{8,12},{9,11},{10,... | collective-permute-start | bytes 1572872 | tf_op jit(solution)/shard_map/ppermute | solution.py:67
  14.6 1.4 %expand0.1 = (f32[2,20,144,128]{3,2,1,0:T(8,128)S(1)}, bf16[16,128,256]{2,1,0:T(8,128)(2,1)S(1)}) custom-call(s32[4]{0:T(128)S(1)} %pad_add_fusion.refs_0_, bf16[512,256]{1,0:T(8,128)(2,1)S(1)} %get-tuple-element.63.refs_1_.refs_2_, f32[1,256]{1,0:T(1,128)S(1)} %get-tuple-element.64.refs_2_, ...), custom_call_target="tpu_custom_call", output_to_operand_aliasing={{0}: (6, {})} | custom-call | flops 1024 | bytes 1024 | tf_op jit(solution)/shard_map/expand0/pallas_call | solution.py:31
  16.6 1.2 %collective-permute-done.refs_3_.refs_10_ = bf16[2,128,512]{2,1,0:T(8,128)(2,1)S(1)} collective-permute-done((bf16[2,128,512]{2,1,0:T(8,128)(2,1)}, bf16[2,128,512]{2,1,0:T(8,128)(2,1)S(1)}, u32[]{:S(2)}, u32[]{:S(2)}) %collective-permute-start) | collective-permute-done | bytes 262176 | tf_op jit(solution)/shard_map/ppermute | solution.py:57
  17.8 2.7 %collective-permute-start.12 = (bf16[2,128,512]{2,1,0:T(8,128)(2,1)}, bf16[2,128,512]{2,1,0:T(8,128)(2,1)S(1)}, u32[]{:S(2)}, u32[]{:S(2)}) collective-permute-start(bf16[2,128,512]{2,1,0:T(8,128)(2,1)} %refs_7_.1), channel_id=1, source_target_pairs={{0,6},{1,7},{2,4},{3,5},{4,2},{5,3},{6,0},{7,1},{8,14},{9,15},{10,... | collective-permute-start | bytes 786440 | tf_op jit(solution)/shard_map/ppermute | solution.py:57
  20.4 1.4 %expand2.1 = (f32[2,20,144,128]{3,2,1,0:T(8,128)S(1)}, bf16[16,128,256]{2,1,0:T(8,128)(2,1)S(1)}) custom-call(s32[4]{0:T(128)S(1)} %pad_add_fusion.refs_0_, bf16[512,256]{1,0:T(8,128)(2,1)S(1)} %get-tuple-element.63.refs_1_.refs_2_, f32[1,256]{1,0:T(1,128)S(1)} %get-tuple-element.64.refs_2_, ...), custom_call_target="tpu_custom_call", output_to_operand_aliasing={{0}: (5, {}), {1}: (6, {})} | custom-call | flops 1024 | bytes 1024 | tf_op jit(solution)/shard_map/expand2/pallas_call | solution.py:31
  21.9 1.8 %expand6.1 = (f32[2,20,144,128]{3,2,1,0:T(8,128)S(1)}, bf16[16,128,256]{2,1,0:T(8,128)(2,1)S(1)}) custom-call(s32[4]{0:T(128)S(1)} %pad_add_fusion.refs_0_, bf16[512,256]{1,0:T(8,128)(2,1)S(1)} %get-tuple-element.63.refs_1_.refs_2_, f32[1,256]{1,0:T(1,128)S(1)} %get-tuple-element.64.refs_2_, ...), custom_call_target="tpu_custom_call", output_to_operand_aliasing={{0}: (6, {}), {1}: (7, {})} | custom-call | flops 1024 | bytes 1024 | tf_op jit(solution)/shard_map/expand6/pallas_call | solution.py:31
  23.7 0.9 %expand7.1 = (f32[2,20,144,128]{3,2,1,0:T(8,128)S(1)}, bf16[16,128,256]{2,1,0:T(8,128)(2,1)S(1)}, bf16[2,128,256]{2,1,0:T(8,128)(2,1)S(1)}, bf16[2,128,256]{2,1,0:T(8,128)(2,1)S(1)}) custom-call(s32[4]{0:T(128)S(1)} %pad_add_fusion.refs_0_, bf16[512,256]{1,0:T(8,128)(2,1)S(1)} %get-tuple-element.63.refs_1_.refs_2_, ...), custom_call_target="tpu_custom_call", output_to_operand_aliasing={{0}: (4, {}), {1}: (5, {})} | custom-call | flops 1024 | bytes 1024 | tf_op jit(solution)/shard_map/expand7/pallas_call | solution.py:31
  24.9 1.6 %collective-permute-start.8 = (bf16[2,128,256]{2,1,0:T(8,128)(2,1)S(1)}, bf16[2,128,256]{2,1,0:T(8,128)(2,1)S(1)}, u32[]{:S(2)}, u32[]{:S(2)}) collective-permute-start(bf16[2,128,256]{2,1,0:T(8,128)(2,1)S(1)} %get-tuple-element.76), channel_id=1, source_target_pairs={{0,8},{1,9},{2,10},{3,11},{4,12},{5,13},{6,14},{7,15},{8,0},{9,1},... | collective-permute-start | bytes 393224 | tf_op jit(solution)/shard_map/ppermute | solution.py:77
  26.5 0.7 collective-permute-start.9
  27.1 4.8 %inner.1 = (bf16[16,128,256]{2,1,0:T(8,128)(2,1)S(1)}, f32[16,128,256]{2,1,0:T(8,128)S(1)}) custom-call(s32[4]{0:T(128)S(1)} %pad_add_fusion.refs_0_, f32[25,256]{1,0:T(8,128)S(1)} %get-tuple-element.60.refs_1_, f32[1,256]{1,0:T(1,128)S(1)} %get-tuple-element.62.refs_2_, f32[2,20,144,128]{3,2,1,0:T(8,128)S(1)} %get-tuple-element.78.refs_3_.refs_7_), custom_call_target="tpu_custom_call" | custom-call | flops 1024 | bytes 1024 | tf_op jit(solution)/shard_map/inner/pallas_call | solution.py:31
  31.9 2.1 %outer.1 = (bf16[16,128,256]{2,1,0:T(8,128)(2,1)S(1)}, f32[16,128,256]{2,1,0:T(8,128)S(1)}, f32[2,20,144,128]{3,2,1,0:T(8,128)S(1)}) custom-call(s32[4]{0:T(128)S(1)} %pad_add_fusion.refs_0_, f32[25,256]{1,0:T(8,128)S(1)} %get-tuple-element.60.refs_1_, ...), custom_call_target="tpu_custom_call", output_to_operand_aliasing={{0}: (5, {}), {1}: (6, {}), {2}: (7, {})} | custom-call | flops 1024 | bytes 1024 | tf_op jit(solution)/shard_map/outer/pallas_call | solution.py:31
  34.3 1.1 %project0.1.refs_8_.refs_6_ = f32[2,20,144,128]{3,2,1,0:T(8,128)S(1)} custom-call(s32[4]{0:T(128)S(1)} %pad_add_fusion.refs_0_, bf16[256,512]{1,0:T(8,128)(2,1)S(1)} %get-tuple-element.61.refs_1_, f32[16,128,256]{2,1,0:T(8,128)S(1)} %get-tuple-element.81.refs_2_, ...), custom_call_target="tpu_custom_call", output_to_operand_aliasing={{}: (7, {})} | custom-call | flops 1024 | bytes 1024 | tf_op jit(solution)/shard_map/project0/pallas_call | solution.py:31
  35.7 1.3 %w2.1 = (f32[64,512]{1,0:T(8,128)S(1)}, bf16[64,512]{1,0:T(8,128)(2,1)S(1)}, bf16[64,512]{1,0:T(8,128)(2,1)S(1)}, bf16[64,512]{1,0:T(8,128)(2,1)S(1)}) custom-call(s32[4]{0:T(128)S(1)} %pad_add_fusion.refs_0_, bf16[16,128,256]{2,1,0:T(8,128)(2,1)S(1)} %get-tuple-element.86.refs_1_, bf16[2,128,512]{2,1,0:T(8,128)(2,1)S(1)} %get-tuple-element.59.refs_3_.refs_2_.refs_1_, ...), custom_call_target="tpu_custom_call" | custom-call | flops 1024 | bytes 1024 | tf_op jit(solution)/shard_map/w2/pallas_call | solution.py:31
  37.0 4.7 %collective-permute-start.16 = (bf16[2,64,512]{2,1,0:T(8,128)(2,1)S(1)}, bf16[2,64,512]{2,1,0:T(8,128)(2,1)S(1)}, u32[]{:S(2)}, u32[]{:S(2)}) collective-permute-start(bf16[2,64,512]{2,1,0:T(8,128)(2,1)S(1)} %pad_maximum_fusion.1), channel_id=1, source_target_pairs={{0,16},{1,17},{2,18},{3,19},{4,20},{5,21},{6,22},{7,23},{8,24},{9,... | collective-permute-start | bytes 393224 | tf_op jit(solution)/shard_map/ppermute | solution.py:57
  41.7 1.0 %project4.1 = (f32[2,20,144,128]{3,2,1,0:T(8,128)S(1)}, bf16[2,128,256]{2,1,0:T(8,128)(2,1)S(1)}, bf16[2,128,256]{2,1,0:T(8,128)(2,1)S(1)}) custom-call(s32[4]{0:T(128)S(1)} %pad_add_fusion.refs_0_, bf16[256,512]{1,0:T(8,128)(2,1)S(1)} %get-tuple-element.61.refs_1_, f32[16,128,256]{2,1,0:T(8,128)S(1)} %get-tuple-element.81.refs_2_, ...), custom_call_target="tpu_custom_call", output_to_operand_aliasing={{0}: (6, {})} | custom-call | flops 1024 | bytes 1024 | tf_op jit(solution)/shard_map/project4/pallas_call | solution.py:31
  42.7 0.7 collective-permute-start.14
  43.4 1.9 %collective-permute-start.15 = (bf16[2,128,256]{2,1,0:T(8,128)(2,1)S(1)}, bf16[2,128,256]{2,1,0:T(8,128)(2,1)S(1)}, u32[]{:S(2)}, u32[]{:S(2)}) collective-permute-start(bf16[2,128,256]{2,1,0:T(8,128)(2,1)S(1)} %get-tuple-element.91), channel_id=1, source_target_pairs={{0,8},{1,9},{2,10},{3,11},{4,12},{5,13},{6,14},{7,15},{8,0},{9,1},... | collective-permute-start | bytes 393224 | tf_op jit(solution)/shard_map/ppermute | solution.py:77
  45.3 4.3 %taps.1.refs_5_.refs_2_ = f32[64,256]{1,0:T(8,128)S(1)} custom-call(s32[4]{0:T(128)S(1)} %pad_add_fusion.refs_0_, f32[2,20,144,128]{3,2,1,0:T(8,128)S(1)} %get-tuple-element.92.refs_1_, f32[2,20,144,128]{3,2,1,0:T(8,128)S(1)} %get-tuple-element.93.refs_2_.refs_8_), custom_call_target="tpu_custom_call" | custom-call | flops 1024 | bytes 1024 | tf_op jit(solution)/shard_map/taps/pallas_call | solution.py:31
  49.9 4.5 %back.1 = (f32[2,20,144,128]{3,2,1,0:T(8,128)S(1)}, bf16[16,128,256]{2,1,0:T(8,128)(2,1)S(1)}, f32[1,256]{1,0:T(1,128)S(1)}) custom-call(s32[4]{0:T(128)S(1)} %pad_add_fusion.refs_0_, f32[25,256]{1,0:T(8,128)S(1)} %get-tuple-element.60.refs_1_, bf16[2,128,256]{2,1,0:T(8,128)(2,1)S(1)} %collective-permute-done.14.refs_2_, ...), custom_call_target="tpu_custom_call", output_to_operand_aliasing={{0}: (8, {})} | custom-call | flops 1024 | bytes 1024 | tf_op jit(solution)/shard_map/back/pallas_call | solution.py:31
  54.5 1.0 %core.1.refs_13_ = bf16[4,2,128,512]{3,2,1,0:T(8,128)(2,1)S(1)} custom-call(s32[4]{0:T(128)S(1)} %pad_add_fusion.refs_0_, bf16[16,128,256]{2,1,0:T(8,128)(2,1)S(1)} %get-tuple-element.97.refs_1_, bf16[512,256]{1,0:T(8,128)(2,1)S(1)} %get-tuple-element.63.refs_1_.refs_2_, bf16[64,512]{1,0:T(8,128)(2,1)S(1)} %add_convert_fusion.refs_3_.refs_12_.refs_1_), custom_call_target="tpu_custom_call" | custom-call | flops 1024 | bytes 1024 | tf_op jit(solution)/shard_map/core/pallas_call | solution.py:31
  55.6 2.6 %collective-permute-start.25 = (bf16[64,512]{1,0:T(8,128)(2,1)S(1)}, bf16[64,512]{1,0:T(8,128)(2,1)S(1)}, u32[]{:S(2)}, u32[]{:S(2)}) collective-permute-start(bf16[64,512]{1,0:T(8,128)(2,1)S(1)} %add_convert_fusion.refs_3_.refs_12_.refs_1_), channel_id=1, source_target_pairs={{0,16},{1,17},{2,18},{3,19},{4,20},{5,21},{6,22},{7,23},{8,24},{9,... | collective-permute-start | bytes 196616 | tf_op jit(solution)/shard_map/ppermute | solution.py:57
  58.1 1.3 %w1.1 = (f32[144,256]{1,0:T(8,128)S(1)}, bf16[144,256]{1,0:T(8,128)(2,1)S(1)}, bf16[144,256]{1,0:T(8,128)(2,1)S(1)}, bf16[144,256]{1,0:T(8,128)(2,1)S(1)}) custom-call(s32[4]{0:T(128)S(1)} %pad_add_fusion.refs_0_, bf16[16,128,256]{2,1,0:T(8,128)(2,1)S(1)} %get-tuple-element.97.refs_1_, f32[64,256]{1,0:T(8,128)S(1)} %taps.1.refs_5_.refs_2_, ...), custom_call_target="tpu_custom_call" | custom-call | flops 1024 | bytes 1024 | tf_op jit(solution)/shard_map/w1/pallas_call | solution.py:31
  59.9 1.9 %collective-permute-start.21 = (bf16[144,256]{1,0:T(8,128)(2,1)S(1)}, bf16[144,256]{1,0:T(8,128)(2,1)S(1)}, u32[]{:S(2)}, u32[]{:S(2)}) collective-permute-start(bf16[144,256]{1,0:T(8,128)(2,1)S(1)} %get-tuple-element.103), channel_id=1, source_target_pairs={{0,16},{1,17},{2,18},{3,19},{4,20},{5,21},{6,22},{7,23},{8,24},{9,... | collective-permute-start | bytes 221192 | tf_op jit(solution)/shard_map/ppermute | solution.py:57
  61.8 2.1 %collective-permute-start.22 = (bf16[144,256]{1,0:T(8,128)(2,1)S(1)}, bf16[144,256]{1,0:T(8,128)(2,1)S(1)}, u32[]{:S(2)}, u32[]{:S(2)}) collective-permute-start(bf16[144,256]{1,0:T(8,128)(2,1)S(1)} %get-tuple-element.104), channel_id=1, source_target_pairs={{0,24},{1,25},{2,26},{3,27},{4,28},{5,29},{6,30},{7,31},{8,16},{9,... | collective-permute-start | bytes 221192 | tf_op jit(solution)/shard_map/ppermute | solution.py:57
  64.0 0.9 chip_send.1.refs_4_
  64.8 1.5 %collective-permute-start.19 = (bf16[2,2,128,512]{3,2,1,0:T(8,128)(2,1)S(1)}, bf16[2,2,128,512]{3,2,1,0:T(8,128)(2,1)S(1)}, u32[]{:S(2)}, u32[]{:S(2)}) collective-permute-start(bf16[2,2,128,512]{3,2,1,0:T(8,128)(2,1)S(1)} %chip_send.1.refs_4_), channel_id=1, source_target_pairs={{0,4},{1,3},{2,6},{3,1},{4,0},{5,7},{6,2},{7,5},{8,12},{9,11},{10,... | collective-permute-start | bytes 1572872 | tf_op jit(solution)/shard_map/ppermute | solution.py:67
  66.4 0.9 chip_keep.1.refs_5_.refs_1_.refs_2_
  67.3 1.6 %collective-permute-done.21.refs_3_ = bf16[144,256]{1,0:T(8,128)(2,1)S(1)} collective-permute-done((bf16[144,256]{1,0:T(8,128)(2,1)S(1)}, bf16[144,256]{1,0:T(8,128)(2,1)S(1)}, u32[]{:S(2)}, u32[]{:S(2)}) %collective-permute-start.21) | collective-permute-done | bytes 73760 | tf_op jit(solution)/shard_map/ppermute | solution.py:57
  69.4 1.5 %collective-permute-start.23 = (bf16[144,256]{1,0:T(8,128)(2,1)S(1)}, bf16[144,256]{1,0:T(8,128)(2,1)S(1)}, u32[]{:S(2)}, u32[]{:S(2)}) collective-permute-start(bf16[144,256]{1,0:T(8,128)(2,1)S(1)} %sum.1.refs_5_.refs_7_), channel_id=1, source_target_pairs={{0,4},{1,5},{2,6},{3,7},{4,0},{5,1},{6,2},{7,3},{8,12},{9,13},{10,... | collective-permute-start | bytes 221192 | tf_op jit(solution)/shard_map/ppermute | solution.py:57
  71.0 1.8 %collective-permute-start.30 = (bf16[144,256]{1,0:T(8,128)(2,1)S(1)}, bf16[144,256]{1,0:T(8,128)(2,1)S(1)}, u32[]{:S(2)}, u32[]{:S(2)}) collective-permute-start(bf16[144,256]{1,0:T(8,128)(2,1)S(1)} %sum.1.refs_5_.refs_7_), channel_id=1, source_target_pairs={{0,24},{1,25},{2,26},{3,27},{4,28},{5,29},{6,30},{7,31},{8,16},{9,... | collective-permute-start | bytes 221192 | tf_op jit(solution)/shard_map/ppermute | solution.py:57
  73.2 2.1 %collective-permute-start.29 = (bf16[144,256]{1,0:T(8,128)(2,1)S(1)}, bf16[144,256]{1,0:T(8,128)(2,1)S(1)}, u32[]{:S(2)}, u32[]{:S(2)}) collective-permute-start(bf16[144,256]{1,0:T(8,128)(2,1)S(1)} %sum.1.refs_5_.refs_7_), channel_id=1, source_target_pairs={{0,16},{1,17},{2,18},{3,19},{4,20},{5,21},{6,22},{7,23},{8,24},{9,... | collective-permute-start | bytes 221192 | tf_op jit(solution)/shard_map/ppermute | solution.py:57
  75.9 2.2 %collective-permute-start.27 = (bf16[4,64,512]{2,1,0:T(8,128)(2,1)S(1)}, bf16[4,64,512]{2,1,0:T(8,128)(2,1)S(1)}, u32[]{:S(2)}, u32[]{:S(2)}) collective-permute-start(bf16[4,64,512]{2,1,0:T(8,128)(2,1)S(1)} %column.1.refs_5_), channel_id=1, source_target_pairs={{0,4},{1,5},{2,6},{3,7},{4,0},{5,1},{6,2},{7,3},{8,12},{9,13},{10,... | collective-permute-start | bytes 786440 | tf_op jit(solution)/shard_map/ppermute | solution.py:57
  78.1 0.6 forward.1
  79.9 2.5 %collective-permute-start.32 = (bf16[144,256]{1,0:T(8,128)(2,1)S(1)}, bf16[144,256]{1,0:T(8,128)(2,1)S(1)}, u32[]{:S(2)}, u32[]{:S(2)}) collective-permute-start(bf16[144,256]{1,0:T(8,128)(2,1)S(1)} %side.1.refs_11_), channel_id=1, source_target_pairs={{0,16},{1,17},{2,18},{3,19},{4,20},{5,21},{6,22},{7,23},{8,24},{9,... | collective-permute-start | bytes 221192 | tf_op jit(solution)/shard_map/ppermute | solution.py:57
  82.5 1.6 %collective-permute-start.33 = (bf16[144,256]{1,0:T(8,128)(2,1)S(1)}, bf16[144,256]{1,0:T(8,128)(2,1)S(1)}, u32[]{:S(2)}, u32[]{:S(2)}) collective-permute-start(bf16[144,256]{1,0:T(8,128)(2,1)S(1)} %side.1.refs_11_), channel_id=1, source_target_pairs={{0,24},{1,25},{2,26},{3,27},{4,28},{5,29},{6,30},{7,31},{8,16},{9,... | collective-permute-start | bytes 221192 | tf_op jit(solution)/shard_map/ppermute | solution.py:57
  84.1 1.1 %collective-permute-done.32.refs_13_ = bf16[144,256]{1,0:T(8,128)(2,1)S(1)} collective-permute-done((bf16[144,256]{1,0:T(8,128)(2,1)S(1)}, bf16[144,256]{1,0:T(8,128)(2,1)S(1)}, u32[]{:S(2)}, u32[]{:S(2)}) %collective-permute-start.32) | collective-permute-done | bytes 73760 | tf_op jit(solution)/shard_map/ppermute | solution.py:57
  85.2 3.4 %collective-permute-done.33.refs_14_ = bf16[144,256]{1,0:T(8,128)(2,1)S(1)} collective-permute-done((bf16[144,256]{1,0:T(8,128)(2,1)S(1)}, bf16[144,256]{1,0:T(8,128)(2,1)S(1)}, u32[]{:S(2)}, u32[]{:S(2)}) %collective-permute-start.33) | collective-permute-done | bytes 73760 | tf_op jit(solution)/shard_map/ppermute | solution.py:57
  88.6 2.0 %last.1 = (bf16[2,128,512]{2,1,0:T(8,128)(2,1)}, f32[512,512]{1,0:T(8,128)}, f32[512,512]{1,0:T(8,128)}, f32[25,512]{1,0:T(8,128)}, f32[1,512]{1,0:T(1,128)}, /*index=5*/f32[1,512]{1,0:T(1,128)}) custom-call(s32[4]{0:T(128)S(1)} %pad_add_fusion.refs_0_, bf16[2,128,512]{2,1,0:T(8,128)(2,1)S(1)} %get-tuple-element.59.refs_3_.refs_2_.refs_1_, ...), custom_call_target="tpu_custom_call" | custom-call | tf_op jit(solution)/shard_map/last/pallas_call | solution.py:31
  (62 shorter events, 5.9 us)
Async XLA Ops:
  0.6 11.1 %collective-permute-start.2 = (bf16[2,128,512]{2,1,0:T(8,128)(2,1)}, bf16[2,128,512]{2,1,0:T(8,128)(2,1)S(1)}, u32[]{:S(2)}, u32[]{:S(2)}) collective-permute-start(bf16[2,128,512]{2,1,0:T(8,128)(2,1)} %refs_7_.1), channel_id=1, source_target_pairs={{0,1},{1,0},{2,3},{3,2},{4,5},{5,4},{6,7},{7,6},{8,9},{9,8},{10,11... | collective-permute-start | bytes 786440 | tf_op jit(solution)/shard_map/ppermute | solution.py:57
  1.1 10.7 %collective-permute-start.4 = (bf16[2,128,512]{2,1,0:T(8,128)(2,1)}, bf16[2,128,512]{2,1,0:T(8,128)(2,1)S(1)}, u32[]{:S(2)}, u32[]{:S(2)}) collective-permute-start(bf16[2,128,512]{2,1,0:T(8,128)(2,1)} %refs_6_.1), channel_id=1, source_target_pairs={{0,2},{1,3},{2,0},{3,1},{4,6},{5,7},{6,4},{7,5},{8,10},{9,11},{10,... | collective-permute-start | bytes 786440 | tf_op jit(solution)/shard_map/ppermute | solution.py:57
  3.7 9.4 %collective-permute-start.6 = (bf16[2,128,512]{2,1,0:T(8,128)(2,1)}, bf16[2,128,512]{2,1,0:T(8,128)(2,1)S(1)}, u32[]{:S(2)}, u32[]{:S(2)}) collective-permute-start(bf16[2,128,512]{2,1,0:T(8,128)(2,1)} %refs_6_.1), channel_id=1, source_target_pairs={{0,4},{1,5},{2,6},{3,7},{4,0},{5,1},{6,2},{7,3},{8,12},{9,13},{10,... | collective-permute-start | bytes 786440 | tf_op jit(solution)/shard_map/ppermute | solution.py:57
  5.2 9.4 %collective-permute-start.1 = (bf16[2,128,512]{2,1,0:T(8,128)(2,1)}, bf16[2,128,512]{2,1,0:T(8,128)(2,1)S(1)}, u32[]{:S(2)}, u32[]{:S(2)}) collective-permute-start(bf16[2,128,512]{2,1,0:T(8,128)(2,1)} %refs_6_.1), channel_id=1, source_target_pairs={{0,1},{1,0},{2,3},{3,2},{4,5},{5,4},{6,7},{7,6},{8,9},{9,8},{10,11... | collective-permute-start | bytes 786440 | tf_op jit(solution)/shard_map/ppermute | solution.py:57
  5.2 12.5 %collective-permute-start = (bf16[2,128,512]{2,1,0:T(8,128)(2,1)}, bf16[2,128,512]{2,1,0:T(8,128)(2,1)S(1)}, u32[]{:S(2)}, u32[]{:S(2)}) collective-permute-start(bf16[2,128,512]{2,1,0:T(8,128)(2,1)} %refs_6_.1), channel_id=1, source_target_pairs={{0,6},{1,7},{2,4},{3,5},{4,2},{5,3},{6,0},{7,1},{8,14},{9,15},{10,... | collective-permute-start | bytes 786440 | tf_op jit(solution)/shard_map/ppermute | solution.py:57
  5.4 1.0 %copy-start = (bf16[512,512]{1,0:T(8,128)(2,1)S(1)}, bf16[512,512]{1,0:T(8,128)(2,1)}, u32[]{:S(2)}) copy-start(bf16[512,512]{1,0:T(8,128)(2,1)} %refs_1_.1) | copy-start | bytes 1572868
  6.5 1.0 %copy-start.1 = (bf16[512,512]{1,0:T(8,128)(2,1)S(1)}, bf16[512,512]{1,0:T(8,128)(2,1)}, u32[]{:S(2)}) copy-start(bf16[512,512]{1,0:T(8,128)(2,1)} %refs_5_.1) | copy-start | bytes 1572868
  7.5 0.9 %copy-start.2 = (bf16[2,128,512]{2,1,0:T(8,128)(2,1)S(1)}, bf16[2,128,512]{2,1,0:T(8,128)(2,1)}, u32[]{:S(2)}) copy-start(bf16[2,128,512]{2,1,0:T(8,128)(2,1)} %refs_6_.1) | copy-start | bytes 786436
  8.5 0.8 copy-start.3
  9.3 0.7 copy-start.4
  10.0 0.7 copy-start.5
  13.1 11.8 %collective-permute-start.10 = (bf16[2,2,128,512]{3,2,1,0:T(8,128)(2,1)S(1)}, bf16[2,2,128,512]{3,2,1,0:T(8,128)(2,1)S(1)}, u32[]{:S(2)}, u32[]{:S(2)}) collective-permute-start(bf16[2,2,128,512]{3,2,1,0:T(8,128)(2,1)S(1)} %pad_maximum_fusion), channel_id=1, source_target_pairs={{0,4},{1,3},{2,6},{3,1},{4,0},{5,7},{6,2},{7,5},{8,12},{9,11},{10,... | collective-permute-start | bytes 1572872 | tf_op jit(solution)/shard_map/ppermute | solution.py:67
  16.0 5.8 %collective-permute-start.5 = (bf16[2,128,512]{2,1,0:T(8,128)(2,1)S(1)}, bf16[2,128,512]{2,1,0:T(8,128)(2,1)S(1)}, u32[]{:S(2)}, u32[]{:S(2)}) collective-permute-start(bf16[2,128,512]{2,1,0:T(8,128)(2,1)S(1)} %collective-permute-done.4.refs_3_.refs_6_), channel_id=1, source_target_pairs={{0,1},{1,0},{2,3},{3,2},{4,5},{5,4},{6,7},{7,6},{8,9},{9,8},{10,11... | collective-permute-start | bytes 786440 | tf_op jit(solution)/shard_map/ppermute | solution.py:57
  16.1 5.8 %collective-permute-start.7 = (bf16[2,128,512]{2,1,0:T(8,128)(2,1)S(1)}, bf16[2,128,512]{2,1,0:T(8,128)(2,1)S(1)}, u32[]{:S(2)}, u32[]{:S(2)}) collective-permute-start(bf16[2,128,512]{2,1,0:T(8,128)(2,1)S(1)} %collective-permute-done.6.refs_4_.refs_8_), channel_id=1, source_target_pairs={{0,1},{1,0},{2,3},{3,2},{4,5},{5,4},{6,7},{7,6},{8,9},{9,8},{10,11... | collective-permute-start | bytes 786440 | tf_op jit(solution)/shard_map/ppermute | solution.py:57
  17.8 5.9 %collective-permute-start.3 = (bf16[2,128,512]{2,1,0:T(8,128)(2,1)S(1)}, bf16[2,128,512]{2,1,0:T(8,128)(2,1)S(1)}, u32[]{:S(2)}, u32[]{:S(2)}) collective-permute-start(bf16[2,128,512]{2,1,0:T(8,128)(2,1)S(1)} %collective-permute-done.refs_3_.refs_10_), channel_id=1, source_target_pairs={{0,1},{1,0},{2,3},{3,2},{4,5},{5,4},{6,7},{7,6},{8,9},{9,8},{10,11... | collective-permute-start | bytes 786440 | tf_op jit(solution)/shard_map/ppermute | solution.py:57
  17.8 16.3 %collective-permute-start.12 = (bf16[2,128,512]{2,1,0:T(8,128)(2,1)}, bf16[2,128,512]{2,1,0:T(8,128)(2,1)S(1)}, u32[]{:S(2)}, u32[]{:S(2)}) collective-permute-start(bf16[2,128,512]{2,1,0:T(8,128)(2,1)} %refs_7_.1), channel_id=1, source_target_pairs={{0,6},{1,7},{2,4},{3,5},{4,2},{5,3},{6,0},{7,1},{8,14},{9,15},{10,... | collective-permute-start | bytes 786440 | tf_op jit(solution)/shard_map/ppermute | solution.py:57
  24.9 10.8 %collective-permute-start.11 = (bf16[2,2,128,512]{3,2,1,0:T(8,128)(2,1)S(1)}, bf16[2,2,128,512]{3,2,1,0:T(8,128)(2,1)S(1)}, u32[]{:S(2)}, u32[]{:S(2)}) collective-permute-start(bf16[2,2,128,512]{3,2,1,0:T(8,128)(2,1)S(1)} %collective-permute-done.10.refs_5_.refs_4_), channel_id=1, source_target_pairs={{0,1},{1,0},{2,3},{3,2},{4,5},{5,4},{6,7},{7,6},{8,9},{9,8},{10,11... | collective-permute-start | bytes 1572872 | tf_op jit(solution)/shard_map/ppermute | solution.py:57
  24.9 7.0 %collective-permute-start.8 = (bf16[2,128,256]{2,1,0:T(8,128)(2,1)S(1)}, bf16[2,128,256]{2,1,0:T(8,128)(2,1)S(1)}, u32[]{:S(2)}, u32[]{:S(2)}) collective-permute-start(bf16[2,128,256]{2,1,0:T(8,128)(2,1)S(1)} %get-tuple-element.76), channel_id=1, source_target_pairs={{0,8},{1,9},{2,10},{3,11},{4,12},{5,13},{6,14},{7,15},{8,0},{9,1},... | collective-permute-start | bytes 393224 | tf_op jit(solution)/shard_map/ppermute | solution.py:77
  26.5 5.4 %collective-permute-start.9 = (bf16[2,128,256]{2,1,0:T(8,128)(2,1)S(1)}, bf16[2,128,256]{2,1,0:T(8,128)(2,1)S(1)}, u32[]{:S(2)}, u32[]{:S(2)}) collective-permute-start(bf16[2,128,256]{2,1,0:T(8,128)(2,1)S(1)} %get-tuple-element.77), channel_id=1, source_target_pairs={{8,16},{9,17},{10,18},{11,19},{12,20},{13,21},{14,22},{15,23},{16,... | collective-permute-start | bytes 393224 | tf_op jit(solution)/shard_map/ppermute | solution.py:77
  34.1 1.6 %collective-permute-start.13 = (bf16[2,128,512]{2,1,0:T(8,128)(2,1)S(1)}, bf16[2,128,512]{2,1,0:T(8,128)(2,1)S(1)}, u32[]{:S(2)}, u32[]{:S(2)}) collective-permute-start(bf16[2,128,512]{2,1,0:T(8,128)(2,1)S(1)} %collective-permute-done.12.refs_6_.refs_5_), channel_id=1, source_target_pairs={{0,1},{1,0},{2,3},{3,2},{4,5},{5,4},{6,7},{7,6},{8,9},{9,8},{10,11... | collective-permute-start | bytes 786440 | tf_op jit(solution)/shard_map/ppermute | solution.py:57
  37.0 12.6 %collective-permute-start.16 = (bf16[2,64,512]{2,1,0:T(8,128)(2,1)S(1)}, bf16[2,64,512]{2,1,0:T(8,128)(2,1)S(1)}, u32[]{:S(2)}, u32[]{:S(2)}) collective-permute-start(bf16[2,64,512]{2,1,0:T(8,128)(2,1)S(1)} %pad_maximum_fusion.1), channel_id=1, source_target_pairs={{0,16},{1,17},{2,18},{3,19},{4,20},{5,21},{6,22},{7,23},{8,24},{9,... | collective-permute-start | bytes 393224 | tf_op jit(solution)/shard_map/ppermute | solution.py:57
  42.7 7.2 %collective-permute-start.14 = (bf16[2,128,256]{2,1,0:T(8,128)(2,1)S(1)}, bf16[2,128,256]{2,1,0:T(8,128)(2,1)S(1)}, u32[]{:S(2)}, u32[]{:S(2)}) collective-permute-start(bf16[2,128,256]{2,1,0:T(8,128)(2,1)S(1)} %get-tuple-element.90), channel_id=1, source_target_pairs={{8,16},{9,17},{10,18},{11,19},{12,20},{13,21},{14,22},{15,23},{16,... | collective-permute-start | bytes 393224 | tf_op jit(solution)/shard_map/ppermute | solution.py:77
  43.4 6.6 %collective-permute-start.15 = (bf16[2,128,256]{2,1,0:T(8,128)(2,1)S(1)}, bf16[2,128,256]{2,1,0:T(8,128)(2,1)S(1)}, u32[]{:S(2)}, u32[]{:S(2)}) collective-permute-start(bf16[2,128,256]{2,1,0:T(8,128)(2,1)S(1)} %get-tuple-element.91), channel_id=1, source_target_pairs={{0,8},{1,9},{2,10},{3,11},{4,12},{5,13},{6,14},{7,15},{8,0},{9,1},... | collective-permute-start | bytes 393224 | tf_op jit(solution)/shard_map/ppermute | solution.py:77
  49.7 4.8 %collective-permute-start.17 = (bf16[64,512]{1,0:T(8,128)(2,1)S(1)}, bf16[64,512]{1,0:T(8,128)(2,1)S(1)}, u32[]{:S(2)}, u32[]{:S(2)}) collective-permute-start(bf16[64,512]{1,0:T(8,128)(2,1)S(1)} %convert_element_type.17), channel_id=1, source_target_pairs={{0,8},{1,9},{2,10},{3,11},{4,12},{5,13},{6,14},{7,15},{8,0},{9,1},... | collective-permute-start | bytes 196616 | tf_op jit(solution)/shard_map/ppermute | solution.py:57
  55.5 8.4 %collective-permute-start.18 = (bf16[4,2,128,512]{3,2,1,0:T(8,128)(2,1)S(1)}, bf16[4,2,128,512]{3,2,1,0:T(8,128)(2,1)S(1)}, u32[]{:S(2)}, u32[]{:S(2)}) collective-permute-start(bf16[4,2,128,512]{3,2,1,0:T(8,128)(2,1)S(1)} %core.1.refs_13_), channel_id=1, source_target_pairs={{0,1},{1,0},{2,3},{3,2},{4,5},{5,4},{6,7},{7,6},{8,9},{9,8},{10,11... | collective-permute-start | bytes 3145736 | tf_op jit(solution)/shard_map/ppermute | solution.py:57
  55.6 8.3 %collective-permute-start.25 = (bf16[64,512]{1,0:T(8,128)(2,1)S(1)}, bf16[64,512]{1,0:T(8,128)(2,1)S(1)}, u32[]{:S(2)}, u32[]{:S(2)}) collective-permute-start(bf16[64,512]{1,0:T(8,128)(2,1)S(1)} %add_convert_fusion.refs_3_.refs_12_.refs_1_), channel_id=1, source_target_pairs={{0,16},{1,17},{2,18},{3,19},{4,20},{5,21},{6,22},{7,23},{8,24},{9,... | collective-permute-start | bytes 196616 | tf_op jit(solution)/shard_map/ppermute | solution.py:57
  59.5 7.8 %collective-permute-start.20 = (bf16[144,256]{1,0:T(8,128)(2,1)S(1)}, bf16[144,256]{1,0:T(8,128)(2,1)S(1)}, u32[]{:S(2)}, u32[]{:S(2)}) collective-permute-start(bf16[144,256]{1,0:T(8,128)(2,1)S(1)} %get-tuple-element.102), channel_id=1, source_target_pairs={{0,8},{1,9},{2,10},{3,11},{4,12},{5,13},{6,14},{7,15},{8,0},{9,1},... | collective-permute-start | bytes 221192 | tf_op jit(solution)/shard_map/ppermute | solution.py:57
  59.9 8.9 %collective-permute-start.21 = (bf16[144,256]{1,0:T(8,128)(2,1)S(1)}, bf16[144,256]{1,0:T(8,128)(2,1)S(1)}, u32[]{:S(2)}, u32[]{:S(2)}) collective-permute-start(bf16[144,256]{1,0:T(8,128)(2,1)S(1)} %get-tuple-element.103), channel_id=1, source_target_pairs={{0,16},{1,17},{2,18},{3,19},{4,20},{5,21},{6,22},{7,23},{8,24},{9,... | collective-permute-start | bytes 221192 | tf_op jit(solution)/shard_map/ppermute | solution.py:57
  61.8 7.0 %collective-permute-start.22 = (bf16[144,256]{1,0:T(8,128)(2,1)S(1)}, bf16[144,256]{1,0:T(8,128)(2,1)S(1)}, u32[]{:S(2)}, u32[]{:S(2)}) collective-permute-start(bf16[144,256]{1,0:T(8,128)(2,1)S(1)} %get-tuple-element.104), channel_id=1, source_target_pairs={{0,24},{1,25},{2,26},{3,27},{4,28},{5,29},{6,30},{7,31},{8,16},{9,... | collective-permute-start | bytes 221192 | tf_op jit(solution)/shard_map/ppermute | solution.py:57
  64.8 13.3 %collective-permute-start.19 = (bf16[2,2,128,512]{3,2,1,0:T(8,128)(2,1)S(1)}, bf16[2,2,128,512]{3,2,1,0:T(8,128)(2,1)S(1)}, u32[]{:S(2)}, u32[]{:S(2)}) collective-permute-start(bf16[2,2,128,512]{3,2,1,0:T(8,128)(2,1)S(1)} %chip_send.1.refs_4_), channel_id=1, source_target_pairs={{0,4},{1,3},{2,6},{3,1},{4,0},{5,7},{6,2},{7,5},{8,12},{9,11},{10,... | collective-permute-start | bytes 1572872 | tf_op jit(solution)/shard_map/ppermute | solution.py:67
  66.4 6.9 %collective-permute-start.26 = (bf16[2,64,512]{2,1,0:T(8,128)(2,1)S(1)}, bf16[2,64,512]{2,1,0:T(8,128)(2,1)S(1)}, u32[]{:S(2)}, u32[]{:S(2)}) collective-permute-start(bf16[2,64,512]{2,1,0:T(8,128)(2,1)S(1)} %pad_maximum_fusion.2), channel_id=1, source_target_pairs={{0,8},{1,9},{2,10},{3,11},{4,12},{5,13},{6,14},{7,15},{8,0},{9,1},... | collective-permute-start | bytes 393224 | tf_op jit(solution)/shard_map/ppermute | solution.py:57
  69.4 6.5 %collective-permute-start.23 = (bf16[144,256]{1,0:T(8,128)(2,1)S(1)}, bf16[144,256]{1,0:T(8,128)(2,1)S(1)}, u32[]{:S(2)}, u32[]{:S(2)}) collective-permute-start(bf16[144,256]{1,0:T(8,128)(2,1)S(1)} %sum.1.refs_5_.refs_7_), channel_id=1, source_target_pairs={{0,4},{1,5},{2,6},{3,7},{4,0},{5,1},{6,2},{7,3},{8,12},{9,13},{10,... | collective-permute-start | bytes 221192 | tf_op jit(solution)/shard_map/ppermute | solution.py:57
  71.0 8.1 %collective-permute-start.30 = (bf16[144,256]{1,0:T(8,128)(2,1)S(1)}, bf16[144,256]{1,0:T(8,128)(2,1)S(1)}, u32[]{:S(2)}, u32[]{:S(2)}) collective-permute-start(bf16[144,256]{1,0:T(8,128)(2,1)S(1)} %sum.1.refs_5_.refs_7_), channel_id=1, source_target_pairs={{0,24},{1,25},{2,26},{3,27},{4,28},{5,29},{6,30},{7,31},{8,16},{9,... | collective-permute-start | bytes 221192 | tf_op jit(solution)/shard_map/ppermute | solution.py:57
  72.8 7.2 %collective-permute-start.28 = (bf16[144,256]{1,0:T(8,128)(2,1)S(1)}, bf16[144,256]{1,0:T(8,128)(2,1)S(1)}, u32[]{:S(2)}, u32[]{:S(2)}) collective-permute-start(bf16[144,256]{1,0:T(8,128)(2,1)S(1)} %sum.1.refs_5_.refs_7_), channel_id=1, source_target_pairs={{0,8},{1,9},{2,10},{3,11},{4,12},{5,13},{6,14},{7,15},{8,0},{9,1},... | collective-permute-start | bytes 221192 | tf_op jit(solution)/shard_map/ppermute | solution.py:57
  73.2 9.3 %collective-permute-start.29 = (bf16[144,256]{1,0:T(8,128)(2,1)S(1)}, bf16[144,256]{1,0:T(8,128)(2,1)S(1)}, u32[]{:S(2)}, u32[]{:S(2)}) collective-permute-start(bf16[144,256]{1,0:T(8,128)(2,1)S(1)} %sum.1.refs_5_.refs_7_), channel_id=1, source_target_pairs={{0,16},{1,17},{2,18},{3,19},{4,20},{5,21},{6,22},{7,23},{8,24},{9,... | collective-permute-start | bytes 221192 | tf_op jit(solution)/shard_map/ppermute | solution.py:57
  75.9 12.7 %collective-permute-start.27 = (bf16[4,64,512]{2,1,0:T(8,128)(2,1)S(1)}, bf16[4,64,512]{2,1,0:T(8,128)(2,1)S(1)}, u32[]{:S(2)}, u32[]{:S(2)}) collective-permute-start(bf16[4,64,512]{2,1,0:T(8,128)(2,1)S(1)} %column.1.refs_5_), channel_id=1, source_target_pairs={{0,4},{1,5},{2,6},{3,7},{4,0},{5,1},{6,2},{7,3},{8,12},{9,13},{10,... | collective-permute-start | bytes 786440 | tf_op jit(solution)/shard_map/ppermute | solution.py:57
  78.7 9.9 %collective-permute-start.24 = (bf16[2,128,512]{2,1,0:T(8,128)(2,1)S(1)}, bf16[2,128,512]{2,1,0:T(8,128)(2,1)S(1)}, u32[]{:S(2)}, u32[]{:S(2)}) collective-permute-start(bf16[2,128,512]{2,1,0:T(8,128)(2,1)S(1)} %forward.1), channel_id=1, source_target_pairs={{0,2},{1,5},{2,0},{3,7},{4,6},{5,1},{6,4},{7,3},{8,10},{9,13},{10,... | collective-permute-start | bytes 786440 | tf_op jit(solution)/shard_map/ppermute | solution.py:67
  79.6 4.5 %collective-permute-start.31 = (bf16[144,256]{1,0:T(8,128)(2,1)S(1)}, bf16[144,256]{1,0:T(8,128)(2,1)S(1)}, u32[]{:S(2)}, u32[]{:S(2)}) collective-permute-start(bf16[144,256]{1,0:T(8,128)(2,1)S(1)} %side.1.refs_11_), channel_id=1, source_target_pairs={{0,8},{1,9},{2,10},{3,11},{4,12},{5,13},{6,14},{7,15},{8,0},{9,1},... | collective-permute-start | bytes 221192 | tf_op jit(solution)/shard_map/ppermute | solution.py:57
  79.9 5.3 %collective-permute-start.32 = (bf16[144,256]{1,0:T(8,128)(2,1)S(1)}, bf16[144,256]{1,0:T(8,128)(2,1)S(1)}, u32[]{:S(2)}, u32[]{:S(2)}) collective-permute-start(bf16[144,256]{1,0:T(8,128)(2,1)S(1)} %side.1.refs_11_), channel_id=1, source_target_pairs={{0,16},{1,17},{2,18},{3,19},{4,20},{5,21},{6,22},{7,23},{8,24},{9,... | collective-permute-start | bytes 221192 | tf_op jit(solution)/shard_map/ppermute | solution.py:57
  82.5 6.2 %collective-permute-start.33 = (bf16[144,256]{1,0:T(8,128)(2,1)S(1)}, bf16[144,256]{1,0:T(8,128)(2,1)S(1)}, u32[]{:S(2)}, u32[]{:S(2)}) collective-permute-start(bf16[144,256]{1,0:T(8,128)(2,1)S(1)} %side.1.refs_11_), channel_id=1, source_target_pairs={{0,24},{1,25},{2,26},{3,27},{4,28},{5,29},{6,30},{7,31},{8,16},{9,... | collective-permute-start | bytes 221192 | tf_op jit(solution)/shard_map/ppermute | solution.py:57

commit v5 on v4

--- a/solution.py
+++ b/solution.py
@@ -436,7 +436,7 @@
 
     f32_full = array(nrows, ncols, half, dtype=F32)
     inner = kernel(
-        lambda *refs: middle_kernel(True, *refs), "inner", (full, f32_full), (pos, taps, bd, hidden), **vpu
+        lambda *refs: middle_kernel(True, *refs), "inner", (full, f32_full), (pos, taps, bd, hidden), **long
     )
     mixed, slope_two, hidden = kernel(
         lambda *refs: middle_kernel(False, *refs), "outer", (full, f32_full, padded),

time: 91.1 us -> 89.2 us (0.979)
  starting transfers between devices: 41 us -> 39 us
    ppermute x27, starting transfers between devices: 32.9 us -> 31.5 us  [hop(): return lax.ppermute(value, AXES, pairs)]
where the time goes in v5:
time: 89.2 us; the launch traced here: 88.8 us
  starting transfers between devices  39 us (44%)
  Pallas kernels  33.9 us (38%)
  waiting for transfers between devices  9.47 us (11%)
  local copies, waits for them, and re-layouts  5.24 us (6%)
  between operations  0.98 us (1%)
    pallas_call x21, Pallas kernels, kernel(): pl.pallas_call(run, out_shape=out, in_specs=[SMEM] + [VMEM] * (len(args)...  33.9 us
    ppermute x27, starting transfers between devices, hop(): return lax.ppermute(value, AXES, pairs)  31.5 us
    ppermute x27, waiting for transfers between devices, hop(): return lax.ppermute(value, AXES, pairs)  9.45 us
    unnamed x12, local copies, waits for them, and re-layouts  5.23 us
    ppermute x4, starting transfers between devices, meet(): return lax.ppermute(value, AXES, pairs)  4.85 us
    ppermute x3, starting transfers between devices, cross(): return lax.ppermute(value, AXES, pairs)  2.65 us
  transfers between devices with their start and end apart: 34, of which 7 were waited for; matrix products, arithmetic and copies ran while one was open for 0% of the time, Pallas kernels for 33%

profile of v5, /device:TPU:0, one launch (start us, length us, event | category | flops | bytes accessed | tf_op | source)
XLA Modules:
  0.0 88.8 jit_solution(16172646643509839254)
XLA Ops:
  1.1 2.6 %collective-permute-start.4 = (bf16[2,128,512]{2,1,0:T(8,128)(2,1)}, bf16[2,128,512]{2,1,0:T(8,128)(2,1)S(1)}, u32[]{:S(2)}, u32[]{:S(2)}) collective-permute-start(bf16[2,128,512]{2,1,0:T(8,128)(2,1)} %refs_6_.1), channel_id=1, source_target_pairs={{0,2},{1,3},{2,0},{3,1},{4,6},{5,7},{6,4},{7,5},{8,10},{9,11},{10,... | collective-permute-start | bytes 786440 | tf_op jit(solution)/shard_map/ppermute | solution.py:57
  3.7 1.5 %collective-permute-start.6 = (bf16[2,128,512]{2,1,0:T(8,128)(2,1)}, bf16[2,128,512]{2,1,0:T(8,128)(2,1)S(1)}, u32[]{:S(2)}, u32[]{:S(2)}) collective-permute-start(bf16[2,128,512]{2,1,0:T(8,128)(2,1)} %refs_6_.1), channel_id=1, source_target_pairs={{0,4},{1,5},{2,6},{3,7},{4,0},{5,1},{6,2},{7,3},{8,12},{9,13},{10,... | collective-permute-start | bytes 786440 | tf_op jit(solution)/shard_map/ppermute | solution.py:57
  5.4 1.0 %copy-done = bf16[512,512]{1,0:T(8,128)(2,1)S(1)} copy-done((bf16[512,512]{1,0:T(8,128)(2,1)S(1)}, bf16[512,512]{1,0:T(8,128)(2,1)}, u32[]{:S(2)}) %copy-start) | copy-done | bytes 524312
  6.5 1.0 %copy-done.1 = bf16[512,512]{1,0:T(8,128)(2,1)S(1)} copy-done((bf16[512,512]{1,0:T(8,128)(2,1)S(1)}, bf16[512,512]{1,0:T(8,128)(2,1)}, u32[]{:S(2)}) %copy-start.1) | copy-done | bytes 524312
  7.5 0.9 %copy-done.2 = bf16[2,128,512]{2,1,0:T(8,128)(2,1)S(1)} copy-done((bf16[2,128,512]{2,1,0:T(8,128)(2,1)S(1)}, bf16[2,128,512]{2,1,0:T(8,128)(2,1)}, u32[]{:S(2)}) %copy-start.2) | copy-done | bytes 262168
  8.5 0.8 copy-done.3
  9.3 0.7 copy-done.4
  10.0 0.7 copy-done.5
  10.7 1.1 %prepare.1 = (bf16[512,256]{1,0:T(8,128)(2,1)S(1)}, f32[1,256]{1,0:T(1,128)S(1)}, f32[25,256]{1,0:T(8,128)S(1)}, f32[1,256]{1,0:T(1,128)S(1)}, bf16[256,512]{1,0...) custom-call(s32[4]{0:T(128)S(1)} %pad_add_fusion.refs_0_, ...), custom_call_target="tpu_custom_call" | custom-call | tf_op jit(solution)/shard_map/prepare/pallas_call | solution.py:31
  11.8 1.3 %collective-permute-done.6.refs_4_.refs_8_ = bf16[2,128,512]{2,1,0:T(8,128)(2,1)S(1)} collective-permute-done((bf16[2,128,512]{2,1,0:T(8,128)(2,1)}, bf16[2,128,512]{2,1,0:T(8,128)(2,1)S(1)}, u32[]{:S(2)}, u32[]{:S(2)}) %collective-permute-start.6) | collective-permute-done | bytes 262176 | tf_op jit(solution)/shard_map/ppermute | solution.py:57
  13.1 1.5 %collective-permute-start.10 = (bf16[2,2,128,512]{3,2,1,0:T(8,128)(2,1)S(1)}, bf16[2,2,128,512]{3,2,1,0:T(8,128)(2,1)S(1)}, u32[]{:S(2)}, u32[]{:S(2)}) collective-permute-start(bf16[2,2,128,512]{3,2,1,0:T(8,128)(2,1)S(1)} %pad_maximum_fusion), channel_id=1, source_target_pairs={{0,4},{1,3},{2,6},{3,1},{4,0},{5,7},{6,2},{7,5},{8,12},{9,11},{10,... | collective-permute-start | bytes 1572872 | tf_op jit(solution)/shard_map/ppermute | solution.py:67
  14.6 1.4 %expand0.1 = (f32[2,20,144,128]{3,2,1,0:T(8,128)S(1)}, bf16[16,128,256]{2,1,0:T(8,128)(2,1)S(1)}) custom-call(s32[4]{0:T(128)S(1)} %pad_add_fusion.refs_0_, bf16[512,256]{1,0:T(8,128)(2,1)S(1)} %get-tuple-element.63.refs_1_.refs_2_, f32[1,256]{1,0:T(1,128)S(1)} %get-tuple-element.64.refs_2_, ...), custom_call_target="tpu_custom_call", output_to_operand_aliasing={{0}: (6, {})} | custom-call | flops 1024 | bytes 1024 | tf_op jit(solution)/shard_map/expand0/pallas_call | solution.py:31
  16.6 1.2 %collective-permute-done.refs_3_.refs_10_ = bf16[2,128,512]{2,1,0:T(8,128)(2,1)S(1)} collective-permute-done((bf16[2,128,512]{2,1,0:T(8,128)(2,1)}, bf16[2,128,512]{2,1,0:T(8,128)(2,1)S(1)}, u32[]{:S(2)}, u32[]{:S(2)}) %collective-permute-start) | collective-permute-done | bytes 262176 | tf_op jit(solution)/shard_map/ppermute | solution.py:57
  17.8 2.7 %collective-permute-start.12 = (bf16[2,128,512]{2,1,0:T(8,128)(2,1)}, bf16[2,128,512]{2,1,0:T(8,128)(2,1)S(1)}, u32[]{:S(2)}, u32[]{:S(2)}) collective-permute-start(bf16[2,128,512]{2,1,0:T(8,128)(2,1)} %refs_7_.1), channel_id=1, source_target_pairs={{0,6},{1,7},{2,4},{3,5},{4,2},{5,3},{6,0},{7,1},{8,14},{9,15},{10,... | collective-permute-start | bytes 786440 | tf_op jit(solution)/shard_map/ppermute | solution.py:57
  20.4 1.4 %expand2.1 = (f32[2,20,144,128]{3,2,1,0:T(8,128)S(1)}, bf16[16,128,256]{2,1,0:T(8,128)(2,1)S(1)}) custom-call(s32[4]{0:T(128)S(1)} %pad_add_fusion.refs_0_, bf16[512,256]{1,0:T(8,128)(2,1)S(1)} %get-tuple-element.63.refs_1_.refs_2_, f32[1,256]{1,0:T(1,128)S(1)} %get-tuple-element.64.refs_2_, ...), custom_call_target="tpu_custom_call", output_to_operand_aliasing={{0}: (5, {}), {1}: (6, {})} | custom-call | flops 1024 | bytes 1024 | tf_op jit(solution)/shard_map/expand2/pallas_call | solution.py:31
  21.9 1.8 %expand6.1 = (f32[2,20,144,128]{3,2,1,0:T(8,128)S(1)}, bf16[16,128,256]{2,1,0:T(8,128)(2,1)S(1)}) custom-call(s32[4]{0:T(128)S(1)} %pad_add_fusion.refs_0_, bf16[512,256]{1,0:T(8,128)(2,1)S(1)} %get-tuple-element.63.refs_1_.refs_2_, f32[1,256]{1,0:T(1,128)S(1)} %get-tuple-element.64.refs_2_, ...), custom_call_target="tpu_custom_call", output_to_operand_aliasing={{0}: (6, {}), {1}: (7, {})} | custom-call | flops 1024 | bytes 1024 | tf_op jit(solution)/shard_map/expand6/pallas_call | solution.py:31
  23.7 0.9 %expand7.1 = (f32[2,20,144,128]{3,2,1,0:T(8,128)S(1)}, bf16[16,128,256]{2,1,0:T(8,128)(2,1)S(1)}, bf16[2,128,256]{2,1,0:T(8,128)(2,1)S(1)}, bf16[2,128,256]{2,1,0:T(8,128)(2,1)S(1)}) custom-call(s32[4]{0:T(128)S(1)} %pad_add_fusion.refs_0_, bf16[512,256]{1,0:T(8,128)(2,1)S(1)} %get-tuple-element.63.refs_1_.refs_2_, ...), custom_call_target="tpu_custom_call", output_to_operand_aliasing={{0}: (4, {}), {1}: (5, {})} | custom-call | flops 1024 | bytes 1024 | tf_op jit(solution)/shard_map/expand7/pallas_call | solution.py:31
  24.6 1.6 %collective-permute-start.8 = (bf16[2,128,256]{2,1,0:T(8,128)(2,1)S(1)}, bf16[2,128,256]{2,1,0:T(8,128)(2,1)S(1)}, u32[]{:S(2)}, u32[]{:S(2)}) collective-permute-start(bf16[2,128,256]{2,1,0:T(8,128)(2,1)S(1)} %get-tuple-element.76), channel_id=1, source_target_pairs={{0,8},{1,9},{2,10},{3,11},{4,12},{5,13},{6,14},{7,15},{8,0},{9,1},... | collective-permute-start | bytes 393224 | tf_op jit(solution)/shard_map/ppermute | solution.py:77
  26.3 0.7 collective-permute-start.9
  27.0 4.6 %inner.1 = (bf16[16,128,256]{2,1,0:T(8,128)(2,1)S(1)}, f32[16,128,256]{2,1,0:T(8,128)S(1)}) custom-call(s32[4]{0:T(128)S(1)} %pad_add_fusion.refs_0_, f32[25,256]{1,0:T(8,128)S(1)} %get-tuple-element.60.refs_1_, f32[1,256]{1,0:T(1,128)S(1)} %get-tuple-element.62.refs_2_, f32[2,20,144,128]{3,2,1,0:T(8,128)S(1)} %get-tuple-element.78.refs_3_.refs_7_), custom_call_target="tpu_custom_call" | custom-call | flops 20000000000 | bytes 100000000 | tf_op jit(solution)/shard_map/inner/pallas_call | solution.py:31
  31.7 2.1 %outer.1 = (bf16[16,128,256]{2,1,0:T(8,128)(2,1)S(1)}, f32[16,128,256]{2,1,0:T(8,128)S(1)}, f32[2,20,144,128]{3,2,1,0:T(8,128)S(1)}) custom-call(s32[4]{0:T(128)S(1)} %pad_add_fusion.refs_0_, f32[25,256]{1,0:T(8,128)S(1)} %get-tuple-element.60.refs_1_, ...), custom_call_target="tpu_custom_call", output_to_operand_aliasing={{0}: (5, {}), {1}: (6, {}), {2}: (7, {})} | custom-call | flops 1024 | bytes 1024 | tf_op jit(solution)/shard_map/outer/pallas_call | solution.py:31
  34.3 1.1 %project0.1.refs_8_.refs_6_ = f32[2,20,144,128]{3,2,1,0:T(8,128)S(1)} custom-call(s32[4]{0:T(128)S(1)} %pad_add_fusion.refs_0_, bf16[256,512]{1,0:T(8,128)(2,1)S(1)} %get-tuple-element.61.refs_1_, f32[16,128,256]{2,1,0:T(8,128)S(1)} %get-tuple-element.81.refs_2_, ...), custom_call_target="tpu_custom_call", output_to_operand_aliasing={{}: (7, {})} | custom-call | flops 1024 | bytes 1024 | tf_op jit(solution)/shard_map/project0/pallas_call | solution.py:31
  35.5 1.3 %w2.1 = (f32[64,512]{1,0:T(8,128)S(1)}, bf16[64,512]{1,0:T(8,128)(2,1)S(1)}, bf16[64,512]{1,0:T(8,128)(2,1)S(1)}, bf16[64,512]{1,0:T(8,128)(2,1)S(1)}) custom-call(s32[4]{0:T(128)S(1)} %pad_add_fusion.refs_0_, bf16[16,128,256]{2,1,0:T(8,128)(2,1)S(1)} %get-tuple-element.86.refs_1_, bf16[2,128,512]{2,1,0:T(8,128)(2,1)S(1)} %get-tuple-element.59.refs_3_.refs_2_.refs_1_, ...), custom_call_target="tpu_custom_call" | custom-call | flops 1024 | bytes 1024 | tf_op jit(solution)/shard_map/w2/pallas_call | solution.py:31
  36.8 4.4 %collective-permute-start.16 = (bf16[2,64,512]{2,1,0:T(8,128)(2,1)S(1)}, bf16[2,64,512]{2,1,0:T(8,128)(2,1)S(1)}, u32[]{:S(2)}, u32[]{:S(2)}) collective-permute-start(bf16[2,64,512]{2,1,0:T(8,128)(2,1)S(1)} %pad_maximum_fusion.1), channel_id=1, source_target_pairs={{0,16},{1,17},{2,18},{3,19},{4,20},{5,21},{6,22},{7,23},{8,24},{9,... | collective-permute-start | bytes 393224 | tf_op jit(solution)/shard_map/ppermute | solution.py:57
  41.2 1.0 %project4.1 = (f32[2,20,144,128]{3,2,1,0:T(8,128)S(1)}, bf16[2,128,256]{2,1,0:T(8,128)(2,1)S(1)}, bf16[2,128,256]{2,1,0:T(8,128)(2,1)S(1)}) custom-call(s32[4]{0:T(128)S(1)} %pad_add_fusion.refs_0_, bf16[256,512]{1,0:T(8,128)(2,1)S(1)} %get-tuple-element.61.refs_1_, f32[16,128,256]{2,1,0:T(8,128)S(1)} %get-tuple-element.81.refs_2_, ...), custom_call_target="tpu_custom_call", output_to_operand_aliasing={{0}: (6, {})} | custom-call | flops 1024 | bytes 1024 | tf_op jit(solution)/shard_map/project4/pallas_call | solution.py:31
  42.2 0.7 collective-permute-start.14
  42.9 1.9 %collective-permute-start.15 = (bf16[2,128,256]{2,1,0:T(8,128)(2,1)S(1)}, bf16[2,128,256]{2,1,0:T(8,128)(2,1)S(1)}, u32[]{:S(2)}, u32[]{:S(2)}) collective-permute-start(bf16[2,128,256]{2,1,0:T(8,128)(2,1)S(1)} %get-tuple-element.91), channel_id=1, source_target_pairs={{0,8},{1,9},{2,10},{3,11},{4,12},{5,13},{6,14},{7,15},{8,0},{9,1},... | collective-permute-start | bytes 393224 | tf_op jit(solution)/shard_map/ppermute | solution.py:77
  44.8 4.3 %taps.1.refs_5_.refs_2_ = f32[64,256]{1,0:T(8,128)S(1)} custom-call(s32[4]{0:T(128)S(1)} %pad_add_fusion.refs_0_, f32[2,20,144,128]{3,2,1,0:T(8,128)S(1)} %get-tuple-element.92.refs_1_, f32[2,20,144,128]{3,2,1,0:T(8,128)S(1)} %get-tuple-element.93.refs_2_.refs_8_), custom_call_target="tpu_custom_call" | custom-call | flops 1024 | bytes 1024 | tf_op jit(solution)/shard_map/taps/pallas_call | solution.py:31
  49.4 4.5 %back.1 = (f32[2,20,144,128]{3,2,1,0:T(8,128)S(1)}, bf16[16,128,256]{2,1,0:T(8,128)(2,1)S(1)}, f32[1,256]{1,0:T(1,128)S(1)}) custom-call(s32[4]{0:T(128)S(1)} %pad_add_fusion.refs_0_, f32[25,256]{1,0:T(8,128)S(1)} %get-tuple-element.60.refs_1_, bf16[2,128,256]{2,1,0:T(8,128)(2,1)S(1)} %collective-permute-done.14.refs_2_, ...), custom_call_target="tpu_custom_call", output_to_operand_aliasing={{0}: (8, {})} | custom-call | flops 1024 | bytes 1024 | tf_op jit(solution)/shard_map/back/pallas_call | solution.py:31
  53.9 1.0 %core.1.refs_13_ = bf16[4,2,128,512]{3,2,1,0:T(8,128)(2,1)S(1)} custom-call(s32[4]{0:T(128)S(1)} %pad_add_fusion.refs_0_, bf16[16,128,256]{2,1,0:T(8,128)(2,1)S(1)} %get-tuple-element.97.refs_1_, bf16[512,256]{1,0:T(8,128)(2,1)S(1)} %get-tuple-element.63.refs_1_.refs_2_, bf16[64,512]{1,0:T(8,128)(2,1)S(1)} %add_convert_fusion.refs_3_.refs_12_.refs_1_), custom_call_target="tpu_custom_call" | custom-call | flops 1024 | bytes 1024 | tf_op jit(solution)/shard_map/core/pallas_call | solution.py:31
  55.0 3.1 %collective-permute-start.25 = (bf16[64,512]{1,0:T(8,128)(2,1)S(1)}, bf16[64,512]{1,0:T(8,128)(2,1)S(1)}, u32[]{:S(2)}, u32[]{:S(2)}) collective-permute-start(bf16[64,512]{1,0:T(8,128)(2,1)S(1)} %add_convert_fusion.refs_3_.refs_12_.refs_1_), channel_id=1, source_target_pairs={{0,16},{1,17},{2,18},{3,19},{4,20},{5,21},{6,22},{7,23},{8,24},{9,... | collective-permute-start | bytes 196616 | tf_op jit(solution)/shard_map/ppermute | solution.py:57
  58.1 1.3 %w1.1 = (f32[144,256]{1,0:T(8,128)S(1)}, bf16[144,256]{1,0:T(8,128)(2,1)S(1)}, bf16[144,256]{1,0:T(8,128)(2,1)S(1)}, bf16[144,256]{1,0:T(8,128)(2,1)S(1)}) custom-call(s32[4]{0:T(128)S(1)} %pad_add_fusion.refs_0_, bf16[16,128,256]{2,1,0:T(8,128)(2,1)S(1)} %get-tuple-element.97.refs_1_, f32[64,256]{1,0:T(8,128)S(1)} %taps.1.refs_5_.refs_2_, ...), custom_call_target="tpu_custom_call" | custom-call | flops 1024 | bytes 1024 | tf_op jit(solution)/shard_map/w1/pallas_call | solution.py:31
  59.4 1.0 %collective-permute-start.20 = (bf16[144,256]{1,0:T(8,128)(2,1)S(1)}, bf16[144,256]{1,0:T(8,128)(2,1)S(1)}, u32[]{:S(2)}, u32[]{:S(2)}) collective-permute-start(bf16[144,256]{1,0:T(8,128)(2,1)S(1)} %get-tuple-element.102), channel_id=1, source_target_pairs={{0,8},{1,9},{2,10},{3,11},{4,12},{5,13},{6,14},{7,15},{8,0},{9,1},... | collective-permute-start | bytes 221192 | tf_op jit(solution)/shard_map/ppermute | solution.py:57
  60.4 0.8 collective-permute-start.21
  61.2 2.7 %collective-permute-start.22 = (bf16[144,256]{1,0:T(8,128)(2,1)S(1)}, bf16[144,256]{1,0:T(8,128)(2,1)S(1)}, u32[]{:S(2)}, u32[]{:S(2)}) collective-permute-start(bf16[144,256]{1,0:T(8,128)(2,1)S(1)} %get-tuple-element.104), channel_id=1, source_target_pairs={{0,24},{1,25},{2,26},{3,27},{4,28},{5,29},{6,30},{7,31},{8,16},{9,... | collective-permute-start | bytes 221192 | tf_op jit(solution)/shard_map/ppermute | solution.py:57
  63.9 0.9 chip_send.1.refs_4_
  65.4 0.9 chip_keep.1.refs_5_.refs_1_.refs_2_
  66.3 2.9 %collective-permute-done.21.refs_3_ = bf16[144,256]{1,0:T(8,128)(2,1)S(1)} collective-permute-done((bf16[144,256]{1,0:T(8,128)(2,1)S(1)}, bf16[144,256]{1,0:T(8,128)(2,1)S(1)}, u32[]{:S(2)}, u32[]{:S(2)}) %collective-permute-start.21) | collective-permute-done | bytes 73760 | tf_op jit(solution)/shard_map/ppermute | solution.py:57
  70.3 1.6 %collective-permute-start.30 = (bf16[144,256]{1,0:T(8,128)(2,1)S(1)}, bf16[144,256]{1,0:T(8,128)(2,1)S(1)}, u32[]{:S(2)}, u32[]{:S(2)}) collective-permute-start(bf16[144,256]{1,0:T(8,128)(2,1)S(1)} %sum.1.refs_5_.refs_7_), channel_id=1, source_target_pairs={{0,24},{1,25},{2,26},{3,27},{4,28},{5,29},{6,30},{7,31},{8,16},{9,... | collective-permute-start | bytes 221192 | tf_op jit(solution)/shard_map/ppermute | solution.py:57
  72.4 2.3 %collective-permute-start.29 = (bf16[144,256]{1,0:T(8,128)(2,1)S(1)}, bf16[144,256]{1,0:T(8,128)(2,1)S(1)}, u32[]{:S(2)}, u32[]{:S(2)}) collective-permute-start(bf16[144,256]{1,0:T(8,128)(2,1)S(1)} %sum.1.refs_5_.refs_7_), channel_id=1, source_target_pairs={{0,16},{1,17},{2,18},{3,19},{4,20},{5,21},{6,22},{7,23},{8,24},{9,... | collective-permute-start | bytes 221192 | tf_op jit(solution)/shard_map/ppermute | solution.py:57
  75.7 1.2 %collective-permute-start.27 = (bf16[4,64,512]{2,1,0:T(8,128)(2,1)S(1)}, bf16[4,64,512]{2,1,0:T(8,128)(2,1)S(1)}, u32[]{:S(2)}, u32[]{:S(2)}) collective-permute-start(bf16[4,64,512]{2,1,0:T(8,128)(2,1)S(1)} %column.1.refs_5_), channel_id=1, source_target_pairs={{0,4},{1,5},{2,6},{3,7},{4,0},{5,1},{6,2},{7,3},{8,12},{9,13},{10,... | collective-permute-start | bytes 786440 | tf_op jit(solution)/shard_map/ppermute | solution.py:57
  78.6 0.7 collective-permute-start.31
  79.3 1.2 %collective-permute-start.32 = (bf16[144,256]{1,0:T(8,128)(2,1)S(1)}, bf16[144,256]{1,0:T(8,128)(2,1)S(1)}, u32[]{:S(2)}, u32[]{:S(2)}) collective-permute-start(bf16[144,256]{1,0:T(8,128)(2,1)S(1)} %side.1.refs_11_), channel_id=1, source_target_pairs={{0,16},{1,17},{2,18},{3,19},{4,20},{5,21},{6,22},{7,23},{8,24},{9,... | collective-permute-start | bytes 221192 | tf_op jit(solution)/shard_map/ppermute | solution.py:57
  80.6 2.5 %collective-permute-start.33 = (bf16[144,256]{1,0:T(8,128)(2,1)S(1)}, bf16[144,256]{1,0:T(8,128)(2,1)S(1)}, u32[]{:S(2)}, u32[]{:S(2)}) collective-permute-start(bf16[144,256]{1,0:T(8,128)(2,1)S(1)} %side.1.refs_11_), channel_id=1, source_target_pairs={{0,24},{1,25},{2,26},{3,27},{4,28},{5,29},{6,30},{7,31},{8,16},{9,... | collective-permute-start | bytes 221192 | tf_op jit(solution)/shard_map/ppermute | solution.py:57
  83.1 0.6 collective-permute-done.31.refs_12_
  83.7 0.9 collective-permute-done.32.refs_13_
  84.6 2.2 %collective-permute-done.33.refs_14_ = bf16[144,256]{1,0:T(8,128)(2,1)S(1)} collective-permute-done((bf16[144,256]{1,0:T(8,128)(2,1)S(1)}, bf16[144,256]{1,0:T(8,128)(2,1)S(1)}, u32[]{:S(2)}, u32[]{:S(2)}) %collective-permute-start.33) | collective-permute-done | bytes 73760 | tf_op jit(solution)/shard_map/ppermute | solution.py:57
  86.8 2.0 %last.1 = (bf16[2,128,512]{2,1,0:T(8,128)(2,1)}, f32[512,512]{1,0:T(8,128)}, f32[512,512]{1,0:T(8,128)}, f32[25,512]{1,0:T(8,128)}, f32[1,512]{1,0:T(1,128)}, /*index=5*/f32[1,512]{1,0:T(1,128)}) custom-call(s32[4]{0:T(128)S(1)} %pad_add_fusion.refs_0_, bf16[2,128,512]{2,1,0:T(8,128)(2,1)S(1)} %get-tuple-element.59.refs_3_.refs_2_.refs_1_, ...), custom_call_target="tpu_custom_call" | custom-call | tf_op jit(solution)/shard_map/last/pallas_call | solution.py:31
  (62 shorter events, 7.4 us)
Async XLA Ops:
  0.6 11.1 %collective-permute-start.2 = (bf16[2,128,512]{2,1,0:T(8,128)(2,1)}, bf16[2,128,512]{2,1,0:T(8,128)(2,1)S(1)}, u32[]{:S(2)}, u32[]{:S(2)}) collective-permute-start(bf16[2,128,512]{2,1,0:T(8,128)(2,1)} %refs_7_.1), channel_id=1, source_target_pairs={{0,1},{1,0},{2,3},{3,2},{4,5},{5,4},{6,7},{7,6},{8,9},{9,8},{10,11... | collective-permute-start | bytes 786440 | tf_op jit(solution)/shard_map/ppermute | solution.py:57
  1.1 10.7 %collective-permute-start.4 = (bf16[2,128,512]{2,1,0:T(8,128)(2,1)}, bf16[2,128,512]{2,1,0:T(8,128)(2,1)S(1)}, u32[]{:S(2)}, u32[]{:S(2)}) collective-permute-start(bf16[2,128,512]{2,1,0:T(8,128)(2,1)} %refs_6_.1), channel_id=1, source_target_pairs={{0,2},{1,3},{2,0},{3,1},{4,6},{5,7},{6,4},{7,5},{8,10},{9,11},{10,... | collective-permute-start | bytes 786440 | tf_op jit(solution)/shard_map/ppermute | solution.py:57
  3.7 9.4 %collective-permute-start.6 = (bf16[2,128,512]{2,1,0:T(8,128)(2,1)}, bf16[2,128,512]{2,1,0:T(8,128)(2,1)S(1)}, u32[]{:S(2)}, u32[]{:S(2)}) collective-permute-start(bf16[2,128,512]{2,1,0:T(8,128)(2,1)} %refs_6_.1), channel_id=1, source_target_pairs={{0,4},{1,5},{2,6},{3,7},{4,0},{5,1},{6,2},{7,3},{8,12},{9,13},{10,... | collective-permute-start | bytes 786440 | tf_op jit(solution)/shard_map/ppermute | solution.py:57
  5.2 9.4 %collective-permute-start.1 = (bf16[2,128,512]{2,1,0:T(8,128)(2,1)}, bf16[2,128,512]{2,1,0:T(8,128)(2,1)S(1)}, u32[]{:S(2)}, u32[]{:S(2)}) collective-permute-start(bf16[2,128,512]{2,1,0:T(8,128)(2,1)} %refs_6_.1), channel_id=1, source_target_pairs={{0,1},{1,0},{2,3},{3,2},{4,5},{5,4},{6,7},{7,6},{8,9},{9,8},{10,11... | collective-permute-start | bytes 786440 | tf_op jit(solution)/shard_map/ppermute | solution.py:57
  5.2 12.5 %collective-permute-start = (bf16[2,128,512]{2,1,0:T(8,128)(2,1)}, bf16[2,128,512]{2,1,0:T(8,128)(2,1)S(1)}, u32[]{:S(2)}, u32[]{:S(2)}) collective-permute-start(bf16[2,128,512]{2,1,0:T(8,128)(2,1)} %refs_6_.1), channel_id=1, source_target_pairs={{0,6},{1,7},{2,4},{3,5},{4,2},{5,3},{6,0},{7,1},{8,14},{9,15},{10,... | collective-permute-start | bytes 786440 | tf_op jit(solution)/shard_map/ppermute | solution.py:57
  5.4 1.0 %copy-start = (bf16[512,512]{1,0:T(8,128)(2,1)S(1)}, bf16[512,512]{1,0:T(8,128)(2,1)}, u32[]{:S(2)}) copy-start(bf16[512,512]{1,0:T(8,128)(2,1)} %refs_1_.1) | copy-start | bytes 1572868
  6.5 1.0 %copy-start.1 = (bf16[512,512]{1,0:T(8,128)(2,1)S(1)}, bf16[512,512]{1,0:T(8,128)(2,1)}, u32[]{:S(2)}) copy-start(bf16[512,512]{1,0:T(8,128)(2,1)} %refs_5_.1) | copy-start | bytes 1572868
  7.5 0.9 %copy-start.2 = (bf16[2,128,512]{2,1,0:T(8,128)(2,1)S(1)}, bf16[2,128,512]{2,1,0:T(8,128)(2,1)}, u32[]{:S(2)}) copy-start(bf16[2,128,512]{2,1,0:T(8,128)(2,1)} %refs_6_.1) | copy-start | bytes 786436
  8.5 0.8 copy-start.3
  9.3 0.7 copy-start.4
  10.0 0.7 copy-start.5
  13.1 13.8 %collective-permute-start.10 = (bf16[2,2,128,512]{3,2,1,0:T(8,128)(2,1)S(1)}, bf16[2,2,128,512]{3,2,1,0:T(8,128)(2,1)S(1)}, u32[]{:S(2)}, u32[]{:S(2)}) collective-permute-start(bf16[2,2,128,512]{3,2,1,0:T(8,128)(2,1)S(1)} %pad_maximum_fusion), channel_id=1, source_target_pairs={{0,4},{1,3},{2,6},{3,1},{4,0},{5,7},{6,2},{7,5},{8,12},{9,11},{10,... | collective-permute-start | bytes 1572872 | tf_op jit(solution)/shard_map/ppermute | solution.py:67
  16.0 5.8 %collective-permute-start.5 = (bf16[2,128,512]{2,1,0:T(8,128)(2,1)S(1)}, bf16[2,128,512]{2,1,0:T(8,128)(2,1)S(1)}, u32[]{:S(2)}, u32[]{:S(2)}) collective-permute-start(bf16[2,128,512]{2,1,0:T(8,128)(2,1)S(1)} %collective-permute-done.4.refs_3_.refs_6_), channel_id=1, source_target_pairs={{0,1},{1,0},{2,3},{3,2},{4,5},{5,4},{6,7},{7,6},{8,9},{9,8},{10,11... | collective-permute-start | bytes 786440 | tf_op jit(solution)/shard_map/ppermute | solution.py:57
  16.1 5.8 %collective-permute-start.7 = (bf16[2,128,512]{2,1,0:T(8,128)(2,1)S(1)}, bf16[2,128,512]{2,1,0:T(8,128)(2,1)S(1)}, u32[]{:S(2)}, u32[]{:S(2)}) collective-permute-start(bf16[2,128,512]{2,1,0:T(8,128)(2,1)S(1)} %collective-permute-done.6.refs_4_.refs_8_), channel_id=1, source_target_pairs={{0,1},{1,0},{2,3},{3,2},{4,5},{5,4},{6,7},{7,6},{8,9},{9,8},{10,11... | collective-permute-start | bytes 786440 | tf_op jit(solution)/shard_map/ppermute | solution.py:57
  17.8 5.9 %collective-permute-start.3 = (bf16[2,128,512]{2,1,0:T(8,128)(2,1)S(1)}, bf16[2,128,512]{2,1,0:T(8,128)(2,1)S(1)}, u32[]{:S(2)}, u32[]{:S(2)}) collective-permute-start(bf16[2,128,512]{2,1,0:T(8,128)(2,1)S(1)} %collective-permute-done.refs_3_.refs_10_), channel_id=1, source_target_pairs={{0,1},{1,0},{2,3},{3,2},{4,5},{5,4},{6,7},{7,6},{8,9},{9,8},{10,11... | collective-permute-start | bytes 786440 | tf_op jit(solution)/shard_map/ppermute | solution.py:57
  17.8 16.0 %collective-permute-start.12 = (bf16[2,128,512]{2,1,0:T(8,128)(2,1)}, bf16[2,128,512]{2,1,0:T(8,128)(2,1)S(1)}, u32[]{:S(2)}, u32[]{:S(2)}) collective-permute-start(bf16[2,128,512]{2,1,0:T(8,128)(2,1)} %refs_7_.1), channel_id=1, source_target_pairs={{0,6},{1,7},{2,4},{3,5},{4,2},{5,3},{6,0},{7,1},{8,14},{9,15},{10,... | collective-permute-start | bytes 786440 | tf_op jit(solution)/shard_map/ppermute | solution.py:57
  24.6 7.0 %collective-permute-start.8 = (bf16[2,128,256]{2,1,0:T(8,128)(2,1)S(1)}, bf16[2,128,256]{2,1,0:T(8,128)(2,1)S(1)}, u32[]{:S(2)}, u32[]{:S(2)}) collective-permute-start(bf16[2,128,256]{2,1,0:T(8,128)(2,1)S(1)} %get-tuple-element.76), channel_id=1, source_target_pairs={{0,8},{1,9},{2,10},{3,11},{4,12},{5,13},{6,14},{7,15},{8,0},{9,1},... | collective-permute-start | bytes 393224 | tf_op jit(solution)/shard_map/ppermute | solution.py:77
  26.3 5.4 %collective-permute-start.9 = (bf16[2,128,256]{2,1,0:T(8,128)(2,1)S(1)}, bf16[2,128,256]{2,1,0:T(8,128)(2,1)S(1)}, u32[]{:S(2)}, u32[]{:S(2)}) collective-permute-start(bf16[2,128,256]{2,1,0:T(8,128)(2,1)S(1)} %get-tuple-element.77), channel_id=1, source_target_pairs={{8,16},{9,17},{10,18},{11,19},{12,20},{13,21},{14,22},{15,23},{16,... | collective-permute-start | bytes 393224 | tf_op jit(solution)/shard_map/ppermute | solution.py:77
  26.9 8.6 %collective-permute-start.11 = (bf16[2,2,128,512]{3,2,1,0:T(8,128)(2,1)S(1)}, bf16[2,2,128,512]{3,2,1,0:T(8,128)(2,1)S(1)}, u32[]{:S(2)}, u32[]{:S(2)}) collective-permute-start(bf16[2,2,128,512]{3,2,1,0:T(8,128)(2,1)S(1)} %collective-permute-done.10.refs_5_.refs_4_), channel_id=1, source_target_pairs={{0,1},{1,0},{2,3},{3,2},{4,5},{5,4},{6,7},{7,6},{8,9},{9,8},{10,11... | collective-permute-start | bytes 1572872 | tf_op jit(solution)/shard_map/ppermute | solution.py:57
  33.8 1.7 %collective-permute-start.13 = (bf16[2,128,512]{2,1,0:T(8,128)(2,1)S(1)}, bf16[2,128,512]{2,1,0:T(8,128)(2,1)S(1)}, u32[]{:S(2)}, u32[]{:S(2)}) collective-permute-start(bf16[2,128,512]{2,1,0:T(8,128)(2,1)S(1)} %collective-permute-done.12.refs_6_.refs_5_), channel_id=1, source_target_pairs={{0,1},{1,0},{2,3},{3,2},{4,5},{5,4},{6,7},{7,6},{8,9},{9,8},{10,11... | collective-permute-start | bytes 786440 | tf_op jit(solution)/shard_map/ppermute | solution.py:57
  36.8 12.2 %collective-permute-start.16 = (bf16[2,64,512]{2,1,0:T(8,128)(2,1)S(1)}, bf16[2,64,512]{2,1,0:T(8,128)(2,1)S(1)}, u32[]{:S(2)}, u32[]{:S(2)}) collective-permute-start(bf16[2,64,512]{2,1,0:T(8,128)(2,1)S(1)} %pad_maximum_fusion.1), channel_id=1, source_target_pairs={{0,16},{1,17},{2,18},{3,19},{4,20},{5,21},{6,22},{7,23},{8,24},{9,... | collective-permute-start | bytes 393224 | tf_op jit(solution)/shard_map/ppermute | solution.py:57
  42.2 7.2 %collective-permute-start.14 = (bf16[2,128,256]{2,1,0:T(8,128)(2,1)S(1)}, bf16[2,128,256]{2,1,0:T(8,128)(2,1)S(1)}, u32[]{:S(2)}, u32[]{:S(2)}) collective-permute-start(bf16[2,128,256]{2,1,0:T(8,128)(2,1)S(1)} %get-tuple-element.90), channel_id=1, source_target_pairs={{8,16},{9,17},{10,18},{11,19},{12,20},{13,21},{14,22},{15,23},{16,... | collective-permute-start | bytes 393224 | tf_op jit(solution)/shard_map/ppermute | solution.py:77
  42.9 6.6 %collective-permute-start.15 = (bf16[2,128,256]{2,1,0:T(8,128)(2,1)S(1)}, bf16[2,128,256]{2,1,0:T(8,128)(2,1)S(1)}, u32[]{:S(2)}, u32[]{:S(2)}) collective-permute-start(bf16[2,128,256]{2,1,0:T(8,128)(2,1)S(1)} %get-tuple-element.91), channel_id=1, source_target_pairs={{0,8},{1,9},{2,10},{3,11},{4,12},{5,13},{6,14},{7,15},{8,0},{9,1},... | collective-permute-start | bytes 393224 | tf_op jit(solution)/shard_map/ppermute | solution.py:77
  49.2 4.7 %collective-permute-start.17 = (bf16[64,512]{1,0:T(8,128)(2,1)S(1)}, bf16[64,512]{1,0:T(8,128)(2,1)S(1)}, u32[]{:S(2)}, u32[]{:S(2)}) collective-permute-start(bf16[64,512]{1,0:T(8,128)(2,1)S(1)} %convert_element_type.17), channel_id=1, source_target_pairs={{0,8},{1,9},{2,10},{3,11},{4,12},{5,13},{6,14},{7,15},{8,0},{9,1},... | collective-permute-start | bytes 196616 | tf_op jit(solution)/shard_map/ppermute | solution.py:57
  54.9 9.0 %collective-permute-start.18 = (bf16[4,2,128,512]{3,2,1,0:T(8,128)(2,1)S(1)}, bf16[4,2,128,512]{3,2,1,0:T(8,128)(2,1)S(1)}, u32[]{:S(2)}, u32[]{:S(2)}) collective-permute-start(bf16[4,2,128,512]{3,2,1,0:T(8,128)(2,1)S(1)} %core.1.refs_13_), channel_id=1, source_target_pairs={{0,1},{1,0},{2,3},{3,2},{4,5},{5,4},{6,7},{7,6},{8,9},{9,8},{10,11... | collective-permute-start | bytes 3145736 | tf_op jit(solution)/shard_map/ppermute | solution.py:57
  55.0 8.9 %collective-permute-start.25 = (bf16[64,512]{1,0:T(8,128)(2,1)S(1)}, bf16[64,512]{1,0:T(8,128)(2,1)S(1)}, u32[]{:S(2)}, u32[]{:S(2)}) collective-permute-start(bf16[64,512]{1,0:T(8,128)(2,1)S(1)} %add_convert_fusion.refs_3_.refs_12_.refs_1_), channel_id=1, source_target_pairs={{0,16},{1,17},{2,18},{3,19},{4,20},{5,21},{6,22},{7,23},{8,24},{9,... | collective-permute-start | bytes 196616 | tf_op jit(solution)/shard_map/ppermute | solution.py:57
  59.4 6.9 %collective-permute-start.20 = (bf16[144,256]{1,0:T(8,128)(2,1)S(1)}, bf16[144,256]{1,0:T(8,128)(2,1)S(1)}, u32[]{:S(2)}, u32[]{:S(2)}) collective-permute-start(bf16[144,256]{1,0:T(8,128)(2,1)S(1)} %get-tuple-element.102), channel_id=1, source_target_pairs={{0,8},{1,9},{2,10},{3,11},{4,12},{5,13},{6,14},{7,15},{8,0},{9,1},... | collective-permute-start | bytes 221192 | tf_op jit(solution)/shard_map/ppermute | solution.py:57
  60.4 8.7 %collective-permute-start.21 = (bf16[144,256]{1,0:T(8,128)(2,1)S(1)}, bf16[144,256]{1,0:T(8,128)(2,1)S(1)}, u32[]{:S(2)}, u32[]{:S(2)}) collective-permute-start(bf16[144,256]{1,0:T(8,128)(2,1)S(1)} %get-tuple-element.103), channel_id=1, source_target_pairs={{0,16},{1,17},{2,18},{3,19},{4,20},{5,21},{6,22},{7,23},{8,24},{9,... | collective-permute-start | bytes 221192 | tf_op jit(solution)/shard_map/ppermute | solution.py:57
  61.2 8.0 %collective-permute-start.22 = (bf16[144,256]{1,0:T(8,128)(2,1)S(1)}, bf16[144,256]{1,0:T(8,128)(2,1)S(1)}, u32[]{:S(2)}, u32[]{:S(2)}) collective-permute-start(bf16[144,256]{1,0:T(8,128)(2,1)S(1)} %get-tuple-element.104), channel_id=1, source_target_pairs={{0,24},{1,25},{2,26},{3,27},{4,28},{5,29},{6,30},{7,31},{8,16},{9,... | collective-permute-start | bytes 221192 | tf_op jit(solution)/shard_map/ppermute | solution.py:57
  64.8 12.1 %collective-permute-start.19 = (bf16[2,2,128,512]{3,2,1,0:T(8,128)(2,1)S(1)}, bf16[2,2,128,512]{3,2,1,0:T(8,128)(2,1)S(1)}, u32[]{:S(2)}, u32[]{:S(2)}) collective-permute-start(bf16[2,2,128,512]{3,2,1,0:T(8,128)(2,1)S(1)} %chip_send.1.refs_4_), channel_id=1, source_target_pairs={{0,4},{1,3},{2,6},{3,1},{4,0},{5,7},{6,2},{7,5},{8,12},{9,11},{10,... | collective-permute-start | bytes 1572872 | tf_op jit(solution)/shard_map/ppermute | solution.py:67
  65.4 7.1 %collective-permute-start.26 = (bf16[2,64,512]{2,1,0:T(8,128)(2,1)S(1)}, bf16[2,64,512]{2,1,0:T(8,128)(2,1)S(1)}, u32[]{:S(2)}, u32[]{:S(2)}) collective-permute-start(bf16[2,64,512]{2,1,0:T(8,128)(2,1)S(1)} %pad_maximum_fusion.2), channel_id=1, source_target_pairs={{0,8},{1,9},{2,10},{3,11},{4,12},{5,13},{6,14},{7,15},{8,0},{9,1},... | collective-permute-start | bytes 393224 | tf_op jit(solution)/shard_map/ppermute | solution.py:57
  69.8 5.9 %collective-permute-start.23 = (bf16[144,256]{1,0:T(8,128)(2,1)S(1)}, bf16[144,256]{1,0:T(8,128)(2,1)S(1)}, u32[]{:S(2)}, u32[]{:S(2)}) collective-permute-start(bf16[144,256]{1,0:T(8,128)(2,1)S(1)} %sum.1.refs_5_.refs_7_), channel_id=1, source_target_pairs={{0,4},{1,5},{2,6},{3,7},{4,0},{5,1},{6,2},{7,3},{8,12},{9,13},{10,... | collective-permute-start | bytes 221192 | tf_op jit(solution)/shard_map/ppermute | solution.py:57
  70.3 7.7 %collective-permute-start.30 = (bf16[144,256]{1,0:T(8,128)(2,1)S(1)}, bf16[144,256]{1,0:T(8,128)(2,1)S(1)}, u32[]{:S(2)}, u32[]{:S(2)}) collective-permute-start(bf16[144,256]{1,0:T(8,128)(2,1)S(1)} %sum.1.refs_5_.refs_7_), channel_id=1, source_target_pairs={{0,24},{1,25},{2,26},{3,27},{4,28},{5,29},{6,30},{7,31},{8,16},{9,... | collective-permute-start | bytes 221192 | tf_op jit(solution)/shard_map/ppermute | solution.py:57
  72.0 7.3 %collective-permute-start.28 = (bf16[144,256]{1,0:T(8,128)(2,1)S(1)}, bf16[144,256]{1,0:T(8,128)(2,1)S(1)}, u32[]{:S(2)}, u32[]{:S(2)}) collective-permute-start(bf16[144,256]{1,0:T(8,128)(2,1)S(1)} %sum.1.refs_5_.refs_7_), channel_id=1, source_target_pairs={{0,8},{1,9},{2,10},{3,11},{4,12},{5,13},{6,14},{7,15},{8,0},{9,1},... | collective-permute-start | bytes 221192 | tf_op jit(solution)/shard_map/ppermute | solution.py:57
  72.4 8.1 %collective-permute-start.29 = (bf16[144,256]{1,0:T(8,128)(2,1)S(1)}, bf16[144,256]{1,0:T(8,128)(2,1)S(1)}, u32[]{:S(2)}, u32[]{:S(2)}) collective-permute-start(bf16[144,256]{1,0:T(8,128)(2,1)S(1)} %sum.1.refs_5_.refs_7_), channel_id=1, source_target_pairs={{0,16},{1,17},{2,18},{3,19},{4,20},{5,21},{6,22},{7,23},{8,24},{9,... | collective-permute-start | bytes 221192 | tf_op jit(solution)/shard_map/ppermute | solution.py:57
  75.7 11.1 %collective-permute-start.27 = (bf16[4,64,512]{2,1,0:T(8,128)(2,1)S(1)}, bf16[4,64,512]{2,1,0:T(8,128)(2,1)S(1)}, u32[]{:S(2)}, u32[]{:S(2)}) collective-permute-start(bf16[4,64,512]{2,1,0:T(8,128)(2,1)S(1)} %column.1.refs_5_), channel_id=1, source_target_pairs={{0,4},{1,5},{2,6},{3,7},{4,0},{5,1},{6,2},{7,3},{8,12},{9,13},{10,... | collective-permute-start | bytes 786440 | tf_op jit(solution)/shard_map/ppermute | solution.py:57
  77.5 9.3 %collective-permute-start.24 = (bf16[2,128,512]{2,1,0:T(8,128)(2,1)S(1)}, bf16[2,128,512]{2,1,0:T(8,128)(2,1)S(1)}, u32[]{:S(2)}, u32[]{:S(2)}) collective-permute-start(bf16[2,128,512]{2,1,0:T(8,128)(2,1)S(1)} %forward.1), channel_id=1, source_target_pairs={{0,2},{1,5},{2,0},{3,7},{4,6},{5,1},{6,4},{7,3},{8,10},{9,13},{10,... | collective-permute-start | bytes 786440 | tf_op jit(solution)/shard_map/ppermute | solution.py:67
  78.6 5.1 %collective-permute-start.31 = (bf16[144,256]{1,0:T(8,128)(2,1)S(1)}, bf16[144,256]{1,0:T(8,128)(2,1)S(1)}, u32[]{:S(2)}, u32[]{:S(2)}) collective-permute-start(bf16[144,256]{1,0:T(8,128)(2,1)S(1)} %side.1.refs_11_), channel_id=1, source_target_pairs={{0,8},{1,9},{2,10},{3,11},{4,12},{5,13},{6,14},{7,15},{8,0},{9,1},... | collective-permute-start | bytes 221192 | tf_op jit(solution)/shard_map/ppermute | solution.py:57
  79.3 5.3 %collective-permute-start.32 = (bf16[144,256]{1,0:T(8,128)(2,1)S(1)}, bf16[144,256]{1,0:T(8,128)(2,1)S(1)}, u32[]{:S(2)}, u32[]{:S(2)}) collective-permute-start(bf16[144,256]{1,0:T(8,128)(2,1)S(1)} %side.1.refs_11_), channel_id=1, source_target_pairs={{0,16},{1,17},{2,18},{3,19},{4,20},{5,21},{6,22},{7,23},{8,24},{9,... | collective-permute-start | bytes 221192 | tf_op jit(solution)/shard_map/ppermute | solution.py:57
  80.6 6.2 %collective-permute-start.33 = (bf16[144,256]{1,0:T(8,128)(2,1)S(1)}, bf16[144,256]{1,0:T(8,128)(2,1)S(1)}, u32[]{:S(2)}, u32[]{:S(2)}) collective-permute-start(bf16[144,256]{1,0:T(8,128)(2,1)S(1)} %side.1.refs_11_), channel_id=1, source_target_pairs={{0,24},{1,25},{2,26},{3,27},{4,28},{5,29},{6,30},{7,31},{8,16},{9,... | collective-permute-start | bytes 221192 | tf_op jit(solution)/shard_map/ppermute | solution.py:57

commit v6 on v5

--- a/solution.py
+++ b/solution.py
@@ -424,11 +424,12 @@
     for k, step in steps.items():
         in_pieces[k] = hop(inputs, *step)
     first = expand((0, 1), (hidden,), after=(cot_core,))
-    for k in steps:
+    for k in (4, 2):
         in_pieces[k + 1] = hop(tied(in_pieces[k], first[0]), 0, 1)
     second = expand((2, 4), first)
+    in_pieces[7] = hop(tied(in_pieces[6], second[1]), 0, 1)
     cot_pair = cross(tied(jnp.stack([cot_own, cot_core]), in_pieces[2], in_pieces[4]), 0)
-    cot_far = hop(tied(cotangent, in_pieces[6]), *steps[6])
+    cot_far = hop(tied(cotangent, in_pieces[6], second[1]), *steps[6])
     in_pieces = [in_pieces[k] for k in range(8)]
     edges = (array(2, ncols, half),) * 2
     hidden, slope_one, *sent = expand((7,), expand((6, 3, 5), second), edges=edges)

time: 89.2 us -> 87.9 us (0.985)
  waiting for transfers between devices: 9.47 us -> 8.22 us
    ppermute x27, waiting for transfers between devices: 9.45 us -> 8.2 us  [hop(): return lax.ppermute(value, AXES, pairs)]
  transfers between devices with their start and end apart: 34 -> 34, of which waited for: 7 -> 6; matrix products, arithmetic and copies ran while one was open for 0% -> 0% of each run, Pallas kernels for 33% -> 34%
where the time goes in v6:
time: 87.9 us; the launch traced here: 87.5 us
  starting transfers between devices  38.9 us (44%)
  Pallas kernels  33.9 us (39%)
  waiting for transfers between devices  8.22 us (9%)
  local copies, waits for them, and re-layouts  5.24 us (6%)
  between operations  0.97 us (1%)
    pallas_call x21, Pallas kernels, kernel(): pl.pallas_call(run, out_shape=out, in_specs=[SMEM] + [VMEM] * (len(args)...  33.9 us
    ppermute x27, starting transfers between devices, hop(): return lax.ppermute(value, AXES, pairs)  31.4 us
    ppermute x27, waiting for transfers between devices, hop(): return lax.ppermute(value, AXES, pairs)  8.2 us
    unnamed x12, local copies, waits for them, and re-layouts  5.23 us
    ppermute x4, starting transfers between devices, meet(): return lax.ppermute(value, AXES, pairs)  4.85 us
    ppermute x3, starting transfers between devices, cross(): return lax.ppermute(value, AXES, pairs)  2.68 us
  transfers between devices with their start and end apart: 34, of which 6 were waited for; matrix products, arithmetic and copies ran while one was open for 0% of the time, Pallas kernels for 34%

profile of v6, /device:TPU:0, one launch (start us, length us, event | category | flops | bytes accessed | tf_op | source)
XLA Modules:
  0.0 87.5 jit_solution(7318921205325248969)
XLA Ops:
  1.1 2.6 %collective-permute-start.1 = (bf16[2,128,512]{2,1,0:T(8,128)(2,1)}, bf16[2,128,512]{2,1,0:T(8,128)(2,1)S(1)}, u32[]{:S(2)}, u32[]{:S(2)}) collective-permute-start(bf16[2,128,512]{2,1,0:T(8,128)(2,1)} %refs_6_.1), channel_id=1, source_target_pairs={{0,2},{1,3},{2,0},{3,1},{4,6},{5,7},{6,4},{7,5},{8,10},{9,11},{10,... | collective-permute-start | bytes 786440 | tf_op jit(solution)/shard_map/ppermute | solution.py:57
  3.7 1.5 %collective-permute-start.2 = (bf16[2,128,512]{2,1,0:T(8,128)(2,1)}, bf16[2,128,512]{2,1,0:T(8,128)(2,1)S(1)}, u32[]{:S(2)}, u32[]{:S(2)}) collective-permute-start(bf16[2,128,512]{2,1,0:T(8,128)(2,1)} %refs_6_.1), channel_id=1, source_target_pairs={{0,4},{1,5},{2,6},{3,7},{4,0},{5,1},{6,2},{7,3},{8,12},{9,13},{10,... | collective-permute-start | bytes 786440 | tf_op jit(solution)/shard_map/ppermute | solution.py:57
  5.4 1.0 %copy-done = bf16[512,512]{1,0:T(8,128)(2,1)S(1)} copy-done((bf16[512,512]{1,0:T(8,128)(2,1)S(1)}, bf16[512,512]{1,0:T(8,128)(2,1)}, u32[]{:S(2)}) %copy-start) | copy-done | bytes 524312
  6.5 1.0 %copy-done.1 = bf16[512,512]{1,0:T(8,128)(2,1)S(1)} copy-done((bf16[512,512]{1,0:T(8,128)(2,1)S(1)}, bf16[512,512]{1,0:T(8,128)(2,1)}, u32[]{:S(2)}) %copy-start.1) | copy-done | bytes 524312
  7.5 0.9 %copy-done.2 = bf16[2,128,512]{2,1,0:T(8,128)(2,1)S(1)} copy-done((bf16[2,128,512]{2,1,0:T(8,128)(2,1)S(1)}, bf16[2,128,512]{2,1,0:T(8,128)(2,1)}, u32[]{:S(2)}) %copy-start.2) | copy-done | bytes 262168
  8.5 0.8 copy-done.3
  9.3 0.7 copy-done.4
  10.0 0.7 copy-done.5
  10.7 1.1 %prepare.1 = (bf16[512,256]{1,0:T(8,128)(2,1)S(1)}, f32[1,256]{1,0:T(1,128)S(1)}, f32[25,256]{1,0:T(8,128)S(1)}, f32[1,256]{1,0:T(1,128)S(1)}, bf16[256,512]{1,0...) custom-call(s32[4]{0:T(128)S(1)} %pad_add_fusion.refs_0_, ...), custom_call_target="tpu_custom_call" | custom-call | tf_op jit(solution)/shard_map/prepare/pallas_call | solution.py:31
  11.8 1.3 %collective-permute-done.2.refs_4_.refs_8_ = bf16[2,128,512]{2,1,0:T(8,128)(2,1)S(1)} collective-permute-done((bf16[2,128,512]{2,1,0:T(8,128)(2,1)}, bf16[2,128,512]{2,1,0:T(8,128)(2,1)S(1)}, u32[]{:S(2)}, u32[]{:S(2)}) %collective-permute-start.2) | collective-permute-done | bytes 262176 | tf_op jit(solution)/shard_map/ppermute | solution.py:57
  13.1 1.5 %collective-permute-start.10 = (bf16[2,2,128,512]{3,2,1,0:T(8,128)(2,1)S(1)}, bf16[2,2,128,512]{3,2,1,0:T(8,128)(2,1)S(1)}, u32[]{:S(2)}, u32[]{:S(2)}) collective-permute-start(bf16[2,2,128,512]{3,2,1,0:T(8,128)(2,1)S(1)} %pad_maximum_fusion), channel_id=1, source_target_pairs={{0,4},{1,3},{2,6},{3,1},{4,0},{5,7},{6,2},{7,5},{8,12},{9,11},{10,... | collective-permute-start | bytes 1572872 | tf_op jit(solution)/shard_map/ppermute | solution.py:67
  14.6 1.4 %expand0.1 = (f32[2,20,144,128]{3,2,1,0:T(8,128)S(1)}, bf16[16,128,256]{2,1,0:T(8,128)(2,1)S(1)}) custom-call(s32[4]{0:T(128)S(1)} %pad_add_fusion.refs_0_, bf16[512,256]{1,0:T(8,128)(2,1)S(1)} %get-tuple-element.63.refs_1_.refs_2_, f32[1,256]{1,0:T(1,128)S(1)} %get-tuple-element.64.refs_2_, ...), custom_call_target="tpu_custom_call", output_to_operand_aliasing={{0}: (6, {})} | custom-call | flops 1024 | bytes 1024 | tf_op jit(solution)/shard_map/expand0/pallas_call | solution.py:31
  16.6 1.4 %expand2.1 = (f32[2,20,144,128]{3,2,1,0:T(8,128)S(1)}, bf16[16,128,256]{2,1,0:T(8,128)(2,1)S(1)}) custom-call(s32[4]{0:T(128)S(1)} %pad_add_fusion.refs_0_, bf16[512,256]{1,0:T(8,128)(2,1)S(1)} %get-tuple-element.63.refs_1_.refs_2_, f32[1,256]{1,0:T(1,128)S(1)} %get-tuple-element.64.refs_2_, ...), custom_call_target="tpu_custom_call", output_to_operand_aliasing={{0}: (5, {}), {1}: (6, {})} | custom-call | flops 1024 | bytes 1024 | tf_op jit(solution)/shard_map/expand2/pallas_call | solution.py:31
  18.1 2.3 %collective-permute-start.12 = (bf16[2,128,512]{2,1,0:T(8,128)(2,1)}, bf16[2,128,512]{2,1,0:T(8,128)(2,1)S(1)}, u32[]{:S(2)}, u32[]{:S(2)}) collective-permute-start(bf16[2,128,512]{2,1,0:T(8,128)(2,1)} %refs_7_.1), channel_id=1, source_target_pairs={{0,6},{1,7},{2,4},{3,5},{4,2},{5,3},{6,0},{7,1},{8,14},{9,15},{10,... | collective-permute-start | bytes 786440 | tf_op jit(solution)/shard_map/ppermute | solution.py:57
  20.5 1.8 %expand6.1 = (f32[2,20,144,128]{3,2,1,0:T(8,128)S(1)}, bf16[16,128,256]{2,1,0:T(8,128)(2,1)S(1)}) custom-call(s32[4]{0:T(128)S(1)} %pad_add_fusion.refs_0_, bf16[512,256]{1,0:T(8,128)(2,1)S(1)} %get-tuple-element.63.refs_1_.refs_2_, f32[1,256]{1,0:T(1,128)S(1)} %get-tuple-element.64.refs_2_, ...), custom_call_target="tpu_custom_call", output_to_operand_aliasing={{0}: (6, {}), {1}: (7, {})} | custom-call | flops 1024 | bytes 1024 | tf_op jit(solution)/shard_map/expand6/pallas_call | solution.py:31
  22.2 0.9 %expand7.1 = (f32[2,20,144,128]{3,2,1,0:T(8,128)S(1)}, bf16[16,128,256]{2,1,0:T(8,128)(2,1)S(1)}, bf16[2,128,256]{2,1,0:T(8,128)(2,1)S(1)}, bf16[2,128,256]{2,1,0:T(8,128)(2,1)S(1)}) custom-call(s32[4]{0:T(128)S(1)} %pad_add_fusion.refs_0_, bf16[512,256]{1,0:T(8,128)(2,1)S(1)} %get-tuple-element.63.refs_1_.refs_2_, ...), custom_call_target="tpu_custom_call", output_to_operand_aliasing={{0}: (4, {}), {1}: (5, {})} | custom-call | flops 1024 | bytes 1024 | tf_op jit(solution)/shard_map/expand7/pallas_call | solution.py:31
  23.2 1.6 %collective-permute-start.8 = (bf16[2,128,256]{2,1,0:T(8,128)(2,1)S(1)}, bf16[2,128,256]{2,1,0:T(8,128)(2,1)S(1)}, u32[]{:S(2)}, u32[]{:S(2)}) collective-permute-start(bf16[2,128,256]{2,1,0:T(8,128)(2,1)S(1)} %get-tuple-element.76), channel_id=1, source_target_pairs={{0,8},{1,9},{2,10},{3,11},{4,12},{5,13},{6,14},{7,15},{8,0},{9,1},... | collective-permute-start | bytes 393224 | tf_op jit(solution)/shard_map/ppermute | solution.py:77
  24.8 0.7 collective-permute-start.9
  25.6 4.6 %inner.1 = (bf16[16,128,256]{2,1,0:T(8,128)(2,1)S(1)}, f32[16,128,256]{2,1,0:T(8,128)S(1)}) custom-call(s32[4]{0:T(128)S(1)} %pad_add_fusion.refs_0_, f32[25,256]{1,0:T(8,128)S(1)} %get-tuple-element.60.refs_1_, f32[1,256]{1,0:T(1,128)S(1)} %get-tuple-element.62.refs_2_, f32[2,20,144,128]{3,2,1,0:T(8,128)S(1)} %get-tuple-element.78.refs_3_.refs_7_), custom_call_target="tpu_custom_call" | custom-call | flops 20000000000 | bytes 100000000 | tf_op jit(solution)/shard_map/inner/pallas_call | solution.py:31
  30.2 2.1 %outer.1 = (bf16[16,128,256]{2,1,0:T(8,128)(2,1)S(1)}, f32[16,128,256]{2,1,0:T(8,128)S(1)}, f32[2,20,144,128]{3,2,1,0:T(8,128)S(1)}) custom-call(s32[4]{0:T(128)S(1)} %pad_add_fusion.refs_0_, f32[25,256]{1,0:T(8,128)S(1)} %get-tuple-element.60.refs_1_, ...), custom_call_target="tpu_custom_call", output_to_operand_aliasing={{0}: (5, {}), {1}: (6, {}), {2}: (7, {})} | custom-call | flops 1024 | bytes 1024 | tf_op jit(solution)/shard_map/outer/pallas_call | solution.py:31
  32.9 1.1 %project0.1.refs_8_.refs_6_ = f32[2,20,144,128]{3,2,1,0:T(8,128)S(1)} custom-call(s32[4]{0:T(128)S(1)} %pad_add_fusion.refs_0_, bf16[256,512]{1,0:T(8,128)(2,1)S(1)} %get-tuple-element.61.refs_1_, f32[16,128,256]{2,1,0:T(8,128)S(1)} %get-tuple-element.81.refs_2_, ...), custom_call_target="tpu_custom_call", output_to_operand_aliasing={{}: (7, {})} | custom-call | flops 1024 | bytes 1024 | tf_op jit(solution)/shard_map/project0/pallas_call | solution.py:31
  34.1 1.3 %w2.1 = (f32[64,512]{1,0:T(8,128)S(1)}, bf16[64,512]{1,0:T(8,128)(2,1)S(1)}, bf16[64,512]{1,0:T(8,128)(2,1)S(1)}, bf16[64,512]{1,0:T(8,128)(2,1)S(1)}) custom-call(s32[4]{0:T(128)S(1)} %pad_add_fusion.refs_0_, bf16[16,128,256]{2,1,0:T(8,128)(2,1)S(1)} %get-tuple-element.86.refs_1_, bf16[2,128,512]{2,1,0:T(8,128)(2,1)S(1)} %get-tuple-element.59.refs_3_.refs_2_.refs_1_, ...), custom_call_target="tpu_custom_call" | custom-call | flops 1024 | bytes 1024 | tf_op jit(solution)/shard_map/w2/pallas_call | solution.py:31
  35.4 4.4 %collective-permute-start.16 = (bf16[2,64,512]{2,1,0:T(8,128)(2,1)S(1)}, bf16[2,64,512]{2,1,0:T(8,128)(2,1)S(1)}, u32[]{:S(2)}, u32[]{:S(2)}) collective-permute-start(bf16[2,64,512]{2,1,0:T(8,128)(2,1)S(1)} %pad_maximum_fusion.1), channel_id=1, source_target_pairs={{0,16},{1,17},{2,18},{3,19},{4,20},{5,21},{6,22},{7,23},{8,24},{9,... | collective-permute-start | bytes 393224 | tf_op jit(solution)/shard_map/ppermute | solution.py:57
  39.8 1.0 %project4.1 = (f32[2,20,144,128]{3,2,1,0:T(8,128)S(1)}, bf16[2,128,256]{2,1,0:T(8,128)(2,1)S(1)}, bf16[2,128,256]{2,1,0:T(8,128)(2,1)S(1)}) custom-call(s32[4]{0:T(128)S(1)} %pad_add_fusion.refs_0_, bf16[256,512]{1,0:T(8,128)(2,1)S(1)} %get-tuple-element.61.refs_1_, f32[16,128,256]{2,1,0:T(8,128)S(1)} %get-tuple-element.81.refs_2_, ...), custom_call_target="tpu_custom_call", output_to_operand_aliasing={{0}: (6, {})} | custom-call | flops 1024 | bytes 1024 | tf_op jit(solution)/shard_map/project4/pallas_call | solution.py:31
  40.8 0.7 collective-permute-start.14
  41.5 1.9 %collective-permute-start.15 = (bf16[2,128,256]{2,1,0:T(8,128)(2,1)S(1)}, bf16[2,128,256]{2,1,0:T(8,128)(2,1)S(1)}, u32[]{:S(2)}, u32[]{:S(2)}) collective-permute-start(bf16[2,128,256]{2,1,0:T(8,128)(2,1)S(1)} %get-tuple-element.91), channel_id=1, source_target_pairs={{0,8},{1,9},{2,10},{3,11},{4,12},{5,13},{6,14},{7,15},{8,0},{9,1},... | collective-permute-start | bytes 393224 | tf_op jit(solution)/shard_map/ppermute | solution.py:77
  43.3 4.3 %taps.1.refs_5_.refs_2_ = f32[64,256]{1,0:T(8,128)S(1)} custom-call(s32[4]{0:T(128)S(1)} %pad_add_fusion.refs_0_, f32[2,20,144,128]{3,2,1,0:T(8,128)S(1)} %get-tuple-element.92.refs_1_, f32[2,20,144,128]{3,2,1,0:T(8,128)S(1)} %get-tuple-element.93.refs_2_.refs_8_), custom_call_target="tpu_custom_call" | custom-call | flops 1024 | bytes 1024 | tf_op jit(solution)/shard_map/taps/pallas_call | solution.py:31
  48.0 4.5 %back.1 = (f32[2,20,144,128]{3,2,1,0:T(8,128)S(1)}, bf16[16,128,256]{2,1,0:T(8,128)(2,1)S(1)}, f32[1,256]{1,0:T(1,128)S(1)}) custom-call(s32[4]{0:T(128)S(1)} %pad_add_fusion.refs_0_, f32[25,256]{1,0:T(8,128)S(1)} %get-tuple-element.60.refs_1_, bf16[2,128,256]{2,1,0:T(8,128)(2,1)S(1)} %collective-permute-done.14.refs_2_, ...), custom_call_target="tpu_custom_call", output_to_operand_aliasing={{0}: (8, {})} | custom-call | flops 1024 | bytes 1024 | tf_op jit(solution)/shard_map/back/pallas_call | solution.py:31
  52.5 1.0 %core.1.refs_13_ = bf16[4,2,128,512]{3,2,1,0:T(8,128)(2,1)S(1)} custom-call(s32[4]{0:T(128)S(1)} %pad_add_fusion.refs_0_, bf16[16,128,256]{2,1,0:T(8,128)(2,1)S(1)} %get-tuple-element.97.refs_1_, bf16[512,256]{1,0:T(8,128)(2,1)S(1)} %get-tuple-element.63.refs_1_.refs_2_, bf16[64,512]{1,0:T(8,128)(2,1)S(1)} %add_convert_fusion.refs_3_.refs_12_.refs_1_), custom_call_target="tpu_custom_call" | custom-call | flops 1024 | bytes 1024 | tf_op jit(solution)/shard_map/core/pallas_call | solution.py:31
  53.6 3.1 %collective-permute-start.25 = (bf16[64,512]{1,0:T(8,128)(2,1)S(1)}, bf16[64,512]{1,0:T(8,128)(2,1)S(1)}, u32[]{:S(2)}, u32[]{:S(2)}) collective-permute-start(bf16[64,512]{1,0:T(8,128)(2,1)S(1)} %add_convert_fusion.refs_3_.refs_12_.refs_1_), channel_id=1, source_target_pairs={{0,16},{1,17},{2,18},{3,19},{4,20},{5,21},{6,22},{7,23},{8,24},{9,... | collective-permute-start | bytes 196616 | tf_op jit(solution)/shard_map/ppermute | solution.py:57
  56.7 1.3 %w1.1 = (f32[144,256]{1,0:T(8,128)S(1)}, bf16[144,256]{1,0:T(8,128)(2,1)S(1)}, bf16[144,256]{1,0:T(8,128)(2,1)S(1)}, bf16[144,256]{1,0:T(8,128)(2,1)S(1)}) custom-call(s32[4]{0:T(128)S(1)} %pad_add_fusion.refs_0_, bf16[16,128,256]{2,1,0:T(8,128)(2,1)S(1)} %get-tuple-element.97.refs_1_, f32[64,256]{1,0:T(8,128)S(1)} %taps.1.refs_5_.refs_2_, ...), custom_call_target="tpu_custom_call" | custom-call | flops 1024 | bytes 1024 | tf_op jit(solution)/shard_map/w1/pallas_call | solution.py:31
  58.0 1.0 %collective-permute-start.20 = (bf16[144,256]{1,0:T(8,128)(2,1)S(1)}, bf16[144,256]{1,0:T(8,128)(2,1)S(1)}, u32[]{:S(2)}, u32[]{:S(2)}) collective-permute-start(bf16[144,256]{1,0:T(8,128)(2,1)S(1)} %get-tuple-element.102), channel_id=1, source_target_pairs={{0,8},{1,9},{2,10},{3,11},{4,12},{5,13},{6,14},{7,15},{8,0},{9,1},... | collective-permute-start | bytes 221192 | tf_op jit(solution)/shard_map/ppermute | solution.py:57
  59.0 0.8 collective-permute-start.21
  59.8 2.6 %collective-permute-start.22 = (bf16[144,256]{1,0:T(8,128)(2,1)S(1)}, bf16[144,256]{1,0:T(8,128)(2,1)S(1)}, u32[]{:S(2)}, u32[]{:S(2)}) collective-permute-start(bf16[144,256]{1,0:T(8,128)(2,1)S(1)} %get-tuple-element.104), channel_id=1, source_target_pairs={{0,24},{1,25},{2,26},{3,27},{4,28},{5,29},{6,30},{7,31},{8,16},{9,... | collective-permute-start | bytes 221192 | tf_op jit(solution)/shard_map/ppermute | solution.py:57
  62.5 0.9 chip_send.1.refs_4_
  64.0 0.9 chip_keep.1.refs_5_.refs_1_.refs_2_
  64.9 2.8 %collective-permute-done.21.refs_3_ = bf16[144,256]{1,0:T(8,128)(2,1)S(1)} collective-permute-done((bf16[144,256]{1,0:T(8,128)(2,1)S(1)}, bf16[144,256]{1,0:T(8,128)(2,1)S(1)}, u32[]{:S(2)}, u32[]{:S(2)}) %collective-permute-start.21) | collective-permute-done | bytes 73760 | tf_op jit(solution)/shard_map/ppermute | solution.py:57
  68.3 0.6 collective-permute-start.23
  68.9 1.4 %collective-permute-start.30 = (bf16[144,256]{1,0:T(8,128)(2,1)S(1)}, bf16[144,256]{1,0:T(8,128)(2,1)S(1)}, u32[]{:S(2)}, u32[]{:S(2)}) collective-permute-start(bf16[144,256]{1,0:T(8,128)(2,1)S(1)} %sum.1.refs_5_.refs_7_), channel_id=1, source_target_pairs={{0,24},{1,25},{2,26},{3,27},{4,28},{5,29},{6,30},{7,31},{8,16},{9,... | collective-permute-start | bytes 221192 | tf_op jit(solution)/shard_map/ppermute | solution.py:57
  70.4 0.7 collective-permute-start.28
  71.0 2.3 %collective-permute-start.29 = (bf16[144,256]{1,0:T(8,128)(2,1)S(1)}, bf16[144,256]{1,0:T(8,128)(2,1)S(1)}, u32[]{:S(2)}, u32[]{:S(2)}) collective-permute-start(bf16[144,256]{1,0:T(8,128)(2,1)S(1)} %sum.1.refs_5_.refs_7_), channel_id=1, source_target_pairs={{0,16},{1,17},{2,18},{3,19},{4,20},{5,21},{6,22},{7,23},{8,24},{9,... | collective-permute-start | bytes 221192 | tf_op jit(solution)/shard_map/ppermute | solution.py:57
  74.2 1.3 %collective-permute-start.27 = (bf16[4,64,512]{2,1,0:T(8,128)(2,1)S(1)}, bf16[4,64,512]{2,1,0:T(8,128)(2,1)S(1)}, u32[]{:S(2)}, u32[]{:S(2)}) collective-permute-start(bf16[4,64,512]{2,1,0:T(8,128)(2,1)S(1)} %column.1.refs_5_), channel_id=1, source_target_pairs={{0,4},{1,5},{2,6},{3,7},{4,0},{5,1},{6,2},{7,3},{8,12},{9,13},{10,... | collective-permute-start | bytes 786440 | tf_op jit(solution)/shard_map/ppermute | solution.py:57
  77.2 1.3 %collective-permute-start.31 = (bf16[144,256]{1,0:T(8,128)(2,1)S(1)}, bf16[144,256]{1,0:T(8,128)(2,1)S(1)}, u32[]{:S(2)}, u32[]{:S(2)}) collective-permute-start(bf16[144,256]{1,0:T(8,128)(2,1)S(1)} %side.1.refs_11_), channel_id=1, source_target_pairs={{0,8},{1,9},{2,10},{3,11},{4,12},{5,13},{6,14},{7,15},{8,0},{9,1},... | collective-permute-start | bytes 221192 | tf_op jit(solution)/shard_map/ppermute | solution.py:57
  78.5 0.7 collective-permute-start.32
  79.2 2.5 %collective-permute-start.33 = (bf16[144,256]{1,0:T(8,128)(2,1)S(1)}, bf16[144,256]{1,0:T(8,128)(2,1)S(1)}, u32[]{:S(2)}, u32[]{:S(2)}) collective-permute-start(bf16[144,256]{1,0:T(8,128)(2,1)S(1)} %side.1.refs_11_), channel_id=1, source_target_pairs={{0,24},{1,25},{2,26},{3,27},{4,28},{5,29},{6,30},{7,31},{8,16},{9,... | collective-permute-start | bytes 221192 | tf_op jit(solution)/shard_map/ppermute | solution.py:57
  81.9 2.6 %collective-permute-done.32.refs_13_ = bf16[144,256]{1,0:T(8,128)(2,1)S(1)} collective-permute-done((bf16[144,256]{1,0:T(8,128)(2,1)S(1)}, bf16[144,256]{1,0:T(8,128)(2,1)S(1)}, u32[]{:S(2)}, u32[]{:S(2)}) %collective-permute-start.32) | collective-permute-done | bytes 73760 | tf_op jit(solution)/shard_map/ppermute | solution.py:57
  84.5 0.9 %collective-permute-done.33.refs_14_ = bf16[144,256]{1,0:T(8,128)(2,1)S(1)} collective-permute-done((bf16[144,256]{1,0:T(8,128)(2,1)S(1)}, bf16[144,256]{1,0:T(8,128)(2,1)S(1)}, u32[]{:S(2)}, u32[]{:S(2)}) %collective-permute-start.33) | collective-permute-done | bytes 73760 | tf_op jit(solution)/shard_map/ppermute | solution.py:57
  85.4 2.0 %last.1 = (bf16[2,128,512]{2,1,0:T(8,128)(2,1)}, f32[512,512]{1,0:T(8,128)}, f32[512,512]{1,0:T(8,128)}, f32[25,512]{1,0:T(8,128)}, f32[1,512]{1,0:T(1,128)}, /*index=5*/f32[1,512]{1,0:T(1,128)}) custom-call(s32[4]{0:T(128)S(1)} %pad_add_fusion.refs_0_, bf16[2,128,512]{2,1,0:T(8,128)(2,1)S(1)} %get-tuple-element.59.refs_3_.refs_2_.refs_1_, ...), custom_call_target="tpu_custom_call" | custom-call | tf_op jit(solution)/shard_map/last/pallas_call | solution.py:31
  (62 shorter events, 6.7 us)
Async XLA Ops:
  0.6 11.1 %collective-permute-start.4 = (bf16[2,128,512]{2,1,0:T(8,128)(2,1)}, bf16[2,128,512]{2,1,0:T(8,128)(2,1)S(1)}, u32[]{:S(2)}, u32[]{:S(2)}) collective-permute-start(bf16[2,128,512]{2,1,0:T(8,128)(2,1)} %refs_7_.1), channel_id=1, source_target_pairs={{0,1},{1,0},{2,3},{3,2},{4,5},{5,4},{6,7},{7,6},{8,9},{9,8},{10,11... | collective-permute-start | bytes 786440 | tf_op jit(solution)/shard_map/ppermute | solution.py:57
  1.1 10.7 %collective-permute-start.1 = (bf16[2,128,512]{2,1,0:T(8,128)(2,1)}, bf16[2,128,512]{2,1,0:T(8,128)(2,1)S(1)}, u32[]{:S(2)}, u32[]{:S(2)}) collective-permute-start(bf16[2,128,512]{2,1,0:T(8,128)(2,1)} %refs_6_.1), channel_id=1, source_target_pairs={{0,2},{1,3},{2,0},{3,1},{4,6},{5,7},{6,4},{7,5},{8,10},{9,11},{10,... | collective-permute-start | bytes 786440 | tf_op jit(solution)/shard_map/ppermute | solution.py:57
  3.7 9.4 %collective-permute-start.2 = (bf16[2,128,512]{2,1,0:T(8,128)(2,1)}, bf16[2,128,512]{2,1,0:T(8,128)(2,1)S(1)}, u32[]{:S(2)}, u32[]{:S(2)}) collective-permute-start(bf16[2,128,512]{2,1,0:T(8,128)(2,1)} %refs_6_.1), channel_id=1, source_target_pairs={{0,4},{1,5},{2,6},{3,7},{4,0},{5,1},{6,2},{7,3},{8,12},{9,13},{10,... | collective-permute-start | bytes 786440 | tf_op jit(solution)/shard_map/ppermute | solution.py:57
  5.2 9.4 %collective-permute-start.3 = (bf16[2,128,512]{2,1,0:T(8,128)(2,1)}, bf16[2,128,512]{2,1,0:T(8,128)(2,1)S(1)}, u32[]{:S(2)}, u32[]{:S(2)}) collective-permute-start(bf16[2,128,512]{2,1,0:T(8,128)(2,1)} %refs_6_.1), channel_id=1, source_target_pairs={{0,1},{1,0},{2,3},{3,2},{4,5},{5,4},{6,7},{7,6},{8,9},{9,8},{10,11... | collective-permute-start | bytes 786440 | tf_op jit(solution)/shard_map/ppermute | solution.py:57
  5.2 12.7 %collective-permute-start = (bf16[2,128,512]{2,1,0:T(8,128)(2,1)}, bf16[2,128,512]{2,1,0:T(8,128)(2,1)S(1)}, u32[]{:S(2)}, u32[]{:S(2)}) collective-permute-start(bf16[2,128,512]{2,1,0:T(8,128)(2,1)} %refs_6_.1), channel_id=1, source_target_pairs={{0,6},{1,7},{2,4},{3,5},{4,2},{5,3},{6,0},{7,1},{8,14},{9,15},{10,... | collective-permute-start | bytes 786440 | tf_op jit(solution)/shard_map/ppermute | solution.py:57
  5.4 1.0 %copy-start = (bf16[512,512]{1,0:T(8,128)(2,1)S(1)}, bf16[512,512]{1,0:T(8,128)(2,1)}, u32[]{:S(2)}) copy-start(bf16[512,512]{1,0:T(8,128)(2,1)} %refs_1_.1) | copy-start | bytes 1572868
  6.5 1.0 %copy-start.1 = (bf16[512,512]{1,0:T(8,128)(2,1)S(1)}, bf16[512,512]{1,0:T(8,128)(2,1)}, u32[]{:S(2)}) copy-start(bf16[512,512]{1,0:T(8,128)(2,1)} %refs_5_.1) | copy-start | bytes 1572868
  7.5 0.9 %copy-start.2 = (bf16[2,128,512]{2,1,0:T(8,128)(2,1)S(1)}, bf16[2,128,512]{2,1,0:T(8,128)(2,1)}, u32[]{:S(2)}) copy-start(bf16[2,128,512]{2,1,0:T(8,128)(2,1)} %refs_6_.1) | copy-start | bytes 786436
  8.5 0.8 copy-start.3
  9.3 0.7 copy-start.4
  10.0 0.7 copy-start.5
  13.1 12.4 %collective-permute-start.10 = (bf16[2,2,128,512]{3,2,1,0:T(8,128)(2,1)S(1)}, bf16[2,2,128,512]{3,2,1,0:T(8,128)(2,1)S(1)}, u32[]{:S(2)}, u32[]{:S(2)}) collective-permute-start(bf16[2,2,128,512]{3,2,1,0:T(8,128)(2,1)S(1)} %pad_maximum_fusion), channel_id=1, source_target_pairs={{0,4},{1,3},{2,6},{3,1},{4,0},{5,7},{6,2},{7,5},{8,12},{9,11},{10,... | collective-permute-start | bytes 1572872 | tf_op jit(solution)/shard_map/ppermute | solution.py:67
  16.0 4.4 %collective-permute-start.6 = (bf16[2,128,512]{2,1,0:T(8,128)(2,1)S(1)}, bf16[2,128,512]{2,1,0:T(8,128)(2,1)S(1)}, u32[]{:S(2)}, u32[]{:S(2)}) collective-permute-start(bf16[2,128,512]{2,1,0:T(8,128)(2,1)S(1)} %collective-permute-done.1.refs_3_.refs_6_), channel_id=1, source_target_pairs={{0,1},{1,0},{2,3},{3,2},{4,5},{5,4},{6,7},{7,6},{8,9},{9,8},{10,11... | collective-permute-start | bytes 786440 | tf_op jit(solution)/shard_map/ppermute | solution.py:57
  16.1 4.4 %collective-permute-start.7 = (bf16[2,128,512]{2,1,0:T(8,128)(2,1)S(1)}, bf16[2,128,512]{2,1,0:T(8,128)(2,1)S(1)}, u32[]{:S(2)}, u32[]{:S(2)}) collective-permute-start(bf16[2,128,512]{2,1,0:T(8,128)(2,1)S(1)} %collective-permute-done.2.refs_4_.refs_8_), channel_id=1, source_target_pairs={{0,1},{1,0},{2,3},{3,2},{4,5},{5,4},{6,7},{7,6},{8,9},{9,8},{10,11... | collective-permute-start | bytes 786440 | tf_op jit(solution)/shard_map/ppermute | solution.py:57
  18.0 4.2 %collective-permute-start.5 = (bf16[2,128,512]{2,1,0:T(8,128)(2,1)S(1)}, bf16[2,128,512]{2,1,0:T(8,128)(2,1)S(1)}, u32[]{:S(2)}, u32[]{:S(2)}) collective-permute-start(bf16[2,128,512]{2,1,0:T(8,128)(2,1)S(1)} %collective-permute-done.refs_3_.refs_10_), channel_id=1, source_target_pairs={{0,1},{1,0},{2,3},{3,2},{4,5},{5,4},{6,7},{7,6},{8,9},{9,8},{10,11... | collective-permute-start | bytes 786440 | tf_op jit(solution)/shard_map/ppermute | solution.py:57
  18.1 14.2 %collective-permute-start.12 = (bf16[2,128,512]{2,1,0:T(8,128)(2,1)}, bf16[2,128,512]{2,1,0:T(8,128)(2,1)S(1)}, u32[]{:S(2)}, u32[]{:S(2)}) collective-permute-start(bf16[2,128,512]{2,1,0:T(8,128)(2,1)} %refs_7_.1), channel_id=1, source_target_pairs={{0,6},{1,7},{2,4},{3,5},{4,2},{5,3},{6,0},{7,1},{8,14},{9,15},{10,... | collective-permute-start | bytes 786440 | tf_op jit(solution)/shard_map/ppermute | solution.py:57
  23.2 7.0 %collective-permute-start.8 = (bf16[2,128,256]{2,1,0:T(8,128)(2,1)S(1)}, bf16[2,128,256]{2,1,0:T(8,128)(2,1)S(1)}, u32[]{:S(2)}, u32[]{:S(2)}) collective-permute-start(bf16[2,128,256]{2,1,0:T(8,128)(2,1)S(1)} %get-tuple-element.76), channel_id=1, source_target_pairs={{0,8},{1,9},{2,10},{3,11},{4,12},{5,13},{6,14},{7,15},{8,0},{9,1},... | collective-permute-start | bytes 393224 | tf_op jit(solution)/shard_map/ppermute | solution.py:77
  24.8 5.4 %collective-permute-start.9 = (bf16[2,128,256]{2,1,0:T(8,128)(2,1)S(1)}, bf16[2,128,256]{2,1,0:T(8,128)(2,1)S(1)}, u32[]{:S(2)}, u32[]{:S(2)}) collective-permute-start(bf16[2,128,256]{2,1,0:T(8,128)(2,1)S(1)} %get-tuple-element.77), channel_id=1, source_target_pairs={{8,16},{9,17},{10,18},{11,19},{12,20},{13,21},{14,22},{15,23},{16,... | collective-permute-start | bytes 393224 | tf_op jit(solution)/shard_map/ppermute | solution.py:77
  25.5 8.6 %collective-permute-start.11 = (bf16[2,2,128,512]{3,2,1,0:T(8,128)(2,1)S(1)}, bf16[2,2,128,512]{3,2,1,0:T(8,128)(2,1)S(1)}, u32[]{:S(2)}, u32[]{:S(2)}) collective-permute-start(bf16[2,2,128,512]{3,2,1,0:T(8,128)(2,1)S(1)} %collective-permute-done.10.refs_5_.refs_4_), channel_id=1, source_target_pairs={{0,1},{1,0},{2,3},{3,2},{4,5},{5,4},{6,7},{7,6},{8,9},{9,8},{10,11... | collective-permute-start | bytes 1572872 | tf_op jit(solution)/shard_map/ppermute | solution.py:57
  32.3 1.7 %collective-permute-start.13 = (bf16[2,128,512]{2,1,0:T(8,128)(2,1)S(1)}, bf16[2,128,512]{2,1,0:T(8,128)(2,1)S(1)}, u32[]{:S(2)}, u32[]{:S(2)}) collective-permute-start(bf16[2,128,512]{2,1,0:T(8,128)(2,1)S(1)} %collective-permute-done.12.refs_6_.refs_5_), channel_id=1, source_target_pairs={{0,1},{1,0},{2,3},{3,2},{4,5},{5,4},{6,7},{7,6},{8,9},{9,8},{10,11... | collective-permute-start | bytes 786440 | tf_op jit(solution)/shard_map/ppermute | solution.py:57
  35.4 12.2 %collective-permute-start.16 = (bf16[2,64,512]{2,1,0:T(8,128)(2,1)S(1)}, bf16[2,64,512]{2,1,0:T(8,128)(2,1)S(1)}, u32[]{:S(2)}, u32[]{:S(2)}) collective-permute-start(bf16[2,64,512]{2,1,0:T(8,128)(2,1)S(1)} %pad_maximum_fusion.1), channel_id=1, source_target_pairs={{0,16},{1,17},{2,18},{3,19},{4,20},{5,21},{6,22},{7,23},{8,24},{9,... | collective-permute-start | bytes 393224 | tf_op jit(solution)/shard_map/ppermute | solution.py:57
  40.8 7.2 %collective-permute-start.14 = (bf16[2,128,256]{2,1,0:T(8,128)(2,1)S(1)}, bf16[2,128,256]{2,1,0:T(8,128)(2,1)S(1)}, u32[]{:S(2)}, u32[]{:S(2)}) collective-permute-start(bf16[2,128,256]{2,1,0:T(8,128)(2,1)S(1)} %get-tuple-element.90), channel_id=1, source_target_pairs={{8,16},{9,17},{10,18},{11,19},{12,20},{13,21},{14,22},{15,23},{16,... | collective-permute-start | bytes 393224 | tf_op jit(solution)/shard_map/ppermute | solution.py:77
  41.5 6.6 %collective-permute-start.15 = (bf16[2,128,256]{2,1,0:T(8,128)(2,1)S(1)}, bf16[2,128,256]{2,1,0:T(8,128)(2,1)S(1)}, u32[]{:S(2)}, u32[]{:S(2)}) collective-permute-start(bf16[2,128,256]{2,1,0:T(8,128)(2,1)S(1)} %get-tuple-element.91), channel_id=1, source_target_pairs={{0,8},{1,9},{2,10},{3,11},{4,12},{5,13},{6,14},{7,15},{8,0},{9,1},... | collective-permute-start | bytes 393224 | tf_op jit(solution)/shard_map/ppermute | solution.py:77
  47.7 4.7 %collective-permute-start.17 = (bf16[64,512]{1,0:T(8,128)(2,1)S(1)}, bf16[64,512]{1,0:T(8,128)(2,1)S(1)}, u32[]{:S(2)}, u32[]{:S(2)}) collective-permute-start(bf16[64,512]{1,0:T(8,128)(2,1)S(1)} %convert_element_type.17), channel_id=1, source_target_pairs={{0,8},{1,9},{2,10},{3,11},{4,12},{5,13},{6,14},{7,15},{8,0},{9,1},... | collective-permute-start | bytes 196616 | tf_op jit(solution)/shard_map/ppermute | solution.py:57
  53.5 8.9 %collective-permute-start.18 = (bf16[4,2,128,512]{3,2,1,0:T(8,128)(2,1)S(1)}, bf16[4,2,128,512]{3,2,1,0:T(8,128)(2,1)S(1)}, u32[]{:S(2)}, u32[]{:S(2)}) collective-permute-start(bf16[4,2,128,512]{3,2,1,0:T(8,128)(2,1)S(1)} %core.1.refs_13_), channel_id=1, source_target_pairs={{0,1},{1,0},{2,3},{3,2},{4,5},{5,4},{6,7},{7,6},{8,9},{9,8},{10,11... | collective-permute-start | bytes 3145736 | tf_op jit(solution)/shard_map/ppermute | solution.py:57
  53.6 8.8 %collective-permute-start.25 = (bf16[64,512]{1,0:T(8,128)(2,1)S(1)}, bf16[64,512]{1,0:T(8,128)(2,1)S(1)}, u32[]{:S(2)}, u32[]{:S(2)}) collective-permute-start(bf16[64,512]{1,0:T(8,128)(2,1)S(1)} %add_convert_fusion.refs_3_.refs_12_.refs_1_), channel_id=1, source_target_pairs={{0,16},{1,17},{2,18},{3,19},{4,20},{5,21},{6,22},{7,23},{8,24},{9,... | collective-permute-start | bytes 196616 | tf_op jit(solution)/shard_map/ppermute | solution.py:57
  58.0 6.9 %collective-permute-start.20 = (bf16[144,256]{1,0:T(8,128)(2,1)S(1)}, bf16[144,256]{1,0:T(8,128)(2,1)S(1)}, u32[]{:S(2)}, u32[]{:S(2)}) collective-permute-start(bf16[144,256]{1,0:T(8,128)(2,1)S(1)} %get-tuple-element.102), channel_id=1, source_target_pairs={{0,8},{1,9},{2,10},{3,11},{4,12},{5,13},{6,14},{7,15},{8,0},{9,1},... | collective-permute-start | bytes 221192 | tf_op jit(solution)/shard_map/ppermute | solution.py:57
  59.0 8.7 %collective-permute-start.21 = (bf16[144,256]{1,0:T(8,128)(2,1)S(1)}, bf16[144,256]{1,0:T(8,128)(2,1)S(1)}, u32[]{:S(2)}, u32[]{:S(2)}) collective-permute-start(bf16[144,256]{1,0:T(8,128)(2,1)S(1)} %get-tuple-element.103), channel_id=1, source_target_pairs={{0,16},{1,17},{2,18},{3,19},{4,20},{5,21},{6,22},{7,23},{8,24},{9,... | collective-permute-start | bytes 221192 | tf_op jit(solution)/shard_map/ppermute | solution.py:57
  59.8 7.9 %collective-permute-start.22 = (bf16[144,256]{1,0:T(8,128)(2,1)S(1)}, bf16[144,256]{1,0:T(8,128)(2,1)S(1)}, u32[]{:S(2)}, u32[]{:S(2)}) collective-permute-start(bf16[144,256]{1,0:T(8,128)(2,1)S(1)} %get-tuple-element.104), channel_id=1, source_target_pairs={{0,24},{1,25},{2,26},{3,27},{4,28},{5,29},{6,30},{7,31},{8,16},{9,... | collective-permute-start | bytes 221192 | tf_op jit(solution)/shard_map/ppermute | solution.py:57
  63.4 12.1 %collective-permute-start.19 = (bf16[2,2,128,512]{3,2,1,0:T(8,128)(2,1)S(1)}, bf16[2,2,128,512]{3,2,1,0:T(8,128)(2,1)S(1)}, u32[]{:S(2)}, u32[]{:S(2)}) collective-permute-start(bf16[2,2,128,512]{3,2,1,0:T(8,128)(2,1)S(1)} %chip_send.1.refs_4_), channel_id=1, source_target_pairs={{0,4},{1,3},{2,6},{3,1},{4,0},{5,7},{6,2},{7,5},{8,12},{9,11},{10,... | collective-permute-start | bytes 1572872 | tf_op jit(solution)/shard_map/ppermute | solution.py:67
  64.0 7.1 %collective-permute-start.26 = (bf16[2,64,512]{2,1,0:T(8,128)(2,1)S(1)}, bf16[2,64,512]{2,1,0:T(8,128)(2,1)S(1)}, u32[]{:S(2)}, u32[]{:S(2)}) collective-permute-start(bf16[2,64,512]{2,1,0:T(8,128)(2,1)S(1)} %pad_maximum_fusion.2), channel_id=1, source_target_pairs={{0,8},{1,9},{2,10},{3,11},{4,12},{5,13},{6,14},{7,15},{8,0},{9,1},... | collective-permute-start | bytes 393224 | tf_op jit(solution)/shard_map/ppermute | solution.py:57
  68.3 5.8 %collective-permute-start.23 = (bf16[144,256]{1,0:T(8,128)(2,1)S(1)}, bf16[144,256]{1,0:T(8,128)(2,1)S(1)}, u32[]{:S(2)}, u32[]{:S(2)}) collective-permute-start(bf16[144,256]{1,0:T(8,128)(2,1)S(1)} %sum.1.refs_5_.refs_7_), channel_id=1, source_target_pairs={{0,4},{1,5},{2,6},{3,7},{4,0},{5,1},{6,2},{7,3},{8,12},{9,13},{10,... | collective-permute-start | bytes 221192 | tf_op jit(solution)/shard_map/ppermute | solution.py:57
  68.9 7.7 %collective-permute-start.30 = (bf16[144,256]{1,0:T(8,128)(2,1)S(1)}, bf16[144,256]{1,0:T(8,128)(2,1)S(1)}, u32[]{:S(2)}, u32[]{:S(2)}) collective-permute-start(bf16[144,256]{1,0:T(8,128)(2,1)S(1)} %sum.1.refs_5_.refs_7_), channel_id=1, source_target_pairs={{0,24},{1,25},{2,26},{3,27},{4,28},{5,29},{6,30},{7,31},{8,16},{9,... | collective-permute-start | bytes 221192 | tf_op jit(solution)/shard_map/ppermute | solution.py:57
  70.4 8.1 %collective-permute-start.28 = (bf16[144,256]{1,0:T(8,128)(2,1)S(1)}, bf16[144,256]{1,0:T(8,128)(2,1)S(1)}, u32[]{:S(2)}, u32[]{:S(2)}) collective-permute-start(bf16[144,256]{1,0:T(8,128)(2,1)S(1)} %sum.1.refs_5_.refs_7_), channel_id=1, source_target_pairs={{0,8},{1,9},{2,10},{3,11},{4,12},{5,13},{6,14},{7,15},{8,0},{9,1},... | collective-permute-start | bytes 221192 | tf_op jit(solution)/shard_map/ppermute | solution.py:57
  71.0 8.1 %collective-permute-start.29 = (bf16[144,256]{1,0:T(8,128)(2,1)S(1)}, bf16[144,256]{1,0:T(8,128)(2,1)S(1)}, u32[]{:S(2)}, u32[]{:S(2)}) collective-permute-start(bf16[144,256]{1,0:T(8,128)(2,1)S(1)} %sum.1.refs_5_.refs_7_), channel_id=1, source_target_pairs={{0,16},{1,17},{2,18},{3,19},{4,20},{5,21},{6,22},{7,23},{8,24},{9,... | collective-permute-start | bytes 221192 | tf_op jit(solution)/shard_map/ppermute | solution.py:57
  74.2 11.3 %collective-permute-start.27 = (bf16[4,64,512]{2,1,0:T(8,128)(2,1)S(1)}, bf16[4,64,512]{2,1,0:T(8,128)(2,1)S(1)}, u32[]{:S(2)}, u32[]{:S(2)}) collective-permute-start(bf16[4,64,512]{2,1,0:T(8,128)(2,1)S(1)} %column.1.refs_5_), channel_id=1, source_target_pairs={{0,4},{1,5},{2,6},{3,7},{4,0},{5,1},{6,2},{7,3},{8,12},{9,13},{10,... | collective-permute-start | bytes 786440 | tf_op jit(solution)/shard_map/ppermute | solution.py:57
  76.1 9.4 %collective-permute-start.24 = (bf16[2,128,512]{2,1,0:T(8,128)(2,1)S(1)}, bf16[2,128,512]{2,1,0:T(8,128)(2,1)S(1)}, u32[]{:S(2)}, u32[]{:S(2)}) collective-permute-start(bf16[2,128,512]{2,1,0:T(8,128)(2,1)S(1)} %forward.1), channel_id=1, source_target_pairs={{0,2},{1,5},{2,0},{3,7},{4,6},{5,1},{6,4},{7,3},{8,10},{9,13},{10,... | collective-permute-start | bytes 786440 | tf_op jit(solution)/shard_map/ppermute | solution.py:67
  77.2 4.7 %collective-permute-start.31 = (bf16[144,256]{1,0:T(8,128)(2,1)S(1)}, bf16[144,256]{1,0:T(8,128)(2,1)S(1)}, u32[]{:S(2)}, u32[]{:S(2)}) collective-permute-start(bf16[144,256]{1,0:T(8,128)(2,1)S(1)} %side.1.refs_11_), channel_id=1, source_target_pairs={{0,8},{1,9},{2,10},{3,11},{4,12},{5,13},{6,14},{7,15},{8,0},{9,1},... | collective-permute-start | bytes 221192 | tf_op jit(solution)/shard_map/ppermute | solution.py:57
  78.5 6.0 %collective-permute-start.32 = (bf16[144,256]{1,0:T(8,128)(2,1)S(1)}, bf16[144,256]{1,0:T(8,128)(2,1)S(1)}, u32[]{:S(2)}, u32[]{:S(2)}) collective-permute-start(bf16[144,256]{1,0:T(8,128)(2,1)S(1)} %side.1.refs_11_), channel_id=1, source_target_pairs={{0,16},{1,17},{2,18},{3,19},{4,20},{5,21},{6,22},{7,23},{8,24},{9,... | collective-permute-start | bytes 221192 | tf_op jit(solution)/shard_map/ppermute | solution.py:57
  79.2 6.3 %collective-permute-start.33 = (bf16[144,256]{1,0:T(8,128)(2,1)S(1)}, bf16[144,256]{1,0:T(8,128)(2,1)S(1)}, u32[]{:S(2)}, u32[]{:S(2)}) collective-permute-start(bf16[144,256]{1,0:T(8,128)(2,1)S(1)} %side.1.refs_11_), channel_id=1, source_target_pairs={{0,24},{1,25},{2,26},{3,27},{4,28},{5,29},{6,30},{7,31},{8,16},{9,... | collective-permute-start | bytes 221192 | tf_op jit(solution)/shard_map/ppermute | solution.py:57

commit v7 on v6

--- a/solution.py
+++ b/solution.py
@@ -293,6 +293,11 @@
         ref[n:, :] = total[pl.ds(pl.multiple_of(cin + at * m, m), m), :].astype(ref.dtype)
 
 
+def back_core_kernel(pos, taps, near, far, slope, w, pad, act, grad_b, to_core, total):
+    back_kernel(pos, taps, near, far, slope, pad, act, grad_b, total)
+    core_kernel(pos, act, w, to_core)
+
+
 def share(pos, act, w, chip_xor, core):
     ncols, half = act.shape[1:]
     n = act.shape[0] // 8
@@ -308,12 +313,12 @@
 
 
 def chip_send_kernel(pos, act, w, other, out):
-    for i, k in enumerate((2 - pos[3], 3)):
+    for i, k in enumerate((1 + pos[3], 3)):
         out[i] = (share(pos, act, w, k, pos[3]) + other[k].astype(F32)).astype(BF)
 
 
 def chip_keep_kernel(pos, act, w, other, out):
-    for i, k in enumerate((0, 1 + pos[3])):
+    for i, k in enumerate((0, 2 - pos[3])):
         out[i] = share(pos, act, w, k, pos[3]) + other[k].astype(F32)
 
 
@@ -467,10 +472,14 @@
     small = kernel(taps_kernel, "taps", array(tail, half, dtype=F32), (pos, hidden, grad_pre), **vpu)
     four = groups == 4
     w2_halves = halved(w2_chunks) if four else w2_chunks[:1]
-    _, grad_act, grad_b1 = kernel(
-        back_kernel, "back", (padded, full, array(1, half, dtype=F32)), (pos, taps, gp_near, gp_far, slope_one),
-        [pltpu.VMEM((8, LANES), F32)], after=(small, *w2_halves), into=(grad_pre,), **vpu,
-    )
+    block = (own_rows, ncols, cin)
+    two = (2, *block)
+    _, grad_act, grad_b1, to_core = kernel(
+        back_core_kernel, "back", (padded, full, array(1, half, dtype=F32), array(4, *block)),
+        (pos, taps, gp_near, gp_far, slope_one, w1), [pltpu.VMEM((8, LANES), F32)],
+        after=(small, *w2_halves), into=(grad_pre,), **vpu,
+    )
+    from_core = hop(to_core, 0, 1)
     if four:
         w2_sent = hop(tied(w2_halves[1], small).astype(BF), 2 * (3 - FIRST), 0).astype(F32)
         w2_chunk = (tied(w2_halves[0], grad_act) + w2_sent).astype(BF)
@@ -478,13 +487,9 @@
         w2_chunk = summed(tied(w2_chunks[0], grad_act), w2_chunks[1:])
     w2_two = jnp.stack([w2_chunk, hop(w2_chunk, 4, 0)]) if four else None
 
-    block = (own_rows, ncols, cin)
-    two = (2, *block)
-    to_core = kernel(core_kernel, "core", array(4, *block), (pos, grad_act, w1), after=(w2_chunk,), **mm)
-    from_core = hop(to_core, 0, 1)
     w1_own, *w1_sends = kernel(
         w1_kernel, "w1", chunk_outs((cin + tail) // groups, half), (pos, grad_act, small, grad_b1, *in_pieces),
-        [pltpu.VMEM((cin + tail, half), F32)], after=(w2_chunk, to_core), **mm,
+        [pltpu.VMEM((cin + tail, half), F32)], after=(w2_chunk,), **long,
     )
     going = kernel(
         chip_send_kernel, "chip_send", array(*two), (pos, grad_act, w1, from_core), after=(w1_own,), **mm
@@ -494,7 +499,7 @@
         w2_blocks = [w2_two[0], w2_far[0], w2_two[1], w2_far[1]]
     else:
         w2_blocks = [hop(w2_chunk, 2 * k, 0) if k else w2_chunk for k in range(groups)]
-    arrived = cross(going, 0)
+    arrived = cross(going, 1)
     kept = kernel(chip_keep_kernel, "chip_keep", array(*two, dtype=F32), (pos, grad_act, w1, from_core), after=(going,), **mm)
     w1_parts = [hop(send, 2 * (k + 1), 0) for k, send in enumerate(w1_sends)]
     w1_chunk = kernel(sum_kernel, "sum", array(*w1_own.shape), (pos, w1_own, *w1_parts), after=(kept,), **long)
@@ -507,7 +512,7 @@
     forward = kernel(
         forward_kernel, "forward", array(*block), (pos, kept, arrived), after=(w1_side,), **mm
     )
-    onward = cross(forward, 1)
+    onward = cross(forward, 0)
     w1_side = kernel(copy_kernel, "side", array(*w1_side.shape), (pos, w1_side), after=(w1_near[-1],), **long)
     w1_blocks = w1_near + [hop(w1_side, 2 * k, 0) if k else w1_side for k in range(groups)]
     line = array(1, hslice, dtype=F32)

time: 87.9 us -> 87.7 us (level)
    pallas_call x21 -> x20, Pallas kernels: 33.9 us -> 33.5 us  [kernel(): pl.pallas_call(run, out_shape=out, in_specs=[SMEM] + [VMEM] * (len(args)...]
  transfers between devices with their start and end apart: 34 -> 34, of which waited for: 6 -> 3; matrix products, arithmetic and copies ran while one was open for 0% -> 0% of each run, Pallas kernels for 34% -> 35%
where the time goes in v7:
time: 87.7 us; the launch traced here: 87.3 us
  starting transfers between devices  39.3 us (45%)
  Pallas kernels  33.5 us (38%)
  waiting for transfers between devices  7.98 us (9%)
  local copies, waits for them, and re-layouts  5.24 us (6%)
  between operations  1 us (1%)
    pallas_call x20, Pallas kernels, kernel(): pl.pallas_call(run, out_shape=out, in_specs=[SMEM] + [VMEM] * (len(args)...  33.5 us
    ppermute x27, starting transfers between devices, hop(): return lax.ppermute(value, AXES, pairs)  31.8 us
    ppermute x27, waiting for transfers between devices, hop(): return lax.ppermute(value, AXES, pairs)  7.96 us
    unnamed x12, local copies, waits for them, and re-layouts  5.23 us
    ppermute x4, starting transfers between devices, meet(): return lax.ppermute(value, AXES, pairs)  4.85 us
    ppermute x3, starting transfers between devices, cross(): return lax.ppermute(value, AXES, pairs)  2.69 us
  transfers between devices with their start and end apart: 34, of which 3 were waited for; matrix products, arithmetic and copies ran while one was open for 0% of the time, Pallas kernels for 35%

profile of v7, /device:TPU:0, one launch (start us, length us, event | category | flops | bytes accessed | tf_op | source)
XLA Modules:
  0.0 87.3 jit_solution(3651887521830293320)
XLA Ops:
  1.1 2.6 %collective-permute-start.1 = (bf16[2,128,512]{2,1,0:T(8,128)(2,1)}, bf16[2,128,512]{2,1,0:T(8,128)(2,1)S(1)}, u32[]{:S(2)}, u32[]{:S(2)}) collective-permute-start(bf16[2,128,512]{2,1,0:T(8,128)(2,1)} %refs_6_.1), channel_id=1, source_target_pairs={{0,2},{1,3},{2,0},{3,1},{4,6},{5,7},{6,4},{7,5},{8,10},{9,11},{10,... | collective-permute-start | bytes 786440 | tf_op jit(solution)/shard_map/ppermute | solution.py:57
  3.7 1.5 %collective-permute-start.2 = (bf16[2,128,512]{2,1,0:T(8,128)(2,1)}, bf16[2,128,512]{2,1,0:T(8,128)(2,1)S(1)}, u32[]{:S(2)}, u32[]{:S(2)}) collective-permute-start(bf16[2,128,512]{2,1,0:T(8,128)(2,1)} %refs_6_.1), channel_id=1, source_target_pairs={{0,4},{1,5},{2,6},{3,7},{4,0},{5,1},{6,2},{7,3},{8,12},{9,13},{10,... | collective-permute-start | bytes 786440 | tf_op jit(solution)/shard_map/ppermute | solution.py:57
  5.4 1.0 %copy-done = bf16[512,512]{1,0:T(8,128)(2,1)S(1)} copy-done((bf16[512,512]{1,0:T(8,128)(2,1)S(1)}, bf16[512,512]{1,0:T(8,128)(2,1)}, u32[]{:S(2)}) %copy-start) | copy-done | bytes 524312
  6.5 1.0 %copy-done.1 = bf16[512,512]{1,0:T(8,128)(2,1)S(1)} copy-done((bf16[512,512]{1,0:T(8,128)(2,1)S(1)}, bf16[512,512]{1,0:T(8,128)(2,1)}, u32[]{:S(2)}) %copy-start.1) | copy-done | bytes 524312
  7.5 0.9 %copy-done.2 = bf16[2,128,512]{2,1,0:T(8,128)(2,1)S(1)} copy-done((bf16[2,128,512]{2,1,0:T(8,128)(2,1)S(1)}, bf16[2,128,512]{2,1,0:T(8,128)(2,1)}, u32[]{:S(2)}) %copy-start.2) | copy-done | bytes 262168
  8.5 0.8 copy-done.3
  9.3 0.7 copy-done.4
  10.0 0.7 copy-done.5
  10.7 1.1 %prepare.1 = (bf16[512,256]{1,0:T(8,128)(2,1)S(1)}, f32[1,256]{1,0:T(1,128)S(1)}, f32[25,256]{1,0:T(8,128)S(1)}, f32[1,256]{1,0:T(1,128)S(1)}, bf16[256,512]{1,0...) custom-call(s32[4]{0:T(128)S(1)} %pad_add_fusion.refs_0_, ...), custom_call_target="tpu_custom_call" | custom-call | tf_op jit(solution)/shard_map/prepare/pallas_call | solution.py:31
  11.8 1.3 %collective-permute-done.2.refs_4_.refs_8_ = bf16[2,128,512]{2,1,0:T(8,128)(2,1)S(1)} collective-permute-done((bf16[2,128,512]{2,1,0:T(8,128)(2,1)}, bf16[2,128,512]{2,1,0:T(8,128)(2,1)S(1)}, u32[]{:S(2)}, u32[]{:S(2)}) %collective-permute-start.2) | collective-permute-done | bytes 262176 | tf_op jit(solution)/shard_map/ppermute | solution.py:57
  13.1 1.5 %collective-permute-start.10 = (bf16[2,2,128,512]{3,2,1,0:T(8,128)(2,1)S(1)}, bf16[2,2,128,512]{3,2,1,0:T(8,128)(2,1)S(1)}, u32[]{:S(2)}, u32[]{:S(2)}) collective-permute-start(bf16[2,2,128,512]{3,2,1,0:T(8,128)(2,1)S(1)} %pad_maximum_fusion), channel_id=1, source_target_pairs={{0,4},{1,3},{2,6},{3,1},{4,0},{5,7},{6,2},{7,5},{8,12},{9,11},{10,... | collective-permute-start | bytes 1572872 | tf_op jit(solution)/shard_map/ppermute | solution.py:67
  14.6 1.4 %expand0.1 = (f32[2,20,144,128]{3,2,1,0:T(8,128)S(1)}, bf16[16,128,256]{2,1,0:T(8,128)(2,1)S(1)}) custom-call(s32[4]{0:T(128)S(1)} %pad_add_fusion.refs_0_, bf16[512,256]{1,0:T(8,128)(2,1)S(1)} %get-tuple-element.64.refs_1_.refs_5_.refs_2_, f32[1,256]{1,0:T(1,128)S(1)} %get-tuple-element.65.refs_2_, ...), custom_call_target="tpu_custom_call", output_to_operand_aliasing={{0}: (6, {})} | custom-call | flops 1024 | bytes 1024 | tf_op jit(solution)/shard_map/expand0/pallas_call | solution.py:31
  16.6 1.4 %expand2.1 = (f32[2,20,144,128]{3,2,1,0:T(8,128)S(1)}, bf16[16,128,256]{2,1,0:T(8,128)(2,1)S(1)}) custom-call(s32[4]{0:T(128)S(1)} %pad_add_fusion.refs_0_, bf16[512,256]{1,0:T(8,128)(2,1)S(1)} %get-tuple-element.64.refs_1_.refs_5_.refs_2_, f32[1,256]{1,0:T(1,128)S(1)} %get-tuple-element.65.refs_2_, ...), custom_call_target="tpu_custom_call", output_to_operand_aliasing={{0}: (5, {}), {1}: (6, {})} | custom-call | flops 1024 | bytes 1024 | tf_op jit(solution)/shard_map/expand2/pallas_call | solution.py:31
  18.1 2.3 %collective-permute-start.12 = (bf16[2,128,512]{2,1,0:T(8,128)(2,1)}, bf16[2,128,512]{2,1,0:T(8,128)(2,1)S(1)}, u32[]{:S(2)}, u32[]{:S(2)}) collective-permute-start(bf16[2,128,512]{2,1,0:T(8,128)(2,1)} %refs_7_.1), channel_id=1, source_target_pairs={{0,6},{1,7},{2,4},{3,5},{4,2},{5,3},{6,0},{7,1},{8,14},{9,15},{10,... | collective-permute-start | bytes 786440 | tf_op jit(solution)/shard_map/ppermute | solution.py:57
  20.5 1.8 %expand6.1 = (f32[2,20,144,128]{3,2,1,0:T(8,128)S(1)}, bf16[16,128,256]{2,1,0:T(8,128)(2,1)S(1)}) custom-call(s32[4]{0:T(128)S(1)} %pad_add_fusion.refs_0_, bf16[512,256]{1,0:T(8,128)(2,1)S(1)} %get-tuple-element.64.refs_1_.refs_5_.refs_2_, f32[1,256]{1,0:T(1,128)S(1)} %get-tuple-element.65.refs_2_, ...), custom_call_target="tpu_custom_call", output_to_operand_aliasing={{0}: (6, {}), {1}: (7, {})} | custom-call | flops 1024 | bytes 1024 | tf_op jit(solution)/shard_map/expand6/pallas_call | solution.py:31
  22.2 0.9 %expand7.1 = (f32[2,20,144,128]{3,2,1,0:T(8,128)S(1)}, bf16[16,128,256]{2,1,0:T(8,128)(2,1)S(1)}, bf16[2,128,256]{2,1,0:T(8,128)(2,1)S(1)}, bf16[2,128,256]{2,1,0:T(8,128)(2,1)S(1)}) custom-call(s32[4]{0:T(128)S(1)} %pad_add_fusion.refs_0_, ...), custom_call_target="tpu_custom_call", output_to_operand_aliasing={{0}: (4, {}), {1}: (5, {})} | custom-call | flops 1024 | bytes 1024 | tf_op jit(solution)/shard_map/expand7/pallas_call | solution.py:31
  23.2 1.6 %collective-permute-start.8 = (bf16[2,128,256]{2,1,0:T(8,128)(2,1)S(1)}, bf16[2,128,256]{2,1,0:T(8,128)(2,1)S(1)}, u32[]{:S(2)}, u32[]{:S(2)}) collective-permute-start(bf16[2,128,256]{2,1,0:T(8,128)(2,1)S(1)} %get-tuple-element.77), channel_id=1, source_target_pairs={{0,8},{1,9},{2,10},{3,11},{4,12},{5,13},{6,14},{7,15},{8,0},{9,1},... | collective-permute-start | bytes 393224 | tf_op jit(solution)/shard_map/ppermute | solution.py:77
  24.8 0.7 collective-permute-start.9
  25.6 4.8 %inner.1 = (bf16[16,128,256]{2,1,0:T(8,128)(2,1)S(1)}, f32[16,128,256]{2,1,0:T(8,128)S(1)}) custom-call(s32[4]{0:T(128)S(1)} %pad_add_fusion.refs_0_, f32[25,256]{1,0:T(8,128)S(1)} %get-tuple-element.61.refs_1_, f32[1,256]{1,0:T(1,128)S(1)} %get-tuple-element.63.refs_2_, f32[2,20,144,128]{3,2,1,0:T(8,128)S(1)} %get-tuple-element.79.refs_3_.refs_7_), custom_call_target="tpu_custom_call" | custom-call | flops 20000000000 | bytes 100000000 | tf_op jit(solution)/shard_map/inner/pallas_call | solution.py:31
  30.4 2.1 %outer.1 = (bf16[16,128,256]{2,1,0:T(8,128)(2,1)S(1)}, f32[16,128,256]{2,1,0:T(8,128)S(1)}, f32[2,20,144,128]{3,2,1,0:T(8,128)S(1)}) custom-call(s32[4]{0:T(128)S(1)} %pad_add_fusion.refs_0_, f32[25,256]{1,0:T(8,128)S(1)} %get-tuple-element.61.refs_1_, ...), custom_call_target="tpu_custom_call", output_to_operand_aliasing={{0}: (5, {}), {1}: (6, {}), {2}: (7, {})} | custom-call | flops 1024 | bytes 1024 | tf_op jit(solution)/shard_map/outer/pallas_call | solution.py:31
  33.1 1.1 %project0.1.refs_8_.refs_6_ = f32[2,20,144,128]{3,2,1,0:T(8,128)S(1)} custom-call(s32[4]{0:T(128)S(1)} %pad_add_fusion.refs_0_, bf16[256,512]{1,0:T(8,128)(2,1)S(1)} %get-tuple-element.62.refs_1_, f32[16,128,256]{2,1,0:T(8,128)S(1)} %get-tuple-element.82.refs_2_, ...), custom_call_target="tpu_custom_call", output_to_operand_aliasing={{}: (7, {})} | custom-call | flops 1024 | bytes 1024 | tf_op jit(solution)/shard_map/project0/pallas_call | solution.py:31
  34.2 1.3 %w2.1 = (f32[64,512]{1,0:T(8,128)S(1)}, bf16[64,512]{1,0:T(8,128)(2,1)S(1)}, bf16[64,512]{1,0:T(8,128)(2,1)S(1)}, bf16[64,512]{1,0:T(8,128)(2,1)S(1)}) custom-call(s32[4]{0:T(128)S(1)} %pad_add_fusion.refs_0_, bf16[16,128,256]{2,1,0:T(8,128)(2,1)S(1)} %get-tuple-element.87.refs_1_, bf16[2,128,512]{2,1,0:T(8,128)(2,1)S(1)} %get-tuple-element.60.refs_3_.refs_2_.refs_1_, ...), custom_call_target="tpu_custom_call" | custom-call | flops 1024 | bytes 1024 | tf_op jit(solution)/shard_map/w2/pallas_call | solution.py:31
  35.6 4.2 %collective-permute-start.16 = (bf16[2,64,512]{2,1,0:T(8,128)(2,1)S(1)}, bf16[2,64,512]{2,1,0:T(8,128)(2,1)S(1)}, u32[]{:S(2)}, u32[]{:S(2)}) collective-permute-start(bf16[2,64,512]{2,1,0:T(8,128)(2,1)S(1)} %pad_maximum_fusion.1), channel_id=1, source_target_pairs={{0,16},{1,17},{2,18},{3,19},{4,20},{5,21},{6,22},{7,23},{8,24},{9,... | collective-permute-start | bytes 393224 | tf_op jit(solution)/shard_map/ppermute | solution.py:57
  39.8 1.0 %project4.1 = (f32[2,20,144,128]{3,2,1,0:T(8,128)S(1)}, bf16[2,128,256]{2,1,0:T(8,128)(2,1)S(1)}, bf16[2,128,256]{2,1,0:T(8,128)(2,1)S(1)}) custom-call(s32[4]{0:T(128)S(1)} %pad_add_fusion.refs_0_, bf16[256,512]{1,0:T(8,128)(2,1)S(1)} %get-tuple-element.62.refs_1_, f32[16,128,256]{2,1,0:T(8,128)S(1)} %get-tuple-element.82.refs_2_, ...), custom_call_target="tpu_custom_call", output_to_operand_aliasing={{0}: (6, {})} | custom-call | flops 1024 | bytes 1024 | tf_op jit(solution)/shard_map/project4/pallas_call | solution.py:31
  40.8 0.7 collective-permute-start.14
  41.5 1.9 %collective-permute-start.15 = (bf16[2,128,256]{2,1,0:T(8,128)(2,1)S(1)}, bf16[2,128,256]{2,1,0:T(8,128)(2,1)S(1)}, u32[]{:S(2)}, u32[]{:S(2)}) collective-permute-start(bf16[2,128,256]{2,1,0:T(8,128)(2,1)S(1)} %get-tuple-element.92), channel_id=1, source_target_pairs={{0,8},{1,9},{2,10},{3,11},{4,12},{5,13},{6,14},{7,15},{8,0},{9,1},... | collective-permute-start | bytes 393224 | tf_op jit(solution)/shard_map/ppermute | solution.py:77
  43.4 4.3 %taps.1.refs_6_.refs_2_ = f32[64,256]{1,0:T(8,128)S(1)} custom-call(s32[4]{0:T(128)S(1)} %pad_add_fusion.refs_0_, f32[2,20,144,128]{3,2,1,0:T(8,128)S(1)} %get-tuple-element.93.refs_1_, f32[2,20,144,128]{3,2,1,0:T(8,128)S(1)} %get-tuple-element.94.refs_2_.refs_9_), custom_call_target="tpu_custom_call" | custom-call | flops 1024 | bytes 1024 | tf_op jit(solution)/shard_map/taps/pallas_call | solution.py:31
  48.0 5.0 %back.1 = (f32[2,20,144,128]{3,2,1,0:T(8,128)S(1)}, bf16[16,128,256]{2,1,0:T(8,128)(2,1)S(1)}, f32[1,256]{1,0:T(1,128)S(1)}, bf16[4,2,128,512]{3,2,1,0:T(8,128)(2,1)S(1)}) custom-call(s32[4]{0:T(128)S(1)} %pad_add_fusion.refs_0_, f32[25,256]{1,0:T(8,128)S(1)} %get-tuple-element.61.refs_1_, ...), custom_call_target="tpu_custom_call", output_to_operand_aliasing={{0}: (9, {})} | custom-call | flops 1024 | bytes 1024 | tf_op jit(solution)/shard_map/back/pallas_call | solution.py:31
  53.1 3.2 %collective-permute-start.25 = (bf16[64,512]{1,0:T(8,128)(2,1)S(1)}, bf16[64,512]{1,0:T(8,128)(2,1)S(1)}, u32[]{:S(2)}, u32[]{:S(2)}) collective-permute-start(bf16[64,512]{1,0:T(8,128)(2,1)S(1)} %add_convert_fusion.refs_12_.refs_1_), channel_id=1, source_target_pairs={{0,16},{1,17},{2,18},{3,19},{4,20},{5,21},{6,22},{7,23},{8,24},{9,... | collective-permute-start | bytes 196616 | tf_op jit(solution)/shard_map/ppermute | solution.py:57
  56.3 1.3 %w1.1 = (f32[144,256]{1,0:T(8,128)S(1)}, bf16[144,256]{1,0:T(8,128)(2,1)S(1)}, bf16[144,256]{1,0:T(8,128)(2,1)S(1)}, bf16[144,256]{1,0:T(8,128)(2,1)S(1)}) custom-call(s32[4]{0:T(128)S(1)} %pad_add_fusion.refs_0_, bf16[16,128,256]{2,1,0:T(8,128)(2,1)S(1)} %get-tuple-element.98.refs_1_, f32[64,256]{1,0:T(8,128)S(1)} %taps.1.refs_6_.refs_2_, ...), custom_call_target="tpu_custom_call" | custom-call | flops 20000000000 | bytes 100000000 | tf_op jit(solution)/shard_map/w1/pallas_call | solution.py:31
  57.7 1.1 %collective-permute-start.20 = (bf16[144,256]{1,0:T(8,128)(2,1)S(1)}, bf16[144,256]{1,0:T(8,128)(2,1)S(1)}, u32[]{:S(2)}, u32[]{:S(2)}) collective-permute-start(bf16[144,256]{1,0:T(8,128)(2,1)S(1)} %get-tuple-element.104), channel_id=1, source_target_pairs={{0,8},{1,9},{2,10},{3,11},{4,12},{5,13},{6,14},{7,15},{8,0},{9,1},... | collective-permute-start | bytes 221192 | tf_op jit(solution)/shard_map/ppermute | solution.py:57
  59.3 2.8 %collective-permute-start.22 = (bf16[144,256]{1,0:T(8,128)(2,1)S(1)}, bf16[144,256]{1,0:T(8,128)(2,1)S(1)}, u32[]{:S(2)}, u32[]{:S(2)}) collective-permute-start(bf16[144,256]{1,0:T(8,128)(2,1)S(1)} %get-tuple-element.106), channel_id=1, source_target_pairs={{0,24},{1,25},{2,26},{3,27},{4,28},{5,29},{6,30},{7,31},{8,16},{9,... | collective-permute-start | bytes 221192 | tf_op jit(solution)/shard_map/ppermute | solution.py:57
  62.1 0.9 chip_send.1.refs_4_
  63.0 0.6 collective-permute-start.19
  63.8 0.9 chip_keep.1.refs_5_.refs_1_.refs_2_
  64.7 2.8 %collective-permute-done.21.refs_3_ = bf16[144,256]{1,0:T(8,128)(2,1)S(1)} collective-permute-done((bf16[144,256]{1,0:T(8,128)(2,1)S(1)}, bf16[144,256]{1,0:T(8,128)(2,1)S(1)}, u32[]{:S(2)}, u32[]{:S(2)}) %collective-permute-start.21) | collective-permute-done | bytes 73760 | tf_op jit(solution)/shard_map/ppermute | solution.py:57
  67.4 0.6 sum.1.refs_5_.refs_7_
  68.0 0.6 collective-permute-start.23
  68.6 1.4 %collective-permute-start.30 = (bf16[144,256]{1,0:T(8,128)(2,1)S(1)}, bf16[144,256]{1,0:T(8,128)(2,1)S(1)}, u32[]{:S(2)}, u32[]{:S(2)}) collective-permute-start(bf16[144,256]{1,0:T(8,128)(2,1)S(1)} %sum.1.refs_5_.refs_7_), channel_id=1, source_target_pairs={{0,24},{1,25},{2,26},{3,27},{4,28},{5,29},{6,30},{7,31},{8,16},{9,... | collective-permute-start | bytes 221192 | tf_op jit(solution)/shard_map/ppermute | solution.py:57
  70.0 0.9 collective-permute-start.28
  70.9 2.2 %collective-permute-start.29 = (bf16[144,256]{1,0:T(8,128)(2,1)S(1)}, bf16[144,256]{1,0:T(8,128)(2,1)S(1)}, u32[]{:S(2)}, u32[]{:S(2)}) collective-permute-start(bf16[144,256]{1,0:T(8,128)(2,1)S(1)} %sum.1.refs_5_.refs_7_), channel_id=1, source_target_pairs={{0,16},{1,17},{2,18},{3,19},{4,20},{5,21},{6,22},{7,23},{8,24},{9,... | collective-permute-start | bytes 221192 | tf_op jit(solution)/shard_map/ppermute | solution.py:57
  73.6 1.5 %collective-permute-start.27 = (bf16[4,64,512]{2,1,0:T(8,128)(2,1)S(1)}, bf16[4,64,512]{2,1,0:T(8,128)(2,1)S(1)}, u32[]{:S(2)}, u32[]{:S(2)}) collective-permute-start(bf16[4,64,512]{2,1,0:T(8,128)(2,1)S(1)} %column.1.refs_5_), channel_id=1, source_target_pairs={{0,4},{1,5},{2,6},{3,7},{4,0},{5,1},{6,2},{7,3},{8,12},{9,13},{10,... | collective-permute-start | bytes 786440 | tf_op jit(solution)/shard_map/ppermute | solution.py:57
  75.2 0.6 forward.1
  75.8 0.6 collective-permute-start.24
  76.9 1.5 %collective-permute-start.31 = (bf16[144,256]{1,0:T(8,128)(2,1)S(1)}, bf16[144,256]{1,0:T(8,128)(2,1)S(1)}, u32[]{:S(2)}, u32[]{:S(2)}) collective-permute-start(bf16[144,256]{1,0:T(8,128)(2,1)S(1)} %side.1.refs_11_), channel_id=1, source_target_pairs={{0,8},{1,9},{2,10},{3,11},{4,12},{5,13},{6,14},{7,15},{8,0},{9,1},... | collective-permute-start | bytes 221192 | tf_op jit(solution)/shard_map/ppermute | solution.py:57
  79.0 2.4 %collective-permute-start.33 = (bf16[144,256]{1,0:T(8,128)(2,1)S(1)}, bf16[144,256]{1,0:T(8,128)(2,1)S(1)}, u32[]{:S(2)}, u32[]{:S(2)}) collective-permute-start(bf16[144,256]{1,0:T(8,128)(2,1)S(1)} %side.1.refs_11_), channel_id=1, source_target_pairs={{0,24},{1,25},{2,26},{3,27},{4,28},{5,29},{6,30},{7,31},{8,16},{9,... | collective-permute-start | bytes 221192 | tf_op jit(solution)/shard_map/ppermute | solution.py:57
  81.4 3.8 %collective-permute-done.32.refs_13_ = bf16[144,256]{1,0:T(8,128)(2,1)S(1)} collective-permute-done((bf16[144,256]{1,0:T(8,128)(2,1)S(1)}, bf16[144,256]{1,0:T(8,128)(2,1)S(1)}, u32[]{:S(2)}, u32[]{:S(2)}) %collective-permute-start.32) | collective-permute-done | bytes 73760 | tf_op jit(solution)/shard_map/ppermute | solution.py:57
  85.3 2.1 %last.1 = (bf16[2,128,512]{2,1,0:T(8,128)(2,1)}, f32[512,512]{1,0:T(8,128)}, f32[512,512]{1,0:T(8,128)}, f32[25,512]{1,0:T(8,128)}, f32[1,512]{1,0:T(1,128)}, /*index=5*/f32[1,512]{1,0:T(1,128)}) custom-call(s32[4]{0:T(128)S(1)} %pad_add_fusion.refs_0_, bf16[2,128,512]{2,1,0:T(8,128)(2,1)S(1)} %get-tuple-element.60.refs_3_.refs_2_.refs_1_, ...), custom_call_target="tpu_custom_call" | custom-call | tf_op jit(solution)/shard_map/last/pallas_call | solution.py:31
  (61 shorter events, 5.1 us)
Async XLA Ops:
  0.6 11.1 %collective-permute-start.4 = (bf16[2,128,512]{2,1,0:T(8,128)(2,1)}, bf16[2,128,512]{2,1,0:T(8,128)(2,1)S(1)}, u32[]{:S(2)}, u32[]{:S(2)}) collective-permute-start(bf16[2,128,512]{2,1,0:T(8,128)(2,1)} %refs_7_.1), channel_id=1, source_target_pairs={{0,1},{1,0},{2,3},{3,2},{4,5},{5,4},{6,7},{7,6},{8,9},{9,8},{10,11... | collective-permute-start | bytes 786440 | tf_op jit(solution)/shard_map/ppermute | solution.py:57
  1.1 10.7 %collective-permute-start.1 = (bf16[2,128,512]{2,1,0:T(8,128)(2,1)}, bf16[2,128,512]{2,1,0:T(8,128)(2,1)S(1)}, u32[]{:S(2)}, u32[]{:S(2)}) collective-permute-start(bf16[2,128,512]{2,1,0:T(8,128)(2,1)} %refs_6_.1), channel_id=1, source_target_pairs={{0,2},{1,3},{2,0},{3,1},{4,6},{5,7},{6,4},{7,5},{8,10},{9,11},{10,... | collective-permute-start | bytes 786440 | tf_op jit(solution)/shard_map/ppermute | solution.py:57
  3.7 9.4 %collective-permute-start.2 = (bf16[2,128,512]{2,1,0:T(8,128)(2,1)}, bf16[2,128,512]{2,1,0:T(8,128)(2,1)S(1)}, u32[]{:S(2)}, u32[]{:S(2)}) collective-permute-start(bf16[2,128,512]{2,1,0:T(8,128)(2,1)} %refs_6_.1), channel_id=1, source_target_pairs={{0,4},{1,5},{2,6},{3,7},{4,0},{5,1},{6,2},{7,3},{8,12},{9,13},{10,... | collective-permute-start | bytes 786440 | tf_op jit(solution)/shard_map/ppermute | solution.py:57
  5.2 9.4 %collective-permute-start.3 = (bf16[2,128,512]{2,1,0:T(8,128)(2,1)}, bf16[2,128,512]{2,1,0:T(8,128)(2,1)S(1)}, u32[]{:S(2)}, u32[]{:S(2)}) collective-permute-start(bf16[2,128,512]{2,1,0:T(8,128)(2,1)} %refs_6_.1), channel_id=1, source_target_pairs={{0,1},{1,0},{2,3},{3,2},{4,5},{5,4},{6,7},{7,6},{8,9},{9,8},{10,11... | collective-permute-start | bytes 786440 | tf_op jit(solution)/shard_map/ppermute | solution.py:57
  5.2 12.7 %collective-permute-start = (bf16[2,128,512]{2,1,0:T(8,128)(2,1)}, bf16[2,128,512]{2,1,0:T(8,128)(2,1)S(1)}, u32[]{:S(2)}, u32[]{:S(2)}) collective-permute-start(bf16[2,128,512]{2,1,0:T(8,128)(2,1)} %refs_6_.1), channel_id=1, source_target_pairs={{0,6},{1,7},{2,4},{3,5},{4,2},{5,3},{6,0},{7,1},{8,14},{9,15},{10,... | collective-permute-start | bytes 786440 | tf_op jit(solution)/shard_map/ppermute | solution.py:57
  5.4 1.0 %copy-start = (bf16[512,512]{1,0:T(8,128)(2,1)S(1)}, bf16[512,512]{1,0:T(8,128)(2,1)}, u32[]{:S(2)}) copy-start(bf16[512,512]{1,0:T(8,128)(2,1)} %refs_1_.1) | copy-start | bytes 1572868
  6.5 1.0 %copy-start.1 = (bf16[512,512]{1,0:T(8,128)(2,1)S(1)}, bf16[512,512]{1,0:T(8,128)(2,1)}, u32[]{:S(2)}) copy-start(bf16[512,512]{1,0:T(8,128)(2,1)} %refs_5_.1) | copy-start | bytes 1572868
  7.5 0.9 %copy-start.2 = (bf16[2,128,512]{2,1,0:T(8,128)(2,1)S(1)}, bf16[2,128,512]{2,1,0:T(8,128)(2,1)}, u32[]{:S(2)}) copy-start(bf16[2,128,512]{2,1,0:T(8,128)(2,1)} %refs_6_.1) | copy-start | bytes 786436
  8.5 0.8 copy-start.3
  9.3 0.7 copy-start.4
  10.0 0.7 copy-start.5
  13.1 12.4 %collective-permute-start.10 = (bf16[2,2,128,512]{3,2,1,0:T(8,128)(2,1)S(1)}, bf16[2,2,128,512]{3,2,1,0:T(8,128)(2,1)S(1)}, u32[]{:S(2)}, u32[]{:S(2)}) collective-permute-start(bf16[2,2,128,512]{3,2,1,0:T(8,128)(2,1)S(1)} %pad_maximum_fusion), channel_id=1, source_target_pairs={{0,4},{1,3},{2,6},{3,1},{4,0},{5,7},{6,2},{7,5},{8,12},{9,11},{10,... | collective-permute-start | bytes 1572872 | tf_op jit(solution)/shard_map/ppermute | solution.py:67
  16.0 4.4 %collective-permute-start.6 = (bf16[2,128,512]{2,1,0:T(8,128)(2,1)S(1)}, bf16[2,128,512]{2,1,0:T(8,128)(2,1)S(1)}, u32[]{:S(2)}, u32[]{:S(2)}) collective-permute-start(bf16[2,128,512]{2,1,0:T(8,128)(2,1)S(1)} %collective-permute-done.1.refs_3_.refs_6_), channel_id=1, source_target_pairs={{0,1},{1,0},{2,3},{3,2},{4,5},{5,4},{6,7},{7,6},{8,9},{9,8},{10,11... | collective-permute-start | bytes 786440 | tf_op jit(solution)/shard_map/ppermute | solution.py:57
  16.1 4.4 %collective-permute-start.7 = (bf16[2,128,512]{2,1,0:T(8,128)(2,1)S(1)}, bf16[2,128,512]{2,1,0:T(8,128)(2,1)S(1)}, u32[]{:S(2)}, u32[]{:S(2)}) collective-permute-start(bf16[2,128,512]{2,1,0:T(8,128)(2,1)S(1)} %collective-permute-done.2.refs_4_.refs_8_), channel_id=1, source_target_pairs={{0,1},{1,0},{2,3},{3,2},{4,5},{5,4},{6,7},{7,6},{8,9},{9,8},{10,11... | collective-permute-start | bytes 786440 | tf_op jit(solution)/shard_map/ppermute | solution.py:57
  18.0 4.2 %collective-permute-start.5 = (bf16[2,128,512]{2,1,0:T(8,128)(2,1)S(1)}, bf16[2,128,512]{2,1,0:T(8,128)(2,1)S(1)}, u32[]{:S(2)}, u32[]{:S(2)}) collective-permute-start(bf16[2,128,512]{2,1,0:T(8,128)(2,1)S(1)} %collective-permute-done.refs_3_.refs_10_), channel_id=1, source_target_pairs={{0,1},{1,0},{2,3},{3,2},{4,5},{5,4},{6,7},{7,6},{8,9},{9,8},{10,11... | collective-permute-start | bytes 786440 | tf_op jit(solution)/shard_map/ppermute | solution.py:57
  18.1 14.4 %collective-permute-start.12 = (bf16[2,128,512]{2,1,0:T(8,128)(2,1)}, bf16[2,128,512]{2,1,0:T(8,128)(2,1)S(1)}, u32[]{:S(2)}, u32[]{:S(2)}) collective-permute-start(bf16[2,128,512]{2,1,0:T(8,128)(2,1)} %refs_7_.1), channel_id=1, source_target_pairs={{0,6},{1,7},{2,4},{3,5},{4,2},{5,3},{6,0},{7,1},{8,14},{9,15},{10,... | collective-permute-start | bytes 786440 | tf_op jit(solution)/shard_map/ppermute | solution.py:57
  23.2 7.2 %collective-permute-start.8 = (bf16[2,128,256]{2,1,0:T(8,128)(2,1)S(1)}, bf16[2,128,256]{2,1,0:T(8,128)(2,1)S(1)}, u32[]{:S(2)}, u32[]{:S(2)}) collective-permute-start(bf16[2,128,256]{2,1,0:T(8,128)(2,1)S(1)} %get-tuple-element.77), channel_id=1, source_target_pairs={{0,8},{1,9},{2,10},{3,11},{4,12},{5,13},{6,14},{7,15},{8,0},{9,1},... | collective-permute-start | bytes 393224 | tf_op jit(solution)/shard_map/ppermute | solution.py:77
  24.8 5.5 %collective-permute-start.9 = (bf16[2,128,256]{2,1,0:T(8,128)(2,1)S(1)}, bf16[2,128,256]{2,1,0:T(8,128)(2,1)S(1)}, u32[]{:S(2)}, u32[]{:S(2)}) collective-permute-start(bf16[2,128,256]{2,1,0:T(8,128)(2,1)S(1)} %get-tuple-element.78), channel_id=1, source_target_pairs={{8,16},{9,17},{10,18},{11,19},{12,20},{13,21},{14,22},{15,23},{16,... | collective-permute-start | bytes 393224 | tf_op jit(solution)/shard_map/ppermute | solution.py:77
  25.5 8.7 %collective-permute-start.11 = (bf16[2,2,128,512]{3,2,1,0:T(8,128)(2,1)S(1)}, bf16[2,2,128,512]{3,2,1,0:T(8,128)(2,1)S(1)}, u32[]{:S(2)}, u32[]{:S(2)}) collective-permute-start(bf16[2,2,128,512]{3,2,1,0:T(8,128)(2,1)S(1)} %collective-permute-done.10.refs_5_.refs_4_), channel_id=1, source_target_pairs={{0,1},{1,0},{2,3},{3,2},{4,5},{5,4},{6,7},{7,6},{8,9},{9,8},{10,11... | collective-permute-start | bytes 1572872 | tf_op jit(solution)/shard_map/ppermute | solution.py:57
  32.5 1.7 %collective-permute-start.13 = (bf16[2,128,512]{2,1,0:T(8,128)(2,1)S(1)}, bf16[2,128,512]{2,1,0:T(8,128)(2,1)S(1)}, u32[]{:S(2)}, u32[]{:S(2)}) collective-permute-start(bf16[2,128,512]{2,1,0:T(8,128)(2,1)S(1)} %collective-permute-done.12.refs_6_.refs_5_), channel_id=1, source_target_pairs={{0,1},{1,0},{2,3},{3,2},{4,5},{5,4},{6,7},{7,6},{8,9},{9,8},{10,11... | collective-permute-start | bytes 786440 | tf_op jit(solution)/shard_map/ppermute | solution.py:57
  35.6 12.1 %collective-permute-start.16 = (bf16[2,64,512]{2,1,0:T(8,128)(2,1)S(1)}, bf16[2,64,512]{2,1,0:T(8,128)(2,1)S(1)}, u32[]{:S(2)}, u32[]{:S(2)}) collective-permute-start(bf16[2,64,512]{2,1,0:T(8,128)(2,1)S(1)} %pad_maximum_fusion.1), channel_id=1, source_target_pairs={{0,16},{1,17},{2,18},{3,19},{4,20},{5,21},{6,22},{7,23},{8,24},{9,... | collective-permute-start | bytes 393224 | tf_op jit(solution)/shard_map/ppermute | solution.py:57
  40.8 7.2 %collective-permute-start.14 = (bf16[2,128,256]{2,1,0:T(8,128)(2,1)S(1)}, bf16[2,128,256]{2,1,0:T(8,128)(2,1)S(1)}, u32[]{:S(2)}, u32[]{:S(2)}) collective-permute-start(bf16[2,128,256]{2,1,0:T(8,128)(2,1)S(1)} %get-tuple-element.91), channel_id=1, source_target_pairs={{8,16},{9,17},{10,18},{11,19},{12,20},{13,21},{14,22},{15,23},{16,... | collective-permute-start | bytes 393224 | tf_op jit(solution)/shard_map/ppermute | solution.py:77
  41.5 6.6 %collective-permute-start.15 = (bf16[2,128,256]{2,1,0:T(8,128)(2,1)S(1)}, bf16[2,128,256]{2,1,0:T(8,128)(2,1)S(1)}, u32[]{:S(2)}, u32[]{:S(2)}) collective-permute-start(bf16[2,128,256]{2,1,0:T(8,128)(2,1)S(1)} %get-tuple-element.92), channel_id=1, source_target_pairs={{0,8},{1,9},{2,10},{3,11},{4,12},{5,13},{6,14},{7,15},{8,0},{9,1},... | collective-permute-start | bytes 393224 | tf_op jit(solution)/shard_map/ppermute | solution.py:77
  47.8 5.3 %collective-permute-start.18 = (bf16[64,512]{1,0:T(8,128)(2,1)S(1)}, bf16[64,512]{1,0:T(8,128)(2,1)S(1)}, u32[]{:S(2)}, u32[]{:S(2)}) collective-permute-start(bf16[64,512]{1,0:T(8,128)(2,1)S(1)} %convert_element_type.17), channel_id=1, source_target_pairs={{0,8},{1,9},{2,10},{3,11},{4,12},{5,13},{6,14},{7,15},{8,0},{9,1},... | collective-permute-start | bytes 196616 | tf_op jit(solution)/shard_map/ppermute | solution.py:57
  53.0 9.1 %collective-permute-start.17 = (bf16[4,2,128,512]{3,2,1,0:T(8,128)(2,1)S(1)}, bf16[4,2,128,512]{3,2,1,0:T(8,128)(2,1)S(1)}, u32[]{:S(2)}, u32[]{:S(2)}) collective-permute-start(bf16[4,2,128,512]{3,2,1,0:T(8,128)(2,1)S(1)} %get-tuple-element.99), channel_id=1, source_target_pairs={{0,1},{1,0},{2,3},{3,2},{4,5},{5,4},{6,7},{7,6},{8,9},{9,8},{10,11... | collective-permute-start | bytes 3145736 | tf_op jit(solution)/shard_map/ppermute | solution.py:57
  53.1 9.0 %collective-permute-start.25 = (bf16[64,512]{1,0:T(8,128)(2,1)S(1)}, bf16[64,512]{1,0:T(8,128)(2,1)S(1)}, u32[]{:S(2)}, u32[]{:S(2)}) collective-permute-start(bf16[64,512]{1,0:T(8,128)(2,1)S(1)} %add_convert_fusion.refs_12_.refs_1_), channel_id=1, source_target_pairs={{0,16},{1,17},{2,18},{3,19},{4,20},{5,21},{6,22},{7,23},{8,24},{9,... | collective-permute-start | bytes 196616 | tf_op jit(solution)/shard_map/ppermute | solution.py:57
  57.7 7.0 %collective-permute-start.20 = (bf16[144,256]{1,0:T(8,128)(2,1)S(1)}, bf16[144,256]{1,0:T(8,128)(2,1)S(1)}, u32[]{:S(2)}, u32[]{:S(2)}) collective-permute-start(bf16[144,256]{1,0:T(8,128)(2,1)S(1)} %get-tuple-element.104), channel_id=1, source_target_pairs={{0,8},{1,9},{2,10},{3,11},{4,12},{5,13},{6,14},{7,15},{8,0},{9,1},... | collective-permute-start | bytes 221192 | tf_op jit(solution)/shard_map/ppermute | solution.py:57
  58.8 8.7 %collective-permute-start.21 = (bf16[144,256]{1,0:T(8,128)(2,1)S(1)}, bf16[144,256]{1,0:T(8,128)(2,1)S(1)}, u32[]{:S(2)}, u32[]{:S(2)}) collective-permute-start(bf16[144,256]{1,0:T(8,128)(2,1)S(1)} %get-tuple-element.105), channel_id=1, source_target_pairs={{0,16},{1,17},{2,18},{3,19},{4,20},{5,21},{6,22},{7,23},{8,24},{9,... | collective-permute-start | bytes 221192 | tf_op jit(solution)/shard_map/ppermute | solution.py:57
  59.3 8.1 %collective-permute-start.22 = (bf16[144,256]{1,0:T(8,128)(2,1)S(1)}, bf16[144,256]{1,0:T(8,128)(2,1)S(1)}, u32[]{:S(2)}, u32[]{:S(2)}) collective-permute-start(bf16[144,256]{1,0:T(8,128)(2,1)S(1)} %get-tuple-element.106), channel_id=1, source_target_pairs={{0,24},{1,25},{2,26},{3,27},{4,28},{5,29},{6,30},{7,31},{8,16},{9,... | collective-permute-start | bytes 221192 | tf_op jit(solution)/shard_map/ppermute | solution.py:57
  63.0 12.2 %collective-permute-start.19 = (bf16[2,2,128,512]{3,2,1,0:T(8,128)(2,1)S(1)}, bf16[2,2,128,512]{3,2,1,0:T(8,128)(2,1)S(1)}, u32[]{:S(2)}, u32[]{:S(2)}) collective-permute-start(bf16[2,2,128,512]{3,2,1,0:T(8,128)(2,1)S(1)} %chip_send.1.refs_4_), channel_id=1, source_target_pairs={{0,2},{1,5},{2,0},{3,7},{4,6},{5,1},{6,4},{7,3},{8,10},{9,13},{10,... | collective-permute-start | bytes 1572872 | tf_op jit(solution)/shard_map/ppermute | solution.py:67
  63.6 7.3 %collective-permute-start.26 = (bf16[2,64,512]{2,1,0:T(8,128)(2,1)S(1)}, bf16[2,64,512]{2,1,0:T(8,128)(2,1)S(1)}, u32[]{:S(2)}, u32[]{:S(2)}) collective-permute-start(bf16[2,64,512]{2,1,0:T(8,128)(2,1)S(1)} %pad_maximum_fusion.2), channel_id=1, source_target_pairs={{0,8},{1,9},{2,10},{3,11},{4,12},{5,13},{6,14},{7,15},{8,0},{9,1},... | collective-permute-start | bytes 393224 | tf_op jit(solution)/shard_map/ppermute | solution.py:57
  68.0 5.6 %collective-permute-start.23 = (bf16[144,256]{1,0:T(8,128)(2,1)S(1)}, bf16[144,256]{1,0:T(8,128)(2,1)S(1)}, u32[]{:S(2)}, u32[]{:S(2)}) collective-permute-start(bf16[144,256]{1,0:T(8,128)(2,1)S(1)} %sum.1.refs_5_.refs_7_), channel_id=1, source_target_pairs={{0,4},{1,5},{2,6},{3,7},{4,0},{5,1},{6,2},{7,3},{8,12},{9,13},{10,... | collective-permute-start | bytes 221192 | tf_op jit(solution)/shard_map/ppermute | solution.py:57
  68.6 7.7 %collective-permute-start.30 = (bf16[144,256]{1,0:T(8,128)(2,1)S(1)}, bf16[144,256]{1,0:T(8,128)(2,1)S(1)}, u32[]{:S(2)}, u32[]{:S(2)}) collective-permute-start(bf16[144,256]{1,0:T(8,128)(2,1)S(1)} %sum.1.refs_5_.refs_7_), channel_id=1, source_target_pairs={{0,24},{1,25},{2,26},{3,27},{4,28},{5,29},{6,30},{7,31},{8,16},{9,... | collective-permute-start | bytes 221192 | tf_op jit(solution)/shard_map/ppermute | solution.py:57
  70.0 8.4 %collective-permute-start.28 = (bf16[144,256]{1,0:T(8,128)(2,1)S(1)}, bf16[144,256]{1,0:T(8,128)(2,1)S(1)}, u32[]{:S(2)}, u32[]{:S(2)}) collective-permute-start(bf16[144,256]{1,0:T(8,128)(2,1)S(1)} %sum.1.refs_5_.refs_7_), channel_id=1, source_target_pairs={{0,8},{1,9},{2,10},{3,11},{4,12},{5,13},{6,14},{7,15},{8,0},{9,1},... | collective-permute-start | bytes 221192 | tf_op jit(solution)/shard_map/ppermute | solution.py:57
  70.9 8.1 %collective-permute-start.29 = (bf16[144,256]{1,0:T(8,128)(2,1)S(1)}, bf16[144,256]{1,0:T(8,128)(2,1)S(1)}, u32[]{:S(2)}, u32[]{:S(2)}) collective-permute-start(bf16[144,256]{1,0:T(8,128)(2,1)S(1)} %sum.1.refs_5_.refs_7_), channel_id=1, source_target_pairs={{0,16},{1,17},{2,18},{3,19},{4,20},{5,21},{6,22},{7,23},{8,24},{9,... | collective-permute-start | bytes 221192 | tf_op jit(solution)/shard_map/ppermute | solution.py:57
  73.6 11.6 %collective-permute-start.27 = (bf16[4,64,512]{2,1,0:T(8,128)(2,1)S(1)}, bf16[4,64,512]{2,1,0:T(8,128)(2,1)S(1)}, u32[]{:S(2)}, u32[]{:S(2)}) collective-permute-start(bf16[4,64,512]{2,1,0:T(8,128)(2,1)S(1)} %column.1.refs_5_), channel_id=1, source_target_pairs={{0,4},{1,5},{2,6},{3,7},{4,0},{5,1},{6,2},{7,3},{8,12},{9,13},{10,... | collective-permute-start | bytes 786440 | tf_op jit(solution)/shard_map/ppermute | solution.py:57
  75.8 9.5 %collective-permute-start.24 = (bf16[2,128,512]{2,1,0:T(8,128)(2,1)S(1)}, bf16[2,128,512]{2,1,0:T(8,128)(2,1)S(1)}, u32[]{:S(2)}, u32[]{:S(2)}) collective-permute-start(bf16[2,128,512]{2,1,0:T(8,128)(2,1)S(1)} %forward.1), channel_id=1, source_target_pairs={{0,4},{1,3},{2,6},{3,1},{4,0},{5,7},{6,2},{7,5},{8,12},{9,11},{10,... | collective-permute-start | bytes 786440 | tf_op jit(solution)/shard_map/ppermute | solution.py:67
  76.9 4.5 %collective-permute-start.31 = (bf16[144,256]{1,0:T(8,128)(2,1)S(1)}, bf16[144,256]{1,0:T(8,128)(2,1)S(1)}, u32[]{:S(2)}, u32[]{:S(2)}) collective-permute-start(bf16[144,256]{1,0:T(8,128)(2,1)S(1)} %side.1.refs_11_), channel_id=1, source_target_pairs={{0,8},{1,9},{2,10},{3,11},{4,12},{5,13},{6,14},{7,15},{8,0},{9,1},... | collective-permute-start | bytes 221192 | tf_op jit(solution)/shard_map/ppermute | solution.py:57
  78.4 6.8 %collective-permute-start.32 = (bf16[144,256]{1,0:T(8,128)(2,1)S(1)}, bf16[144,256]{1,0:T(8,128)(2,1)S(1)}, u32[]{:S(2)}, u32[]{:S(2)}) collective-permute-start(bf16[144,256]{1,0:T(8,128)(2,1)S(1)} %side.1.refs_11_), channel_id=1, source_target_pairs={{0,16},{1,17},{2,18},{3,19},{4,20},{5,21},{6,22},{7,23},{8,24},{9,... | collective-permute-start | bytes 221192 | tf_op jit(solution)/shard_map/ppermute | solution.py:57
  79.0 6.3 %collective-permute-start.33 = (bf16[144,256]{1,0:T(8,128)(2,1)S(1)}, bf16[144,256]{1,0:T(8,128)(2,1)S(1)}, u32[]{:S(2)}, u32[]{:S(2)}) collective-permute-start(bf16[144,256]{1,0:T(8,128)(2,1)S(1)} %side.1.refs_11_), channel_id=1, source_target_pairs={{0,24},{1,25},{2,26},{3,27},{4,28},{5,29},{6,30},{7,31},{8,16},{9,... | collective-permute-start | bytes 221192 | tf_op jit(solution)/shard_map/ppermute | solution.py:57

commit v8 on v7

--- a/solution.py
+++ b/solution.py
@@ -233,6 +233,12 @@
     n = outs[0].shape[0]
     for k, ref in enumerate(outs):
         ref[...] = total[pl.ds(pl.multiple_of((pos[2] ^ k) * n, n), n), :].astype(ref.dtype)
+
+
+def products_kernel(pos, weights, slope, mixed, *refs):
+    pieces, (gp, near, far, *outs) = refs[:6], refs[6:]
+    project_kernel((4, 5), pos, weights, slope, *pieces[4:], gp, near, far)
+    w2_kernel(pos, mixed, *pieces, *outs)
 
 
 def taps_kernel(pos, hid, gp, small):
@@ -462,11 +468,11 @@
         return (array(rows, width, dtype=F32),) + (array(rows, width),) * (groups - 1)
 
     half_done = project((0, 1, 2, 3), (grad_pre,))
-    w2_chunks = kernel(
-        w2_kernel, "w2", chunk_outs(half // groups, cin), (pos, mixed, *cot_pieces),
-        [pltpu.VMEM((half, cin), F32)], after=half_done, **mm,
-    )
-    grad_pre, *sent = project((4, 5), half_done, (w2_chunks[0],), edges)
+    grad_pre, *rest = kernel(
+        products_kernel, "products", (padded,) + edges + chunk_outs(half // groups, cin),
+        (pos, w2, slope_two, mixed, *cot_pieces), [pltpu.VMEM((half, cin), F32)], into=half_done, **mm,
+    )
+    sent, w2_chunks = rest[:2], rest[2:]
     gp_near, gp_far = meet(sent[0], FLIP_GP), meet(sent[1], 1 - FLIP_GP)
     tail = 16 * groups
     small = kernel(taps_kernel, "taps", array(tail, half, dtype=F32), (pos, hidden, grad_pre), **vpu)

time: 87.7 us -> 87.3 us (level)
  Pallas kernels: 33.5 us -> 32.5 us
    pallas_call x20 -> x19, Pallas kernels: 33.5 us -> 32.5 us  [kernel(): pl.pallas_call(run, out_shape=out, in_specs=[SMEM] + [VMEM] * (len(args)...]
  transfers between devices with their start and end apart: 34 -> 34, of which waited for: 3 -> 5; matrix products, arithmetic and copies ran while one was open for 0% -> 0% of each run, Pallas kernels for 35% -> 33%
where the time goes in v8:
time: 87.3 us; the launch traced here: 86.9 us
  starting transfers between devices  40.1 us (46%)
  Pallas kernels  32.5 us (37%)
  waiting for transfers between devices  7.8 us (9%)
  local copies, waits for them, and re-layouts  5.24 us (6%)
  between operations  0.98 us (1%)
    ppermute x27, starting transfers between devices, hop(): return lax.ppermute(value, AXES, pairs)  32.6 us
    pallas_call x19, Pallas kernels, kernel(): pl.pallas_call(run, out_shape=out, in_specs=[SMEM] + [VMEM] * (len(args)...  32.5 us
    ppermute x27, waiting for transfers between devices, hop(): return lax.ppermute(value, AXES, pairs)  7.78 us
    unnamed x12, local copies, waits for them, and re-layouts  5.23 us
    ppermute x4, starting transfers between devices, meet(): return lax.ppermute(value, AXES, pairs)  4.85 us
    ppermute x3, starting transfers between devices, cross(): return lax.ppermute(value, AXES, pairs)  2.67 us
  transfers between devices with their start and end apart: 34, of which 5 were waited for; matrix products, arithmetic and copies ran while one was open for 0% of the time, Pallas kernels for 33%

profile of v8, /device:TPU:0, one launch (start us, length us, event | category | flops | bytes accessed | tf_op | source)
XLA Modules:
  0.0 86.9 jit_solution(8630004843730218208)
XLA Ops:
  1.1 2.6 %collective-permute-start.1 = (bf16[2,128,512]{2,1,0:T(8,128)(2,1)}, bf16[2,128,512]{2,1,0:T(8,128)(2,1)S(1)}, u32[]{:S(2)}, u32[]{:S(2)}) collective-permute-start(bf16[2,128,512]{2,1,0:T(8,128)(2,1)} %refs_6_.1), channel_id=1, source_target_pairs={{0,2},{1,3},{2,0},{3,1},{4,6},{5,7},{6,4},{7,5},{8,10},{9,11},{10,... | collective-permute-start | bytes 786440 | tf_op jit(solution)/shard_map/ppermute | solution.py:57
  3.7 1.5 %collective-permute-start.2 = (bf16[2,128,512]{2,1,0:T(8,128)(2,1)}, bf16[2,128,512]{2,1,0:T(8,128)(2,1)S(1)}, u32[]{:S(2)}, u32[]{:S(2)}) collective-permute-start(bf16[2,128,512]{2,1,0:T(8,128)(2,1)} %refs_6_.1), channel_id=1, source_target_pairs={{0,4},{1,5},{2,6},{3,7},{4,0},{5,1},{6,2},{7,3},{8,12},{9,13},{10,... | collective-permute-start | bytes 786440 | tf_op jit(solution)/shard_map/ppermute | solution.py:57
  5.4 1.0 %copy-done = bf16[512,512]{1,0:T(8,128)(2,1)S(1)} copy-done((bf16[512,512]{1,0:T(8,128)(2,1)S(1)}, bf16[512,512]{1,0:T(8,128)(2,1)}, u32[]{:S(2)}) %copy-start) | copy-done | bytes 524312
  6.5 1.0 %copy-done.1 = bf16[512,512]{1,0:T(8,128)(2,1)S(1)} copy-done((bf16[512,512]{1,0:T(8,128)(2,1)S(1)}, bf16[512,512]{1,0:T(8,128)(2,1)}, u32[]{:S(2)}) %copy-start.1) | copy-done | bytes 524312
  7.5 0.9 %copy-done.2 = bf16[2,128,512]{2,1,0:T(8,128)(2,1)S(1)} copy-done((bf16[2,128,512]{2,1,0:T(8,128)(2,1)S(1)}, bf16[2,128,512]{2,1,0:T(8,128)(2,1)}, u32[]{:S(2)}) %copy-start.2) | copy-done | bytes 262168
  8.5 0.8 copy-done.3
  9.3 0.7 copy-done.4
  10.0 0.7 copy-done.5
  10.7 1.1 %prepare.1 = (bf16[512,256]{1,0:T(8,128)(2,1)S(1)}, f32[1,256]{1,0:T(1,128)S(1)}, f32[25,256]{1,0:T(8,128)S(1)}, f32[1,256]{1,0:T(1,128)S(1)}, bf16[256,512]{1,0...) custom-call(s32[4]{0:T(128)S(1)} %pad_add_fusion.refs_0_, ...), custom_call_target="tpu_custom_call" | custom-call | tf_op jit(solution)/shard_map/prepare/pallas_call | solution.py:31
  11.8 1.3 %collective-permute-done.2.refs_4_.refs_8_ = bf16[2,128,512]{2,1,0:T(8,128)(2,1)S(1)} collective-permute-done((bf16[2,128,512]{2,1,0:T(8,128)(2,1)}, bf16[2,128,512]{2,1,0:T(8,128)(2,1)S(1)}, u32[]{:S(2)}, u32[]{:S(2)}) %collective-permute-start.2) | collective-permute-done | bytes 262176 | tf_op jit(solution)/shard_map/ppermute | solution.py:57
  13.1 1.5 %collective-permute-start.10 = (bf16[2,2,128,512]{3,2,1,0:T(8,128)(2,1)S(1)}, bf16[2,2,128,512]{3,2,1,0:T(8,128)(2,1)S(1)}, u32[]{:S(2)}, u32[]{:S(2)}) collective-permute-start(bf16[2,2,128,512]{3,2,1,0:T(8,128)(2,1)S(1)} %pad_maximum_fusion), channel_id=1, source_target_pairs={{0,4},{1,3},{2,6},{3,1},{4,0},{5,7},{6,2},{7,5},{8,12},{9,11},{10,... | collective-permute-start | bytes 1572872 | tf_op jit(solution)/shard_map/ppermute | solution.py:67
  14.6 1.4 %expand0.1 = (f32[2,20,144,128]{3,2,1,0:T(8,128)S(1)}, bf16[16,128,256]{2,1,0:T(8,128)(2,1)S(1)}) custom-call(s32[4]{0:T(128)S(1)} %pad_add_fusion.refs_0_, bf16[512,256]{1,0:T(8,128)(2,1)S(1)} %get-tuple-element.64.refs_1_.refs_5_.refs_2_, f32[1,256]{1,0:T(1,128)S(1)} %get-tuple-element.65.refs_2_, ...), custom_call_target="tpu_custom_call", output_to_operand_aliasing={{0}: (6, {})} | custom-call | flops 1024 | bytes 1024 | tf_op jit(solution)/shard_map/expand0/pallas_call | solution.py:31
  16.6 1.4 %expand2.1 = (f32[2,20,144,128]{3,2,1,0:T(8,128)S(1)}, bf16[16,128,256]{2,1,0:T(8,128)(2,1)S(1)}) custom-call(s32[4]{0:T(128)S(1)} %pad_add_fusion.refs_0_, bf16[512,256]{1,0:T(8,128)(2,1)S(1)} %get-tuple-element.64.refs_1_.refs_5_.refs_2_, f32[1,256]{1,0:T(1,128)S(1)} %get-tuple-element.65.refs_2_, ...), custom_call_target="tpu_custom_call", output_to_operand_aliasing={{0}: (5, {}), {1}: (6, {})} | custom-call | flops 1024 | bytes 1024 | tf_op jit(solution)/shard_map/expand2/pallas_call | solution.py:31
  18.1 2.3 %collective-permute-start.11 = (bf16[2,128,512]{2,1,0:T(8,128)(2,1)}, bf16[2,128,512]{2,1,0:T(8,128)(2,1)S(1)}, u32[]{:S(2)}, u32[]{:S(2)}) collective-permute-start(bf16[2,128,512]{2,1,0:T(8,128)(2,1)} %refs_7_.1), channel_id=1, source_target_pairs={{0,6},{1,7},{2,4},{3,5},{4,2},{5,3},{6,0},{7,1},{8,14},{9,15},{10,... | collective-permute-start | bytes 786440 | tf_op jit(solution)/shard_map/ppermute | solution.py:57
  20.5 1.8 %expand6.1 = (f32[2,20,144,128]{3,2,1,0:T(8,128)S(1)}, bf16[16,128,256]{2,1,0:T(8,128)(2,1)S(1)}) custom-call(s32[4]{0:T(128)S(1)} %pad_add_fusion.refs_0_, bf16[512,256]{1,0:T(8,128)(2,1)S(1)} %get-tuple-element.64.refs_1_.refs_5_.refs_2_, f32[1,256]{1,0:T(1,128)S(1)} %get-tuple-element.65.refs_2_, ...), custom_call_target="tpu_custom_call", output_to_operand_aliasing={{0}: (6, {}), {1}: (7, {})} | custom-call | flops 1024 | bytes 1024 | tf_op jit(solution)/shard_map/expand6/pallas_call | solution.py:31
  22.2 0.9 %expand7.1 = (f32[2,20,144,128]{3,2,1,0:T(8,128)S(1)}, bf16[16,128,256]{2,1,0:T(8,128)(2,1)S(1)}, bf16[2,128,256]{2,1,0:T(8,128)(2,1)S(1)}, bf16[2,128,256]{2,1,0:T(8,128)(2,1)S(1)}) custom-call(s32[4]{0:T(128)S(1)} %pad_add_fusion.refs_0_, ...), custom_call_target="tpu_custom_call", output_to_operand_aliasing={{0}: (4, {}), {1}: (5, {})} | custom-call | flops 1024 | bytes 1024 | tf_op jit(solution)/shard_map/expand7/pallas_call | solution.py:31
  23.2 1.6 %collective-permute-start.8 = (bf16[2,128,256]{2,1,0:T(8,128)(2,1)S(1)}, bf16[2,128,256]{2,1,0:T(8,128)(2,1)S(1)}, u32[]{:S(2)}, u32[]{:S(2)}) collective-permute-start(bf16[2,128,256]{2,1,0:T(8,128)(2,1)S(1)} %get-tuple-element.77), channel_id=1, source_target_pairs={{0,8},{1,9},{2,10},{3,11},{4,12},{5,13},{6,14},{7,15},{8,0},{9,1},... | collective-permute-start | bytes 393224 | tf_op jit(solution)/shard_map/ppermute | solution.py:77
  24.8 0.7 collective-permute-start.9
  25.6 4.6 %inner.1 = (bf16[16,128,256]{2,1,0:T(8,128)(2,1)S(1)}, f32[16,128,256]{2,1,0:T(8,128)S(1)}) custom-call(s32[4]{0:T(128)S(1)} %pad_add_fusion.refs_0_, f32[25,256]{1,0:T(8,128)S(1)} %get-tuple-element.61.refs_1_, f32[1,256]{1,0:T(1,128)S(1)} %get-tuple-element.63.refs_2_, f32[2,20,144,128]{3,2,1,0:T(8,128)S(1)} %get-tuple-element.79.refs_3_.refs_7_), custom_call_target="tpu_custom_call" | custom-call | flops 20000000000 | bytes 100000000 | tf_op jit(solution)/shard_map/inner/pallas_call | solution.py:31
  30.2 2.0 %outer.1 = (bf16[16,128,256]{2,1,0:T(8,128)(2,1)S(1)}, f32[16,128,256]{2,1,0:T(8,128)S(1)}, f32[2,20,144,128]{3,2,1,0:T(8,128)S(1)}) custom-call(s32[4]{0:T(128)S(1)} %pad_add_fusion.refs_0_, f32[25,256]{1,0:T(8,128)S(1)} %get-tuple-element.61.refs_1_, ...), custom_call_target="tpu_custom_call", output_to_operand_aliasing={{0}: (5, {}), {1}: (6, {}), {2}: (7, {})} | custom-call | flops 1024 | bytes 1024 | tf_op jit(solution)/shard_map/outer/pallas_call | solution.py:31
  32.8 1.1 %project0.1.refs_10_ = f32[2,20,144,128]{3,2,1,0:T(8,128)S(1)} custom-call(s32[4]{0:T(128)S(1)} %pad_add_fusion.refs_0_, bf16[256,512]{1,0:T(8,128)(2,1)S(1)} %get-tuple-element.62.refs_1_, f32[16,128,256]{2,1,0:T(8,128)S(1)} %get-tuple-element.82.refs_2_, ...), custom_call_target="tpu_custom_call", output_to_operand_aliasing={{}: (7, {})} | custom-call | flops 1024 | bytes 1024 | tf_op jit(solution)/shard_map/project0/pallas_call | solution.py:31
  34.0 1.6 %products.1 = (f32[2,20,144,128]{3,2,1,0:T(8,128)S(1)}, bf16[2,128,256]{2,1,0:T(8,128)(2,1)S(1)}, bf16[2,128,256]{2,1,0:T(8,128)(2,1)S(1)}, f32[64,512]{1,0:T(8,...) custom-call(s32[4]{0:T(128)S(1)} %pad_add_fusion.refs_0_, ...), custom_call_target="tpu_custom_call", output_to_operand_aliasing={{0}: (10, {})} | custom-call | flops 1024 | bytes 1024 | tf_op jit(solution)/shard_map/products/pallas_call | solution.py:31
  35.6 4.4 %collective-permute-start.16 = (bf16[2,64,512]{2,1,0:T(8,128)(2,1)S(1)}, bf16[2,64,512]{2,1,0:T(8,128)(2,1)S(1)}, u32[]{:S(2)}, u32[]{:S(2)}) collective-permute-start(bf16[2,64,512]{2,1,0:T(8,128)(2,1)S(1)} %pad_maximum_fusion.1), channel_id=1, source_target_pairs={{0,16},{1,17},{2,18},{3,19},{4,20},{5,21},{6,22},{7,23},{8,24},{9,... | collective-permute-start | bytes 393224 | tf_op jit(solution)/shard_map/ppermute | solution.py:57
  39.9 0.7 collective-permute-start.14
  40.6 1.9 %collective-permute-start.15 = (bf16[2,128,256]{2,1,0:T(8,128)(2,1)S(1)}, bf16[2,128,256]{2,1,0:T(8,128)(2,1)S(1)}, u32[]{:S(2)}, u32[]{:S(2)}) collective-permute-start(bf16[2,128,256]{2,1,0:T(8,128)(2,1)S(1)} %get-tuple-element.91), channel_id=1, source_target_pairs={{0,8},{1,9},{2,10},{3,11},{4,12},{5,13},{6,14},{7,15},{8,0},{9,1},... | collective-permute-start | bytes 393224 | tf_op jit(solution)/shard_map/ppermute | solution.py:77
  42.5 4.3 %taps.1.refs_6_.refs_2_ = f32[64,256]{1,0:T(8,128)S(1)} custom-call(s32[4]{0:T(128)S(1)} %pad_add_fusion.refs_0_, f32[2,20,144,128]{3,2,1,0:T(8,128)S(1)} %get-tuple-element.92.refs_1_, f32[2,20,144,128]{3,2,1,0:T(8,128)S(1)} %get-tuple-element.93.refs_2_.refs_9_), custom_call_target="tpu_custom_call" | custom-call | flops 1024 | bytes 1024 | tf_op jit(solution)/shard_map/taps/pallas_call | solution.py:31
  47.5 4.9 %back.1 = (f32[2,20,144,128]{3,2,1,0:T(8,128)S(1)}, bf16[16,128,256]{2,1,0:T(8,128)(2,1)S(1)}, f32[1,256]{1,0:T(1,128)S(1)}, bf16[4,2,128,512]{3,2,1,0:T(8,128)(2,1)S(1)}) custom-call(s32[4]{0:T(128)S(1)} %pad_add_fusion.refs_0_, f32[25,256]{1,0:T(8,128)S(1)} %get-tuple-element.61.refs_1_, ...), custom_call_target="tpu_custom_call", output_to_operand_aliasing={{0}: (9, {})} | custom-call | flops 1024 | bytes 1024 | tf_op jit(solution)/shard_map/back/pallas_call | solution.py:31
  52.5 3.8 %collective-permute-start.25 = (bf16[64,512]{1,0:T(8,128)(2,1)S(1)}, bf16[64,512]{1,0:T(8,128)(2,1)S(1)}, u32[]{:S(2)}, u32[]{:S(2)}) collective-permute-start(bf16[64,512]{1,0:T(8,128)(2,1)S(1)} %add_convert_fusion.refs_12_.refs_1_), channel_id=1, source_target_pairs={{0,16},{1,17},{2,18},{3,19},{4,20},{5,21},{6,22},{7,23},{8,24},{9,... | collective-permute-start | bytes 196616 | tf_op jit(solution)/shard_map/ppermute | solution.py:57
  56.3 1.3 %w1.1 = (f32[144,256]{1,0:T(8,128)S(1)}, bf16[144,256]{1,0:T(8,128)(2,1)S(1)}, bf16[144,256]{1,0:T(8,128)(2,1)S(1)}, bf16[144,256]{1,0:T(8,128)(2,1)S(1)}) custom-call(s32[4]{0:T(128)S(1)} %pad_add_fusion.refs_0_, bf16[16,128,256]{2,1,0:T(8,128)(2,1)S(1)} %get-tuple-element.98.refs_1_, f32[64,256]{1,0:T(8,128)S(1)} %taps.1.refs_6_.refs_2_, ...), custom_call_target="tpu_custom_call" | custom-call | flops 20000000000 | bytes 100000000 | tf_op jit(solution)/shard_map/w1/pallas_call | solution.py:31
  57.7 1.7 %collective-permute-start.21 = (bf16[144,256]{1,0:T(8,128)(2,1)S(1)}, bf16[144,256]{1,0:T(8,128)(2,1)S(1)}, u32[]{:S(2)}, u32[]{:S(2)}) collective-permute-start(bf16[144,256]{1,0:T(8,128)(2,1)S(1)} %get-tuple-element.105), channel_id=1, source_target_pairs={{0,16},{1,17},{2,18},{3,19},{4,20},{5,21},{6,22},{7,23},{8,24},{9,... | collective-permute-start | bytes 221192 | tf_op jit(solution)/shard_map/ppermute | solution.py:57
  59.4 2.7 %collective-permute-start.22 = (bf16[144,256]{1,0:T(8,128)(2,1)S(1)}, bf16[144,256]{1,0:T(8,128)(2,1)S(1)}, u32[]{:S(2)}, u32[]{:S(2)}) collective-permute-start(bf16[144,256]{1,0:T(8,128)(2,1)S(1)} %get-tuple-element.106), channel_id=1, source_target_pairs={{0,24},{1,25},{2,26},{3,27},{4,28},{5,29},{6,30},{7,31},{8,16},{9,... | collective-permute-start | bytes 221192 | tf_op jit(solution)/shard_map/ppermute | solution.py:57
  62.1 0.9 %chip_send.1.refs_4_ = bf16[2,2,128,512]{3,2,1,0:T(8,128)(2,1)S(1)} custom-call(s32[4]{0:T(128)S(1)} %pad_add_fusion.refs_0_, bf16[16,128,256]{2,1,0:T(8,128)(2,1)S(1)} %get-tuple-element.98.refs_1_, bf16[512,256]{1,0:T(8,128)(2,1)S(1)} %get-tuple-element.64.refs_1_.refs_5_.refs_2_, bf16[4,2,128,512]{3,2,1,0:T(8,128)(2,1)S(1)} %collective-permute-done.17.refs_3_, ...), custom_call_target="tpu_custom_call" | custom-call | flops 1024 | bytes 1024 | tf_op jit(solution)/shard_map/chip_send/pallas_call | solution.py:31
  63.0 0.6 collective-permute-start.19
  63.6 0.9 %chip_keep.1.refs_5_.refs_1_.refs_2_ = f32[2,2,128,512]{3,2,1,0:T(8,128)S(1)} custom-call(s32[4]{0:T(128)S(1)} %pad_add_fusion.refs_0_, bf16[16,128,256]{2,1,0:T(8,128)(2,1)S(1)} %get-tuple-element.98.refs_1_, bf16[512,256]{1,0:T(8,128)(2,1)S(1)} %get-tuple-element.64.refs_1_.refs_5_.refs_2_, bf16[4,2,128,512]{3,2,1,0:T(8,128)(2,1)S(1)} %collective-permute-done.17.refs_3_, ...), custom_call_target="tpu_custom_call" | custom-call | flops 1024 | bytes 1024 | tf_op jit(solution)/shard_map/chip_keep/pallas_call | solution.py:31
  64.4 2.5 %collective-permute-done.21.refs_3_ = bf16[144,256]{1,0:T(8,128)(2,1)S(1)} collective-permute-done((bf16[144,256]{1,0:T(8,128)(2,1)S(1)}, bf16[144,256]{1,0:T(8,128)(2,1)S(1)}, u32[]{:S(2)}, u32[]{:S(2)}) %collective-permute-start.21) | collective-permute-done | bytes 73760 | tf_op jit(solution)/shard_map/ppermute | solution.py:57
  66.9 0.6 sum.1.refs_5_.refs_7_
  67.5 0.6 collective-permute-start.23
  68.1 1.6 %collective-permute-start.30 = (bf16[144,256]{1,0:T(8,128)(2,1)S(1)}, bf16[144,256]{1,0:T(8,128)(2,1)S(1)}, u32[]{:S(2)}, u32[]{:S(2)}) collective-permute-start(bf16[144,256]{1,0:T(8,128)(2,1)S(1)} %sum.1.refs_5_.refs_7_), channel_id=1, source_target_pairs={{0,24},{1,25},{2,26},{3,27},{4,28},{5,29},{6,30},{7,31},{8,16},{9,... | collective-permute-start | bytes 221192 | tf_op jit(solution)/shard_map/ppermute | solution.py:57
  70.0 2.5 %collective-permute-start.29 = (bf16[144,256]{1,0:T(8,128)(2,1)S(1)}, bf16[144,256]{1,0:T(8,128)(2,1)S(1)}, u32[]{:S(2)}, u32[]{:S(2)}) collective-permute-start(bf16[144,256]{1,0:T(8,128)(2,1)S(1)} %sum.1.refs_5_.refs_7_), channel_id=1, source_target_pairs={{0,16},{1,17},{2,18},{3,19},{4,20},{5,21},{6,22},{7,23},{8,24},{9,... | collective-permute-start | bytes 221192 | tf_op jit(solution)/shard_map/ppermute | solution.py:57
  73.1 1.6 %collective-permute-start.27 = (bf16[4,64,512]{2,1,0:T(8,128)(2,1)S(1)}, bf16[4,64,512]{2,1,0:T(8,128)(2,1)S(1)}, u32[]{:S(2)}, u32[]{:S(2)}) collective-permute-start(bf16[4,64,512]{2,1,0:T(8,128)(2,1)S(1)} %column.1.refs_5_), channel_id=1, source_target_pairs={{0,4},{1,5},{2,6},{3,7},{4,0},{5,1},{6,2},{7,3},{8,12},{9,13},{10,... | collective-permute-start | bytes 786440 | tf_op jit(solution)/shard_map/ppermute | solution.py:57
  74.7 0.6 forward.1
  75.3 0.6 collective-permute-start.24
  76.4 0.6 collective-permute-start.31
  77.0 1.7 %collective-permute-start.32 = (bf16[144,256]{1,0:T(8,128)(2,1)S(1)}, bf16[144,256]{1,0:T(8,128)(2,1)S(1)}, u32[]{:S(2)}, u32[]{:S(2)}) collective-permute-start(bf16[144,256]{1,0:T(8,128)(2,1)S(1)} %side.1.refs_11_), channel_id=1, source_target_pairs={{0,16},{1,17},{2,18},{3,19},{4,20},{5,21},{6,22},{7,23},{8,24},{9,... | collective-permute-start | bytes 221192 | tf_op jit(solution)/shard_map/ppermute | solution.py:57
  78.7 2.2 %collective-permute-start.33 = (bf16[144,256]{1,0:T(8,128)(2,1)S(1)}, bf16[144,256]{1,0:T(8,128)(2,1)S(1)}, u32[]{:S(2)}, u32[]{:S(2)}) collective-permute-start(bf16[144,256]{1,0:T(8,128)(2,1)S(1)} %side.1.refs_11_), channel_id=1, source_target_pairs={{0,24},{1,25},{2,26},{3,27},{4,28},{5,29},{6,30},{7,31},{8,16},{9,... | collective-permute-start | bytes 221192 | tf_op jit(solution)/shard_map/ppermute | solution.py:57
  81.1 1.1 %collective-permute-done.32.refs_13_ = bf16[144,256]{1,0:T(8,128)(2,1)S(1)} collective-permute-done((bf16[144,256]{1,0:T(8,128)(2,1)S(1)}, bf16[144,256]{1,0:T(8,128)(2,1)S(1)}, u32[]{:S(2)}, u32[]{:S(2)}) %collective-permute-start.32) | collective-permute-done | bytes 73760 | tf_op jit(solution)/shard_map/ppermute | solution.py:57
  82.2 2.6 %collective-permute-done.33.refs_14_ = bf16[144,256]{1,0:T(8,128)(2,1)S(1)} collective-permute-done((bf16[144,256]{1,0:T(8,128)(2,1)S(1)}, bf16[144,256]{1,0:T(8,128)(2,1)S(1)}, u32[]{:S(2)}, u32[]{:S(2)}) %collective-permute-start.33) | collective-permute-done | bytes 73760 | tf_op jit(solution)/shard_map/ppermute | solution.py:57
  84.8 2.0 %last.1 = (bf16[2,128,512]{2,1,0:T(8,128)(2,1)}, f32[512,512]{1,0:T(8,128)}, f32[512,512]{1,0:T(8,128)}, f32[25,512]{1,0:T(8,128)}, f32[1,512]{1,0:T(1,128)}, /*index=5*/f32[1,512]{1,0:T(1,128)}) custom-call(s32[4]{0:T(128)S(1)} %pad_add_fusion.refs_0_, bf16[2,128,512]{2,1,0:T(8,128)(2,1)S(1)} %get-tuple-element.60.refs_3_.refs_4_.refs_1_, ...), custom_call_target="tpu_custom_call" | custom-call | tf_op jit(solution)/shard_map/last/pallas_call | solution.py:31
  (60 shorter events, 4.7 us)
Async XLA Ops:
  0.6 11.1 %collective-permute-start.4 = (bf16[2,128,512]{2,1,0:T(8,128)(2,1)}, bf16[2,128,512]{2,1,0:T(8,128)(2,1)S(1)}, u32[]{:S(2)}, u32[]{:S(2)}) collective-permute-start(bf16[2,128,512]{2,1,0:T(8,128)(2,1)} %refs_7_.1), channel_id=1, source_target_pairs={{0,1},{1,0},{2,3},{3,2},{4,5},{5,4},{6,7},{7,6},{8,9},{9,8},{10,11... | collective-permute-start | bytes 786440 | tf_op jit(solution)/shard_map/ppermute | solution.py:57
  1.1 10.7 %collective-permute-start.1 = (bf16[2,128,512]{2,1,0:T(8,128)(2,1)}, bf16[2,128,512]{2,1,0:T(8,128)(2,1)S(1)}, u32[]{:S(2)}, u32[]{:S(2)}) collective-permute-start(bf16[2,128,512]{2,1,0:T(8,128)(2,1)} %refs_6_.1), channel_id=1, source_target_pairs={{0,2},{1,3},{2,0},{3,1},{4,6},{5,7},{6,4},{7,5},{8,10},{9,11},{10,... | collective-permute-start | bytes 786440 | tf_op jit(solution)/shard_map/ppermute | solution.py:57
  3.7 9.4 %collective-permute-start.2 = (bf16[2,128,512]{2,1,0:T(8,128)(2,1)}, bf16[2,128,512]{2,1,0:T(8,128)(2,1)S(1)}, u32[]{:S(2)}, u32[]{:S(2)}) collective-permute-start(bf16[2,128,512]{2,1,0:T(8,128)(2,1)} %refs_6_.1), channel_id=1, source_target_pairs={{0,4},{1,5},{2,6},{3,7},{4,0},{5,1},{6,2},{7,3},{8,12},{9,13},{10,... | collective-permute-start | bytes 786440 | tf_op jit(solution)/shard_map/ppermute | solution.py:57
  5.2 9.4 %collective-permute-start.3 = (bf16[2,128,512]{2,1,0:T(8,128)(2,1)}, bf16[2,128,512]{2,1,0:T(8,128)(2,1)S(1)}, u32[]{:S(2)}, u32[]{:S(2)}) collective-permute-start(bf16[2,128,512]{2,1,0:T(8,128)(2,1)} %refs_6_.1), channel_id=1, source_target_pairs={{0,1},{1,0},{2,3},{3,2},{4,5},{5,4},{6,7},{7,6},{8,9},{9,8},{10,11... | collective-permute-start | bytes 786440 | tf_op jit(solution)/shard_map/ppermute | solution.py:57
  5.2 12.7 %collective-permute-start = (bf16[2,128,512]{2,1,0:T(8,128)(2,1)}, bf16[2,128,512]{2,1,0:T(8,128)(2,1)S(1)}, u32[]{:S(2)}, u32[]{:S(2)}) collective-permute-start(bf16[2,128,512]{2,1,0:T(8,128)(2,1)} %refs_6_.1), channel_id=1, source_target_pairs={{0,6},{1,7},{2,4},{3,5},{4,2},{5,3},{6,0},{7,1},{8,14},{9,15},{10,... | collective-permute-start | bytes 786440 | tf_op jit(solution)/shard_map/ppermute | solution.py:57
  5.4 1.0 %copy-start = (bf16[512,512]{1,0:T(8,128)(2,1)S(1)}, bf16[512,512]{1,0:T(8,128)(2,1)}, u32[]{:S(2)}) copy-start(bf16[512,512]{1,0:T(8,128)(2,1)} %refs_1_.1) | copy-start | bytes 1572868
  6.5 1.0 %copy-start.1 = (bf16[512,512]{1,0:T(8,128)(2,1)S(1)}, bf16[512,512]{1,0:T(8,128)(2,1)}, u32[]{:S(2)}) copy-start(bf16[512,512]{1,0:T(8,128)(2,1)} %refs_5_.1) | copy-start | bytes 1572868
  7.5 0.9 %copy-start.2 = (bf16[2,128,512]{2,1,0:T(8,128)(2,1)S(1)}, bf16[2,128,512]{2,1,0:T(8,128)(2,1)}, u32[]{:S(2)}) copy-start(bf16[2,128,512]{2,1,0:T(8,128)(2,1)} %refs_6_.1) | copy-start | bytes 786436
  8.5 0.8 copy-start.3
  9.3 0.7 copy-start.4
  10.0 0.7 copy-start.5
  13.1 12.4 %collective-permute-start.10 = (bf16[2,2,128,512]{3,2,1,0:T(8,128)(2,1)S(1)}, bf16[2,2,128,512]{3,2,1,0:T(8,128)(2,1)S(1)}, u32[]{:S(2)}, u32[]{:S(2)}) collective-permute-start(bf16[2,2,128,512]{3,2,1,0:T(8,128)(2,1)S(1)} %pad_maximum_fusion), channel_id=1, source_target_pairs={{0,4},{1,3},{2,6},{3,1},{4,0},{5,7},{6,2},{7,5},{8,12},{9,11},{10,... | collective-permute-start | bytes 1572872 | tf_op jit(solution)/shard_map/ppermute | solution.py:67
  16.0 4.4 %collective-permute-start.6 = (bf16[2,128,512]{2,1,0:T(8,128)(2,1)S(1)}, bf16[2,128,512]{2,1,0:T(8,128)(2,1)S(1)}, u32[]{:S(2)}, u32[]{:S(2)}) collective-permute-start(bf16[2,128,512]{2,1,0:T(8,128)(2,1)S(1)} %collective-permute-done.1.refs_3_.refs_6_), channel_id=1, source_target_pairs={{0,1},{1,0},{2,3},{3,2},{4,5},{5,4},{6,7},{7,6},{8,9},{9,8},{10,11... | collective-permute-start | bytes 786440 | tf_op jit(solution)/shard_map/ppermute | solution.py:57
  16.1 4.4 %collective-permute-start.7 = (bf16[2,128,512]{2,1,0:T(8,128)(2,1)S(1)}, bf16[2,128,512]{2,1,0:T(8,128)(2,1)S(1)}, u32[]{:S(2)}, u32[]{:S(2)}) collective-permute-start(bf16[2,128,512]{2,1,0:T(8,128)(2,1)S(1)} %collective-permute-done.2.refs_4_.refs_8_), channel_id=1, source_target_pairs={{0,1},{1,0},{2,3},{3,2},{4,5},{5,4},{6,7},{7,6},{8,9},{9,8},{10,11... | collective-permute-start | bytes 786440 | tf_op jit(solution)/shard_map/ppermute | solution.py:57
  18.0 4.2 %collective-permute-start.5 = (bf16[2,128,512]{2,1,0:T(8,128)(2,1)S(1)}, bf16[2,128,512]{2,1,0:T(8,128)(2,1)S(1)}, u32[]{:S(2)}, u32[]{:S(2)}) collective-permute-start(bf16[2,128,512]{2,1,0:T(8,128)(2,1)S(1)} %collective-permute-done.refs_3_.refs_10_), channel_id=1, source_target_pairs={{0,1},{1,0},{2,3},{3,2},{4,5},{5,4},{6,7},{7,6},{8,9},{9,8},{10,11... | collective-permute-start | bytes 786440 | tf_op jit(solution)/shard_map/ppermute | solution.py:57
  18.1 14.1 %collective-permute-start.11 = (bf16[2,128,512]{2,1,0:T(8,128)(2,1)}, bf16[2,128,512]{2,1,0:T(8,128)(2,1)S(1)}, u32[]{:S(2)}, u32[]{:S(2)}) collective-permute-start(bf16[2,128,512]{2,1,0:T(8,128)(2,1)} %refs_7_.1), channel_id=1, source_target_pairs={{0,6},{1,7},{2,4},{3,5},{4,2},{5,3},{6,0},{7,1},{8,14},{9,15},{10,... | collective-permute-start | bytes 786440 | tf_op jit(solution)/shard_map/ppermute | solution.py:57
  23.2 7.0 %collective-permute-start.8 = (bf16[2,128,256]{2,1,0:T(8,128)(2,1)S(1)}, bf16[2,128,256]{2,1,0:T(8,128)(2,1)S(1)}, u32[]{:S(2)}, u32[]{:S(2)}) collective-permute-start(bf16[2,128,256]{2,1,0:T(8,128)(2,1)S(1)} %get-tuple-element.77), channel_id=1, source_target_pairs={{0,8},{1,9},{2,10},{3,11},{4,12},{5,13},{6,14},{7,15},{8,0},{9,1},... | collective-permute-start | bytes 393224 | tf_op jit(solution)/shard_map/ppermute | solution.py:77
  24.8 5.4 %collective-permute-start.9 = (bf16[2,128,256]{2,1,0:T(8,128)(2,1)S(1)}, bf16[2,128,256]{2,1,0:T(8,128)(2,1)S(1)}, u32[]{:S(2)}, u32[]{:S(2)}) collective-permute-start(bf16[2,128,256]{2,1,0:T(8,128)(2,1)S(1)} %get-tuple-element.78), channel_id=1, source_target_pairs={{8,16},{9,17},{10,18},{11,19},{12,20},{13,21},{14,22},{15,23},{16,... | collective-permute-start | bytes 393224 | tf_op jit(solution)/shard_map/ppermute | solution.py:77
  25.5 8.5 %collective-permute-start.12 = (bf16[2,2,128,512]{3,2,1,0:T(8,128)(2,1)S(1)}, bf16[2,2,128,512]{3,2,1,0:T(8,128)(2,1)S(1)}, u32[]{:S(2)}, u32[]{:S(2)}) collective-permute-start(bf16[2,2,128,512]{3,2,1,0:T(8,128)(2,1)S(1)} %collective-permute-done.10.refs_5_.refs_6_), channel_id=1, source_target_pairs={{0,1},{1,0},{2,3},{3,2},{4,5},{5,4},{6,7},{7,6},{8,9},{9,8},{10,11... | collective-permute-start | bytes 1572872 | tf_op jit(solution)/shard_map/ppermute | solution.py:57
  32.3 1.7 %collective-permute-start.13 = (bf16[2,128,512]{2,1,0:T(8,128)(2,1)S(1)}, bf16[2,128,512]{2,1,0:T(8,128)(2,1)S(1)}, u32[]{:S(2)}, u32[]{:S(2)}) collective-permute-start(bf16[2,128,512]{2,1,0:T(8,128)(2,1)S(1)} %collective-permute-done.11.refs_6_.refs_7_), channel_id=1, source_target_pairs={{0,1},{1,0},{2,3},{3,2},{4,5},{5,4},{6,7},{7,6},{8,9},{9,8},{10,11... | collective-permute-start | bytes 786440 | tf_op jit(solution)/shard_map/ppermute | solution.py:57
  35.6 11.2 %collective-permute-start.16 = (bf16[2,64,512]{2,1,0:T(8,128)(2,1)S(1)}, bf16[2,64,512]{2,1,0:T(8,128)(2,1)S(1)}, u32[]{:S(2)}, u32[]{:S(2)}) collective-permute-start(bf16[2,64,512]{2,1,0:T(8,128)(2,1)S(1)} %pad_maximum_fusion.1), channel_id=1, source_target_pairs={{0,16},{1,17},{2,18},{3,19},{4,20},{5,21},{6,22},{7,23},{8,24},{9,... | collective-permute-start | bytes 393224 | tf_op jit(solution)/shard_map/ppermute | solution.py:57
  39.9 7.5 %collective-permute-start.14 = (bf16[2,128,256]{2,1,0:T(8,128)(2,1)S(1)}, bf16[2,128,256]{2,1,0:T(8,128)(2,1)S(1)}, u32[]{:S(2)}, u32[]{:S(2)}) collective-permute-start(bf16[2,128,256]{2,1,0:T(8,128)(2,1)S(1)} %get-tuple-element.90), channel_id=1, source_target_pairs={{8,16},{9,17},{10,18},{11,19},{12,20},{13,21},{14,22},{15,23},{16,... | collective-permute-start | bytes 393224 | tf_op jit(solution)/shard_map/ppermute | solution.py:77
  40.6 6.9 %collective-permute-start.15 = (bf16[2,128,256]{2,1,0:T(8,128)(2,1)S(1)}, bf16[2,128,256]{2,1,0:T(8,128)(2,1)S(1)}, u32[]{:S(2)}, u32[]{:S(2)}) collective-permute-start(bf16[2,128,256]{2,1,0:T(8,128)(2,1)S(1)} %get-tuple-element.91), channel_id=1, source_target_pairs={{0,8},{1,9},{2,10},{3,11},{4,12},{5,13},{6,14},{7,15},{8,0},{9,1},... | collective-permute-start | bytes 393224 | tf_op jit(solution)/shard_map/ppermute | solution.py:77
  46.9 5.6 %collective-permute-start.18 = (bf16[64,512]{1,0:T(8,128)(2,1)S(1)}, bf16[64,512]{1,0:T(8,128)(2,1)S(1)}, u32[]{:S(2)}, u32[]{:S(2)}) collective-permute-start(bf16[64,512]{1,0:T(8,128)(2,1)S(1)} %convert_element_type.17), channel_id=1, source_target_pairs={{0,8},{1,9},{2,10},{3,11},{4,12},{5,13},{6,14},{7,15},{8,0},{9,1},... | collective-permute-start | bytes 196616 | tf_op jit(solution)/shard_map/ppermute | solution.py:57
  52.4 9.7 %collective-permute-start.17 = (bf16[4,2,128,512]{3,2,1,0:T(8,128)(2,1)S(1)}, bf16[4,2,128,512]{3,2,1,0:T(8,128)(2,1)S(1)}, u32[]{:S(2)}, u32[]{:S(2)}) collective-permute-start(bf16[4,2,128,512]{3,2,1,0:T(8,128)(2,1)S(1)} %get-tuple-element.99), channel_id=1, source_target_pairs={{0,1},{1,0},{2,3},{3,2},{4,5},{5,4},{6,7},{7,6},{8,9},{9,8},{10,11... | collective-permute-start | bytes 3145736 | tf_op jit(solution)/shard_map/ppermute | solution.py:57
  52.5 9.6 %collective-permute-start.25 = (bf16[64,512]{1,0:T(8,128)(2,1)S(1)}, bf16[64,512]{1,0:T(8,128)(2,1)S(1)}, u32[]{:S(2)}, u32[]{:S(2)}) collective-permute-start(bf16[64,512]{1,0:T(8,128)(2,1)S(1)} %add_convert_fusion.refs_12_.refs_1_), channel_id=1, source_target_pairs={{0,16},{1,17},{2,18},{3,19},{4,20},{5,21},{6,22},{7,23},{8,24},{9,... | collective-permute-start | bytes 196616 | tf_op jit(solution)/shard_map/ppermute | solution.py:57
  57.6 6.8 %collective-permute-start.20 = (bf16[144,256]{1,0:T(8,128)(2,1)S(1)}, bf16[144,256]{1,0:T(8,128)(2,1)S(1)}, u32[]{:S(2)}, u32[]{:S(2)}) collective-permute-start(bf16[144,256]{1,0:T(8,128)(2,1)S(1)} %get-tuple-element.104), channel_id=1, source_target_pairs={{0,8},{1,9},{2,10},{3,11},{4,12},{5,13},{6,14},{7,15},{8,0},{9,1},... | collective-permute-start | bytes 221192 | tf_op jit(solution)/shard_map/ppermute | solution.py:57
  57.7 9.2 %collective-permute-start.21 = (bf16[144,256]{1,0:T(8,128)(2,1)S(1)}, bf16[144,256]{1,0:T(8,128)(2,1)S(1)}, u32[]{:S(2)}, u32[]{:S(2)}) collective-permute-start(bf16[144,256]{1,0:T(8,128)(2,1)S(1)} %get-tuple-element.105), channel_id=1, source_target_pairs={{0,16},{1,17},{2,18},{3,19},{4,20},{5,21},{6,22},{7,23},{8,24},{9,... | collective-permute-start | bytes 221192 | tf_op jit(solution)/shard_map/ppermute | solution.py:57
  59.4 7.6 %collective-permute-start.22 = (bf16[144,256]{1,0:T(8,128)(2,1)S(1)}, bf16[144,256]{1,0:T(8,128)(2,1)S(1)}, u32[]{:S(2)}, u32[]{:S(2)}) collective-permute-start(bf16[144,256]{1,0:T(8,128)(2,1)S(1)} %get-tuple-element.106), channel_id=1, source_target_pairs={{0,24},{1,25},{2,26},{3,27},{4,28},{5,29},{6,30},{7,31},{8,16},{9,... | collective-permute-start | bytes 221192 | tf_op jit(solution)/shard_map/ppermute | solution.py:57
  63.0 11.7 %collective-permute-start.19 = (bf16[2,2,128,512]{3,2,1,0:T(8,128)(2,1)S(1)}, bf16[2,2,128,512]{3,2,1,0:T(8,128)(2,1)S(1)}, u32[]{:S(2)}, u32[]{:S(2)}) collective-permute-start(bf16[2,2,128,512]{3,2,1,0:T(8,128)(2,1)S(1)} %chip_send.1.refs_4_), channel_id=1, source_target_pairs={{0,2},{1,5},{2,0},{3,7},{4,6},{5,1},{6,4},{7,3},{8,10},{9,13},{10,... | collective-permute-start | bytes 1572872 | tf_op jit(solution)/shard_map/ppermute | solution.py:67
  63.6 6.5 %collective-permute-start.26 = (bf16[2,64,512]{2,1,0:T(8,128)(2,1)S(1)}, bf16[2,64,512]{2,1,0:T(8,128)(2,1)S(1)}, u32[]{:S(2)}, u32[]{:S(2)}) collective-permute-start(bf16[2,64,512]{2,1,0:T(8,128)(2,1)S(1)} %pad_maximum_fusion.2), channel_id=1, source_target_pairs={{0,8},{1,9},{2,10},{3,11},{4,12},{5,13},{6,14},{7,15},{8,0},{9,1},... | collective-permute-start | bytes 393224 | tf_op jit(solution)/shard_map/ppermute | solution.py:57
  67.5 5.6 %collective-permute-start.23 = (bf16[144,256]{1,0:T(8,128)(2,1)S(1)}, bf16[144,256]{1,0:T(8,128)(2,1)S(1)}, u32[]{:S(2)}, u32[]{:S(2)}) collective-permute-start(bf16[144,256]{1,0:T(8,128)(2,1)S(1)} %sum.1.refs_5_.refs_7_), channel_id=1, source_target_pairs={{0,4},{1,5},{2,6},{3,7},{4,0},{5,1},{6,2},{7,3},{8,12},{9,13},{10,... | collective-permute-start | bytes 221192 | tf_op jit(solution)/shard_map/ppermute | solution.py:57
  68.1 7.7 %collective-permute-start.30 = (bf16[144,256]{1,0:T(8,128)(2,1)S(1)}, bf16[144,256]{1,0:T(8,128)(2,1)S(1)}, u32[]{:S(2)}, u32[]{:S(2)}) collective-permute-start(bf16[144,256]{1,0:T(8,128)(2,1)S(1)} %sum.1.refs_5_.refs_7_), channel_id=1, source_target_pairs={{0,24},{1,25},{2,26},{3,27},{4,28},{5,29},{6,30},{7,31},{8,16},{9,... | collective-permute-start | bytes 221192 | tf_op jit(solution)/shard_map/ppermute | solution.py:57
  69.7 7.3 %collective-permute-start.28 = (bf16[144,256]{1,0:T(8,128)(2,1)S(1)}, bf16[144,256]{1,0:T(8,128)(2,1)S(1)}, u32[]{:S(2)}, u32[]{:S(2)}) collective-permute-start(bf16[144,256]{1,0:T(8,128)(2,1)S(1)} %sum.1.refs_5_.refs_7_), channel_id=1, source_target_pairs={{0,8},{1,9},{2,10},{3,11},{4,12},{5,13},{6,14},{7,15},{8,0},{9,1},... | collective-permute-start | bytes 221192 | tf_op jit(solution)/shard_map/ppermute | solution.py:57
  70.0 8.6 %collective-permute-start.29 = (bf16[144,256]{1,0:T(8,128)(2,1)S(1)}, bf16[144,256]{1,0:T(8,128)(2,1)S(1)}, u32[]{:S(2)}, u32[]{:S(2)}) collective-permute-start(bf16[144,256]{1,0:T(8,128)(2,1)S(1)} %sum.1.refs_5_.refs_7_), channel_id=1, source_target_pairs={{0,16},{1,17},{2,18},{3,19},{4,20},{5,21},{6,22},{7,23},{8,24},{9,... | collective-permute-start | bytes 221192 | tf_op jit(solution)/shard_map/ppermute | solution.py:57
  73.1 11.7 %collective-permute-start.27 = (bf16[4,64,512]{2,1,0:T(8,128)(2,1)S(1)}, bf16[4,64,512]{2,1,0:T(8,128)(2,1)S(1)}, u32[]{:S(2)}, u32[]{:S(2)}) collective-permute-start(bf16[4,64,512]{2,1,0:T(8,128)(2,1)S(1)} %column.1.refs_5_), channel_id=1, source_target_pairs={{0,4},{1,5},{2,6},{3,7},{4,0},{5,1},{6,2},{7,3},{8,12},{9,13},{10,... | collective-permute-start | bytes 786440 | tf_op jit(solution)/shard_map/ppermute | solution.py:57
  75.3 9.6 %collective-permute-start.24 = (bf16[2,128,512]{2,1,0:T(8,128)(2,1)S(1)}, bf16[2,128,512]{2,1,0:T(8,128)(2,1)S(1)}, u32[]{:S(2)}, u32[]{:S(2)}) collective-permute-start(bf16[2,128,512]{2,1,0:T(8,128)(2,1)S(1)} %forward.1), channel_id=1, source_target_pairs={{0,4},{1,3},{2,6},{3,1},{4,0},{5,7},{6,2},{7,5},{8,12},{9,11},{10,... | collective-permute-start | bytes 786440 | tf_op jit(solution)/shard_map/ppermute | solution.py:67
  76.4 4.7 %collective-permute-start.31 = (bf16[144,256]{1,0:T(8,128)(2,1)S(1)}, bf16[144,256]{1,0:T(8,128)(2,1)S(1)}, u32[]{:S(2)}, u32[]{:S(2)}) collective-permute-start(bf16[144,256]{1,0:T(8,128)(2,1)S(1)} %side.1.refs_11_), channel_id=1, source_target_pairs={{0,8},{1,9},{2,10},{3,11},{4,12},{5,13},{6,14},{7,15},{8,0},{9,1},... | collective-permute-start | bytes 221192 | tf_op jit(solution)/shard_map/ppermute | solution.py:57
  77.0 5.3 %collective-permute-start.32 = (bf16[144,256]{1,0:T(8,128)(2,1)S(1)}, bf16[144,256]{1,0:T(8,128)(2,1)S(1)}, u32[]{:S(2)}, u32[]{:S(2)}) collective-permute-start(bf16[144,256]{1,0:T(8,128)(2,1)S(1)} %side.1.refs_11_), channel_id=1, source_target_pairs={{0,16},{1,17},{2,18},{3,19},{4,20},{5,21},{6,22},{7,23},{8,24},{9,... | collective-permute-start | bytes 221192 | tf_op jit(solution)/shard_map/ppermute | solution.py:57
  78.7 6.2 %collective-permute-start.33 = (bf16[144,256]{1,0:T(8,128)(2,1)S(1)}, bf16[144,256]{1,0:T(8,128)(2,1)S(1)}, u32[]{:S(2)}, u32[]{:S(2)}) collective-permute-start(bf16[144,256]{1,0:T(8,128)(2,1)S(1)} %side.1.refs_11_), channel_id=1, source_target_pairs={{0,24},{1,25},{2,26},{3,27},{4,28},{5,29},{6,30},{7,31},{8,16},{9,... | collective-permute-start | bytes 221192 | tf_op jit(solution)/shard_map/ppermute | solution.py:57
